TPU v7x, 32 devices: a whole 2x2x4 slice. The times are simulated.
32 devices in a mesh: group: 2 (over x), tm: 8 (over z, y), space: 2 (over core).
Axes of the slice: x: 2, y: 2, z: 4, core: 2. Of those that a mesh axis runs over, the one named last changes fastest.
Arguments:
- iterate: float32 [1024, 128, 512], P(('group', 'space'), 'tm'), parts along dimension 0, may hold values from -3 to 3
- initial: float32 [1024, 512], P(('group', 'space')), parts along dimension 0, may hold values from -4 to 4
Outputs:
- new_iterate: float32 [1024, 128, 512], P(('group', 'space'), 'tm'), parts along dimension 0
There are 2 independent parts, one for each index of `group`. A program takes and returns all parts, laid end to end along the dimension named above; each array names one. Nothing has to cross between parts.
All inputs are finite; a program needn't handle non-finite values.
Results may differ from a plain program's by a relative error of at most 0.0003.
Values sent between devices are 32-bit elements; how exact they have to be, the bound alone decides.
No kernel may reach another device: no remote copies, remote signals or barrier semaphores. Data moves between devices by JAX's collectives and lax.ppermute only.
A program may use at most 192 MiB of HBM per device.

v0:
```python
import functools
import math

import jax
import jax.numpy as jnp
import numpy as np
from jax import lax
from jax.experimental import pallas as pl
from jax.experimental.pallas import tpu as pltpu
from jax.sharding import PartitionSpec as P

circulant_alpha = 0.01
DIFFUSION = 2.0
REACTION_STEP = 0.5
VMEM_BYTES = 56 * 1024 * 1024
LANES = 128
SUBLANES = 8


def sine_table(row_index, column_index, length):
    product = np.outer(row_index + 1, column_index + 1) % (2 * (length + 1))
    return math.sqrt(2.0 / (length + 1)) * np.sin(product * (math.pi / (length + 1)))


def stencil_eigen(mode_index, length):
    return 4.0 * np.sin((mode_index + 1) * (math.pi / (2.0 * (length + 1)))) ** 2


def constant(table):
    return jnp.asarray(np.asarray(table, np.float32))


def second_tables(width):
    half = width // 2
    return np.stack([sine_table(np.arange(half), np.arange(s, width, 2), width) for s in (0, 1)])


def first_tables(total):
    rows = total // 2
    return np.stack(
        [
            np.stack(
                [sine_table(np.arange(c, total, 2), s * rows + np.arange(rows), total) for c in (0, 1)]
            )
            for s in (0, 1)
        ]
    )


def decay_tables(total, width):
    first, second = stencil_eigen(np.arange(total), total), stencil_eigen(np.arange(width), width)
    decay = 1.0 / (1.0 + DIFFUSION * (first[:, None] + second[None, :]))
    return np.stack(
        [np.stack([decay[c::2, s::2] for c in (0, 1)]) for s in (0, 1)]
    )


def dot(first, second):
    return lax.dot_general(
        first,
        second,
        (((1,), (0,)), ((), ())),
        precision=lax.Precision.HIGH,
        preferred_element_type=jnp.float32,
    )


def lanes_reversed(block):
    index = LANES - 1 - lax.broadcasted_iota(jnp.int32, (block.shape[0], LANES), 1)
    parts = [
        jnp.take_along_axis(block[:, at : at + LANES], index, axis=1, mode="promise_in_bounds")
        for at in range(0, block.shape[1], LANES)
    ]
    return jnp.concatenate(parts[::-1], axis=1)


def store_rows_reversed(ref, at, block):
    rows, width = block.shape
    index = SUBLANES - 1 - lax.broadcasted_iota(jnp.int32, (SUBLANES, width), 0)
    for row in range(0, rows, SUBLANES):
        ref[at, pl.ds(rows - SUBLANES - row, SUBLANES), :] = jnp.take_along_axis(
            block[row : row + SUBLANES], index, axis=0, mode="promise_in_bounds"
        )


def forward_second_kernel(place, field, initial, own_table, other_table, keep, send):
    rows, steps, width = field.shape
    half = width // 2
    cells = field[...]
    force = jnp.swapaxes(REACTION_STEP * (cells - cells * cells * cells), 0, 1)
    is_first = (place[0] == 0).astype(jnp.float32)
    head = force[0] + is_first * initial[...]
    stacked = jnp.concatenate(
        [head, force[1:].reshape((steps - 1) * rows, width), field[:, steps - 1, :]], axis=0
    )
    sign = 1.0 - 2.0 * place[1].astype(jnp.float32)
    lower = stacked[:, :half]
    upper = sign * lanes_reversed(stacked[:, half:])
    keep[...] = dot(lower + upper, own_table[0]).reshape(keep.shape)
    other = dot(lower - upper, other_table[0])
    for step in range(steps + 1):
        store_rows_reversed(send, step, other[step * rows : (step + 1) * rows])


def forward_second(place, field, initial, tables):
    rows, steps, width = field.shape
    half = width // 2
    block = min(32, rows)
    count = rows // block
    out = jax.ShapeDtypeStruct((steps + 1, rows, half), jnp.float32)
    table = (1, half, half)
    return pl.pallas_call(
        forward_second_kernel,
        grid_spec=pltpu.PrefetchScalarGridSpec(
            num_scalar_prefetch=1,
            grid=(count,),
            in_specs=[
                pl.BlockSpec((block, steps, width), lambda i, place: (i, 0, 0)),
                pl.BlockSpec((block, width), lambda i, place: (i, 0)),
                pl.BlockSpec(table, lambda i, place: (place[1], 0, 0)),
                pl.BlockSpec(table, lambda i, place: (1 - place[1], 0, 0)),
            ],
            out_specs=[
                pl.BlockSpec((steps + 1, block, half), lambda i, place: (0, i, 0)),
                pl.BlockSpec((steps + 1, block, half), lambda i, place: (0, count - 1 - i, 0)),
            ],
        ),
        out_shape=[out, out],
        compiler_params=pltpu.CompilerParams(vmem_limit_bytes=VMEM_BYTES),
        name="forward_second",
    )(place, field, initial, tables, tables)


def forward_first_kernel(steps, slabs, place, keep, got, table, decay, modes, last, state):
    step = pl.program_id(0)
    near, far = keep[0], got[0]

    @pl.when(step == 0)
    def _():
        state[...] = jnp.zeros_like(state)

    parts = [dot(table[0, 0], near + far), dot(table[0, 1], near - far)]

    @pl.when(step < steps)
    def _():
        for c in (0, 1):
            modes[0, c] = parts[c]
            state[c] = decay[0, c] * (state[c] + parts[c])

    @pl.when(step == steps)
    def _():
        is_last = (place[0] == slabs - 1).astype(jnp.float32)
        for c in (0, 1):
            last[c] = state[c] - is_last * parts[c]


def forward_first(place, keep, got, tables, decays, slabs):
    steps, rows, half = keep.shape
    steps = steps - 1
    return pl.pallas_call(
        functools.partial(forward_first_kernel, steps, slabs),
        grid_spec=pltpu.PrefetchScalarGridSpec(
            num_scalar_prefetch=1,
            grid=(steps + 1,),
            in_specs=[
                pl.BlockSpec((1, rows, half), lambda i, place: (i, 0, 0)),
                pl.BlockSpec((1, rows, half), lambda i, place: (i, 0, 0)),
                pl.BlockSpec((1, 2, rows, rows), lambda i, place: (place[1], 0, 0, 0)),
                pl.BlockSpec((1, 2, rows, half), lambda i, place: (place[1], 0, 0, 0)),
            ],
            out_specs=[
                pl.BlockSpec((1, 2, rows, half), lambda i, place: (jnp.minimum(i, steps - 1), 0, 0, 0)),
                pl.BlockSpec((2, rows, half), lambda i, place: (0, 0, 0)),
            ],
            scratch_shapes=[pltpu.VMEM((2, rows, half), jnp.float32)],
        ),
        out_shape=[
            jax.ShapeDtypeStruct((steps, 2, rows, half), jnp.float32),
            jax.ShapeDtypeStruct((2, rows, half), jnp.float32),
        ],
        compiler_params=pltpu.CompilerParams(vmem_limit_bytes=VMEM_BYTES),
        name="forward_first",
    )(place, keep, got, tables, decays)


def close_kernel(place, lasts, decay, gain, befores):
    slabs = lasts.shape[0]
    state = lasts[0]
    for slab in range(1, slabs):
        state = lasts[slab] + decay[0] * state
    state = gain[0] * state
    for slab in range(slabs):
        befores[slab] = state
        if slab < slabs - 1:
            state = lasts[slab] + decay[0] * state


def close(place, lasts, slab_decays, gains):
    slabs, rows, half = lasts.shape
    table = pl.BlockSpec((1, rows, half), lambda i, place: (place[1], place[0], 0))
    whole = pl.BlockSpec((slabs, rows, half), lambda i, place: (0, 0, 0))
    return pl.pallas_call(
        close_kernel,
        grid_spec=pltpu.PrefetchScalarGridSpec(
            num_scalar_prefetch=1, grid=(1,), in_specs=[whole, table, table], out_specs=whole
        ),
        out_shape=jax.ShapeDtypeStruct(lasts.shape, jnp.float32),
        compiler_params=pltpu.CompilerParams(vmem_limit_bytes=VMEM_BYTES),
        name="close",
    )(place, lasts, slab_decays, gains)


def inverse_first_kernel(place, modes, before, table, decay, keep, send, state):
    @pl.when(pl.program_id(0) == 0)
    def _():
        state[...] = before[...]

    parts = []
    for c in (0, 1):
        solved = decay[0, c] * (state[c] + modes[0, c])
        state[c] = solved
        parts.append(dot(table[0, c], solved))
    keep[0] = parts[0] + parts[1]
    store_rows_reversed(send, 0, parts[0] - parts[1])


def inverse_first(place, modes, before, tables, decays):
    steps, _, rows, half = modes.shape
    out = jax.ShapeDtypeStruct((steps, rows, half), jnp.float32)
    return pl.pallas_call(
        inverse_first_kernel,
        grid_spec=pltpu.PrefetchScalarGridSpec(
            num_scalar_prefetch=1,
            grid=(steps,),
            in_specs=[
                pl.BlockSpec((1, 2, rows, half), lambda i, place: (i, 0, 0, 0)),
                pl.BlockSpec((2, rows, half), lambda i, place: (0, 0, 0)),
                pl.BlockSpec((1, 2, rows, rows), lambda i, place: (place[1], 0, 0, 0)),
                pl.BlockSpec((1, 2, rows, half), lambda i, place: (place[1], 0, 0, 0)),
            ],
            out_specs=[
                pl.BlockSpec((1, rows, half), lambda i, place: (i, 0, 0)),
                pl.BlockSpec((1, rows, half), lambda i, place: (i, 0, 0)),
            ],
            scratch_shapes=[pltpu.VMEM((2, rows, half), jnp.float32)],
        ),
        out_shape=[out, out],
        compiler_params=pltpu.CompilerParams(vmem_limit_bytes=VMEM_BYTES),
        name="inverse_first",
    )(place, modes, before, tables, decays)


def inverse_second_kernel(place, keep, got, own_table, other_table, out):
    steps, rows, half = keep.shape
    own = dot(keep[...].reshape(steps * rows, half), own_table[0])
    other = dot(got[...].reshape(steps * rows, half), other_table[0])
    sign = 1.0 - 2.0 * place[1].astype(jnp.float32)
    lower = own + other
    upper = lanes_reversed(sign * (own - other))
    for part, at in ((lower, 0), (upper, half)):
        out[:, :, at : at + half] = jnp.swapaxes(part.reshape(steps, rows, half), 0, 1)


def inverse_second(place, keep, got, tables):
    steps, rows, half = keep.shape
    block = min(32, rows)
    table = (1, half, half)
    slab = pl.BlockSpec((steps, block, half), lambda i, place: (0, i, 0))
    return pl.pallas_call(
        inverse_second_kernel,
        grid_spec=pltpu.PrefetchScalarGridSpec(
            num_scalar_prefetch=1,
            grid=(rows // block,),
            in_specs=[
                slab,
                slab,
                pl.BlockSpec(table, lambda i, place: (place[1], 0, 0)),
                pl.BlockSpec(table, lambda i, place: (1 - place[1], 0, 0)),
            ],
            out_specs=pl.BlockSpec((block, steps, 2 * half), lambda i, place: (i, 0, 0)),
        ),
        out_shape=jax.ShapeDtypeStruct((rows, steps, 2 * half), jnp.float32),
        compiler_params=pltpu.CompilerParams(vmem_limit_bytes=VMEM_BYTES),
        name="inverse_second",
    )(place, keep, got, tables, tables)


def swapped(block):
    return lax.ppermute(block, "space", [(0, 1), (1, 0)])


def shards(iterate, initial):
    rows, steps, width = iterate.shape
    slabs = lax.axis_size("tm")
    total = rows * lax.axis_size("space")
    half = width // 2
    place = jnp.stack([lax.axis_index("tm"), lax.axis_index("space")]).astype(jnp.int32)
    second = second_tables(width)
    first = first_tables(total)
    decay = decay_tables(total, width)
    slab_decay = decay**steps
    gain = circulant_alpha / (1.0 - circulant_alpha * slab_decay**slabs)
    flat = (2, total, half)
    keep, send = forward_second(place, iterate, initial, constant(second))
    modes, last = forward_first(place, keep, swapped(send), constant(first), constant(decay), slabs)
    lasts = lax.all_to_all(last.reshape(slabs, total // slabs, half), "tm", 0, 0, tiled=True)
    befores = close(place, lasts, constant(slab_decay.reshape(flat)), constant(gain.reshape(flat)))
    before = lax.all_to_all(befores, "tm", 0, 0, tiled=True).reshape(last.shape)
    keep, send = inverse_first(
        place, modes, before, constant(np.swapaxes(first, 2, 3)), constant(decay)
    )
    return inverse_second(place, keep, swapped(send), constant(np.swapaxes(second, 1, 2)))


def solution(mesh):
    return jax.shard_map(
        shards,
        mesh=mesh,
        in_specs=(P(("group", "space"), "tm", None), P(("group", "space"), None)),
        out_specs=P(("group", "space"), "tm", None),
        check_vma=False,
    )
```

profile of v0, /device:TPU:0, one launch (start us, length us, event | category | flops | bytes accessed | tf_op | source)
XLA Modules:
  0.0 121.2 jit_solution(16008663525697663193)
XLA Ops:
  0.0 0.7 pad_add_fusion.place
  0.7 13.2 %forward_second.1 = (f32[17,256,256]{2,1,0:T(8,128)}, f32[17,256,256]{2,1,0:T(8,128)}) custom-call(s32[2]{0:T(128)} %pad_add_fusion.place, f32[256,16,512]{2,1,0:T(8,128)} %field.1, f32[256,512]{1,0:T(8,128)} %initial.1, f32[2,256,256]{2,1,0:T(8,128)} %constant.22.clone.own_table.other_table, f32[2,256,256]{2,1,0:T(8,128)} %constant.22.clone.own_table.other_table), custom_call_target="tpu_custom_call" | custom-call | tf_op jit(solution)/shard_map/forward_second/pallas_call | solution.py:112
  13.8 0.5 collective-permute-start
  14.3 7.4 %collective-permute-done.got = f32[17,256,256]{2,1,0:T(8,128)S(1)} collective-permute-done((f32[17,256,256]{2,1,0:T(8,128)}, f32[17,256,256]{2,1,0:T(8,128)S(1)}, u32[]{:S(2)}, u32[]{:S(2)}) %collective-permute-start) | collective-permute-done | bytes 4456480 | tf_op jit(solution)/shard_map/ppermute | solution.py:289
  21.6 0.0 copy-start
  21.6 2.1 %copy-done = f32[17,256,256]{2,1,0:T(8,128)} copy-done((f32[17,256,256]{2,1,0:T(8,128)}, f32[17,256,256]{2,1,0:T(8,128)S(1)}, u32[]{:S(2)}) %copy-start) | copy-done | bytes 4456472
  23.7 17.7 %forward_first.1 = (f32[16,2,256,256]{3,2,1,0:T(8,128)}, f32[2,256,256]{2,1,0:T(8,128)}) custom-call(s32[2]{0:T(128)} %pad_add_fusion.place, f32[17,256,256]{2,1,0:T(8,128)} %get-tuple-element.11.keep, f32[17,256,256]{2,1,0:T(8,128)} %copy-done, f32[2,2,256,256]{3,2,1,0:T(8,128)} %constant.23.clone.table, f32[2,2,256,256]{3,2,1,0:T(8,128)} %constant.24.clone.decay), custom_call_target="tpu_custom_call" | custom-call | tf_op jit(solution)/shard_map/forward_first/pallas_call | solution.py:160
  41.5 22.1 %all_to_all.10.lasts = f32[8,64,256]{2,1,0:T(8,128)} all-to-all(f32[8,64,256]{2,1,0:T(8,128)} %bitcast.5), channel_id=1, replica_groups=mesh['group'=2,'tm'=8,'space'=2] {'tm'}, dimensions={0} | all-to-all | bytes 1048576 | tf_op jit(solution)/shard_map/all_to_all | solution.py:306
  63.6 2.6 %close.1 = f32[8,64,256]{2,1,0:T(8,128)} custom-call(s32[2]{0:T(128)} %pad_add_fusion.place, f32[8,64,256]{2,1,0:T(8,128)} %all_to_all.10.lasts, f32[2,512,256]{2,1,0:T(8,128)} %constant.25.clone.decay, f32[2,512,256]{2,1,0:T(8,128)} %constant.26.clone.gain), custom_call_target="tpu_custom_call" | custom-call | tf_op jit(solution)/shard_map/close/pallas_call | solution.py:202
  66.1 17.9 %all_to_all.11 = f32[8,64,256]{2,1,0:T(8,128)} all-to-all(f32[8,64,256]{2,1,0:T(8,128)} %close.1), channel_id=1, replica_groups=mesh['group'=2,'tm'=8,'space'=2] {'tm'}, dimensions={0} | all-to-all | bytes 1048576 | tf_op jit(solution)/shard_map/all_to_all | solution.py:308
  84.0 16.0 %inverse_first.1 = (f32[16,256,256]{2,1,0:T(8,128)}, f32[16,256,256]{2,1,0:T(8,128)}) custom-call(s32[2]{0:T(128)} %pad_add_fusion.place, f32[16,2,256,256]{3,2,1,0:T(8,128)} %get-tuple-element.13.modes, f32[2,256,256]{2,1,0:T(8,128)} %bitcast.4, f32[2,2,256,256]{3,2,1,0:T(8,128)} %constant.27.clone.table, f32[2,2,256,256]{3,2,1,0:T(8,128)} %constant.24.clone.decay), custom_call_target="tpu_custom_call" | custom-call | tf_op jit(solution)/shard_map/inverse_first/pallas_call | solution.py:230
  100.1 0.0 collective-permute-start.1
  100.1 7.4 %collective-permute-done.1.got = f32[16,256,256]{2,1,0:T(8,128)S(1)} collective-permute-done((f32[16,256,256]{2,1,0:T(8,128)}, f32[16,256,256]{2,1,0:T(8,128)S(1)}, u32[]{:S(2)}, u32[]{:S(2)}) %collective-permute-start.1) | collective-permute-done | bytes 4194336 | tf_op jit(solution)/shard_map/ppermute | solution.py:289
  107.4 0.0 copy-start.1
  107.4 2.0 %copy-done.1 = f32[16,256,256]{2,1,0:T(8,128)} copy-done((f32[16,256,256]{2,1,0:T(8,128)}, f32[16,256,256]{2,1,0:T(8,128)S(1)}, u32[]{:S(2)}) %copy-start.1) | copy-done | bytes 4194328
  109.4 11.8 %inverse_second.1 = f32[256,16,512]{2,1,0:T(8,128)} custom-call(s32[2]{0:T(128)} %pad_add_fusion.place, f32[16,256,256]{2,1,0:T(8,128)} %get-tuple-element.15.keep, f32[16,256,256]{2,1,0:T(8,128)} %copy-done.1, f32[2,256,256]{2,1,0:T(8,128)} %constant.28.clone.own_table.other_table, f32[2,256,256]{2,1,0:T(8,128)} %constant.28.clone.own_table.other_table), custom_call_target="tpu_custom_call" | custom-call | tf_op jit(solution)/shard_map/inverse_second/pallas_call | solution.py:269
Async XLA Ops:
  13.8 7.8 %collective-permute-start = (f32[17,256,256]{2,1,0:T(8,128)}, f32[17,256,256]{2,1,0:T(8,128)S(1)}, u32[]{:S(2)}, u32[]{:S(2)}) collective-permute-start(f32[17,256,256]{2,1,0:T(8,128)} %get-tuple-element.12), channel_id=1, source_target_pairs={{0,1},{1,0},{2,3},{3,2},{4,5},{5,4},{6,7},{7,6},{8,9},{9,8},{10,11... | collective-permute-start | bytes 13369352 | tf_op jit(solution)/shard_map/ppermute | solution.py:289
  21.6 2.1 %copy-start = (f32[17,256,256]{2,1,0:T(8,128)}, f32[17,256,256]{2,1,0:T(8,128)S(1)}, u32[]{:S(2)}) copy-start(f32[17,256,256]{2,1,0:T(8,128)S(1)} %collective-permute-done.got) | copy-start | bytes 13369348
  100.1 7.4 %collective-permute-start.1 = (f32[16,256,256]{2,1,0:T(8,128)}, f32[16,256,256]{2,1,0:T(8,128)S(1)}, u32[]{:S(2)}, u32[]{:S(2)}) collective-permute-start(f32[16,256,256]{2,1,0:T(8,128)} %get-tuple-element.16), channel_id=1, source_target_pairs={{0,1},{1,0},{2,3},{3,2},{4,5},{5,4},{6,7},{7,6},{8,9},{9,8},{10,11... | collective-permute-start | bytes 12582920 | tf_op jit(solution)/shard_map/ppermute | solution.py:289
  107.4 2.0 %copy-start.1 = (f32[16,256,256]{2,1,0:T(8,128)}, f32[16,256,256]{2,1,0:T(8,128)S(1)}, u32[]{:S(2)}) copy-start(f32[16,256,256]{2,1,0:T(8,128)S(1)} %collective-permute-done.1.got) | copy-start | bytes 12582916
where the time goes:
time: 123 us; the launch traced here: 121 us
  Pallas kernels  61.3 us (50%)
  blocking collectives  40 us (33%)
  waiting for transfers between devices  14.7 us (12%)
  local copies, waits for them, and re-layouts  4.07 us (3%)
    all_to_all x1, blocking collectives, shards(): lax.all_to_all(last.reshape(slabs, total // slabs, half), 'tm', 0, 0, til...  22.1 us
    all_to_all x1, blocking collectives, shards(): before = lax.all_to_all(befores, 'tm', 0, 0, tiled=True).reshape(last.shape)  17.9 us
    pallas_call x1, Pallas kernels, forward_first(): pl.pallas_call(functools.partial(forward_first_kernel, steps, slabs), gri...  17.7 us
    pallas_call x1, Pallas kernels, inverse_first(): pl.pallas_call(inverse_first_kernel, grid_spec=pltpu.PrefetchScalarGridSp...  16 us
    ppermute x2, waiting for transfers between devices, swapped(): return lax.ppermute(block, 'space', [(0, 1), (1, 0)])  14.7 us
    pallas_call x1, Pallas kernels, forward_second(): pl.pallas_call(forward_second_kernel, grid_spec=pltpu.PrefetchScalarGridS...  13.2 us
    pallas_call x1, Pallas kernels, inverse_second(): pl.pallas_call(inverse_second_kernel, grid_spec=pltpu.PrefetchScalarGridS...  11.8 us
    unnamed x4, local copies, waits for them, and re-layouts  4.07 us
  transfers between devices with their start and end apart: 2, of which 2 were waited for; matrix products, arithmetic and copies ran while one was open for 0% of the time, Pallas kernels for 0%

commit v1 on v0

v1 whole, which is shorter than its diff:
```python
import functools
import math

import jax
import jax.numpy as jnp
import numpy as np
from jax import lax
from jax.experimental import pallas as pl
from jax.experimental.pallas import tpu as pltpu
from jax.sharding import PartitionSpec as P

circulant_alpha = 0.01
DIFFUSION = 2.0
REACTION_STEP = 0.5
VMEM_BYTES = 28 * 1024 * 1024
LANES = 128
SUBLANES = 8
TILE = 16


def sine_table(row_index, column_index, length):
    product = np.outer(row_index + 1, column_index + 1) % (2 * (length + 1))
    return math.sqrt(2.0 / (length + 1)) * np.sin(product * (math.pi / (length + 1)))


def stencil_eigen(mode_index, length):
    return 4.0 * np.sin((mode_index + 1) * (math.pi / (2.0 * (length + 1)))) ** 2


def second_tables(width):
    half = width // 2
    return np.stack([sine_table(np.arange(half), np.arange(s, width, 2), width) for s in (0, 1)])


def first_tables(total):
    rows = total // 2
    return np.stack(
        [
            np.stack(
                [sine_table(s * rows + np.arange(rows), np.arange(c, total, 2), total) for c in (0, 1)]
            )
            for s in (0, 1)
        ]
    )


def decay_tables(total, width):
    first, second = stencil_eigen(np.arange(total), total), stencil_eigen(np.arange(width), width)
    decay = 1.0 / (1.0 + DIFFUSION * (second[:, None] + first[None, :]))
    return np.stack([np.stack([decay[s::2, c::2] for c in (0, 1)]) for s in (0, 1)])


def constant(table):
    return jnp.asarray(np.asarray(table, np.float32))


def split_constant(table):
    table = np.asarray(table, np.float32)
    high = table.astype(jnp.bfloat16)
    low = (table - high.astype(np.float32)).astype(jnp.bfloat16)
    return jnp.asarray(np.concatenate([high, high, low], axis=-2))


def store_split(ref, at, lane, block):
    depth = ref.shape[-1] // 3
    width = block.shape[-1]
    high = block.astype(jnp.bfloat16)
    low = (block - high.astype(jnp.float32)).astype(jnp.bfloat16)
    for part, value in enumerate((high, low, high)):
        ref[(*at, pl.ds(part * depth + lane, width))] = value


def dot(first, second):
    return jnp.dot(first, second, preferred_element_type=jnp.float32)


def lanes_reversed(block):
    index = LANES - 1 - lax.broadcasted_iota(jnp.int32, (block.shape[0], LANES), 1)
    return jnp.take_along_axis(block, index, axis=1, mode="promise_in_bounds")


def store_rows_reversed(ref, at, block):
    rows, width = block.shape
    index = SUBLANES - 1 - lax.broadcasted_iota(jnp.int32, (SUBLANES, width), 0)
    for row in range(0, rows, SUBLANES):
        ref[at, pl.ds(rows - SUBLANES - row, SUBLANES), :] = jnp.take_along_axis(
            block[row : row + SUBLANES], index, axis=0, mode="promise_in_bounds"
        )


def forward_second_kernel(place, field, initial, own_table, other_table, keep, send, own, other):
    rows, steps, width = field.shape
    half = width // 2
    group = min(SUBLANES, steps)
    is_first = (place[0] == 0).astype(jnp.float32)
    sign = 1.0 - 2.0 * place[1].astype(jnp.float32)

    def put(at, lane, lower, upper):
        shape = lower.shape
        upper = sign * lanes_reversed(upper.reshape(-1, LANES)).reshape(shape)
        store_split(own, at, lane, lower + upper)
        store_split(other, at, lane, lower - upper)

    for row in range(0, rows, TILE):
        cells_at = pl.ds(row, TILE)
        for lane in range(0, half, LANES):
            lanes = (lane, width - LANES - lane)
            for step in range(0, steps, group):
                forces = []
                for at in lanes:
                    cells = field[cells_at, pl.ds(step, group), pl.ds(at, LANES)]
                    force = REACTION_STEP * (cells - cells * cells * cells)
                    force = jnp.swapaxes(force, 0, 1)
                    if step == 0:
                        head = force[:1] + is_first * initial[cells_at, pl.ds(at, LANES)][None]
                        force = jnp.concatenate([head, force[1:]], axis=0)
                    forces.append(force)
                put((pl.ds(step, group), cells_at), lane, *forces)
            ends = [field[cells_at, steps - 1, pl.ds(at, LANES)][None] for at in lanes]
            put((pl.ds(steps, 1), cells_at), lane, *ends)
    keep[...] = dot(own[...].reshape(-1, 3 * half), own_table[0]).reshape(keep.shape)
    result = dot(other[...].reshape(-1, 3 * half), other_table[0])
    for step in range(steps + 1):
        store_rows_reversed(send, step, result[step * rows : (step + 1) * rows])


def forward_second(place, field, initial, tables):
    rows, steps, width = field.shape
    half = width // 2
    block = min(64, rows)
    count = rows // block
    out = jax.ShapeDtypeStruct((steps + 1, rows, half), jnp.float32)
    table = (1, 3 * half, half)
    return pl.pallas_call(
        forward_second_kernel,
        grid_spec=pltpu.PrefetchScalarGridSpec(
            num_scalar_prefetch=1,
            grid=(count,),
            in_specs=[
                pl.BlockSpec((block, steps, width), lambda i, place: (i, 0, 0)),
                pl.BlockSpec((block, width), lambda i, place: (i, 0)),
                pl.BlockSpec(table, lambda i, place: (place[1], 0, 0)),
                pl.BlockSpec(table, lambda i, place: (1 - place[1], 0, 0)),
            ],
            out_specs=[
                pl.BlockSpec((steps + 1, block, half), lambda i, place: (0, i, 0)),
                pl.BlockSpec((steps + 1, block, half), lambda i, place: (0, count - 1 - i, 0)),
            ],
            scratch_shapes=[pltpu.VMEM((steps + 1, block, 3 * half), jnp.bfloat16)] * 2,
        ),
        out_shape=[out, out],
        compiler_params=pltpu.CompilerParams(vmem_limit_bytes=VMEM_BYTES),
        name="forward_second",
    )(place, field, initial, tables, tables)


def forward_first_kernel(
    slabs, place, keep, keep_end, got, got_end, table, decay, modes, last, state, split, split_end
):
    step = pl.program_id(0)
    block, rows, half = keep.shape

    @pl.when(step == 0)
    def _():
        state[...] = jnp.zeros_like(state)

    for at in range(block):
        near, far = keep[at], got[at]
        for c, cells in enumerate((near + far, near - far)):
            store_split(split, (c, pl.ds(at * half, half)), 0, cells.T)
    for c in (0, 1):
        modes[:, c] = dot(split[c], table[0, c]).reshape(block, half, rows)
    for c in (0, 1):
        for row in range(0, half, TILE):
            tile = pl.ds(row, TILE)
            value, rate = state[c, tile], decay[0, c, tile]
            for at in range(block):
                value = rate * (value + modes[at, c, tile])
            state[c, tile] = value

    @pl.when(step == pl.num_programs(0) - 1)
    def _():
        is_last = (place[0] == slabs - 1).astype(jnp.float32)
        near, far = keep_end[0], got_end[0]
        for c, cells in enumerate((near + far, near - far)):
            store_split(split_end, (c, slice(None)), 0, cells.T)
            last[c] = state[c] - is_last * dot(split_end[c], table[0, c])


def forward_first(place, keep, got, tables, decays, slabs):
    steps, rows, half = keep.shape
    steps = steps - 1
    block = min(4, steps)
    step_block = pl.BlockSpec((block, rows, half), lambda i, place: (i, 0, 0))
    end_block = pl.BlockSpec((1, rows, half), lambda i, place: (steps, 0, 0))
    return pl.pallas_call(
        functools.partial(forward_first_kernel, slabs),
        grid_spec=pltpu.PrefetchScalarGridSpec(
            num_scalar_prefetch=1,
            grid=(steps // block,),
            in_specs=[
                step_block,
                end_block,
                step_block,
                end_block,
                pl.BlockSpec((1, 2, 3 * rows, rows), lambda i, place: (place[1], 0, 0, 0)),
                pl.BlockSpec((1, 2, half, rows), lambda i, place: (place[1], 0, 0, 0)),
            ],
            out_specs=[
                pl.BlockSpec((block, 2, half, rows), lambda i, place: (i, 0, 0, 0)),
                pl.BlockSpec((2, half, rows), lambda i, place: (0, 0, 0)),
            ],
            scratch_shapes=[
                pltpu.VMEM((2, half, rows), jnp.float32),
                pltpu.VMEM((2, block * half, 3 * rows), jnp.bfloat16),
                pltpu.VMEM((2, half, 3 * rows), jnp.bfloat16),
            ],
        ),
        out_shape=[
            jax.ShapeDtypeStruct((steps, 2, half, rows), jnp.float32),
            jax.ShapeDtypeStruct((2, half, rows), jnp.float32),
        ],
        compiler_params=pltpu.CompilerParams(vmem_limit_bytes=VMEM_BYTES),
        name="forward_first",
    )(place, keep, keep, got, got, tables, decays)


def close_kernel(place, lasts, decay, gain, before):
    slabs = lasts.shape[0]
    slab = place[0]
    rate = decay[0]
    state = lasts[slab]
    for step in range(1, slabs):
        at = lax.rem(slab + step, slabs)
        state = state * jnp.where(at == 0, circulant_alpha, 1.0)
        state = lasts[at] + rate * state
    state = state * jnp.where(slab == 0, circulant_alpha, 1.0)
    before[...] = gain[0] * state


def close(place, lasts, slab_decays, gains):
    slabs, rows, width = lasts.shape
    block = min(64, rows)
    table = pl.BlockSpec((1, block, width), lambda i, place: (place[1], i, 0))
    return pl.pallas_call(
        close_kernel,
        grid_spec=pltpu.PrefetchScalarGridSpec(
            num_scalar_prefetch=1,
            grid=(rows // block,),
            in_specs=[
                pl.BlockSpec((slabs, block, width), lambda i, place: (0, i, 0)),
                table,
                table,
            ],
            out_specs=pl.BlockSpec((block, width), lambda i, place: (i, 0)),
        ),
        out_shape=jax.ShapeDtypeStruct((rows, width), jnp.float32),
        compiler_params=pltpu.CompilerParams(vmem_limit_bytes=VMEM_BYTES),
        name="close",
    )(place, lasts, slab_decays, gains)


def inverse_first_kernel(place, modes, before, table, decay, keep, send, state, split):
    block, _, half, rows = modes.shape

    @pl.when(pl.program_id(0) == 0)
    def _():
        state[...] = before[...]

    for c in (0, 1):
        for row in range(0, half, TILE):
            tile = pl.ds(row, TILE)
            value, rate = state[c, tile], decay[0, c, tile]
            for at in range(block):
                value = rate * (value + modes[at, c, tile])
                store_split(split, (c, pl.ds(at * half + row, TILE)), 0, value)
            state[c, tile] = value
    even = dot(split[0], table[0, 0])
    odd = dot(split[1], table[0, 1])
    for at in range(block):
        part = slice(at * half, (at + 1) * half)
        keep[at] = (even[part] + odd[part]).T
        store_rows_reversed(send, at, (even[part] - odd[part]).T)


def inverse_first(place, modes, before, tables, decays):
    steps, _, half, rows = modes.shape
    block = min(4, steps)
    out = jax.ShapeDtypeStruct((steps, rows, half), jnp.float32)
    return pl.pallas_call(
        inverse_first_kernel,
        grid_spec=pltpu.PrefetchScalarGridSpec(
            num_scalar_prefetch=1,
            grid=(steps // block,),
            in_specs=[
                pl.BlockSpec((block, 2, half, rows), lambda i, place: (i, 0, 0, 0)),
                pl.BlockSpec((2, half, rows), lambda i, place: (0, 0, 0)),
                pl.BlockSpec((1, 2, 3 * rows, rows), lambda i, place: (place[1], 0, 0, 0)),
                pl.BlockSpec((1, 2, half, rows), lambda i, place: (place[1], 0, 0, 0)),
            ],
            out_specs=[
                pl.BlockSpec((block, rows, half), lambda i, place: (i, 0, 0)),
                pl.BlockSpec((block, rows, half), lambda i, place: (i, 0, 0)),
            ],
            scratch_shapes=[
                pltpu.VMEM((2, half, rows), jnp.float32),
                pltpu.VMEM((2, block * half, 3 * rows), jnp.bfloat16),
            ],
        ),
        out_shape=[out, out],
        compiler_params=pltpu.CompilerParams(vmem_limit_bytes=VMEM_BYTES),
        name="inverse_first",
    )(place, modes, before, tables, decays)


def inverse_second_kernel(
    place, keep, got, own_table, other_table, out, own, other, own_result, other_result
):
    steps, rows, half = keep.shape
    width = 2 * half
    group = min(SUBLANES, steps)
    sign = 1.0 - 2.0 * place[1].astype(jnp.float32)
    for step in range(steps):
        for row in range(0, rows, TILE):
            tile = pl.ds(row, TILE)
            store_split(own, (step, tile), 0, keep[step, tile])
            store_split(other, (step, tile), 0, got[step, tile])
    shape = own_result.shape
    own_result[...] = dot(own[...].reshape(-1, 3 * half), own_table[0]).reshape(shape)
    other_result[...] = dot(other[...].reshape(-1, 3 * half), other_table[0]).reshape(shape)
    for row in range(0, rows, SUBLANES):
        for step in range(0, steps, group):
            for lane in range(0, half, LANES):
                at = (pl.ds(step, group), pl.ds(row, SUBLANES), pl.ds(lane, LANES))
                first, second = own_result[at], other_result[at]
                upper = sign * (first - second)
                upper = lanes_reversed(upper.reshape(-1, LANES)).reshape(upper.shape)
                place_at = (pl.ds(row, SUBLANES), pl.ds(step, group))
                out[(*place_at, pl.ds(lane, LANES))] = jnp.swapaxes(first + second, 0, 1)
                out[(*place_at, pl.ds(width - LANES - lane, LANES))] = jnp.swapaxes(upper, 0, 1)


def inverse_second(place, keep, got, tables):
    steps, rows, half = keep.shape
    block = min(64, rows)
    table = (1, 3 * half, half)
    slab = pl.BlockSpec((steps, block, half), lambda i, place: (0, i, 0))
    return pl.pallas_call(
        inverse_second_kernel,
        grid_spec=pltpu.PrefetchScalarGridSpec(
            num_scalar_prefetch=1,
            grid=(rows // block,),
            in_specs=[
                slab,
                slab,
                pl.BlockSpec(table, lambda i, place: (place[1], 0, 0)),
                pl.BlockSpec(table, lambda i, place: (1 - place[1], 0, 0)),
            ],
            out_specs=pl.BlockSpec((block, steps, 2 * half), lambda i, place: (i, 0, 0)),
            scratch_shapes=[pltpu.VMEM((steps, block, 3 * half), jnp.bfloat16)] * 2
            + [pltpu.VMEM((steps, block, half), jnp.float32)] * 2,
        ),
        out_shape=jax.ShapeDtypeStruct((rows, steps, 2 * half), jnp.float32),
        compiler_params=pltpu.CompilerParams(vmem_limit_bytes=VMEM_BYTES),
        name="inverse_second",
    )(place, keep, got, tables, tables)


def swapped(block):
    return lax.ppermute(block, "space", [(0, 1), (1, 0)])


def shards(iterate, initial):
    rows, steps, width = iterate.shape
    slabs = lax.axis_size("tm")
    total = rows * lax.axis_size("space")
    half = width // 2
    place = jnp.stack([lax.axis_index("tm"), lax.axis_index("space")]).astype(jnp.int32)
    second = second_tables(width)
    first = first_tables(total)
    decay = decay_tables(total, width)
    slab_decay = (decay**steps).reshape(2, width, rows)
    gain = 1.0 / (1.0 - circulant_alpha * slab_decay**slabs)
    keep, send = forward_second(place, iterate, initial, split_constant(second))
    modes, last = forward_first(
        place, keep, swapped(send), split_constant(first), constant(decay), slabs
    )
    lasts = lax.all_gather(last.reshape(width, rows), "tm")
    before = close(place, lasts, constant(slab_decay), constant(gain)).reshape(last.shape)
    keep, send = inverse_first(
        place, modes, before, split_constant(np.swapaxes(first, 2, 3)), constant(decay)
    )
    return inverse_second(place, keep, swapped(send), split_constant(np.swapaxes(second, 1, 2)))


def solution(mesh):
    return jax.shard_map(
        shards,
        mesh=mesh,
        in_specs=(P(("group", "space"), "tm", None), P(("group", "space"), None)),
        out_specs=P(("group", "space"), "tm", None),
        check_vma=False,
    )
```

time: 123 us -> 155 us (1.26); the launches traced: 121 us -> 155 us
  waiting for transfers between devices: 14.7 us -> 90.5 us
  blocking collectives: 40 us -> 0 us
  Pallas kernels: 61.3 us -> 33.2 us
  between operations: 0.01 us -> 13.5 us
  local copies, waits for them, and re-layouts: 4.07 us -> 17 us
    all_gather x0 -> x1, waiting for transfers between devices: none -> 76.2 us  [shards(): lasts = lax.all_gather(last.reshape(width, rows), 'tm')]
    all_to_all x2 -> x0, blocking collectives: 40 us -> none  [the longest x1 22.1 us: shards(): lax.all_to_all(last.reshape(slabs, total // slabs, half), 'tm', 0, 0, til...]
    unnamed x4 -> x24, local copies, waits for them, and re-layouts: 4.07 us -> 17 us
    pallas_call x1, Pallas kernels: 17.7 us -> 7.75 us  [forward_first(): pl.pallas_call(functools.partial(forward_first_kernel, slabs), grid_spec=...]
    pallas_call x1, Pallas kernels: 16 us -> 6.68 us  [inverse_first(): pl.pallas_call(inverse_first_kernel, grid_spec=pltpu.PrefetchScalarGridSp...]
    pallas_call x1, Pallas kernels: 11.8 us -> 7.87 us  [inverse_second(): pl.pallas_call(inverse_second_kernel, grid_spec=pltpu.PrefetchScalarGridS...]
    pallas_call x1, Pallas kernels: 13.2 us -> 9.47 us  [forward_second(): pl.pallas_call(forward_second_kernel, grid_spec=pltpu.PrefetchScalarGridS...]
  transfers between devices with their start and end apart: 2 -> 3, of which waited for: 2 -> 3; matrix products, arithmetic and copies ran while one was open for 0% -> 0% of each run, Pallas kernels for 0% -> 0%
where the time goes in v1:
time: 155 us
  waiting for transfers between devices  90.5 us (58%)
  Pallas kernels  33.2 us (21%)
  local copies, waits for them, and re-layouts  17 us (11%)
  between operations  13.5 us (9%)
    all_gather x1, waiting for transfers between devices, shards(): lasts = lax.all_gather(last.reshape(width, rows), 'tm')  76.2 us
    unnamed x24, local copies, waits for them, and re-layouts  17 us
    ppermute x2, waiting for transfers between devices, swapped(): return lax.ppermute(block, 'space', [(0, 1), (1, 0)])  14.3 us
    pallas_call x1, Pallas kernels, forward_second(): pl.pallas_call(forward_second_kernel, grid_spec=pltpu.PrefetchScalarGridS...  9.47 us
    pallas_call x1, Pallas kernels, inverse_second(): pl.pallas_call(inverse_second_kernel, grid_spec=pltpu.PrefetchScalarGridS...  7.87 us
    pallas_call x1, Pallas kernels, forward_first(): pl.pallas_call(functools.partial(forward_first_kernel, slabs), grid_spec=...  7.75 us
    pallas_call x1, Pallas kernels, inverse_first(): pl.pallas_call(inverse_first_kernel, grid_spec=pltpu.PrefetchScalarGridSp...  6.68 us
  transfers between devices with their start and end apart: 3, of which 3 were waited for; matrix products, arithmetic and copies ran while one was open for 0% of the time, Pallas kernels for 0%

profile of v1, /device:TPU:0, one launch (start us, length us, event | category | flops | bytes accessed | tf_op | source)
XLA Modules:
  0.0 154.8 jit_solution(12253104642412672043)
XLA Ops:
  6.5 0.0 all-gather.2.cloned.1.call-start
  6.5 0.1 pad_add_fusion.place
  6.6 0.0 copy-start
  6.6 3.4 %copy-done = f32[256,16,512]{2,1,0:T(8,128)S(1)} copy-done((f32[256,16,512]{2,1,0:T(8,128)S(1)}, f32[256,16,512]{2,1,0:T(8,128)}, u32[]{:S(2)}) %copy-start) | copy-done | bytes 8388632
  10.0 0.0 copy-start.6
  10.0 1.1 copy-done.6
  11.1 0.0 copy-start.11
  11.1 1.0 copy-done.11
  12.2 0.0 copy-start.3
  12.2 0.0 copy-start.7
  12.2 9.5 %forward_second.1 = (f32[17,256,256]{2,1,0:T(8,128)S(1)}, f32[17,256,256]{2,1,0:T(8,128)S(1)}) custom-call(s32[2]{0:T(128)S(1)} %pad_add_fusion.place, f32[256,16,512]{2,1,0:T(8,128)S(1)} %copy-done, f32[256,512]{1,0:T(8,128)S(1)} %copy-done.11, bf16[2,768,256]{2,1,0:T(8,128)(2,1)S(1)} %copy-done.6, bf16[2,768,256]{2,1,0:T(8,128)(2,1)S(1)} %copy-done.6), custom_call_target="tpu_custom_call" | custom-call | tf_op jit(solution)/shard_map/forward_second/pallas_call | solution.py:134
  21.7 0.5 collective-permute-start
  22.2 7.2 %collective-permute-done.got.got_end = f32[17,256,256]{2,1,0:T(8,128)S(1)} collective-permute-done((f32[17,256,256]{2,1,0:T(8,128)S(1)}, f32[17,256,256]{2,1,0:T(8,128)S(1)}, u32[]{:S(2)}, u32[]{:S(2)}) %collective-permute-start) | collective-permute-done | bytes 4456480 | tf_op jit(solution)/shard_map/ppermute | solution.py:370
  29.3 0.0 copy-done.3
  29.3 0.0 copy-done.7
  29.3 0.0 copy-start.8
  29.3 7.8 %forward_first.1 = (f32[16,2,256,256]{3,2,1,0:T(8,128)S(1)}, f32[2,256,256]{2,1,0:T(8,128)}) custom-call(s32[2]{0:T(128)S(1)} %pad_add_fusion.place, f32[17,256,256]{2,1,0:T(8,128)S(1)} %get-tuple-element.11.keep.keep_end, f32[17,256,256]{2,1,0:T(8,128)S(1)} %get-tuple-element.11.keep.keep_end, f32[17,256,256]{2,1,0:T(8,128)S(1)} %collective-permute-done.got.got_end, ...), custom_call_target="tpu_custom_call" | custom-call | tf_op jit(solution)/shard_map/forward_first/pallas_call | solution.py:196
  37.1 3.4 %copy-done.1 = f32[16,2,256,256]{3,2,1,0:T(8,128)} copy-done((f32[16,2,256,256]{3,2,1,0:T(8,128)}, f32[16,2,256,256]{3,2,1,0:T(8,128)S(1)}, u32[]{:S(2)}) %copy-start.1) | copy-done | bytes 8388632
  40.5 0.0 all-gather.2.cloned.1.call-update
  40.5 76.2 %all-gather.2.cloned.1.call-done.lasts = f32[8,512,256]{2,1,0:T(8,128)} async-done(((f32[1,512,256]{2,1,0:T(8,128)}), f32[8,512,256]{2,1,0:T(8,128)}) %all-gather.2.cloned.1.call-update) | async-done | bytes 4194320 | tf_op jit(solution)/shard_map/all_gather | solution.py:388
  116.7 2.2 %copy-done.4 = f32[8,512,256]{2,1,0:T(8,128)S(1)} copy-done((f32[8,512,256]{2,1,0:T(8,128)S(1)}, f32[8,512,256]{2,1,0:T(8,128)}, u32[]{:S(2)}) %copy-start.4) | copy-done | bytes 4194328
  118.9 1.2 copy-done.9
  120.1 1.2 copy-done.10
  121.3 1.5 close.1
  122.8 0.0 copy-done.8
  122.8 0.0 copy-start.2
  122.8 3.4 %copy-done.2 = f32[16,2,256,256]{3,2,1,0:T(8,128)S(1)} copy-done((f32[16,2,256,256]{3,2,1,0:T(8,128)S(1)}, f32[16,2,256,256]{3,2,1,0:T(8,128)}, u32[]{:S(2)}) %copy-start.2) | copy-done | bytes 8388632
  126.2 6.7 %inverse_first.1 = (f32[16,256,256]{2,1,0:T(8,128)S(1)}, f32[16,256,256]{2,1,0:T(8,128)S(1)}) custom-call(s32[2]{0:T(128)S(1)} %pad_add_fusion.place, f32[16,2,256,256]{3,2,1,0:T(8,128)S(1)} %copy-done.2, f32[2,256,256]{2,1,0:T(8,128)S(1)} %bitcast.4, bf16[2,2,768,256]{3,2,1,0:T(8,128)(2,1)S(1)} %copy-done.8, f32[2,2,256,256]{3,2,1,0:T(8,128)S(1)} %copy-done.3), custom_call_target="tpu_custom_call" | custom-call | tf_op jit(solution)/shard_map/inverse_first/pallas_call | solution.py:290
  132.9 0.1 collective-permute-start.1
  133.0 7.1 %collective-permute-done.1.got = f32[16,256,256]{2,1,0:T(8,128)S(1)} collective-permute-done((f32[16,256,256]{2,1,0:T(8,128)S(1)}, f32[16,256,256]{2,1,0:T(8,128)S(1)}, u32[]{:S(2)}, u32[]{:S(2)}) %collective-permute-start.1) | collective-permute-done | bytes 4194336 | tf_op jit(solution)/shard_map/ppermute | solution.py:370
  140.1 0.0 copy-done.5
  140.1 7.9 %inverse_second.1 = f32[256,16,512]{2,1,0:T(8,128)} custom-call(s32[2]{0:T(128)S(1)} %pad_add_fusion.place, f32[16,256,256]{2,1,0:T(8,128)S(1)} %get-tuple-element.15.keep, f32[16,256,256]{2,1,0:T(8,128)S(1)} %collective-permute-done.1.got, bf16[2,768,256]{2,1,0:T(8,128)(2,1)S(1)} %copy-done.5, bf16[2,768,256]{2,1,0:T(8,128)(2,1)S(1)} %copy-done.5), custom_call_target="tpu_custom_call" | custom-call | tf_op jit(solution)/shard_map/inverse_second/pallas_call | solution.py:348
  (5 shorter events, 0.0 us)
Async XLA Ops:
  6.5 110.2 %all-gather.2.cloned.1.call-start = ((), (), s32[]{:S(2)}) async-start(), calls=%async_computation | async-start | bytes 4718592 | tf_op jit(solution)/shard_map/all_gather | solution.py:388
  6.6 3.4 %copy-start = (f32[256,16,512]{2,1,0:T(8,128)S(1)}, f32[256,16,512]{2,1,0:T(8,128)}, u32[]{:S(2)}) copy-start(f32[256,16,512]{2,1,0:T(8,128)} %field.1) | copy-start | bytes 25165828
  10.0 1.1 copy-start.6
  11.1 1.0 copy-start.11
  12.2 17.2 %copy-start.3 = (f32[2,2,256,256]{3,2,1,0:T(8,128)S(1)}, f32[2,2,256,256]{3,2,1,0:T(8,128)}, u32[]{:S(2)}) copy-start(f32[2,2,256,256]{3,2,1,0:T(8,128)} %constant.24.clone.decay) | copy-start | bytes 3145732
  12.2 17.2 %copy-start.7 = (bf16[2,2,768,256]{3,2,1,0:T(8,128)(2,1)S(1)}, bf16[2,2,768,256]{3,2,1,0:T(8,128)(2,1)}, u32[]{:S(2)}) copy-start(bf16[2,2,768,256]{3,2,1,0:T(8,128)(2,1)} %constant.23.clone.table) | copy-start | bytes 4718596
  21.7 7.7 %collective-permute-start = (f32[17,256,256]{2,1,0:T(8,128)S(1)}, f32[17,256,256]{2,1,0:T(8,128)S(1)}, u32[]{:S(2)}, u32[]{:S(2)}) collective-permute-start(f32[17,256,256]{2,1,0:T(8,128)S(1)} %get-tuple-element.12), channel_id=1, source_target_pairs={{0,1},{1,0},{2,3},{3,2},{4,5},{5,4},{6,7},{7,6},{8,9},{9,8},{10,11... | collective-permute-start | bytes 13369352 | tf_op jit(solution)/shard_map/ppermute | solution.py:370
  29.3 93.5 %copy-start.8 = (bf16[2,2,768,256]{3,2,1,0:T(8,128)(2,1)S(1)}, bf16[2,2,768,256]{3,2,1,0:T(8,128)(2,1)}, u32[]{:S(2)}) copy-start(bf16[2,2,768,256]{3,2,1,0:T(8,128)(2,1)} %constant.27.clone.table) | copy-start | bytes 4718596
  37.1 3.4 %copy-start.1 = (f32[16,2,256,256]{3,2,1,0:T(8,128)}, f32[16,2,256,256]{3,2,1,0:T(8,128)S(1)}, u32[]{:S(2)}) copy-start(f32[16,2,256,256]{3,2,1,0:T(8,128)S(1)} %get-tuple-element.13.modes) | copy-start | bytes 25165828
  116.7 2.2 %copy-start.4 = (f32[8,512,256]{2,1,0:T(8,128)S(1)}, f32[8,512,256]{2,1,0:T(8,128)}, u32[]{:S(2)}) copy-start(f32[8,512,256]{2,1,0:T(8,128)} %all-gather.2.cloned.1.call-done.lasts) | copy-start | bytes 12582916
  118.9 1.2 copy-start.9
  120.1 1.2 copy-start.10
  122.8 3.4 %copy-start.2 = (f32[16,2,256,256]{3,2,1,0:T(8,128)S(1)}, f32[16,2,256,256]{3,2,1,0:T(8,128)}, u32[]{:S(2)}) copy-start(f32[16,2,256,256]{3,2,1,0:T(8,128)} %copy-done.1) | copy-start | bytes 25165828
  126.2 13.9 %copy-start.5 = (bf16[2,768,256]{2,1,0:T(8,128)(2,1)S(1)}, bf16[2,768,256]{2,1,0:T(8,128)(2,1)}, u32[]{:S(2)}) copy-start(bf16[2,768,256]{2,1,0:T(8,128)(2,1)} %constant.28.clone.own_table.other_table) | copy-start | bytes 2359300
  132.9 7.2 %collective-permute-start.1 = (f32[16,256,256]{2,1,0:T(8,128)S(1)}, f32[16,256,256]{2,1,0:T(8,128)S(1)}, u32[]{:S(2)}, u32[]{:S(2)}) collective-permute-start(f32[16,256,256]{2,1,0:T(8,128)S(1)} %get-tuple-element.16), channel_id=1, source_target_pairs={{0,1},{1,0},{2,3},{3,2},{4,5},{5,4},{6,7},{7,6},{8,9},{9,8},{10,11... | collective-permute-start | bytes 12582920 | tf_op jit(solution)/shard_map/ppermute | solution.py:370
Sparse Core Ops, SparseCore 0:
  40.6 76.0 all-gather.1

commit v2 on v1

v2 whole, which is shorter than its diff:
```python
import functools
import math

import jax
import jax.numpy as jnp
import numpy as np
from jax import lax
from jax.experimental import pallas as pl
from jax.experimental.pallas import tpu as pltpu
from jax.sharding import PartitionSpec as P

circulant_alpha = 0.01
DIFFUSION = 2.0
REACTION_STEP = 0.5
VMEM_BYTES = 28 * 1024 * 1024
LANES = 128
SUBLANES = 8
TILE = 16
CHUNKS = 2


def sine_table(row_index, column_index, length):
    product = np.outer(row_index + 1, column_index + 1) % (2 * (length + 1))
    return math.sqrt(2.0 / (length + 1)) * np.sin(product * (math.pi / (length + 1)))


def stencil_eigen(mode_index, length):
    return 4.0 * np.sin((mode_index + 1) * (math.pi / (2.0 * (length + 1)))) ** 2


def second_tables(width):
    half = width // 2
    return np.stack([sine_table(np.arange(half), np.arange(s, width, 2), width) for s in (0, 1)])


def first_tables(total):
    rows = total // 2
    return np.stack(
        [
            np.stack(
                [sine_table(s * rows + np.arange(rows), np.arange(c, total, 2), total) for c in (0, 1)]
            )
            for s in (0, 1)
        ]
    )


def decay_tables(total, width):
    first, second = stencil_eigen(np.arange(total), total), stencil_eigen(np.arange(width), width)
    decay = 1.0 / (1.0 + DIFFUSION * (second[:, None] + first[None, :]))
    return np.stack([np.stack([decay[s::2, c::2] for c in (0, 1)]) for s in (0, 1)])


def constant(table):
    return jnp.asarray(np.asarray(table, np.float32))


def split_constant(table):
    table = np.asarray(table, np.float32)
    high = table.astype(jnp.bfloat16)
    low = (table - high.astype(np.float32)).astype(jnp.bfloat16)
    return jnp.asarray(np.concatenate([high, high, low], axis=-2))


def store_split(ref, at, lane, block):
    depth = ref.shape[-1] // 3
    width = block.shape[-1]
    high = block.astype(jnp.bfloat16)
    low = (block - high.astype(jnp.float32)).astype(jnp.bfloat16)
    for part, value in enumerate((high, low, high)):
        ref[(*at, pl.ds(part * depth + lane, width))] = value


def dot(first, second):
    return jnp.dot(first, second, preferred_element_type=jnp.float32)


def lanes_reversed(block):
    index = LANES - 1 - lax.broadcasted_iota(jnp.int32, (block.shape[0], LANES), 1)
    return jnp.take_along_axis(block, index, axis=1, mode="promise_in_bounds")


def store_rows_reversed(ref, at, block):
    rows, width = block.shape
    index = SUBLANES - 1 - lax.broadcasted_iota(jnp.int32, (SUBLANES, width), 0)
    for row in range(0, rows, SUBLANES):
        ref[at, pl.ds(rows - SUBLANES - row, SUBLANES), :] = jnp.take_along_axis(
            block[row : row + SUBLANES], index, axis=0, mode="promise_in_bounds"
        )


def in_hbm(array):
    return pltpu.with_memory_space_constraint(array, pltpu.HBM)


def call(kernel, name, grid, in_specs, out_specs, out_shape, scratch, flops):
    return pl.pallas_call(
        kernel,
        grid_spec=pltpu.PrefetchScalarGridSpec(
            num_scalar_prefetch=1,
            grid=(grid,),
            in_specs=in_specs,
            out_specs=out_specs,
            scratch_shapes=scratch,
        ),
        out_shape=out_shape,
        compiler_params=pltpu.CompilerParams(vmem_limit_bytes=VMEM_BYTES),
        cost_estimate=pl.CostEstimate(flops=flops, bytes_accessed=1 << 23, transcendentals=0),
        name=name,
    )


def floats(*shape):
    return jax.ShapeDtypeStruct(shape, jnp.float32)


def forward_second_kernel(place, field, initial, own_table, other_table, *refs):
    keeps, sends, (own, other) = refs[:CHUNKS], refs[CHUNKS : 2 * CHUNKS], refs[2 * CHUNKS :]
    rows, steps, width = field.shape
    half = width // 2
    part = half // CHUNKS
    group = min(SUBLANES, steps)
    is_first = (place[0] == 0).astype(jnp.float32)
    sign = 1.0 - 2.0 * place[1].astype(jnp.float32)

    def put(at, lane, lower, upper):
        shape = lower.shape
        upper = sign * lanes_reversed(upper.reshape(-1, LANES)).reshape(shape)
        store_split(own, at, lane, lower + upper)
        store_split(other, at, lane, lower - upper)

    for row in range(0, rows, TILE):
        cells_at = pl.ds(row, TILE)
        for lane in range(0, half, LANES):
            lanes = (lane, width - LANES - lane)
            for step in range(0, steps, group):
                forces = []
                for at in lanes:
                    cells = field[cells_at, pl.ds(step, group), pl.ds(at, LANES)]
                    force = REACTION_STEP * (cells - cells * cells * cells)
                    force = jnp.swapaxes(force, 0, 1)
                    if step == 0:
                        head = force[:1] + is_first * initial[cells_at, pl.ds(at, LANES)][None]
                        force = jnp.concatenate([head, force[1:]], axis=0)
                    forces.append(force)
                put((pl.ds(step, group), cells_at), lane, *forces)
            ends = [field[cells_at, steps - 1, pl.ds(at, LANES)][None] for at in lanes]
            put((pl.ds(steps, 1), cells_at), lane, *ends)
    kept = dot(own[...].reshape(-1, 3 * half), own_table[0])
    sent = dot(other[...].reshape(-1, 3 * half), other_table[0])
    for chunk in range(CHUNKS):
        lanes = slice(chunk * part, (chunk + 1) * part)
        keeps[chunk][...] = kept[:, lanes].reshape(steps + 1, rows, part)
        for step in range(steps + 1):
            store_rows_reversed(sends[chunk], step, sent[step * rows : (step + 1) * rows, lanes])


def forward_second(place, field, initial, tables):
    rows, steps, width = field.shape
    half = width // 2
    part = half // CHUNKS
    block = min(64, rows)
    count = rows // block
    table = (1, 3 * half, half)
    shape = (steps + 1, block, part)
    outs = call(
        forward_second_kernel,
        "forward_second",
        count,
        [
            pl.BlockSpec((block, steps, width), lambda i, place: (i, 0, 0)),
            pl.BlockSpec((block, width), lambda i, place: (i, 0)),
            pl.BlockSpec(table, lambda i, place: (place[1], 0, 0)),
            pl.BlockSpec(table, lambda i, place: (1 - place[1], 0, 0)),
        ],
        [pl.BlockSpec(shape, lambda i, place: (0, i, 0))] * CHUNKS
        + [pl.BlockSpec(shape, lambda i, place: (0, count - 1 - i, 0))] * CHUNKS,
        [floats(steps + 1, rows, part)] * (2 * CHUNKS),
        [pltpu.VMEM((steps + 1, block, 3 * half), jnp.bfloat16)] * 2,
        1 << 32,
    )(place, in_hbm(field), in_hbm(initial), in_hbm(tables), in_hbm(tables))
    return outs[:CHUNKS], outs[CHUNKS:]


def ranks(slabs):
    return slabs // 2


def forward_first_kernel(slabs, place, keep, keep_end, got, got_end, table, decay, modes, *refs):
    size = ranks(slabs)
    lasts, (state, split, split_end) = refs[:size], refs[size:]
    step = pl.program_id(0)
    block, rows, part = keep.shape

    @pl.when(step == 0)
    def _():
        state[...] = jnp.zeros_like(state)

    for at in range(block):
        near, far = keep[at], got[at]
        for c, cells in enumerate((near + far, near - far)):
            store_split(split, (c, pl.ds(at * part, part)), 0, cells.T)
    for c in (0, 1):
        modes[:, c] = dot(split[c], table[0, c]).reshape(block, part, rows)
    for c in (0, 1):
        for row in range(0, part, TILE):
            tile, at_state = pl.ds(row, TILE), pl.ds(c * part + row, TILE)
            value, rate = state[at_state], decay[0, c, tile]
            for at in range(block):
                value = rate * (value + modes[at, c, tile])
            state[at_state] = value

    @pl.when(step == pl.num_programs(0) - 1)
    def _():
        is_last = (place[0] == slabs - 1).astype(jnp.float32)
        near, far = keep_end[0], got_end[0]
        for c, cells in enumerate((near + far, near - far)):
            store_split(split_end, (c, slice(None)), 0, cells.T)
            at_state = pl.ds(c * part, part)
            state[at_state] = state[at_state] - is_last * dot(split_end[c], table[0, c])
        rank = lax.rem(place[0], size)
        share = 2 * part // size
        for partner in range(size):
            at = pl.multiple_of((rank ^ partner) * share, share)
            lasts[partner][...] = state[pl.ds(at, share)]


def forward_first(place, chunk, keep, got, tables, decays, slabs):
    steps, rows, part = keep.shape
    steps = steps - 1
    block = min(4, steps)
    size = ranks(slabs)
    share = 2 * part // size
    step_block = pl.BlockSpec((block, rows, part), lambda i, place: (i, 0, 0))
    end_block = pl.BlockSpec((1, rows, part), lambda i, place: (steps, 0, 0))
    outs = call(
        functools.partial(forward_first_kernel, slabs),
        "forward_first",
        steps // block,
        [
            step_block,
            end_block,
            step_block,
            end_block,
            pl.BlockSpec((1, 2, 3 * rows, rows), lambda i, place: (place[1], 0, 0, 0)),
            pl.BlockSpec((1, 2, part, rows), lambda i, place: (place[1], 0, chunk, 0)),
        ],
        [pl.BlockSpec((block, 2, part, rows), lambda i, place: (i, 0, 0, 0))]
        + [pl.BlockSpec((share, rows), lambda i, place: (0, 0))] * size,
        [floats(steps, 2, part, rows)] + [floats(share, rows)] * size,
        [
            pltpu.VMEM((2 * part, rows), jnp.float32),
            pltpu.VMEM((2, block * part, 3 * rows), jnp.bfloat16),
            pltpu.VMEM((2, part, 3 * rows), jnp.bfloat16),
        ],
        1 << 31,
    )(place, keep, keep, got, got, in_hbm(tables), in_hbm(decays))
    return outs[0], outs[1:]


def half_sum_kernel(slabs, place, decay, *refs):
    size = ranks(slabs)
    lasts, ordered, total = refs[:size], refs[size], refs[size + 1]
    rank = lax.rem(place[0], size)
    for partner in range(size):
        ordered[rank ^ partner] = lasts[partner][...]
    state = ordered[0]
    for at in range(1, size):
        state = ordered[at] + decay[0] * state
    total[...] = state


def half_sum(place, lasts, slab_decays, slabs):
    size = ranks(slabs)
    share, rows = lasts[0].shape
    whole = pl.BlockSpec((share, rows), lambda i, place: (0, 0))
    return call(
        functools.partial(half_sum_kernel, slabs),
        "half_sum",
        1,
        [pl.BlockSpec((1, share, rows), lambda i, place: (place[1], lax.rem(place[0], size), 0))]
        + [whole] * size,
        [pl.BlockSpec((size, share, rows), lambda i, place: (0, 0, 0)), whole],
        [floats(size, share, rows), floats(share, rows)],
        [],
        1 << 20,
    )(place, in_hbm(slab_decays), *lasts)


def close_kernel(slabs, place, decay, half_decay, gain, ordered, near, far, *refs):
    size = ranks(slabs)
    befores, states = refs[:size], refs[size]
    rank = lax.rem(place[0], size)
    entering = jnp.where(place[0] < size, circulant_alpha, 1.0)
    state = gain[0] * (entering * far[...] + circulant_alpha * half_decay[0] * near[...])
    for at in range(size):
        states[at] = state
        if at < size - 1:
            state = ordered[at] + decay[0] * state
    for partner in range(size):
        befores[partner][...] = states[rank ^ partner]


def close(place, ordered, near, far, slab_decays, half_decays, gains, slabs):
    size, share, rows = ordered.shape
    table = pl.BlockSpec((1, share, rows), lambda i, place: (place[1], lax.rem(place[0], size), 0))
    whole = pl.BlockSpec((share, rows), lambda i, place: (0, 0))
    return call(
        functools.partial(close_kernel, slabs),
        "close",
        1,
        [table] * 3 + [pl.BlockSpec((size, share, rows), lambda i, place: (0, 0, 0)), whole, whole],
        [whole] * size,
        [floats(share, rows)] * size,
        [pltpu.VMEM((size, share, rows), jnp.float32)],
        1 << 20,
    )(place, in_hbm(slab_decays), in_hbm(half_decays), in_hbm(gains), ordered, near, far)


def inverse_first_kernel(slabs, place, modes, table, decay, *refs):
    size = ranks(slabs)
    befores, (keep, send, state, split) = refs[:size], refs[size:]
    block, _, part, rows = modes.shape

    @pl.when(pl.program_id(0) == 0)
    def _():
        rank = lax.rem(place[0], size)
        share = 2 * part // size
        for partner in range(size):
            at = pl.multiple_of((rank ^ partner) * share, share)
            state[pl.ds(at, share)] = befores[partner][...]

    for c in (0, 1):
        for row in range(0, part, TILE):
            tile, at_state = pl.ds(row, TILE), pl.ds(c * part + row, TILE)
            value, rate = state[at_state], decay[0, c, tile]
            for at in range(block):
                value = rate * (value + modes[at, c, tile])
                store_split(split, (c, pl.ds(at * part + row, TILE)), 0, value)
            state[at_state] = value
    even = dot(split[0], table[0, 0])
    odd = dot(split[1], table[0, 1])
    for at in range(block):
        piece = slice(at * part, (at + 1) * part)
        keep[at] = (even[piece] + odd[piece]).T
        store_rows_reversed(send, at, (even[piece] - odd[piece]).T)


def inverse_first(place, chunk, modes, befores, tables, decays, slabs):
    steps, _, part, rows = modes.shape
    block = min(4, steps)
    whole = pl.BlockSpec(befores[0].shape, lambda i, place: (0, 0))
    return call(
        functools.partial(inverse_first_kernel, slabs),
        "inverse_first",
        steps // block,
        [
            pl.BlockSpec((block, 2, part, rows), lambda i, place: (i, 0, 0, 0)),
            pl.BlockSpec((1, 2, 3 * rows, rows), lambda i, place: (place[1], 0, 0, 0)),
            pl.BlockSpec((1, 2, part, rows), lambda i, place: (place[1], 0, chunk, 0)),
        ]
        + [whole] * len(befores),
        [pl.BlockSpec((block, rows, part), lambda i, place: (i, 0, 0))] * 2,
        [floats(steps, rows, part)] * 2,
        [
            pltpu.VMEM((2 * part, rows), jnp.float32),
            pltpu.VMEM((2, block * part, 3 * rows), jnp.bfloat16),
        ],
        1 << 31,
    )(place, modes, in_hbm(tables), in_hbm(decays), *befores)


def inverse_second_kernel(place, own_table, other_table, *refs):
    keeps, gots, refs = refs[:CHUNKS], refs[CHUNKS : 2 * CHUNKS], refs[2 * CHUNKS :]
    out, own, other, own_result, other_result = refs
    steps, rows, part = keeps[0].shape
    half = part * CHUNKS
    width = 2 * half
    group = min(SUBLANES, steps)
    sign = 1.0 - 2.0 * place[1].astype(jnp.float32)
    for step in range(steps):
        for row in range(0, rows, TILE):
            tile = pl.ds(row, TILE)
            for chunk in range(CHUNKS):
                store_split(own, (step, tile), chunk * part, keeps[chunk][step, tile])
                store_split(other, (step, tile), chunk * part, gots[chunk][step, tile])
    shape = own_result.shape
    own_result[...] = dot(own[...].reshape(-1, 3 * half), own_table[0]).reshape(shape)
    other_result[...] = dot(other[...].reshape(-1, 3 * half), other_table[0]).reshape(shape)
    for row in range(0, rows, SUBLANES):
        for step in range(0, steps, group):
            for lane in range(0, half, LANES):
                at = (pl.ds(step, group), pl.ds(row, SUBLANES), pl.ds(lane, LANES))
                first, second = own_result[at], other_result[at]
                upper = sign * (first - second)
                upper = lanes_reversed(upper.reshape(-1, LANES)).reshape(upper.shape)
                place_at = (pl.ds(row, SUBLANES), pl.ds(step, group))
                out[(*place_at, pl.ds(lane, LANES))] = jnp.swapaxes(first + second, 0, 1)
                out[(*place_at, pl.ds(width - LANES - lane, LANES))] = jnp.swapaxes(upper, 0, 1)


def inverse_second(place, keeps, gots, tables):
    steps, rows, part = keeps[0].shape
    half = part * CHUNKS
    block = min(64, rows)
    table = (1, 3 * half, half)
    return call(
        inverse_second_kernel,
        "inverse_second",
        rows // block,
        [
            pl.BlockSpec(table, lambda i, place: (place[1], 0, 0)),
            pl.BlockSpec(table, lambda i, place: (1 - place[1], 0, 0)),
        ]
        + [pl.BlockSpec((steps, block, part), lambda i, place: (0, i, 0))] * (2 * CHUNKS),
        pl.BlockSpec((block, steps, 2 * half), lambda i, place: (i, 0, 0)),
        floats(rows, steps, 2 * half),
        [pltpu.VMEM((steps, block, 3 * half), jnp.bfloat16)] * 2
        + [pltpu.VMEM((steps, block, half), jnp.float32)] * 2,
        1 << 32,
    )(place, in_hbm(tables), in_hbm(tables), *keeps, *gots)


def swapped(block):
    return lax.ppermute(block, "space", [(0, 1), (1, 0)])


def with_partner(block, distance):
    slabs = lax.axis_size("tm")
    return lax.ppermute(block, "tm", [(slab, slab ^ distance) for slab in range(slabs)])


def among_ranks(blocks):
    return [blocks[0]] + [with_partner(block, at) for at, block in enumerate(blocks) if at]


def by_chunk(table, parts):
    strips, _, half, rows = table.shape
    size = half // parts
    return [
        table[:, :, at * size : (at + 1) * size].reshape(strips, 2 * size, rows) for at in range(parts)
    ]


def shards(iterate, initial):
    rows, steps, width = iterate.shape
    slabs = lax.axis_size("tm")
    total = rows * lax.axis_size("space")
    place = jnp.stack([lax.axis_index("tm"), lax.axis_index("space")]).astype(jnp.int32)
    second = second_tables(width)
    first = first_tables(total)
    decay = decay_tables(total, width)
    slab_decay = decay**steps
    half_decay = slab_decay ** ranks(slabs)
    gain = 1.0 / (1.0 - circulant_alpha * half_decay * half_decay)
    closing = [
        [constant(part) for part in parts]
        for parts in zip(*(by_chunk(table, CHUNKS) for table in (slab_decay, half_decay, gain)))
    ]
    first_table, decays = split_constant(first), constant(decay)
    keeps, sends = forward_second(place, iterate, initial, split_constant(second))
    gots = [swapped(send) for send in sends]
    modes, befores = [], []
    for chunk in range(CHUNKS):
        own_modes, lasts = forward_first(
            place, chunk, keeps[chunk], gots[chunk], first_table, decays, slabs
        )
        modes.append(own_modes)
        slab_part, half_part, gain_part = closing[chunk]
        ordered, near = half_sum(place, among_ranks(lasts), slab_part, slabs)
        far = with_partner(near, ranks(slabs))
        befores.append(
            among_ranks(close(place, ordered, near, far, slab_part, half_part, gain_part, slabs))
        )
    inverse_table = split_constant(np.swapaxes(first, 2, 3))
    keeps, sends = zip(
        *(
            inverse_first(place, chunk, modes[chunk], befores[chunk], inverse_table, decays, slabs)
            for chunk in range(CHUNKS)
        )
    )
    gots = [swapped(send) for send in sends]
    return inverse_second(place, keeps, gots, split_constant(np.swapaxes(second, 1, 2)))


def solution(mesh):
    return jax.shard_map(
        shards,
        mesh=mesh,
        in_specs=(P(("group", "space"), "tm", None), P(("group", "space"), None)),
        out_specs=P(("group", "space"), "tm", None),
        check_vma=False,
    )
```

time: 155 us -> 80.1 us (0.52)
  waiting for transfers between devices: 90.5 us -> 9.11 us
  starting transfers between devices: 0.59 us -> 21.4 us
  local copies, waits for them, and re-layouts: 17 us -> 0.83 us
  Pallas kernels: 33.2 us -> 48.1 us
  between operations: 13.5 us -> 0.11 us
    all_gather x1 -> x0, waiting for transfers between devices: 76.2 us -> none  [shards(): lasts = lax.all_gather(last.reshape(width, rows), 'tm')]
    ppermute x0 -> x14, starting transfers between devices: none -> 20.2 us  [with_partner(): lax.ppermute(block, 'tm', [(slab, slab ^ distance) for slab in range(slab...]
    unnamed x24 -> x0, local copies, waits for them, and re-layouts: 17 us -> none
    pallas_call x5 -> x10, Pallas kernels: 33.2 us -> 48.1 us  [the longest x1 11.2 us: forward_second(): call(forward_second_kernel, 'forward_second', count, [pl.BlockSpec((block...]
    ppermute x2 -> x4, waiting for transfers between devices: 14.3 us -> 7.68 us  [swapped(): return lax.ppermute(block, 'space', [(0, 1), (1, 0)])]
  transfers between devices with their start and end apart: 3 -> 18, of which waited for: 3 -> 3; matrix products, arithmetic and copies ran while one was open for 0% -> 1% of each run, Pallas kernels for 0% -> 35%
where the time goes in v2:
time: 80.1 us; the launch traced here: 79.7 us
  Pallas kernels  48.1 us (60%)
  starting transfers between devices  21.4 us (27%)
  waiting for transfers between devices  9.11 us (11%)
  local copies, waits for them, and re-layouts  0.83 us (1%)
    ppermute x14, starting transfers between devices, with_partner(): lax.ppermute(block, 'tm', [(slab, slab ^ distance) for slab in range(slab...  20.2 us
    pallas_call x1, Pallas kernels, forward_second(): call(forward_second_kernel, 'forward_second', count, [pl.BlockSpec((block...  11.2 us
    pallas_call x2, Pallas kernels, forward_first(): call(functools.partial(forward_first_kernel, slabs), 'forward_first', ste...  11.1 us
    pallas_call x2, Pallas kernels, inverse_first(): call(functools.partial(inverse_first_kernel, slabs), 'inverse_first', ste...  11 us
    pallas_call x1, Pallas kernels, inverse_second(): call(inverse_second_kernel, 'inverse_second', rows // block, [pl.BlockSpe...  9.02 us
    ppermute x4, waiting for transfers between devices, swapped(): return lax.ppermute(block, 'space', [(0, 1), (1, 0)])  7.68 us
    pallas_call x2, Pallas kernels, close(): call(functools.partial(close_kernel, slabs), 'close', 1, [table] * 3 + [p...  3 us
    pallas_call x2, Pallas kernels, half_sum(): call(functools.partial(half_sum_kernel, slabs), 'half_sum', 1, [pl.BlockS...  2.86 us
  transfers between devices with their start and end apart: 18, of which 3 were waited for; matrix products, arithmetic and copies ran while one was open for 1% of the time, Pallas kernels for 35%

profile of v2, /device:TPU:0, one launch (start us, length us, event | category | flops | bytes accessed | tf_op | source)
XLA Modules:
  0.0 79.7 jit_solution(1093012120968596185)
XLA Ops:
  0.0 0.1 pad_add_fusion.place
  0.1 11.2 %forward_second.1 = (f32[17,256,128]{2,1,0:T(8,128)S(1)}, f32[17,256,128]{2,1,0:T(8,128)S(1)}, f32[17,256,128]{2,1,0:T(8,128)S(1)}, f32[17,256,128]{2,1,0:T(8,128)S(1)}) custom-call(s32[2]{0:T(128)S(1)} %pad_add_fusion.place, f32[256,16,512]{2,1,0:T(8,128)} %field.1, f32[256,512]{1,0:T(8,128)} %initial.1, ...), custom_call_target="tpu_custom_call" | custom-call | flops 4294967296 | bytes 8388608 | tf_op jit(solution)/shard_map/forward_second/pallas_call | solution.py:166
  11.3 0.5 collective-permute-start
  11.8 0.1 collective-permute-start.8
  11.9 3.9 %collective-permute-done.got.got_end = f32[17,256,128]{2,1,0:T(8,128)S(1)} collective-permute-done((f32[17,256,128]{2,1,0:T(8,128)S(1)}, f32[17,256,128]{2,1,0:T(8,128)S(1)}, u32[]{:S(2)}, u32[]{:S(2)}) %collective-permute-start) | collective-permute-done | bytes 2228256 | tf_op jit(solution)/shard_map/ppermute | solution.py:425
  15.8 5.5 %forward_first.2 = (f32[16,2,128,256]{3,2,1,0:T(8,128)S(1)}, f32[64,256]{1,0:T(8,128)S(1)}, f32[64,256]{1,0:T(8,128)S(1)}, f32[64,256]{1,0:T(8,128)S(1)}, f32[64,256]{1,0:T(8,128)S(1)}) custom-call(s32[2]{0:T(128)S(1)} %pad_add_fusion.place, f32[17,256,128]{2,1,0:T(8,128)S(1)} %get-tuple-element.35.keep.keep_end, ...), custom_call_target="tpu_custom_call" | custom-call | flops 2147483648 | bytes 8388608 | tf_op jit(solution)/shard_map/forward_first/pallas_call | solution.py:236
  21.3 3.0 %collective-permute-start.1 = (f32[64,256]{1,0:T(8,128)S(1)}, f32[64,256]{1,0:T(8,128)S(1)}, u32[]{:S(2)}, u32[]{:S(2)}) collective-permute-start(f32[64,256]{1,0:T(8,128)S(1)} %get-tuple-element.39), channel_id=1, source_target_pairs={{0,2},{2,0},{4,6},{6,4},{8,10},{10,8},{12,14},{14,12},{1,3},{3,1},... | collective-permute-start | bytes 196616 | tf_op jit(solution)/shard_map/ppermute | solution.py:430
  24.3 1.6 %collective-permute-start.2 = (f32[64,256]{1,0:T(8,128)S(1)}, f32[64,256]{1,0:T(8,128)S(1)}, u32[]{:S(2)}, u32[]{:S(2)}) collective-permute-start(f32[64,256]{1,0:T(8,128)S(1)} %get-tuple-element.40), channel_id=1, source_target_pairs={{0,4},{2,6},{4,0},{6,2},{8,12},{10,14},{12,8},{14,10},{1,5},{3,7},... | collective-permute-start | bytes 196616 | tf_op jit(solution)/shard_map/ppermute | solution.py:430
  25.9 0.0 collective-permute-start.3
  25.9 5.5 %forward_first.3 = (f32[16,2,128,256]{3,2,1,0:T(8,128)S(1)}, f32[64,256]{1,0:T(8,128)S(1)}, f32[64,256]{1,0:T(8,128)S(1)}, f32[64,256]{1,0:T(8,128)S(1)}, f32[64,256]{1,0:T(8,128)S(1)}) custom-call(s32[2]{0:T(128)S(1)} %pad_add_fusion.place, f32[17,256,128]{2,1,0:T(8,128)S(1)} %get-tuple-element.49.keep.keep_end, ...), custom_call_target="tpu_custom_call" | custom-call | flops 2147483648 | bytes 8388608 | tf_op jit(solution)/shard_map/forward_first/pallas_call | solution.py:236
  31.5 2.0 %collective-permute-start.9 = (f32[64,256]{1,0:T(8,128)S(1)}, f32[64,256]{1,0:T(8,128)S(1)}, u32[]{:S(2)}, u32[]{:S(2)}) collective-permute-start(f32[64,256]{1,0:T(8,128)S(1)} %get-tuple-element.53), channel_id=1, source_target_pairs={{0,2},{2,0},{4,6},{6,4},{8,10},{10,8},{12,14},{14,12},{1,3},{3,1},... | collective-permute-start | bytes 196616 | tf_op jit(solution)/shard_map/ppermute | solution.py:430
  33.4 1.6 %collective-permute-start.10 = (f32[64,256]{1,0:T(8,128)S(1)}, f32[64,256]{1,0:T(8,128)S(1)}, u32[]{:S(2)}, u32[]{:S(2)}) collective-permute-start(f32[64,256]{1,0:T(8,128)S(1)} %get-tuple-element.54), channel_id=1, source_target_pairs={{0,4},{2,6},{4,0},{6,2},{8,12},{10,14},{12,8},{14,10},{1,5},{3,7},... | collective-permute-start | bytes 196616 | tf_op jit(solution)/shard_map/ppermute | solution.py:430
  35.0 1.4 %half_sum.2 = (f32[4,64,256]{2,1,0:T(8,128)S(1)}, f32[64,256]{1,0:T(8,128)S(1)}) custom-call(s32[2]{0:T(128)S(1)} %pad_add_fusion.place, f32[2,256,256]{2,1,0:T(8,128)} %constant.30.clone.decay, f32[64,256]{1,0:T(8,128)S(1)} %get-tuple-element.38.refs_0_, f32[64,256]{1,0:T(8,128)S(1)} %collective-permute-done.1.refs_1_, ...), custom_call_target="tpu_custom_call" | custom-call | flops 1048576 | bytes 8388608 | tf_op jit(solution)/shard_map/half_sum/pallas_call | solution.py:277
  36.5 3.0 %collective-permute-start.4 = (f32[64,256]{1,0:T(8,128)S(1)}, f32[64,256]{1,0:T(8,128)S(1)}, u32[]{:S(2)}, u32[]{:S(2)}) collective-permute-start(f32[64,256]{1,0:T(8,128)S(1)} %get-tuple-element.43.near), channel_id=1, source_target_pairs={{0,8},{2,10},{4,12},{6,14},{8,0},{10,2},{12,4},{14,6},{1,9},{3,11}... | collective-permute-start | bytes 196616 | tf_op jit(solution)/shard_map/ppermute | solution.py:430
  39.5 1.4 %collective-permute-done.11.refs_3_ = f32[64,256]{1,0:T(8,128)S(1)} collective-permute-done((f32[64,256]{1,0:T(8,128)S(1)}, f32[64,256]{1,0:T(8,128)S(1)}, u32[]{:S(2)}, u32[]{:S(2)}) %collective-permute-start.11) | collective-permute-done | bytes 65568 | tf_op jit(solution)/shard_map/ppermute | solution.py:430
  40.9 1.4 %half_sum.3 = (f32[4,64,256]{2,1,0:T(8,128)S(1)}, f32[64,256]{1,0:T(8,128)S(1)}) custom-call(s32[2]{0:T(128)S(1)} %pad_add_fusion.place, f32[2,256,256]{2,1,0:T(8,128)} %constant.33.clone.decay, f32[64,256]{1,0:T(8,128)S(1)} %get-tuple-element.52.refs_0_, f32[64,256]{1,0:T(8,128)S(1)} %collective-permute-done.9.refs_1_, ...), custom_call_target="tpu_custom_call" | custom-call | flops 1048576 | bytes 8388608 | tf_op jit(solution)/shard_map/half_sum/pallas_call | solution.py:277
  42.3 2.0 %collective-permute-start.12 = (f32[64,256]{1,0:T(8,128)S(1)}, f32[64,256]{1,0:T(8,128)S(1)}, u32[]{:S(2)}, u32[]{:S(2)}) collective-permute-start(f32[64,256]{1,0:T(8,128)S(1)} %get-tuple-element.57.near), channel_id=1, source_target_pairs={{0,8},{2,10},{4,12},{6,14},{8,0},{10,2},{12,4},{14,6},{1,9},{3,11}... | collective-permute-start | bytes 196616 | tf_op jit(solution)/shard_map/ppermute | solution.py:430
  44.3 1.5 %close.2 = (f32[64,256]{1,0:T(8,128)S(1)}, f32[64,256]{1,0:T(8,128)S(1)}, f32[64,256]{1,0:T(8,128)S(1)}, f32[64,256]{1,0:T(8,128)S(1)}) custom-call(s32[2]{0:T(128)S(1)} %pad_add_fusion.place, f32[2,256,256]{2,1,0:T(8,128)} %constant.30.clone.decay, f32[2,256,256]{2,1,0:T(8,128)} %constant.31.clone.half_decay, f32[2,256,256]{2,1,0:T(8,128)} %constant.32.clone.gain, ...), custom_call_target="tpu_custom_call" | custom-call | flops 1048576 | bytes 8388608 | tf_op jit(solution)/shard_map/close/pallas_call | solution.py:308
  45.8 0.5 collective-permute-start.5
  46.4 1.6 %collective-permute-start.6 = (f32[64,256]{1,0:T(8,128)S(1)}, f32[64,256]{1,0:T(8,128)S(1)}, u32[]{:S(2)}, u32[]{:S(2)}) collective-permute-start(f32[64,256]{1,0:T(8,128)S(1)} %get-tuple-element.46), channel_id=1, source_target_pairs={{0,4},{2,6},{4,0},{6,2},{8,12},{10,14},{12,8},{14,10},{1,5},{3,7},... | collective-permute-start | bytes 196616 | tf_op jit(solution)/shard_map/ppermute | solution.py:430
  47.9 1.4 %collective-permute-start.7 = (f32[64,256]{1,0:T(8,128)S(1)}, f32[64,256]{1,0:T(8,128)S(1)}, u32[]{:S(2)}, u32[]{:S(2)}) collective-permute-start(f32[64,256]{1,0:T(8,128)S(1)} %get-tuple-element.47), channel_id=1, source_target_pairs={{0,6},{2,4},{4,2},{6,0},{8,14},{10,12},{12,10},{14,8},{1,7},{3,5},... | collective-permute-start | bytes 196616 | tf_op jit(solution)/shard_map/ppermute | solution.py:430
  49.4 0.8 %jit_solution_.3.gain = f32[2,256,256]{2,1,0:T(8,128)} broadcast(f32[]{:T(128)} %constant.35.clone), dimensions={} | broadcast | bytes 524292 | tf_op jit(solution)
  50.2 1.5 %close.3 = (f32[64,256]{1,0:T(8,128)S(1)}, f32[64,256]{1,0:T(8,128)S(1)}, f32[64,256]{1,0:T(8,128)S(1)}, f32[64,256]{1,0:T(8,128)S(1)}) custom-call(s32[2]{0:T(128)S(1)} %pad_add_fusion.place, f32[2,256,256]{2,1,0:T(8,128)} %constant.33.clone.decay, f32[2,256,256]{2,1,0:T(8,128)} %constant.34.clone.half_decay, f32[2,256,256]{2,1,0:T(8,128)} %jit_solution_.3.gain, ...), custom_call_target="tpu_custom_call" | custom-call | flops 1048576 | bytes 8388608 | tf_op jit(solution)/shard_map/close/pallas_call | solution.py:308
  51.7 0.5 collective-permute-start.13
  52.2 1.6 %collective-permute-start.14 = (f32[64,256]{1,0:T(8,128)S(1)}, f32[64,256]{1,0:T(8,128)S(1)}, u32[]{:S(2)}, u32[]{:S(2)}) collective-permute-start(f32[64,256]{1,0:T(8,128)S(1)} %get-tuple-element.60), channel_id=1, source_target_pairs={{0,4},{2,6},{4,0},{6,2},{8,12},{10,14},{12,8},{14,10},{1,5},{3,7},... | collective-permute-start | bytes 196616 | tf_op jit(solution)/shard_map/ppermute | solution.py:430
  53.8 1.4 %collective-permute-start.15 = (f32[64,256]{1,0:T(8,128)S(1)}, f32[64,256]{1,0:T(8,128)S(1)}, u32[]{:S(2)}, u32[]{:S(2)}) collective-permute-start(f32[64,256]{1,0:T(8,128)S(1)} %get-tuple-element.61), channel_id=1, source_target_pairs={{0,6},{2,4},{4,2},{6,0},{8,14},{10,12},{12,10},{14,8},{1,7},{3,5},... | collective-permute-start | bytes 196616 | tf_op jit(solution)/shard_map/ppermute | solution.py:430
  55.3 5.5 %inverse_first.2 = (f32[16,256,128]{2,1,0:T(8,128)S(1)}, f32[16,256,128]{2,1,0:T(8,128)S(1)}) custom-call(s32[2]{0:T(128)S(1)} %pad_add_fusion.place, f32[16,2,128,256]{3,2,1,0:T(8,128)S(1)} %get-tuple-element.37.modes, bf16[2,2,768,256]{3,2,1,0:T(8,128)(2,1)} %constant.39.clone.table, f32[2,2,256,256]{3,2,1,0:T(8,128)} %constant.37.clone.decay, ...), custom_call_target="tpu_custom_call" | custom-call | flops 2147483648 | bytes 8388608 | tf_op jit(solution)/shard_map/inverse_first/pallas_call | solution.py:353
  60.8 0.1 collective-permute-start.16
  60.9 5.5 %inverse_first.3 = (f32[16,256,128]{2,1,0:T(8,128)S(1)}, f32[16,256,128]{2,1,0:T(8,128)S(1)}) custom-call(s32[2]{0:T(128)S(1)} %pad_add_fusion.place, f32[16,2,128,256]{3,2,1,0:T(8,128)S(1)} %get-tuple-element.51.modes, bf16[2,2,768,256]{3,2,1,0:T(8,128)(2,1)} %constant.39.clone.table, f32[2,2,256,256]{3,2,1,0:T(8,128)} %constant.37.clone.decay, ...), custom_call_target="tpu_custom_call" | custom-call | flops 2147483648 | bytes 8388608 | tf_op jit(solution)/shard_map/inverse_first/pallas_call | solution.py:353
  66.4 0.5 collective-permute-start.17
  66.9 3.8 %collective-permute-done.17.refs_3_ = f32[16,256,128]{2,1,0:T(8,128)S(1)} collective-permute-done((f32[16,256,128]{2,1,0:T(8,128)S(1)}, f32[16,256,128]{2,1,0:T(8,128)S(1)}, u32[]{:S(2)}, u32[]{:S(2)}) %collective-permute-start.17) | collective-permute-done | bytes 2097184 | tf_op jit(solution)/shard_map/ppermute | solution.py:425
  70.7 9.0 %inverse_second.1 = f32[256,16,512]{2,1,0:T(8,128)} custom-call(s32[2]{0:T(128)S(1)} %pad_add_fusion.place, bf16[2,768,256]{2,1,0:T(8,128)(2,1)} %constant.40.clone.own_table.other_table, bf16[2,768,256]{2,1,0:T(8,128)(2,1)} %constant.40.clone.own_table.other_table, f32[16,256,128]{2,1,0:T(8,128)S(1)} %get-tuple-element.48.refs_0_, ...), custom_call_target="tpu_custom_call" | custom-call | flops 4294967296 | bytes 8388608 | tf_op jit(solution)/shard_map/inverse_second/pallas_call | solution.py:407
  (16 shorter events, 0.0 us)
Async XLA Ops:
  11.3 4.5 %collective-permute-start = (f32[17,256,128]{2,1,0:T(8,128)S(1)}, f32[17,256,128]{2,1,0:T(8,128)S(1)}, u32[]{:S(2)}, u32[]{:S(2)}) collective-permute-start(f32[17,256,128]{2,1,0:T(8,128)S(1)} %get-tuple-element.36), channel_id=1, source_target_pairs={{0,1},{1,0},{2,3},{3,2},{4,5},{5,4},{6,7},{7,6},{8,9},{9,8},{10,11... | collective-permute-start | bytes 6684680 | tf_op jit(solution)/shard_map/ppermute | solution.py:425
  11.8 14.1 %collective-permute-start.8 = (f32[17,256,128]{2,1,0:T(8,128)S(1)}, f32[17,256,128]{2,1,0:T(8,128)S(1)}, u32[]{:S(2)}, u32[]{:S(2)}) collective-permute-start(f32[17,256,128]{2,1,0:T(8,128)S(1)} %get-tuple-element.50), channel_id=1, source_target_pairs={{0,1},{1,0},{2,3},{3,2},{4,5},{5,4},{6,7},{7,6},{8,9},{9,8},{10,11... | collective-permute-start | bytes 6684680 | tf_op jit(solution)/shard_map/ppermute | solution.py:425
  21.3 13.7 %collective-permute-start.1 = (f32[64,256]{1,0:T(8,128)S(1)}, f32[64,256]{1,0:T(8,128)S(1)}, u32[]{:S(2)}, u32[]{:S(2)}) collective-permute-start(f32[64,256]{1,0:T(8,128)S(1)} %get-tuple-element.39), channel_id=1, source_target_pairs={{0,2},{2,0},{4,6},{6,4},{8,10},{10,8},{12,14},{14,12},{1,3},{3,1},... | collective-permute-start | bytes 196616 | tf_op jit(solution)/shard_map/ppermute | solution.py:430
  24.3 10.7 %collective-permute-start.2 = (f32[64,256]{1,0:T(8,128)S(1)}, f32[64,256]{1,0:T(8,128)S(1)}, u32[]{:S(2)}, u32[]{:S(2)}) collective-permute-start(f32[64,256]{1,0:T(8,128)S(1)} %get-tuple-element.40), channel_id=1, source_target_pairs={{0,4},{2,6},{4,0},{6,2},{8,12},{10,14},{12,8},{14,10},{1,5},{3,7},... | collective-permute-start | bytes 196616 | tf_op jit(solution)/shard_map/ppermute | solution.py:430
  25.9 9.1 %collective-permute-start.3 = (f32[64,256]{1,0:T(8,128)S(1)}, f32[64,256]{1,0:T(8,128)S(1)}, u32[]{:S(2)}, u32[]{:S(2)}) collective-permute-start(f32[64,256]{1,0:T(8,128)S(1)} %get-tuple-element.41), channel_id=1, source_target_pairs={{0,6},{2,4},{4,2},{6,0},{8,14},{10,12},{12,10},{14,8},{1,7},{3,5},... | collective-permute-start | bytes 196616 | tf_op jit(solution)/shard_map/ppermute | solution.py:430
  31.5 8.0 %collective-permute-start.9 = (f32[64,256]{1,0:T(8,128)S(1)}, f32[64,256]{1,0:T(8,128)S(1)}, u32[]{:S(2)}, u32[]{:S(2)}) collective-permute-start(f32[64,256]{1,0:T(8,128)S(1)} %get-tuple-element.53), channel_id=1, source_target_pairs={{0,2},{2,0},{4,6},{6,4},{8,10},{10,8},{12,14},{14,12},{1,3},{3,1},... | collective-permute-start | bytes 196616 | tf_op jit(solution)/shard_map/ppermute | solution.py:430
  33.4 6.1 %collective-permute-start.10 = (f32[64,256]{1,0:T(8,128)S(1)}, f32[64,256]{1,0:T(8,128)S(1)}, u32[]{:S(2)}, u32[]{:S(2)}) collective-permute-start(f32[64,256]{1,0:T(8,128)S(1)} %get-tuple-element.54), channel_id=1, source_target_pairs={{0,4},{2,6},{4,0},{6,2},{8,12},{10,14},{12,8},{14,10},{1,5},{3,7},... | collective-permute-start | bytes 196616 | tf_op jit(solution)/shard_map/ppermute | solution.py:430
  35.0 5.9 %collective-permute-start.11 = (f32[64,256]{1,0:T(8,128)S(1)}, f32[64,256]{1,0:T(8,128)S(1)}, u32[]{:S(2)}, u32[]{:S(2)}) collective-permute-start(f32[64,256]{1,0:T(8,128)S(1)} %get-tuple-element.55), channel_id=1, source_target_pairs={{0,6},{2,4},{4,2},{6,0},{8,14},{10,12},{12,10},{14,8},{1,7},{3,5},... | collective-permute-start | bytes 196616 | tf_op jit(solution)/shard_map/ppermute | solution.py:430
  36.5 7.8 %collective-permute-start.4 = (f32[64,256]{1,0:T(8,128)S(1)}, f32[64,256]{1,0:T(8,128)S(1)}, u32[]{:S(2)}, u32[]{:S(2)}) collective-permute-start(f32[64,256]{1,0:T(8,128)S(1)} %get-tuple-element.43.near), channel_id=1, source_target_pairs={{0,8},{2,10},{4,12},{6,14},{8,0},{10,2},{12,4},{14,6},{1,9},{3,11}... | collective-permute-start | bytes 196616 | tf_op jit(solution)/shard_map/ppermute | solution.py:430
  42.3 7.1 %collective-permute-start.12 = (f32[64,256]{1,0:T(8,128)S(1)}, f32[64,256]{1,0:T(8,128)S(1)}, u32[]{:S(2)}, u32[]{:S(2)}) collective-permute-start(f32[64,256]{1,0:T(8,128)S(1)} %get-tuple-element.57.near), channel_id=1, source_target_pairs={{0,8},{2,10},{4,12},{6,14},{8,0},{10,2},{12,4},{14,6},{1,9},{3,11}... | collective-permute-start | bytes 196616 | tf_op jit(solution)/shard_map/ppermute | solution.py:430
  45.8 8.0 %collective-permute-start.5 = (f32[64,256]{1,0:T(8,128)S(1)}, f32[64,256]{1,0:T(8,128)S(1)}, u32[]{:S(2)}, u32[]{:S(2)}) collective-permute-start(f32[64,256]{1,0:T(8,128)S(1)} %get-tuple-element.45), channel_id=1, source_target_pairs={{0,2},{2,0},{4,6},{6,4},{8,10},{10,8},{12,14},{14,12},{1,3},{3,1},... | collective-permute-start | bytes 196616 | tf_op jit(solution)/shard_map/ppermute | solution.py:430
  46.4 8.9 %collective-permute-start.6 = (f32[64,256]{1,0:T(8,128)S(1)}, f32[64,256]{1,0:T(8,128)S(1)}, u32[]{:S(2)}, u32[]{:S(2)}) collective-permute-start(f32[64,256]{1,0:T(8,128)S(1)} %get-tuple-element.46), channel_id=1, source_target_pairs={{0,4},{2,6},{4,0},{6,2},{8,12},{10,14},{12,8},{14,10},{1,5},{3,7},... | collective-permute-start | bytes 196616 | tf_op jit(solution)/shard_map/ppermute | solution.py:430
  47.9 7.3 %collective-permute-start.7 = (f32[64,256]{1,0:T(8,128)S(1)}, f32[64,256]{1,0:T(8,128)S(1)}, u32[]{:S(2)}, u32[]{:S(2)}) collective-permute-start(f32[64,256]{1,0:T(8,128)S(1)} %get-tuple-element.47), channel_id=1, source_target_pairs={{0,6},{2,4},{4,2},{6,0},{8,14},{10,12},{12,10},{14,8},{1,7},{3,5},... | collective-permute-start | bytes 196616 | tf_op jit(solution)/shard_map/ppermute | solution.py:430
  51.7 9.1 %collective-permute-start.13 = (f32[64,256]{1,0:T(8,128)S(1)}, f32[64,256]{1,0:T(8,128)S(1)}, u32[]{:S(2)}, u32[]{:S(2)}) collective-permute-start(f32[64,256]{1,0:T(8,128)S(1)} %get-tuple-element.59), channel_id=1, source_target_pairs={{0,2},{2,0},{4,6},{6,4},{8,10},{10,8},{12,14},{14,12},{1,3},{3,1},... | collective-permute-start | bytes 196616 | tf_op jit(solution)/shard_map/ppermute | solution.py:430
  52.2 8.6 %collective-permute-start.14 = (f32[64,256]{1,0:T(8,128)S(1)}, f32[64,256]{1,0:T(8,128)S(1)}, u32[]{:S(2)}, u32[]{:S(2)}) collective-permute-start(f32[64,256]{1,0:T(8,128)S(1)} %get-tuple-element.60), channel_id=1, source_target_pairs={{0,4},{2,6},{4,0},{6,2},{8,12},{10,14},{12,8},{14,10},{1,5},{3,7},... | collective-permute-start | bytes 196616 | tf_op jit(solution)/shard_map/ppermute | solution.py:430
  53.8 7.0 %collective-permute-start.15 = (f32[64,256]{1,0:T(8,128)S(1)}, f32[64,256]{1,0:T(8,128)S(1)}, u32[]{:S(2)}, u32[]{:S(2)}) collective-permute-start(f32[64,256]{1,0:T(8,128)S(1)} %get-tuple-element.61), channel_id=1, source_target_pairs={{0,6},{2,4},{4,2},{6,0},{8,14},{10,12},{12,10},{14,8},{1,7},{3,5},... | collective-permute-start | bytes 196616 | tf_op jit(solution)/shard_map/ppermute | solution.py:430
  60.8 6.1 %collective-permute-start.16 = (f32[16,256,128]{2,1,0:T(8,128)S(1)}, f32[16,256,128]{2,1,0:T(8,128)S(1)}, u32[]{:S(2)}, u32[]{:S(2)}) collective-permute-start(f32[16,256,128]{2,1,0:T(8,128)S(1)} %get-tuple-element.63), channel_id=1, source_target_pairs={{0,1},{1,0},{2,3},{3,2},{4,5},{5,4},{6,7},{7,6},{8,9},{9,8},{10,11... | collective-permute-start | bytes 6291464 | tf_op jit(solution)/shard_map/ppermute | solution.py:425
  66.4 4.3 %collective-permute-start.17 = (f32[16,256,128]{2,1,0:T(8,128)S(1)}, f32[16,256,128]{2,1,0:T(8,128)S(1)}, u32[]{:S(2)}, u32[]{:S(2)}) collective-permute-start(f32[16,256,128]{2,1,0:T(8,128)S(1)} %get-tuple-element.64), channel_id=1, source_target_pairs={{0,1},{1,0},{2,3},{3,2},{4,5},{5,4},{6,7},{7,6},{8,9},{9,8},{10,11... | collective-permute-start | bytes 6291464 | tf_op jit(solution)/shard_map/ppermute | solution.py:425

commit v3 on v2

v3 whole, which is shorter than its diff:
```python
import functools
import math

import jax
import jax.numpy as jnp
import numpy as np
from jax import lax
from jax.experimental import pallas as pl
from jax.experimental.pallas import tpu as pltpu
from jax.sharding import PartitionSpec as P

circulant_alpha = 0.01
DIFFUSION = 2.0
REACTION_STEP = 0.5
VMEM_BYTES = 20 * 1024 * 1024
LANES = 128
SUBLANES = 8
TILE = 16
CHUNKS = 2


def sine_table(row_index, column_index, length):
    product = np.outer(row_index + 1, column_index + 1) % (2 * (length + 1))
    return math.sqrt(2.0 / (length + 1)) * np.sin(product * (math.pi / (length + 1)))


def stencil_eigen(mode_index, length):
    return 4.0 * np.sin((mode_index + 1) * (math.pi / (2.0 * (length + 1)))) ** 2


def second_tables(width):
    half = width // 2
    return np.stack([sine_table(np.arange(half), np.arange(s, width, 2), width) for s in (0, 1)])


def first_tables(total):
    rows = total // 2
    return np.stack(
        [
            np.stack(
                [sine_table(s * rows + np.arange(rows), np.arange(c, total, 2), total) for c in (0, 1)]
            )
            for s in (0, 1)
        ]
    )


def decay_tables(total, width):
    first, second = stencil_eigen(np.arange(total), total), stencil_eigen(np.arange(width), width)
    decay = 1.0 / (1.0 + DIFFUSION * (second[:, None] + first[None, :]))
    return np.stack([np.stack([decay[s::2, c::2] for c in (0, 1)]) for s in (0, 1)])


def constant(table):
    return jnp.asarray(np.asarray(table, np.float32))


def split_constant(table):
    table = np.asarray(table, np.float32)
    high = table.astype(jnp.bfloat16)
    low = (table - high.astype(np.float32)).astype(jnp.bfloat16)
    return jnp.asarray(np.concatenate([high, high, low], axis=-2))


def store_split(ref, at, lane, block):
    depth = ref.shape[-1] // 3
    width = block.shape[-1]
    high = block.astype(jnp.bfloat16)
    low = (block - high.astype(jnp.float32)).astype(jnp.bfloat16)
    for part, value in enumerate((high, low, high)):
        ref[(*at, pl.ds(part * depth + lane, width))] = value


def dot(first, second):
    return jnp.dot(first, second, preferred_element_type=jnp.float32)


def lanes_reversed(block):
    index = LANES - 1 - lax.broadcasted_iota(jnp.int32, (block.shape[0], LANES), 1)
    return jnp.take_along_axis(block, index, axis=1, mode="promise_in_bounds")


def store_rows_reversed(ref, at, start, block):
    rows, width = block.shape
    index = SUBLANES - 1 - lax.broadcasted_iota(jnp.int32, (SUBLANES, width), 0)
    for row in range(0, rows, SUBLANES):
        to = pl.multiple_of(start + rows - SUBLANES - row, SUBLANES)
        ref[at, pl.ds(to, SUBLANES), :] = jnp.take_along_axis(
            block[row : row + SUBLANES], index, axis=0, mode="promise_in_bounds"
        )


IN_VMEM = pl.BlockSpec(memory_space=pltpu.VMEM)
IN_SMEM = pl.BlockSpec(memory_space=pltpu.SMEM)


def in_hbm(array):
    return pltpu.with_memory_space_constraint(array, pltpu.HBM)


def floats(*shape):
    return jax.ShapeDtypeStruct(shape, jnp.float32)


def call(kernel, name, in_specs, out_specs, out_shape, scratch, flops, grid=None):
    if grid is None:
        spec = pl.GridSpec(
            in_specs=[IN_SMEM, *in_specs], out_specs=out_specs, scratch_shapes=scratch
        )
    else:
        spec = pltpu.PrefetchScalarGridSpec(
            num_scalar_prefetch=1,
            grid=(grid,),
            in_specs=in_specs,
            out_specs=out_specs,
            scratch_shapes=scratch,
        )
    return pl.pallas_call(
        kernel,
        grid_spec=spec,
        out_shape=out_shape,
        compiler_params=pltpu.CompilerParams(vmem_limit_bytes=VMEM_BYTES),
        cost_estimate=pl.CostEstimate(flops=flops, bytes_accessed=1 << 23, transcendentals=0),
        name=name,
    )


def forward_second_kernel(place, field, initial, own_table, other_table, *refs):
    keeps, sends, (own, other) = refs[:CHUNKS], refs[CHUNKS : 2 * CHUNKS], refs[2 * CHUNKS :]
    rows, steps, width = field.shape
    half = width // 2
    part = half // CHUNKS
    group = min(SUBLANES, steps)
    is_first = (place[0] == 0).astype(jnp.float32)
    sign = 1.0 - 2.0 * place[1].astype(jnp.float32)
    block = pl.program_id(0)
    kept_at = pl.ds(pl.multiple_of(block * rows, rows), rows)
    sent_at = (pl.num_programs(0) - 1 - block) * rows

    def put(at, lane, lower, upper):
        shape = lower.shape
        upper = sign * lanes_reversed(upper.reshape(-1, LANES)).reshape(shape)
        store_split(own, at, lane, lower + upper)
        store_split(other, at, lane, lower - upper)

    for row in range(0, rows, TILE):
        cells_at = pl.ds(row, TILE)
        for lane in range(0, half, LANES):
            lanes = (lane, width - LANES - lane)
            for step in range(0, steps, group):
                forces = []
                for at in lanes:
                    cells = field[cells_at, pl.ds(step, group), pl.ds(at, LANES)]
                    force = REACTION_STEP * (cells - cells * cells * cells)
                    force = jnp.swapaxes(force, 0, 1)
                    if step == 0:
                        head = force[:1] + is_first * initial[cells_at, pl.ds(at, LANES)][None]
                        force = jnp.concatenate([head, force[1:]], axis=0)
                    forces.append(force)
                put((pl.ds(step, group), cells_at), lane, *forces)
            ends = [field[cells_at, steps - 1, pl.ds(at, LANES)][None] for at in lanes]
            put((pl.ds(steps, 1), cells_at), lane, *ends)
    kept = dot(own[...].reshape(-1, 3 * half), own_table[0])
    sent = dot(other[...].reshape(-1, 3 * half), other_table[0])
    for chunk in range(CHUNKS):
        lanes = slice(chunk * part, (chunk + 1) * part)
        keeps[chunk][:, kept_at, :] = kept[:, lanes].reshape(steps + 1, rows, part)
        for step in range(steps + 1):
            store_rows_reversed(
                sends[chunk], step, sent_at, sent[step * rows : (step + 1) * rows, lanes]
            )


def forward_second(place, field, initial, tables):
    rows, steps, width = field.shape
    half = width // 2
    part = half // CHUNKS
    block = min(32, rows)
    table = (1, 3 * half, half)
    outs = call(
        forward_second_kernel,
        "forward_second",
        [
            pl.BlockSpec((block, steps, width), lambda i, place: (i, 0, 0)),
            pl.BlockSpec((block, width), lambda i, place: (i, 0)),
            pl.BlockSpec(table, lambda i, place: (place[1], 0, 0)),
            pl.BlockSpec(table, lambda i, place: (1 - place[1], 0, 0)),
        ],
        [IN_VMEM] * (2 * CHUNKS),
        [floats(steps + 1, rows, part)] * (2 * CHUNKS),
        [pltpu.VMEM((steps + 1, block, 3 * half), jnp.bfloat16)] * 2,
        1 << 32,
        rows // block,
    )(place, in_hbm(field), in_hbm(initial), in_hbm(tables), in_hbm(tables))
    return outs[:CHUNKS], outs[CHUNKS:]


def ranks(slabs):
    return slabs // 2


def forward_first_kernel(slabs, chunk, place, keep, got, table, decay, modes, *refs):
    size = ranks(slabs)
    lasts, (state, split, split_end) = refs[:size], refs[size:]
    steps, _, part, rows = modes.shape
    block = split.shape[1] // part
    strip = place[1]
    state[...] = jnp.zeros_like(state)
    for step in range(0, steps, block):
        for c in (0, 1):
            for at in range(block):
                near, far = keep[step + at], got[step + at]
                cells = near - far if c else near + far
                store_split(split, (c, pl.ds(at * part, part)), 0, cells.T)
            result = dot(split[c], table[strip, c])
            modes[pl.ds(step, block), c] = result.reshape(block, part, rows)
        for c in (0, 1):
            for row in range(0, part, TILE):
                tile, at_state = pl.ds(row, TILE), pl.ds(c * part + row, TILE)
                value = state[at_state]
                rate = decay[strip, c, pl.ds(chunk * part + row, TILE)]
                for at in range(block):
                    value = rate * (value + modes[step + at, c, tile])
                state[at_state] = value
    is_last = (place[0] == slabs - 1).astype(jnp.float32)
    near, far = keep[steps], got[steps]
    for c, cells in enumerate((near + far, near - far)):
        store_split(split_end, (c, slice(None)), 0, cells.T)
        at_state = pl.ds(c * part, part)
        state[at_state] = state[at_state] - is_last * dot(split_end[c], table[strip, c])
    rank = lax.rem(place[0], size)
    share = 2 * part // size
    for partner in range(size):
        at = pl.multiple_of((rank ^ partner) * share, share)
        lasts[partner][...] = state[pl.ds(at, share)]


def forward_first(place, chunk, keep, got, tables, decays, slabs):
    steps, rows, part = keep.shape
    steps = steps - 1
    block = min(8, steps)
    size = ranks(slabs)
    share = 2 * part // size
    outs = call(
        functools.partial(forward_first_kernel, slabs, chunk),
        "forward_first",
        [IN_VMEM] * 4,
        [IN_VMEM] * (1 + size),
        [floats(steps, 2, part, rows)] + [floats(share, rows)] * size,
        [
            pltpu.VMEM((2 * part, rows), jnp.float32),
            pltpu.VMEM((2, block * part, 3 * rows), jnp.bfloat16),
            pltpu.VMEM((2, part, 3 * rows), jnp.bfloat16),
        ],
        1 << 31,
    )(place, keep, got, tables, decays)
    return outs[0], outs[1:]


def half_sum_kernel(slabs, chunk, place, closing, *refs):
    size = ranks(slabs)
    lasts, ordered, total = refs[:size], refs[size], refs[size + 1]
    share = total.shape[0]
    rank = lax.rem(place[0], size)
    decay = closing[place[1], chunk, 0, pl.ds(pl.multiple_of(rank * share, share), share)]
    for partner in range(size):
        ordered[rank ^ partner] = lasts[partner][...]
    state = ordered[0]
    for at in range(1, size):
        state = ordered[at] + decay * state
    total[...] = state


def half_sum(place, chunk, lasts, closing, slabs):
    size = ranks(slabs)
    share, rows = lasts[0].shape
    return call(
        functools.partial(half_sum_kernel, slabs, chunk),
        "half_sum",
        [IN_VMEM] * (1 + size),
        [IN_VMEM] * 2,
        [floats(size, share, rows), floats(share, rows)],
        [],
        1 << 20,
    )(place, closing, *lasts)


def close_kernel(slabs, chunk, place, closing, ordered, near, far, *refs):
    size = ranks(slabs)
    befores, states = refs[:size], refs[size]
    share = near.shape[0]
    rank = lax.rem(place[0], size)
    at_share = pl.ds(pl.multiple_of(rank * share, share), share)
    decay, half_decay, gain = (closing[place[1], chunk, at, at_share] for at in range(3))
    entering = jnp.where(place[0] < size, circulant_alpha, 1.0)
    state = gain * (entering * far[...] + circulant_alpha * half_decay * near[...])
    for at in range(size):
        states[at] = state
        if at < size - 1:
            state = ordered[at] + decay * state
    for partner in range(size):
        befores[partner][...] = states[rank ^ partner]


def close(place, chunk, ordered, near, far, closing, slabs):
    size, share, rows = ordered.shape
    return call(
        functools.partial(close_kernel, slabs, chunk),
        "close",
        [IN_VMEM] * 4,
        [IN_VMEM] * size,
        [floats(share, rows)] * size,
        [pltpu.VMEM((size, share, rows), jnp.float32)],
        1 << 20,
    )(place, closing, ordered, near, far)


def inverse_first_kernel(slabs, chunk, place, modes, table, decay, *refs):
    size = ranks(slabs)
    befores, (keep, send, state, split) = refs[:size], refs[size:]
    steps, _, part, rows = modes.shape
    block = split.shape[1] // part
    strip = place[1]
    rank = lax.rem(place[0], size)
    share = 2 * part // size
    for partner in range(size):
        at = pl.multiple_of((rank ^ partner) * share, share)
        state[pl.ds(at, share)] = befores[partner][...]
    for step in range(0, steps, block):
        results = []
        for c in (0, 1):
            for row in range(0, part, TILE):
                tile, at_state = pl.ds(row, TILE), pl.ds(c * part + row, TILE)
                value = state[at_state]
                rate = decay[strip, c, pl.ds(chunk * part + row, TILE)]
                for at in range(block):
                    value = rate * (value + modes[step + at, c, tile])
                    store_split(split, (c, pl.ds(at * part + row, TILE)), 0, value)
                state[at_state] = value
            results.append(dot(split[c], table[strip, c]))
        even, odd = results
        for at in range(block):
            piece = slice(at * part, (at + 1) * part)
            keep[step + at] = (even[piece] + odd[piece]).T
            store_rows_reversed(send, step + at, 0, (even[piece] - odd[piece]).T)


def inverse_first(place, chunk, modes, befores, tables, decays, slabs):
    steps, _, part, rows = modes.shape
    block = min(8, steps)
    return call(
        functools.partial(inverse_first_kernel, slabs, chunk),
        "inverse_first",
        [IN_VMEM] * (3 + len(befores)),
        [IN_VMEM] * 2,
        [floats(steps, rows, part)] * 2,
        [
            pltpu.VMEM((2 * part, rows), jnp.float32),
            pltpu.VMEM((2, block * part, 3 * rows), jnp.bfloat16),
        ],
        1 << 31,
    )(place, modes, tables, decays, *befores)


def inverse_second_kernel(place, tables, *refs):
    keeps, gots, refs = refs[:CHUNKS], refs[CHUNKS : 2 * CHUNKS], refs[2 * CHUNKS :]
    out, own, other, own_result, other_result = refs
    rows, steps, width = out.shape
    part = keeps[0].shape[2]
    half = part * CHUNKS
    group = min(SUBLANES, steps)
    strip = place[1]
    sign = 1.0 - 2.0 * strip.astype(jnp.float32)
    start = pl.program_id(0) * rows
    for step in range(steps):
        for row in range(0, rows, TILE):
            tile = pl.ds(row, TILE)
            source = pl.ds(pl.multiple_of(start + row, TILE), TILE)
            for chunk in range(CHUNKS):
                store_split(own, (step, tile), chunk * part, keeps[chunk][step, source])
                store_split(other, (step, tile), chunk * part, gots[chunk][step, source])
    shape = own_result.shape
    own_result[...] = dot(own[...].reshape(-1, 3 * half), tables[strip]).reshape(shape)
    other_result[...] = dot(other[...].reshape(-1, 3 * half), tables[1 - strip]).reshape(shape)
    for row in range(0, rows, SUBLANES):
        for step in range(0, steps, group):
            for lane in range(0, half, LANES):
                at = (pl.ds(step, group), pl.ds(row, SUBLANES), pl.ds(lane, LANES))
                first, second = own_result[at], other_result[at]
                upper = sign * (first - second)
                upper = lanes_reversed(upper.reshape(-1, LANES)).reshape(upper.shape)
                place_at = (pl.ds(row, SUBLANES), pl.ds(step, group))
                out[(*place_at, pl.ds(lane, LANES))] = jnp.swapaxes(first + second, 0, 1)
                out[(*place_at, pl.ds(width - LANES - lane, LANES))] = jnp.swapaxes(upper, 0, 1)


def inverse_second(place, keeps, gots, tables):
    steps, rows, part = keeps[0].shape
    half = part * CHUNKS
    block = min(32, rows)
    return call(
        inverse_second_kernel,
        "inverse_second",
        [IN_VMEM] * (1 + 2 * CHUNKS),
        pl.BlockSpec((block, steps, 2 * half), lambda i, place: (i, 0, 0)),
        floats(rows, steps, 2 * half),
        [pltpu.VMEM((steps, block, 3 * half), jnp.bfloat16)] * 2
        + [pltpu.VMEM((steps, block, half), jnp.float32)] * 2,
        1 << 32,
        rows // block,
    )(place, tables, *keeps, *gots)


def swapped(block):
    return lax.ppermute(block, "space", [(0, 1), (1, 0)])


def with_partner(block, distance):
    slabs = lax.axis_size("tm")
    return lax.ppermute(block, "tm", [(slab, slab ^ distance) for slab in range(slabs)])


def among_ranks(blocks):
    return [blocks[0]] + [with_partner(block, at) for at, block in enumerate(blocks) if at]


def by_chunk(table):
    strips, _, half, rows = table.shape
    parts = table.reshape(strips, 2, CHUNKS, half // CHUNKS, rows)
    return np.swapaxes(parts, 1, 2).reshape(strips, CHUNKS, 2 * half // CHUNKS, rows)


def shards(iterate, initial):
    rows, steps, width = iterate.shape
    slabs = lax.axis_size("tm")
    total = rows * lax.axis_size("space")
    place = jnp.stack([lax.axis_index("tm"), lax.axis_index("space")]).astype(jnp.int32)
    second = second_tables(width)
    first = first_tables(total)
    decay = decay_tables(total, width)
    slab_decay = decay**steps
    half_decay = slab_decay ** ranks(slabs)
    gain = 1.0 / (1.0 - circulant_alpha * half_decay * half_decay)
    closing = constant(
        np.stack([by_chunk(table) for table in (slab_decay, half_decay, gain)], axis=2)
    )
    first_table, decays = split_constant(first), constant(decay)
    keeps, sends = forward_second(place, iterate, initial, split_constant(second))
    gots = [swapped(send) for send in sends]
    modes, befores = [], []
    for chunk in range(CHUNKS):
        own_modes, lasts = forward_first(
            place, chunk, keeps[chunk], gots[chunk], first_table, decays, slabs
        )
        modes.append(own_modes)
        ordered, near = half_sum(place, chunk, among_ranks(lasts), closing, slabs)
        far = with_partner(near, ranks(slabs))
        befores.append(among_ranks(close(place, chunk, ordered, near, far, closing, slabs)))
    inverse_table = split_constant(np.swapaxes(first, 2, 3))
    keeps, sends = zip(
        *(
            inverse_first(place, chunk, modes[chunk], befores[chunk], inverse_table, decays, slabs)
            for chunk in range(CHUNKS)
        )
    )
    gots = [swapped(send) for send in sends]
    return inverse_second(place, keeps, gots, split_constant(np.swapaxes(second, 1, 2)))


def solution(mesh):
    return jax.shard_map(
        shards,
        mesh=mesh,
        in_specs=(P(("group", "space"), "tm", None), P(("group", "space"), None)),
        out_specs=P(("group", "space"), "tm", None),
        check_vma=False,
    )
```

time: 80.1 us -> 67.6 us (0.84)
  Pallas kernels: 48.1 us -> 35.3 us
  waiting for transfers between devices: 9.11 us -> 10.3 us
  local copies, waits for them, and re-layouts: 0.83 us -> 0.02 us
    pallas_call x10, Pallas kernels: 48.1 us -> 35.3 us  [the longest x1 11.6 us: forward_second(): call(forward_second_kernel, 'forward_second', [pl.BlockSpec((block, steps...]
    ppermute x14, waiting for transfers between devices: 1.43 us -> 2.27 us  [with_partner(): lax.ppermute(block, 'tm', [(slab, slab ^ distance) for slab in range(slab...]
    another operation x1 -> x0, local copies, waits for them, and re-layouts: 0.83 us -> none
  transfers between devices with their start and end apart: 18 -> 18, of which waited for: 3 -> 5; matrix products, arithmetic and copies ran while one was open for 1% -> 0% of each run, Pallas kernels for 35% -> 23%
where the time goes in v3:
time: 67.6 us; the launch traced here: 67.3 us
  Pallas kernels  35.3 us (52%)
  starting transfers between devices  21.4 us (32%)
  waiting for transfers between devices  10.3 us (15%)
    ppermute x14, starting transfers between devices, with_partner(): lax.ppermute(block, 'tm', [(slab, slab ^ distance) for slab in range(slab...  20.7 us
    pallas_call x1, Pallas kernels, forward_second(): call(forward_second_kernel, 'forward_second', [pl.BlockSpec((block, steps...  11.6 us
    pallas_call x1, Pallas kernels, inverse_second(): call(inverse_second_kernel, 'inverse_second', [IN_VMEM] * (1 + 2 * CHUNKS...  8.35 us
    ppermute x4, waiting for transfers between devices, swapped(): return lax.ppermute(block, 'space', [(0, 1), (1, 0)])  8.04 us
    pallas_call x2, Pallas kernels, forward_first(): call(functools.partial(forward_first_kernel, slabs, chunk), 'forward_firs...  6.7 us
    pallas_call x2, Pallas kernels, inverse_first(): call(functools.partial(inverse_first_kernel, slabs, chunk), 'inverse_firs...  6.38 us
    ppermute x14, waiting for transfers between devices, with_partner(): lax.ppermute(block, 'tm', [(slab, slab ^ distance) for slab in range(slab...  2.27 us
  transfers between devices with their start and end apart: 18, of which 5 were waited for; matrix products, arithmetic and copies ran while one was open for 0% of the time, Pallas kernels for 23%

profile of v3, /device:TPU:0, one launch (start us, length us, event | category | flops | bytes accessed | tf_op | source)
XLA Modules:
  0.0 67.3 jit_solution(2382344654437571074)
XLA Ops:
  0.0 0.1 pad_add_fusion.place
  0.1 11.6 %forward_second.1 = (f32[17,256,128]{2,1,0:T(8,128)S(1)}, f32[17,256,128]{2,1,0:T(8,128)S(1)}, f32[17,256,128]{2,1,0:T(8,128)S(1)}, f32[17,256,128]{2,1,0:T(8,128)S(1)}) custom-call(s32[2]{0:T(128)S(1)} %pad_add_fusion.place, f32[256,16,512]{2,1,0:T(8,128)} %field.1, f32[256,512]{1,0:T(8,128)} %initial.1, ...), custom_call_target="tpu_custom_call" | custom-call | flops 4294967296 | bytes 8388608 | tf_op jit(solution)/shard_map/forward_second/pallas_call | solution.py:180
  11.6 0.5 collective-permute-start
  12.2 0.1 collective-permute-start.8
  12.2 3.9 %collective-permute-done.got = f32[17,256,128]{2,1,0:T(8,128)S(1)} collective-permute-done((f32[17,256,128]{2,1,0:T(8,128)S(1)}, f32[17,256,128]{2,1,0:T(8,128)S(1)}, u32[]{:S(2)}, u32[]{:S(2)}) %collective-permute-start) | collective-permute-done | bytes 2228256 | tf_op jit(solution)/shard_map/ppermute | solution.py:415
  16.1 3.3 %forward_first.2 = (f32[16,2,128,256]{3,2,1,0:T(8,128)S(1)}, f32[64,256]{1,0:T(8,128)S(1)}, f32[64,256]{1,0:T(8,128)S(1)}, f32[64,256]{1,0:T(8,128)S(1)}, f32[64,256]{1,0:T(8,128)S(1)}) custom-call(s32[2]{0:T(128)S(1)} %pad_add_fusion.place, f32[17,256,128]{2,1,0:T(8,128)S(1)} %get-tuple-element.35.keep, f32[17,256,128]{2,1,0:T(8,128)S(1)} %collective-permute-done.got, ...), custom_call_target="tpu_custom_call" | custom-call | flops 2147483648 | bytes 8388608 | tf_op jit(solution)/shard_map/forward_first/pallas_call | solution.py:244
  19.5 3.0 %collective-permute-start.1 = (f32[64,256]{1,0:T(8,128)S(1)}, f32[64,256]{1,0:T(8,128)S(1)}, u32[]{:S(2)}, u32[]{:S(2)}) collective-permute-start(f32[64,256]{1,0:T(8,128)S(1)} %get-tuple-element.39), channel_id=1, source_target_pairs={{0,2},{2,0},{4,6},{6,4},{8,10},{10,8},{12,14},{14,12},{1,3},{3,1},... | collective-permute-start | bytes 196616 | tf_op jit(solution)/shard_map/ppermute | solution.py:420
  22.5 1.6 %collective-permute-start.2 = (f32[64,256]{1,0:T(8,128)S(1)}, f32[64,256]{1,0:T(8,128)S(1)}, u32[]{:S(2)}, u32[]{:S(2)}) collective-permute-start(f32[64,256]{1,0:T(8,128)S(1)} %get-tuple-element.40), channel_id=1, source_target_pairs={{0,4},{2,6},{4,0},{6,2},{8,12},{10,14},{12,8},{14,10},{1,5},{3,7},... | collective-permute-start | bytes 196616 | tf_op jit(solution)/shard_map/ppermute | solution.py:420
  24.0 3.4 %forward_first.3 = (f32[16,2,128,256]{3,2,1,0:T(8,128)S(1)}, f32[64,256]{1,0:T(8,128)S(1)}, f32[64,256]{1,0:T(8,128)S(1)}, f32[64,256]{1,0:T(8,128)S(1)}, f32[64,256]{1,0:T(8,128)S(1)}) custom-call(s32[2]{0:T(128)S(1)} %pad_add_fusion.place, f32[17,256,128]{2,1,0:T(8,128)S(1)} %get-tuple-element.49.keep, f32[17,256,128]{2,1,0:T(8,128)S(1)} %collective-permute-done.8.got, ...), custom_call_target="tpu_custom_call" | custom-call | flops 2147483648 | bytes 8388608 | tf_op jit(solution)/shard_map/forward_first/pallas_call | solution.py:244
  27.4 2.0 %collective-permute-start.9 = (f32[64,256]{1,0:T(8,128)S(1)}, f32[64,256]{1,0:T(8,128)S(1)}, u32[]{:S(2)}, u32[]{:S(2)}) collective-permute-start(f32[64,256]{1,0:T(8,128)S(1)} %get-tuple-element.53), channel_id=1, source_target_pairs={{0,2},{2,0},{4,6},{6,4},{8,10},{10,8},{12,14},{14,12},{1,3},{3,1},... | collective-permute-start | bytes 196616 | tf_op jit(solution)/shard_map/ppermute | solution.py:420
  29.4 1.6 %collective-permute-start.10 = (f32[64,256]{1,0:T(8,128)S(1)}, f32[64,256]{1,0:T(8,128)S(1)}, u32[]{:S(2)}, u32[]{:S(2)}) collective-permute-start(f32[64,256]{1,0:T(8,128)S(1)} %get-tuple-element.54), channel_id=1, source_target_pairs={{0,4},{2,6},{4,0},{6,2},{8,12},{10,14},{12,8},{14,10},{1,5},{3,7},... | collective-permute-start | bytes 196616 | tf_op jit(solution)/shard_map/ppermute | solution.py:420
  31.0 0.6 half_sum.2
  31.6 3.0 %collective-permute-start.4 = (f32[64,256]{1,0:T(8,128)S(1)}, f32[64,256]{1,0:T(8,128)S(1)}, u32[]{:S(2)}, u32[]{:S(2)}) collective-permute-start(f32[64,256]{1,0:T(8,128)S(1)} %get-tuple-element.43.near), channel_id=1, source_target_pairs={{0,8},{2,10},{4,12},{6,14},{8,0},{10,2},{12,4},{14,6},{1,9},{3,11}... | collective-permute-start | bytes 196616 | tf_op jit(solution)/shard_map/ppermute | solution.py:420
  34.6 1.7 %collective-permute-done.11.refs_3_ = f32[64,256]{1,0:T(8,128)S(1)} collective-permute-done((f32[64,256]{1,0:T(8,128)S(1)}, f32[64,256]{1,0:T(8,128)S(1)}, u32[]{:S(2)}, u32[]{:S(2)}) %collective-permute-start.11) | collective-permute-done | bytes 65568 | tf_op jit(solution)/shard_map/ppermute | solution.py:420
  36.3 0.6 half_sum.3
  36.9 2.4 %collective-permute-start.12 = (f32[64,256]{1,0:T(8,128)S(1)}, f32[64,256]{1,0:T(8,128)S(1)}, u32[]{:S(2)}, u32[]{:S(2)}) collective-permute-start(f32[64,256]{1,0:T(8,128)S(1)} %get-tuple-element.57.near), channel_id=1, source_target_pairs={{0,8},{2,10},{4,12},{6,14},{8,0},{10,2},{12,4},{14,6},{1,9},{3,11}... | collective-permute-start | bytes 196616 | tf_op jit(solution)/shard_map/ppermute | solution.py:420
  39.4 0.6 close.2
  40.0 0.6 collective-permute-start.5
  40.6 1.6 %collective-permute-start.6 = (f32[64,256]{1,0:T(8,128)S(1)}, f32[64,256]{1,0:T(8,128)S(1)}, u32[]{:S(2)}, u32[]{:S(2)}) collective-permute-start(f32[64,256]{1,0:T(8,128)S(1)} %get-tuple-element.46), channel_id=1, source_target_pairs={{0,4},{2,6},{4,0},{6,2},{8,12},{10,14},{12,8},{14,10},{1,5},{3,7},... | collective-permute-start | bytes 196616 | tf_op jit(solution)/shard_map/ppermute | solution.py:420
  42.2 1.4 %collective-permute-start.7 = (f32[64,256]{1,0:T(8,128)S(1)}, f32[64,256]{1,0:T(8,128)S(1)}, u32[]{:S(2)}, u32[]{:S(2)}) collective-permute-start(f32[64,256]{1,0:T(8,128)S(1)} %get-tuple-element.47), channel_id=1, source_target_pairs={{0,6},{2,4},{4,2},{6,0},{8,14},{10,12},{12,10},{14,8},{1,7},{3,5},... | collective-permute-start | bytes 196616 | tf_op jit(solution)/shard_map/ppermute | solution.py:420
  43.6 0.6 close.3
  44.2 0.6 collective-permute-start.13
  44.7 1.6 %collective-permute-start.14 = (f32[64,256]{1,0:T(8,128)S(1)}, f32[64,256]{1,0:T(8,128)S(1)}, u32[]{:S(2)}, u32[]{:S(2)}) collective-permute-start(f32[64,256]{1,0:T(8,128)S(1)} %get-tuple-element.60), channel_id=1, source_target_pairs={{0,4},{2,6},{4,0},{6,2},{8,12},{10,14},{12,8},{14,10},{1,5},{3,7},... | collective-permute-start | bytes 196616 | tf_op jit(solution)/shard_map/ppermute | solution.py:420
  46.4 1.4 %collective-permute-start.15 = (f32[64,256]{1,0:T(8,128)S(1)}, f32[64,256]{1,0:T(8,128)S(1)}, u32[]{:S(2)}, u32[]{:S(2)}) collective-permute-start(f32[64,256]{1,0:T(8,128)S(1)} %get-tuple-element.61), channel_id=1, source_target_pairs={{0,6},{2,4},{4,2},{6,0},{8,14},{10,12},{12,10},{14,8},{1,7},{3,5},... | collective-permute-start | bytes 196616 | tf_op jit(solution)/shard_map/ppermute | solution.py:420
  47.7 3.2 %inverse_first.2 = (f32[16,256,128]{2,1,0:T(8,128)S(1)}, f32[16,256,128]{2,1,0:T(8,128)S(1)}) custom-call(s32[2]{0:T(128)S(1)} %pad_add_fusion.place, f32[16,2,128,256]{3,2,1,0:T(8,128)S(1)} %get-tuple-element.37.modes, bf16[2,2,768,256]{3,2,1,0:T(8,128)(2,1)S(1)} %copy-done.2, f32[2,2,256,256]{3,2,1,0:T(8,128)S(1)} %copy-done.4, ...), custom_call_target="tpu_custom_call" | custom-call | flops 2147483648 | bytes 8388608 | tf_op jit(solution)/shard_map/inverse_first/pallas_call | solution.py:351
  50.9 0.1 collective-permute-start.16
  51.0 0.5 collective-permute-done.15.refs_3_
  51.5 3.2 %inverse_first.3 = (f32[16,256,128]{2,1,0:T(8,128)S(1)}, f32[16,256,128]{2,1,0:T(8,128)S(1)}) custom-call(s32[2]{0:T(128)S(1)} %pad_add_fusion.place, f32[16,2,128,256]{3,2,1,0:T(8,128)S(1)} %get-tuple-element.51.modes, bf16[2,2,768,256]{3,2,1,0:T(8,128)(2,1)S(1)} %copy-done.2, f32[2,2,256,256]{3,2,1,0:T(8,128)S(1)} %copy-done.4, ...), custom_call_target="tpu_custom_call" | custom-call | flops 2147483648 | bytes 8388608 | tf_op jit(solution)/shard_map/inverse_first/pallas_call | solution.py:351
  54.7 0.1 collective-permute-start.17
  54.8 0.4 collective-permute-done.16.refs_2_
  55.2 3.8 %collective-permute-done.17.refs_3_ = f32[16,256,128]{2,1,0:T(8,128)S(1)} collective-permute-done((f32[16,256,128]{2,1,0:T(8,128)S(1)}, f32[16,256,128]{2,1,0:T(8,128)S(1)}, u32[]{:S(2)}, u32[]{:S(2)}) %collective-permute-start.17) | collective-permute-done | bytes 2097184 | tf_op jit(solution)/shard_map/ppermute | solution.py:415
  58.9 8.4 %inverse_second.1 = f32[256,16,512]{2,1,0:T(8,128)} custom-call(s32[2]{0:T(128)S(1)} %pad_add_fusion.place, bf16[2,768,256]{2,1,0:T(8,128)(2,1)S(1)} %copy-done.1, f32[16,256,128]{2,1,0:T(8,128)S(1)} %get-tuple-element.48.refs_0_, f32[16,256,128]{2,1,0:T(8,128)S(1)} %get-tuple-element.62.refs_1_, f32[16,256,128]{2,1,0:T(8,128)S(1)} %collective-permute-done.16.refs_2_, ...), custom_call_target="tpu_custom_call" | custom-call | flops 4294967296 | bytes 8388608 | tf_op jit(solution)/shard_map/inverse_second/pallas_call | solution.py:401
  (25 shorter events, 0.1 us)
Async XLA Ops:
  0.1 16.1 %copy-start.3 = (bf16[2,2,768,256]{3,2,1,0:T(8,128)(2,1)S(1)}, bf16[2,2,768,256]{3,2,1,0:T(8,128)(2,1)}, u32[]{:S(2)}) copy-start(bf16[2,2,768,256]{3,2,1,0:T(8,128)(2,1)} %constant.21.clone.table) | copy-start | bytes 4718596
  0.1 16.1 %copy-start.4 = (f32[2,2,256,256]{3,2,1,0:T(8,128)S(1)}, f32[2,2,256,256]{3,2,1,0:T(8,128)}, u32[]{:S(2)}) copy-start(f32[2,2,256,256]{3,2,1,0:T(8,128)} %constant.22.clone.decay) | copy-start | bytes 3145732
  11.6 4.5 %collective-permute-start = (f32[17,256,128]{2,1,0:T(8,128)S(1)}, f32[17,256,128]{2,1,0:T(8,128)S(1)}, u32[]{:S(2)}, u32[]{:S(2)}) collective-permute-start(f32[17,256,128]{2,1,0:T(8,128)S(1)} %get-tuple-element.36), channel_id=1, source_target_pairs={{0,1},{1,0},{2,3},{3,2},{4,5},{5,4},{6,7},{7,6},{8,9},{9,8},{10,11... | collective-permute-start | bytes 6684680 | tf_op jit(solution)/shard_map/ppermute | solution.py:415
  12.2 11.9 %collective-permute-start.8 = (f32[17,256,128]{2,1,0:T(8,128)S(1)}, f32[17,256,128]{2,1,0:T(8,128)S(1)}, u32[]{:S(2)}, u32[]{:S(2)}) collective-permute-start(f32[17,256,128]{2,1,0:T(8,128)S(1)} %get-tuple-element.50), channel_id=1, source_target_pairs={{0,1},{1,0},{2,3},{3,2},{4,5},{5,4},{6,7},{7,6},{8,9},{9,8},{10,11... | collective-permute-start | bytes 6684680 | tf_op jit(solution)/shard_map/ppermute | solution.py:415
  19.5 11.5 %collective-permute-start.1 = (f32[64,256]{1,0:T(8,128)S(1)}, f32[64,256]{1,0:T(8,128)S(1)}, u32[]{:S(2)}, u32[]{:S(2)}) collective-permute-start(f32[64,256]{1,0:T(8,128)S(1)} %get-tuple-element.39), channel_id=1, source_target_pairs={{0,2},{2,0},{4,6},{6,4},{8,10},{10,8},{12,14},{14,12},{1,3},{3,1},... | collective-permute-start | bytes 196616 | tf_op jit(solution)/shard_map/ppermute | solution.py:420
  22.5 8.5 %collective-permute-start.2 = (f32[64,256]{1,0:T(8,128)S(1)}, f32[64,256]{1,0:T(8,128)S(1)}, u32[]{:S(2)}, u32[]{:S(2)}) collective-permute-start(f32[64,256]{1,0:T(8,128)S(1)} %get-tuple-element.40), channel_id=1, source_target_pairs={{0,4},{2,6},{4,0},{6,2},{8,12},{10,14},{12,8},{14,10},{1,5},{3,7},... | collective-permute-start | bytes 196616 | tf_op jit(solution)/shard_map/ppermute | solution.py:420
  24.0 6.9 %collective-permute-start.3 = (f32[64,256]{1,0:T(8,128)S(1)}, f32[64,256]{1,0:T(8,128)S(1)}, u32[]{:S(2)}, u32[]{:S(2)}) collective-permute-start(f32[64,256]{1,0:T(8,128)S(1)} %get-tuple-element.41), channel_id=1, source_target_pairs={{0,6},{2,4},{4,2},{6,0},{8,14},{10,12},{12,10},{14,8},{1,7},{3,5},... | collective-permute-start | bytes 196616 | tf_op jit(solution)/shard_map/ppermute | solution.py:420
  24.0 6.9 %copy-start = (f32[2,2,3,256,256]{4,3,2,1,0:T(8,128)S(1)}, f32[2,2,3,256,256]{4,3,2,1,0:T(8,128)}, u32[]{:S(2)}) copy-start(f32[2,2,3,256,256]{4,3,2,1,0:T(8,128)} %constant.20.clone.closing) | copy-start | bytes 9437188
  27.4 7.2 %collective-permute-start.9 = (f32[64,256]{1,0:T(8,128)S(1)}, f32[64,256]{1,0:T(8,128)S(1)}, u32[]{:S(2)}, u32[]{:S(2)}) collective-permute-start(f32[64,256]{1,0:T(8,128)S(1)} %get-tuple-element.53), channel_id=1, source_target_pairs={{0,2},{2,0},{4,6},{6,4},{8,10},{10,8},{12,14},{14,12},{1,3},{3,1},... | collective-permute-start | bytes 196616 | tf_op jit(solution)/shard_map/ppermute | solution.py:420
  29.4 5.2 %collective-permute-start.10 = (f32[64,256]{1,0:T(8,128)S(1)}, f32[64,256]{1,0:T(8,128)S(1)}, u32[]{:S(2)}, u32[]{:S(2)}) collective-permute-start(f32[64,256]{1,0:T(8,128)S(1)} %get-tuple-element.54), channel_id=1, source_target_pairs={{0,4},{2,6},{4,0},{6,2},{8,12},{10,14},{12,8},{14,10},{1,5},{3,7},... | collective-permute-start | bytes 196616 | tf_op jit(solution)/shard_map/ppermute | solution.py:420
  31.0 5.4 %collective-permute-start.11 = (f32[64,256]{1,0:T(8,128)S(1)}, f32[64,256]{1,0:T(8,128)S(1)}, u32[]{:S(2)}, u32[]{:S(2)}) collective-permute-start(f32[64,256]{1,0:T(8,128)S(1)} %get-tuple-element.55), channel_id=1, source_target_pairs={{0,6},{2,4},{4,2},{6,0},{8,14},{10,12},{12,10},{14,8},{1,7},{3,5},... | collective-permute-start | bytes 196616 | tf_op jit(solution)/shard_map/ppermute | solution.py:420
  31.6 7.8 %collective-permute-start.4 = (f32[64,256]{1,0:T(8,128)S(1)}, f32[64,256]{1,0:T(8,128)S(1)}, u32[]{:S(2)}, u32[]{:S(2)}) collective-permute-start(f32[64,256]{1,0:T(8,128)S(1)} %get-tuple-element.43.near), channel_id=1, source_target_pairs={{0,8},{2,10},{4,12},{6,14},{8,0},{10,2},{12,4},{14,6},{1,9},{3,11}... | collective-permute-start | bytes 196616 | tf_op jit(solution)/shard_map/ppermute | solution.py:420
  36.9 6.6 %collective-permute-start.12 = (f32[64,256]{1,0:T(8,128)S(1)}, f32[64,256]{1,0:T(8,128)S(1)}, u32[]{:S(2)}, u32[]{:S(2)}) collective-permute-start(f32[64,256]{1,0:T(8,128)S(1)} %get-tuple-element.57.near), channel_id=1, source_target_pairs={{0,8},{2,10},{4,12},{6,14},{8,0},{10,2},{12,4},{14,6},{1,9},{3,11}... | collective-permute-start | bytes 196616 | tf_op jit(solution)/shard_map/ppermute | solution.py:420
  40.0 7.7 %copy-start.2 = (bf16[2,2,768,256]{3,2,1,0:T(8,128)(2,1)S(1)}, bf16[2,2,768,256]{3,2,1,0:T(8,128)(2,1)}, u32[]{:S(2)}) copy-start(bf16[2,2,768,256]{3,2,1,0:T(8,128)(2,1)} %constant.24.clone.table) | copy-start | bytes 4718596
  40.0 6.4 %collective-permute-start.5 = (f32[64,256]{1,0:T(8,128)S(1)}, f32[64,256]{1,0:T(8,128)S(1)}, u32[]{:S(2)}, u32[]{:S(2)}) collective-permute-start(f32[64,256]{1,0:T(8,128)S(1)} %get-tuple-element.45), channel_id=1, source_target_pairs={{0,2},{2,0},{4,6},{6,4},{8,10},{10,8},{12,14},{14,12},{1,3},{3,1},... | collective-permute-start | bytes 196616 | tf_op jit(solution)/shard_map/ppermute | solution.py:420
  40.6 7.2 %collective-permute-start.6 = (f32[64,256]{1,0:T(8,128)S(1)}, f32[64,256]{1,0:T(8,128)S(1)}, u32[]{:S(2)}, u32[]{:S(2)}) collective-permute-start(f32[64,256]{1,0:T(8,128)S(1)} %get-tuple-element.46), channel_id=1, source_target_pairs={{0,4},{2,6},{4,0},{6,2},{8,12},{10,14},{12,8},{14,10},{1,5},{3,7},... | collective-permute-start | bytes 196616 | tf_op jit(solution)/shard_map/ppermute | solution.py:420
  42.2 5.5 %collective-permute-start.7 = (f32[64,256]{1,0:T(8,128)S(1)}, f32[64,256]{1,0:T(8,128)S(1)}, u32[]{:S(2)}, u32[]{:S(2)}) collective-permute-start(f32[64,256]{1,0:T(8,128)S(1)} %get-tuple-element.47), channel_id=1, source_target_pairs={{0,6},{2,4},{4,2},{6,0},{8,14},{10,12},{12,10},{14,8},{1,7},{3,5},... | collective-permute-start | bytes 196616 | tf_op jit(solution)/shard_map/ppermute | solution.py:420
  44.2 6.8 %collective-permute-start.13 = (f32[64,256]{1,0:T(8,128)S(1)}, f32[64,256]{1,0:T(8,128)S(1)}, u32[]{:S(2)}, u32[]{:S(2)}) collective-permute-start(f32[64,256]{1,0:T(8,128)S(1)} %get-tuple-element.59), channel_id=1, source_target_pairs={{0,2},{2,0},{4,6},{6,4},{8,10},{10,8},{12,14},{14,12},{1,3},{3,1},... | collective-permute-start | bytes 196616 | tf_op jit(solution)/shard_map/ppermute | solution.py:420
  44.7 6.3 %collective-permute-start.14 = (f32[64,256]{1,0:T(8,128)S(1)}, f32[64,256]{1,0:T(8,128)S(1)}, u32[]{:S(2)}, u32[]{:S(2)}) collective-permute-start(f32[64,256]{1,0:T(8,128)S(1)} %get-tuple-element.60), channel_id=1, source_target_pairs={{0,4},{2,6},{4,0},{6,2},{8,12},{10,14},{12,8},{14,10},{1,5},{3,7},... | collective-permute-start | bytes 196616 | tf_op jit(solution)/shard_map/ppermute | solution.py:420
  46.4 5.2 %collective-permute-start.15 = (f32[64,256]{1,0:T(8,128)S(1)}, f32[64,256]{1,0:T(8,128)S(1)}, u32[]{:S(2)}, u32[]{:S(2)}) collective-permute-start(f32[64,256]{1,0:T(8,128)S(1)} %get-tuple-element.61), channel_id=1, source_target_pairs={{0,6},{2,4},{4,2},{6,0},{8,14},{10,12},{12,10},{14,8},{1,7},{3,5},... | collective-permute-start | bytes 196616 | tf_op jit(solution)/shard_map/ppermute | solution.py:420
  50.9 4.2 %collective-permute-start.16 = (f32[16,256,128]{2,1,0:T(8,128)S(1)}, f32[16,256,128]{2,1,0:T(8,128)S(1)}, u32[]{:S(2)}, u32[]{:S(2)}) collective-permute-start(f32[16,256,128]{2,1,0:T(8,128)S(1)} %get-tuple-element.63), channel_id=1, source_target_pairs={{0,1},{1,0},{2,3},{3,2},{4,5},{5,4},{6,7},{7,6},{8,9},{9,8},{10,11... | collective-permute-start | bytes 6291464 | tf_op jit(solution)/shard_map/ppermute | solution.py:415
  51.5 7.4 %copy-start.1 = (bf16[2,768,256]{2,1,0:T(8,128)(2,1)S(1)}, bf16[2,768,256]{2,1,0:T(8,128)(2,1)}, u32[]{:S(2)}) copy-start(bf16[2,768,256]{2,1,0:T(8,128)(2,1)} %constant.25.clone.tables) | copy-start | bytes 2359300
  54.7 4.2 %collective-permute-start.17 = (f32[16,256,128]{2,1,0:T(8,128)S(1)}, f32[16,256,128]{2,1,0:T(8,128)S(1)}, u32[]{:S(2)}, u32[]{:S(2)}) collective-permute-start(f32[16,256,128]{2,1,0:T(8,128)S(1)} %get-tuple-element.64), channel_id=1, source_target_pairs={{0,1},{1,0},{2,3},{3,2},{4,5},{5,4},{6,7},{7,6},{8,9},{9,8},{10,11... | collective-permute-start | bytes 6291464 | tf_op jit(solution)/shard_map/ppermute | solution.py:415

commit v4 on v3

--- a/solution.py
+++ b/solution.py
@@ -12,7 +12,7 @@
 circulant_alpha = 0.01
 DIFFUSION = 2.0
 REACTION_STEP = 0.5
-VMEM_BYTES = 20 * 1024 * 1024
+VMEM_BYTES = 24 * 1024 * 1024
 LANES = 128
 SUBLANES = 8
 TILE = 16
@@ -80,12 +80,12 @@
     return jnp.take_along_axis(block, index, axis=1, mode="promise_in_bounds")
 
 
-def store_rows_reversed(ref, at, start, block):
+def store_rows_reversed(ref, start, block):
     rows, width = block.shape
     index = SUBLANES - 1 - lax.broadcasted_iota(jnp.int32, (SUBLANES, width), 0)
     for row in range(0, rows, SUBLANES):
         to = pl.multiple_of(start + rows - SUBLANES - row, SUBLANES)
-        ref[at, pl.ds(to, SUBLANES), :] = jnp.take_along_axis(
+        ref[pl.ds(to, SUBLANES), :] = jnp.take_along_axis(
             block[row : row + SUBLANES], index, axis=0, mode="promise_in_bounds"
         )
 
@@ -126,57 +126,63 @@
 
 
 def forward_second_kernel(place, field, initial, own_table, other_table, *refs):
-    keeps, sends, (own, other) = refs[:CHUNKS], refs[CHUNKS : 2 * CHUNKS], refs[2 * CHUNKS :]
+    keeps, sends, scratch = refs[:CHUNKS], refs[CHUNKS : 2 * CHUNKS], refs[2 * CHUNKS :]
     rows, steps, width = field.shape
     half = width // 2
     part = half // CHUNKS
-    group = min(SUBLANES, steps)
+    count = len(scratch) // 2
+    piece = rows // count
+    group = max(TILE // steps, 1)
+    total = rows * pl.num_programs(0)
+    start = pl.program_id(0) * rows
+    mirror = total - rows - start
     is_first = (place[0] == 0).astype(jnp.float32)
     sign = 1.0 - 2.0 * place[1].astype(jnp.float32)
-    block = pl.program_id(0)
-    kept_at = pl.ds(pl.multiple_of(block * rows, rows), rows)
-    sent_at = (pl.num_programs(0) - 1 - block) * rows
-
-    def put(at, lane, lower, upper):
-        shape = lower.shape
-        upper = sign * lanes_reversed(upper.reshape(-1, LANES)).reshape(shape)
-        store_split(own, at, lane, lower + upper)
-        store_split(other, at, lane, lower - upper)
-
-    for row in range(0, rows, TILE):
-        cells_at = pl.ds(row, TILE)
-        for lane in range(0, half, LANES):
-            lanes = (lane, width - LANES - lane)
-            for step in range(0, steps, group):
-                forces = []
-                for at in lanes:
-                    cells = field[cells_at, pl.ds(step, group), pl.ds(at, LANES)]
-                    force = REACTION_STEP * (cells - cells * cells * cells)
-                    force = jnp.swapaxes(force, 0, 1)
-                    if step == 0:
-                        head = force[:1] + is_first * initial[cells_at, pl.ds(at, LANES)][None]
-                        force = jnp.concatenate([head, force[1:]], axis=0)
-                    forces.append(force)
-                put((pl.ds(step, group), cells_at), lane, *forces)
-            ends = [field[cells_at, steps - 1, pl.ds(at, LANES)][None] for at in lanes]
-            put((pl.ds(steps, 1), cells_at), lane, *ends)
-    kept = dot(own[...].reshape(-1, 3 * half), own_table[0])
-    sent = dot(other[...].reshape(-1, 3 * half), other_table[0])
-    for chunk in range(CHUNKS):
-        lanes = slice(chunk * part, (chunk + 1) * part)
-        keeps[chunk][:, kept_at, :] = kept[:, lanes].reshape(steps + 1, rows, part)
-        for step in range(steps + 1):
-            store_rows_reversed(
-                sends[chunk], step, sent_at, sent[step * rows : (step + 1) * rows, lanes]
-            )
+    ones = lax.broadcasted_iota(jnp.int32, (group, steps, width), 1) == 0
+    ones = jnp.where(ones, is_first, 0.0)
+
+    def put(own, other, at, cells):
+        lower = cells[:, :half]
+        upper = jnp.concatenate(
+            [lanes_reversed(cells[:, lane : lane + LANES]) for lane in range(half, width, LANES)][::-1],
+            axis=1,
+        )
+        store_split(own, (pl.ds(at, TILE),), 0, lower + sign * upper)
+        store_split(other, (pl.ds(at, TILE),), 0, lower - sign * upper)
+
+    for sub in range(count):
+        own, other = scratch[2 * sub : 2 * sub + 2]
+        for row in range(0, piece, group):
+            at = pl.ds(sub * piece + row, group)
+            cells = field[at]
+            force = REACTION_STEP * (cells - cells * cells * cells) + ones * initial[at][:, None, :]
+            put(own, other, row * steps, force.reshape(TILE, width))
+        for row in range(0, piece, TILE):
+            ends = field[pl.ds(sub * piece + row, TILE), steps - 1, :]
+            put(own, other, piece * steps + row, ends)
+        kept = dot(own[...], own_table[0])
+        sent = dot(other[...], other_table[0])
+        body = piece * steps
+        kept_at = pl.multiple_of(start + sub * piece, piece)
+        sent_at = pl.multiple_of(mirror + (count - 1 - sub) * piece, piece)
+        for chunk in range(CHUNKS):
+            keep, send = keeps[chunk], sends[chunk]
+            lanes = slice(chunk * part, (chunk + 1) * part)
+            keep[pl.ds(pl.multiple_of(kept_at * steps, body), body), :] = kept[:body, lanes]
+            keep[pl.ds(total * steps + kept_at, piece), :] = kept[body:, lanes]
+            base = pl.multiple_of(sent_at * steps, body)
+            for row in range(piece):
+                line = sent[row * steps : (row + 1) * steps, lanes]
+                send[pl.ds(base + (piece - 1 - row) * steps, steps), :] = line
+            store_rows_reversed(send, total * steps + sent_at, sent[body:, lanes])
 
 
 def forward_second(place, field, initial, tables):
     rows, steps, width = field.shape
     half = width // 2
-    part = half // CHUNKS
-    block = min(32, rows)
+    block, pieces = min(64, rows), 2
     table = (1, 3 * half, half)
+    depth = (steps + 1) * block // pieces
     outs = call(
         forward_second_kernel,
         "forward_second",
@@ -187,8 +193,8 @@
             pl.BlockSpec(table, lambda i, place: (1 - place[1], 0, 0)),
         ],
         [IN_VMEM] * (2 * CHUNKS),
-        [floats(steps + 1, rows, part)] * (2 * CHUNKS),
-        [pltpu.VMEM((steps + 1, block, 3 * half), jnp.bfloat16)] * 2,
+        [floats((steps + 1) * rows, half // CHUNKS)] * (2 * CHUNKS),
+        [pltpu.VMEM((depth, 3 * half), jnp.bfloat16)] * (2 * pieces),
         1 << 32,
         rows // block,
     )(place, in_hbm(field), in_hbm(initial), in_hbm(tables), in_hbm(tables))
@@ -209,7 +215,8 @@
     for step in range(0, steps, block):
         for c in (0, 1):
             for at in range(block):
-                near, far = keep[step + at], got[step + at]
+                cells_at = pl.ds(step + at, rows, stride=steps)
+                near, far = keep[cells_at, :], got[cells_at, :]
                 cells = near - far if c else near + far
                 store_split(split, (c, pl.ds(at * part, part)), 0, cells.T)
             result = dot(split[c], table[strip, c])
@@ -223,7 +230,7 @@
                     value = rate * (value + modes[step + at, c, tile])
                 state[at_state] = value
     is_last = (place[0] == slabs - 1).astype(jnp.float32)
-    near, far = keep[steps], got[steps]
+    near, far = keep[pl.ds(rows * steps, rows)], got[pl.ds(rows * steps, rows)]
     for c, cells in enumerate((near + far, near - far)):
         store_split(split_end, (c, slice(None)), 0, cells.T)
         at_state = pl.ds(c * part, part)
@@ -236,8 +243,8 @@
 
 
 def forward_first(place, chunk, keep, got, tables, decays, slabs):
-    steps, rows, part = keep.shape
-    steps = steps - 1
+    rows, part = tables.shape[-1], keep.shape[1]
+    steps = keep.shape[0] // rows - 1
     block = min(8, steps)
     size = ranks(slabs)
     share = 2 * part // size
@@ -341,8 +348,9 @@
         even, odd = results
         for at in range(block):
             piece = slice(at * part, (at + 1) * part)
-            keep[step + at] = (even[piece] + odd[piece]).T
-            store_rows_reversed(send, step + at, 0, (even[piece] - odd[piece]).T)
+            cells_at = pl.ds(step + at, rows, stride=steps)
+            keep[cells_at, :] = (even[piece] + odd[piece]).T
+            send[cells_at, :] = (even[piece] - odd[piece]).T
 
 
 def inverse_first(place, chunk, modes, befores, tables, decays, slabs):
@@ -353,7 +361,7 @@
         "inverse_first",
         [IN_VMEM] * (3 + len(befores)),
         [IN_VMEM] * 2,
-        [floats(steps, rows, part)] * 2,
+        [floats(steps * rows, part)] * 2,
         [
             pltpu.VMEM((2 * part, rows), jnp.float32),
             pltpu.VMEM((2, block * part, 3 * rows), jnp.bfloat16),
@@ -364,48 +372,61 @@
 
 def inverse_second_kernel(place, tables, *refs):
     keeps, gots, refs = refs[:CHUNKS], refs[CHUNKS : 2 * CHUNKS], refs[2 * CHUNKS :]
-    out, own, other, own_result, other_result = refs
+    out, scratch = refs[0], refs[1:]
     rows, steps, width = out.shape
-    part = keeps[0].shape[2]
+    part = keeps[0].shape[1]
     half = part * CHUNKS
-    group = min(SUBLANES, steps)
+    count = len(scratch) // 4
+    piece = rows // count
+    group = max(TILE // steps, 1)
     strip = place[1]
     sign = 1.0 - 2.0 * strip.astype(jnp.float32)
+    total = rows * pl.num_programs(0)
     start = pl.program_id(0) * rows
-    for step in range(steps):
-        for row in range(0, rows, TILE):
-            tile = pl.ds(row, TILE)
-            source = pl.ds(pl.multiple_of(start + row, TILE), TILE)
+    mirror = total - rows - start
+    for sub in range(count):
+        own, other, own_result, other_result = scratch[4 * sub : 4 * sub + 4]
+        kept_at = pl.multiple_of((start + sub * piece) * steps, piece * steps)
+        sent_at = pl.multiple_of((mirror + (count - 1 - sub) * piece) * steps, piece * steps)
+        for row in range(0, piece, group):
+            to = (pl.ds(row * steps, TILE),)
             for chunk in range(CHUNKS):
-                store_split(own, (step, tile), chunk * part, keeps[chunk][step, source])
-                store_split(other, (step, tile), chunk * part, gots[chunk][step, source])
-    shape = own_result.shape
-    own_result[...] = dot(own[...].reshape(-1, 3 * half), tables[strip]).reshape(shape)
-    other_result[...] = dot(other[...].reshape(-1, 3 * half), tables[1 - strip]).reshape(shape)
-    for row in range(0, rows, SUBLANES):
-        for step in range(0, steps, group):
-            for lane in range(0, half, LANES):
-                at = (pl.ds(step, group), pl.ds(row, SUBLANES), pl.ds(lane, LANES))
-                first, second = own_result[at], other_result[at]
-                upper = sign * (first - second)
-                upper = lanes_reversed(upper.reshape(-1, LANES)).reshape(upper.shape)
-                place_at = (pl.ds(row, SUBLANES), pl.ds(step, group))
-                out[(*place_at, pl.ds(lane, LANES))] = jnp.swapaxes(first + second, 0, 1)
-                out[(*place_at, pl.ds(width - LANES - lane, LANES))] = jnp.swapaxes(upper, 0, 1)
-
-
-def inverse_second(place, keeps, gots, tables):
-    steps, rows, part = keeps[0].shape
+                store_split(own, to, chunk * part, keeps[chunk][pl.ds(kept_at + row * steps, TILE)])
+                lines = [
+                    gots[chunk][pl.ds(sent_at + (piece - 1 - row - at) * steps, steps)]
+                    for at in range(group)
+                ]
+                store_split(other, to, chunk * part, jnp.concatenate(lines, axis=0))
+        own_result[...] = dot(own[...], tables[strip])
+        other_result[...] = dot(other[...], tables[1 - strip])
+        for row in range(0, piece, group):
+            at = pl.ds(row * steps, TILE)
+            first, second = own_result[at], other_result[at]
+            upper = sign * (first - second)
+            parts = [
+                lanes_reversed(upper[:, lane : lane + LANES]) for lane in range(0, half, LANES)
+            ][::-1]
+            whole = jnp.concatenate([first + second, *parts], axis=1)
+            out[pl.ds(sub * piece + row, group)] = whole.reshape(group, TILE // group, width)
+
+
+def inverse_second(place, keeps, gots, tables, steps):
+    part = keeps[0].shape[1]
+    rows = keeps[0].shape[0] // steps
     half = part * CHUNKS
-    block = min(32, rows)
+    block, pieces = min(64, rows), 2
+    depth = steps * block // pieces
     return call(
         inverse_second_kernel,
         "inverse_second",
         [IN_VMEM] * (1 + 2 * CHUNKS),
         pl.BlockSpec((block, steps, 2 * half), lambda i, place: (i, 0, 0)),
         floats(rows, steps, 2 * half),
-        [pltpu.VMEM((steps, block, 3 * half), jnp.bfloat16)] * 2
-        + [pltpu.VMEM((steps, block, half), jnp.float32)] * 2,
+        (
+            [pltpu.VMEM((depth, 3 * half), jnp.bfloat16)] * 2
+            + [pltpu.VMEM((depth, half), jnp.float32)] * 2
+        )
+        * pieces,
         1 << 32,
         rows // block,
     )(place, tables, *keeps, *gots)
@@ -464,7 +485,7 @@
         )
     )
     gots = [swapped(send) for send in sends]
-    return inverse_second(place, keeps, gots, split_constant(np.swapaxes(second, 1, 2)))
+    return inverse_second(place, keeps, gots, split_constant(np.swapaxes(second, 1, 2)), steps)
 
 
 def solution(mesh):

time: 67.6 us -> 67 us (level)
  waiting for transfers between devices: 10.3 us -> 9.45 us
    pallas_call x1, Pallas kernels: 11.6 us -> 8.24 us  [forward_second(): call(forward_second_kernel, 'forward_second', [pl.BlockSpec((block, steps...]
    pallas_call x2, Pallas kernels: 6.38 us -> 9.41 us  [inverse_first(): call(functools.partial(inverse_first_kernel, slabs, chunk), 'inverse_firs...]
    pallas_call x2, Pallas kernels: 6.7 us -> 8.55 us  [forward_first(): call(functools.partial(forward_first_kernel, slabs, chunk), 'forward_firs...]
    pallas_call x1, Pallas kernels: 8.35 us -> 6.71 us  [inverse_second(): call(inverse_second_kernel, 'inverse_second', [IN_VMEM] * (1 + 2 * CHUNKS...]
  transfers between devices with their start and end apart: 18 -> 18, of which waited for: 5 -> 3; matrix products, arithmetic and copies ran while one was open for 0% -> 0% of each run, Pallas kernels for 23% -> 30%
where the time goes in v4:
time: 67 us; the launch traced here: 66.9 us
  Pallas kernels  35.3 us (53%)
  starting transfers between devices  21.9 us (33%)
  waiting for transfers between devices  9.45 us (14%)
    ppermute x14, starting transfers between devices, with_partner(): lax.ppermute(block, 'tm', [(slab, slab ^ distance) for slab in range(slab...  20.7 us
    pallas_call x2, Pallas kernels, inverse_first(): call(functools.partial(inverse_first_kernel, slabs, chunk), 'inverse_firs...  9.41 us
    pallas_call x2, Pallas kernels, forward_first(): call(functools.partial(forward_first_kernel, slabs, chunk), 'forward_firs...  8.55 us
    pallas_call x1, Pallas kernels, forward_second(): call(forward_second_kernel, 'forward_second', [pl.BlockSpec((block, steps...  8.24 us
    ppermute x4, waiting for transfers between devices, swapped(): return lax.ppermute(block, 'space', [(0, 1), (1, 0)])  7.68 us
    pallas_call x1, Pallas kernels, inverse_second(): call(inverse_second_kernel, 'inverse_second', [IN_VMEM] * (1 + 2 * CHUNKS...  6.71 us
    ppermute x14, waiting for transfers between devices, with_partner(): lax.ppermute(block, 'tm', [(slab, slab ^ distance) for slab in range(slab...  1.77 us
  transfers between devices with their start and end apart: 18, of which 3 were waited for; matrix products, arithmetic and copies ran while one was open for 0% of the time, Pallas kernels for 30%

profile of v4, /device:TPU:0, one launch (start us, length us, event | category | flops | bytes accessed | tf_op | source)
XLA Modules:
  0.0 66.9 jit_solution(10774065759954403079)
XLA Ops:
  0.0 0.1 pad_add_fusion.place
  0.1 8.2 %forward_second.1 = (f32[4352,128]{1,0:T(8,128)S(1)}, f32[4352,128]{1,0:T(8,128)S(1)}, f32[4352,128]{1,0:T(8,128)S(1)}, f32[4352,128]{1,0:T(8,128)S(1)}) custom-call(s32[2]{0:T(128)S(1)} %pad_add_fusion.place, f32[256,16,512]{2,1,0:T(8,128)} %field.1, f32[256,512]{1,0:T(8,128)} %initial.1, bf16[2,768,256]{2,1,0:T(8,128)(2,1)} %constant.23.clone.own_table.other_table, ...), custom_call_target="tpu_custom_call" | custom-call | flops 4294967296 | bytes 8388608 | tf_op jit(solution)/shard_map/forward_second/pallas_call | solution.py:186
  8.3 0.5 collective-permute-start
  8.8 0.1 collective-permute-start.8
  8.9 3.9 %collective-permute-done.got = f32[4352,128]{1,0:T(8,128)S(1)} collective-permute-done((f32[4352,128]{1,0:T(8,128)S(1)}, f32[4352,128]{1,0:T(8,128)S(1)}, u32[]{:S(2)}, u32[]{:S(2)}) %collective-permute-start) | collective-permute-done | bytes 2228256 | tf_op jit(solution)/shard_map/ppermute | solution.py:436
  12.8 4.2 %forward_first.2 = (f32[16,2,128,256]{3,2,1,0:T(8,128)S(1)}, f32[64,256]{1,0:T(8,128)S(1)}, f32[64,256]{1,0:T(8,128)S(1)}, f32[64,256]{1,0:T(8,128)S(1)}, f32[64,256]{1,0:T(8,128)S(1)}) custom-call(s32[2]{0:T(128)S(1)} %pad_add_fusion.place, f32[4352,128]{1,0:T(8,128)S(1)} %get-tuple-element.35.keep, f32[4352,128]{1,0:T(8,128)S(1)} %collective-permute-done.got, ...), custom_call_target="tpu_custom_call" | custom-call | flops 2147483648 | bytes 8388608 | tf_op jit(solution)/shard_map/forward_first/pallas_call | solution.py:251
  17.0 3.0 %collective-permute-start.1 = (f32[64,256]{1,0:T(8,128)S(1)}, f32[64,256]{1,0:T(8,128)S(1)}, u32[]{:S(2)}, u32[]{:S(2)}) collective-permute-start(f32[64,256]{1,0:T(8,128)S(1)} %get-tuple-element.39), channel_id=1, source_target_pairs={{0,2},{2,0},{4,6},{6,4},{8,10},{10,8},{12,14},{14,12},{1,3},{3,1},... | collective-permute-start | bytes 196616 | tf_op jit(solution)/shard_map/ppermute | solution.py:441
  20.0 1.6 %collective-permute-start.2 = (f32[64,256]{1,0:T(8,128)S(1)}, f32[64,256]{1,0:T(8,128)S(1)}, u32[]{:S(2)}, u32[]{:S(2)}) collective-permute-start(f32[64,256]{1,0:T(8,128)S(1)} %get-tuple-element.40), channel_id=1, source_target_pairs={{0,4},{2,6},{4,0},{6,2},{8,12},{10,14},{12,8},{14,10},{1,5},{3,7},... | collective-permute-start | bytes 196616 | tf_op jit(solution)/shard_map/ppermute | solution.py:441
  21.6 4.4 %forward_first.3 = (f32[16,2,128,256]{3,2,1,0:T(8,128)S(1)}, f32[64,256]{1,0:T(8,128)S(1)}, f32[64,256]{1,0:T(8,128)S(1)}, f32[64,256]{1,0:T(8,128)S(1)}, f32[64,256]{1,0:T(8,128)S(1)}) custom-call(s32[2]{0:T(128)S(1)} %pad_add_fusion.place, f32[4352,128]{1,0:T(8,128)S(1)} %get-tuple-element.49.keep, f32[4352,128]{1,0:T(8,128)S(1)} %collective-permute-done.8.got, ...), custom_call_target="tpu_custom_call" | custom-call | flops 2147483648 | bytes 8388608 | tf_op jit(solution)/shard_map/forward_first/pallas_call | solution.py:251
  25.9 2.0 %collective-permute-start.9 = (f32[64,256]{1,0:T(8,128)S(1)}, f32[64,256]{1,0:T(8,128)S(1)}, u32[]{:S(2)}, u32[]{:S(2)}) collective-permute-start(f32[64,256]{1,0:T(8,128)S(1)} %get-tuple-element.53), channel_id=1, source_target_pairs={{0,2},{2,0},{4,6},{6,4},{8,10},{10,8},{12,14},{14,12},{1,3},{3,1},... | collective-permute-start | bytes 196616 | tf_op jit(solution)/shard_map/ppermute | solution.py:441
  27.9 1.6 %collective-permute-start.10 = (f32[64,256]{1,0:T(8,128)S(1)}, f32[64,256]{1,0:T(8,128)S(1)}, u32[]{:S(2)}, u32[]{:S(2)}) collective-permute-start(f32[64,256]{1,0:T(8,128)S(1)} %get-tuple-element.54), channel_id=1, source_target_pairs={{0,4},{2,6},{4,0},{6,2},{8,12},{10,14},{12,8},{14,10},{1,5},{3,7},... | collective-permute-start | bytes 196616 | tf_op jit(solution)/shard_map/ppermute | solution.py:441
  29.5 0.6 half_sum.2
  30.1 3.0 %collective-permute-start.4 = (f32[64,256]{1,0:T(8,128)S(1)}, f32[64,256]{1,0:T(8,128)S(1)}, u32[]{:S(2)}, u32[]{:S(2)}) collective-permute-start(f32[64,256]{1,0:T(8,128)S(1)} %get-tuple-element.43.near), channel_id=1, source_target_pairs={{0,8},{2,10},{4,12},{6,14},{8,0},{10,2},{12,4},{14,6},{1,9},{3,11}... | collective-permute-start | bytes 196616 | tf_op jit(solution)/shard_map/ppermute | solution.py:441
  33.1 1.7 %collective-permute-done.11.refs_3_ = f32[64,256]{1,0:T(8,128)S(1)} collective-permute-done((f32[64,256]{1,0:T(8,128)S(1)}, f32[64,256]{1,0:T(8,128)S(1)}, u32[]{:S(2)}, u32[]{:S(2)}) %collective-permute-start.11) | collective-permute-done | bytes 65568 | tf_op jit(solution)/shard_map/ppermute | solution.py:441
  34.9 0.6 half_sum.3
  35.5 2.5 %collective-permute-start.12 = (f32[64,256]{1,0:T(8,128)S(1)}, f32[64,256]{1,0:T(8,128)S(1)}, u32[]{:S(2)}, u32[]{:S(2)}) collective-permute-start(f32[64,256]{1,0:T(8,128)S(1)} %get-tuple-element.57.near), channel_id=1, source_target_pairs={{0,8},{2,10},{4,12},{6,14},{8,0},{10,2},{12,4},{14,6},{1,9},{3,11}... | collective-permute-start | bytes 196616 | tf_op jit(solution)/shard_map/ppermute | solution.py:441
  37.9 0.6 close.2
  38.5 0.0 copy-start.2
  38.5 0.5 collective-permute-start.5
  39.1 1.6 %collective-permute-start.6 = (f32[64,256]{1,0:T(8,128)S(1)}, f32[64,256]{1,0:T(8,128)S(1)}, u32[]{:S(2)}, u32[]{:S(2)}) collective-permute-start(f32[64,256]{1,0:T(8,128)S(1)} %get-tuple-element.46), channel_id=1, source_target_pairs={{0,4},{2,6},{4,0},{6,2},{8,12},{10,14},{12,8},{14,10},{1,5},{3,7},... | collective-permute-start | bytes 196616 | tf_op jit(solution)/shard_map/ppermute | solution.py:441
  40.7 1.4 %collective-permute-start.7 = (f32[64,256]{1,0:T(8,128)S(1)}, f32[64,256]{1,0:T(8,128)S(1)}, u32[]{:S(2)}, u32[]{:S(2)}) collective-permute-start(f32[64,256]{1,0:T(8,128)S(1)} %get-tuple-element.47), channel_id=1, source_target_pairs={{0,6},{2,4},{4,2},{6,0},{8,14},{10,12},{12,10},{14,8},{1,7},{3,5},... | collective-permute-start | bytes 196616 | tf_op jit(solution)/shard_map/ppermute | solution.py:441
  42.1 0.6 close.3
  42.7 0.5 collective-permute-start.13
  43.3 1.6 %collective-permute-start.14 = (f32[64,256]{1,0:T(8,128)S(1)}, f32[64,256]{1,0:T(8,128)S(1)}, u32[]{:S(2)}, u32[]{:S(2)}) collective-permute-start(f32[64,256]{1,0:T(8,128)S(1)} %get-tuple-element.60), channel_id=1, source_target_pairs={{0,4},{2,6},{4,0},{6,2},{8,12},{10,14},{12,8},{14,10},{1,5},{3,7},... | collective-permute-start | bytes 196616 | tf_op jit(solution)/shard_map/ppermute | solution.py:441
  44.9 1.4 %collective-permute-start.15 = (f32[64,256]{1,0:T(8,128)S(1)}, f32[64,256]{1,0:T(8,128)S(1)}, u32[]{:S(2)}, u32[]{:S(2)}) collective-permute-start(f32[64,256]{1,0:T(8,128)S(1)} %get-tuple-element.61), channel_id=1, source_target_pairs={{0,6},{2,4},{4,2},{6,0},{8,14},{10,12},{12,10},{14,8},{1,7},{3,5},... | collective-permute-start | bytes 196616 | tf_op jit(solution)/shard_map/ppermute | solution.py:441
  46.3 4.6 %inverse_first.2 = (f32[4096,128]{1,0:T(8,128)S(1)}, f32[4096,128]{1,0:T(8,128)S(1)}) custom-call(s32[2]{0:T(128)S(1)} %pad_add_fusion.place, f32[16,2,128,256]{3,2,1,0:T(8,128)S(1)} %get-tuple-element.37.modes, bf16[2,2,768,256]{3,2,1,0:T(8,128)(2,1)S(1)} %copy-done.2, f32[2,2,256,256]{3,2,1,0:T(8,128)S(1)} %copy-done.4, ...), custom_call_target="tpu_custom_call" | custom-call | flops 2147483648 | bytes 8388608 | tf_op jit(solution)/shard_map/inverse_first/pallas_call | solution.py:359
  50.9 0.1 collective-permute-start.16
  51.0 0.0 copy-start.1
  51.0 4.8 %inverse_first.3 = (f32[4096,128]{1,0:T(8,128)S(1)}, f32[4096,128]{1,0:T(8,128)S(1)}) custom-call(s32[2]{0:T(128)S(1)} %pad_add_fusion.place, f32[16,2,128,256]{3,2,1,0:T(8,128)S(1)} %get-tuple-element.51.modes, bf16[2,2,768,256]{3,2,1,0:T(8,128)(2,1)S(1)} %copy-done.2, f32[2,2,256,256]{3,2,1,0:T(8,128)S(1)} %copy-done.4, ...), custom_call_target="tpu_custom_call" | custom-call | flops 2147483648 | bytes 8388608 | tf_op jit(solution)/shard_map/inverse_first/pallas_call | solution.py:359
  55.8 0.5 collective-permute-start.17
  56.4 3.8 %collective-permute-done.17.refs_3_ = f32[4096,128]{1,0:T(8,128)S(1)} collective-permute-done((f32[4096,128]{1,0:T(8,128)S(1)}, f32[4096,128]{1,0:T(8,128)S(1)}, u32[]{:S(2)}, u32[]{:S(2)}) %collective-permute-start.17) | collective-permute-done | bytes 2097184 | tf_op jit(solution)/shard_map/ppermute | solution.py:436
  60.2 6.7 %inverse_second.1 = f32[256,16,512]{2,1,0:T(8,128)} custom-call(s32[2]{0:T(128)S(1)} %pad_add_fusion.place, bf16[2,768,256]{2,1,0:T(8,128)(2,1)S(1)} %copy-done.1, f32[4096,128]{1,0:T(8,128)S(1)} %get-tuple-element.48.refs_0_, f32[4096,128]{1,0:T(8,128)S(1)} %get-tuple-element.62.refs_1_, f32[4096,128]{1,0:T(8,128)S(1)} %collective-permute-done.16.refs_2_, ...), custom_call_target="tpu_custom_call" | custom-call | flops 4294967296 | bytes 8388608 | tf_op jit(solution)/shard_map/inverse_second/pallas_call | solution.py:419
  (25 shorter events, 0.1 us)
Async XLA Ops:
  0.1 12.7 %copy-start.3 = (bf16[2,2,768,256]{3,2,1,0:T(8,128)(2,1)S(1)}, bf16[2,2,768,256]{3,2,1,0:T(8,128)(2,1)}, u32[]{:S(2)}) copy-start(bf16[2,2,768,256]{3,2,1,0:T(8,128)(2,1)} %constant.21.clone.table) | copy-start | bytes 4718596
  0.1 12.7 %copy-start.4 = (f32[2,2,256,256]{3,2,1,0:T(8,128)S(1)}, f32[2,2,256,256]{3,2,1,0:T(8,128)}, u32[]{:S(2)}) copy-start(f32[2,2,256,256]{3,2,1,0:T(8,128)} %constant.22.clone.decay) | copy-start | bytes 3145732
  8.3 4.5 %collective-permute-start = (f32[4352,128]{1,0:T(8,128)S(1)}, f32[4352,128]{1,0:T(8,128)S(1)}, u32[]{:S(2)}, u32[]{:S(2)}) collective-permute-start(f32[4352,128]{1,0:T(8,128)S(1)} %get-tuple-element.36), channel_id=1, source_target_pairs={{0,1},{1,0},{2,3},{3,2},{4,5},{5,4},{6,7},{7,6},{8,9},{9,8},{10,11... | collective-permute-start | bytes 6684680 | tf_op jit(solution)/shard_map/ppermute | solution.py:436
  8.8 12.7 %collective-permute-start.8 = (f32[4352,128]{1,0:T(8,128)S(1)}, f32[4352,128]{1,0:T(8,128)S(1)}, u32[]{:S(2)}, u32[]{:S(2)}) collective-permute-start(f32[4352,128]{1,0:T(8,128)S(1)} %get-tuple-element.50), channel_id=1, source_target_pairs={{0,1},{1,0},{2,3},{3,2},{4,5},{5,4},{6,7},{7,6},{8,9},{9,8},{10,11... | collective-permute-start | bytes 6684680 | tf_op jit(solution)/shard_map/ppermute | solution.py:436
  17.0 12.5 %collective-permute-start.1 = (f32[64,256]{1,0:T(8,128)S(1)}, f32[64,256]{1,0:T(8,128)S(1)}, u32[]{:S(2)}, u32[]{:S(2)}) collective-permute-start(f32[64,256]{1,0:T(8,128)S(1)} %get-tuple-element.39), channel_id=1, source_target_pairs={{0,2},{2,0},{4,6},{6,4},{8,10},{10,8},{12,14},{14,12},{1,3},{3,1},... | collective-permute-start | bytes 196616 | tf_op jit(solution)/shard_map/ppermute | solution.py:441
  20.0 9.5 %collective-permute-start.2 = (f32[64,256]{1,0:T(8,128)S(1)}, f32[64,256]{1,0:T(8,128)S(1)}, u32[]{:S(2)}, u32[]{:S(2)}) collective-permute-start(f32[64,256]{1,0:T(8,128)S(1)} %get-tuple-element.40), channel_id=1, source_target_pairs={{0,4},{2,6},{4,0},{6,2},{8,12},{10,14},{12,8},{14,10},{1,5},{3,7},... | collective-permute-start | bytes 196616 | tf_op jit(solution)/shard_map/ppermute | solution.py:441
  21.6 7.9 %collective-permute-start.3 = (f32[64,256]{1,0:T(8,128)S(1)}, f32[64,256]{1,0:T(8,128)S(1)}, u32[]{:S(2)}, u32[]{:S(2)}) collective-permute-start(f32[64,256]{1,0:T(8,128)S(1)} %get-tuple-element.41), channel_id=1, source_target_pairs={{0,6},{2,4},{4,2},{6,0},{8,14},{10,12},{12,10},{14,8},{1,7},{3,5},... | collective-permute-start | bytes 196616 | tf_op jit(solution)/shard_map/ppermute | solution.py:441
  21.6 8.0 %copy-start = (f32[2,2,3,256,256]{4,3,2,1,0:T(8,128)S(1)}, f32[2,2,3,256,256]{4,3,2,1,0:T(8,128)}, u32[]{:S(2)}) copy-start(f32[2,2,3,256,256]{4,3,2,1,0:T(8,128)} %constant.20.clone.closing) | copy-start | bytes 9437188
  25.9 7.2 %collective-permute-start.9 = (f32[64,256]{1,0:T(8,128)S(1)}, f32[64,256]{1,0:T(8,128)S(1)}, u32[]{:S(2)}, u32[]{:S(2)}) collective-permute-start(f32[64,256]{1,0:T(8,128)S(1)} %get-tuple-element.53), channel_id=1, source_target_pairs={{0,2},{2,0},{4,6},{6,4},{8,10},{10,8},{12,14},{14,12},{1,3},{3,1},... | collective-permute-start | bytes 196616 | tf_op jit(solution)/shard_map/ppermute | solution.py:441
  27.9 5.2 %collective-permute-start.10 = (f32[64,256]{1,0:T(8,128)S(1)}, f32[64,256]{1,0:T(8,128)S(1)}, u32[]{:S(2)}, u32[]{:S(2)}) collective-permute-start(f32[64,256]{1,0:T(8,128)S(1)} %get-tuple-element.54), channel_id=1, source_target_pairs={{0,4},{2,6},{4,0},{6,2},{8,12},{10,14},{12,8},{14,10},{1,5},{3,7},... | collective-permute-start | bytes 196616 | tf_op jit(solution)/shard_map/ppermute | solution.py:441
  29.5 5.4 %collective-permute-start.11 = (f32[64,256]{1,0:T(8,128)S(1)}, f32[64,256]{1,0:T(8,128)S(1)}, u32[]{:S(2)}, u32[]{:S(2)}) collective-permute-start(f32[64,256]{1,0:T(8,128)S(1)} %get-tuple-element.55), channel_id=1, source_target_pairs={{0,6},{2,4},{4,2},{6,0},{8,14},{10,12},{12,10},{14,8},{1,7},{3,5},... | collective-permute-start | bytes 196616 | tf_op jit(solution)/shard_map/ppermute | solution.py:441
  30.1 7.8 %collective-permute-start.4 = (f32[64,256]{1,0:T(8,128)S(1)}, f32[64,256]{1,0:T(8,128)S(1)}, u32[]{:S(2)}, u32[]{:S(2)}) collective-permute-start(f32[64,256]{1,0:T(8,128)S(1)} %get-tuple-element.43.near), channel_id=1, source_target_pairs={{0,8},{2,10},{4,12},{6,14},{8,0},{10,2},{12,4},{14,6},{1,9},{3,11}... | collective-permute-start | bytes 196616 | tf_op jit(solution)/shard_map/ppermute | solution.py:441
  35.5 6.6 %collective-permute-start.12 = (f32[64,256]{1,0:T(8,128)S(1)}, f32[64,256]{1,0:T(8,128)S(1)}, u32[]{:S(2)}, u32[]{:S(2)}) collective-permute-start(f32[64,256]{1,0:T(8,128)S(1)} %get-tuple-element.57.near), channel_id=1, source_target_pairs={{0,8},{2,10},{4,12},{6,14},{8,0},{10,2},{12,4},{14,6},{1,9},{3,11}... | collective-permute-start | bytes 196616 | tf_op jit(solution)/shard_map/ppermute | solution.py:441
  38.5 7.7 %copy-start.2 = (bf16[2,2,768,256]{3,2,1,0:T(8,128)(2,1)S(1)}, bf16[2,2,768,256]{3,2,1,0:T(8,128)(2,1)}, u32[]{:S(2)}) copy-start(bf16[2,2,768,256]{3,2,1,0:T(8,128)(2,1)} %constant.24.clone.table) | copy-start | bytes 4718596
  38.5 6.3 %collective-permute-start.5 = (f32[64,256]{1,0:T(8,128)S(1)}, f32[64,256]{1,0:T(8,128)S(1)}, u32[]{:S(2)}, u32[]{:S(2)}) collective-permute-start(f32[64,256]{1,0:T(8,128)S(1)} %get-tuple-element.45), channel_id=1, source_target_pairs={{0,2},{2,0},{4,6},{6,4},{8,10},{10,8},{12,14},{14,12},{1,3},{3,1},... | collective-permute-start | bytes 196616 | tf_op jit(solution)/shard_map/ppermute | solution.py:441
  39.1 7.2 %collective-permute-start.6 = (f32[64,256]{1,0:T(8,128)S(1)}, f32[64,256]{1,0:T(8,128)S(1)}, u32[]{:S(2)}, u32[]{:S(2)}) collective-permute-start(f32[64,256]{1,0:T(8,128)S(1)} %get-tuple-element.46), channel_id=1, source_target_pairs={{0,4},{2,6},{4,0},{6,2},{8,12},{10,14},{12,8},{14,10},{1,5},{3,7},... | collective-permute-start | bytes 196616 | tf_op jit(solution)/shard_map/ppermute | solution.py:441
  40.7 5.6 %collective-permute-start.7 = (f32[64,256]{1,0:T(8,128)S(1)}, f32[64,256]{1,0:T(8,128)S(1)}, u32[]{:S(2)}, u32[]{:S(2)}) collective-permute-start(f32[64,256]{1,0:T(8,128)S(1)} %get-tuple-element.47), channel_id=1, source_target_pairs={{0,6},{2,4},{4,2},{6,0},{8,14},{10,12},{12,10},{14,8},{1,7},{3,5},... | collective-permute-start | bytes 196616 | tf_op jit(solution)/shard_map/ppermute | solution.py:441
  42.7 8.3 %collective-permute-start.13 = (f32[64,256]{1,0:T(8,128)S(1)}, f32[64,256]{1,0:T(8,128)S(1)}, u32[]{:S(2)}, u32[]{:S(2)}) collective-permute-start(f32[64,256]{1,0:T(8,128)S(1)} %get-tuple-element.59), channel_id=1, source_target_pairs={{0,2},{2,0},{4,6},{6,4},{8,10},{10,8},{12,14},{14,12},{1,3},{3,1},... | collective-permute-start | bytes 196616 | tf_op jit(solution)/shard_map/ppermute | solution.py:441
  43.3 7.7 %collective-permute-start.14 = (f32[64,256]{1,0:T(8,128)S(1)}, f32[64,256]{1,0:T(8,128)S(1)}, u32[]{:S(2)}, u32[]{:S(2)}) collective-permute-start(f32[64,256]{1,0:T(8,128)S(1)} %get-tuple-element.60), channel_id=1, source_target_pairs={{0,4},{2,6},{4,0},{6,2},{8,12},{10,14},{12,8},{14,10},{1,5},{3,7},... | collective-permute-start | bytes 196616 | tf_op jit(solution)/shard_map/ppermute | solution.py:441
  44.9 6.1 %collective-permute-start.15 = (f32[64,256]{1,0:T(8,128)S(1)}, f32[64,256]{1,0:T(8,128)S(1)}, u32[]{:S(2)}, u32[]{:S(2)}) collective-permute-start(f32[64,256]{1,0:T(8,128)S(1)} %get-tuple-element.61), channel_id=1, source_target_pairs={{0,6},{2,4},{4,2},{6,0},{8,14},{10,12},{12,10},{14,8},{1,7},{3,5},... | collective-permute-start | bytes 196616 | tf_op jit(solution)/shard_map/ppermute | solution.py:441
  50.9 5.5 %collective-permute-start.16 = (f32[4096,128]{1,0:T(8,128)S(1)}, f32[4096,128]{1,0:T(8,128)S(1)}, u32[]{:S(2)}, u32[]{:S(2)}) collective-permute-start(f32[4096,128]{1,0:T(8,128)S(1)} %get-tuple-element.63), channel_id=1, source_target_pairs={{0,1},{1,0},{2,3},{3,2},{4,5},{5,4},{6,7},{7,6},{8,9},{9,8},{10,11... | collective-permute-start | bytes 6291464 | tf_op jit(solution)/shard_map/ppermute | solution.py:436
  51.0 9.2 %copy-start.1 = (bf16[2,768,256]{2,1,0:T(8,128)(2,1)S(1)}, bf16[2,768,256]{2,1,0:T(8,128)(2,1)}, u32[]{:S(2)}) copy-start(bf16[2,768,256]{2,1,0:T(8,128)(2,1)} %constant.25.clone.tables) | copy-start | bytes 2359300
  55.8 4.3 %collective-permute-start.17 = (f32[4096,128]{1,0:T(8,128)S(1)}, f32[4096,128]{1,0:T(8,128)S(1)}, u32[]{:S(2)}, u32[]{:S(2)}) collective-permute-start(f32[4096,128]{1,0:T(8,128)S(1)} %get-tuple-element.64), channel_id=1, source_target_pairs={{0,1},{1,0},{2,3},{3,2},{4,5},{5,4},{6,7},{7,6},{8,9},{9,8},{10,11... | collective-permute-start | bytes 6291464 | tf_op jit(solution)/shard_map/ppermute | solution.py:436

commit v5 on v4

--- a/solution.py
+++ b/solution.py
@@ -125,52 +125,50 @@
     )
 
 
-def forward_second_kernel(place, field, initial, own_table, other_table, *refs):
-    keeps, sends, scratch = refs[:CHUNKS], refs[CHUNKS : 2 * CHUNKS], refs[2 * CHUNKS :]
+def forward_second_kernel(place, field, initial, table, sums, *refs):
+    sends, scratch = refs[:CHUNKS], refs[CHUNKS:]
     rows, steps, width = field.shape
     half = width // 2
     part = half // CHUNKS
-    count = len(scratch) // 2
-    piece = rows // count
+    piece = rows // len(scratch)
     group = max(TILE // steps, 1)
+    head = min(steps, SUBLANES)
     total = rows * pl.num_programs(0)
     start = pl.program_id(0) * rows
     mirror = total - rows - start
     is_first = (place[0] == 0).astype(jnp.float32)
     sign = 1.0 - 2.0 * place[1].astype(jnp.float32)
-    ones = lax.broadcasted_iota(jnp.int32, (group, steps, width), 1) == 0
-    ones = jnp.where(ones, is_first, 0.0)
-
-    def put(own, other, at, cells):
+    firsts = lax.broadcasted_iota(jnp.int32, (group, head, width), 1) == 0
+    firsts = jnp.where(firsts, is_first, 0.0)
+
+    def put(other, at, sums_at, cells):
         lower = cells[:, :half]
-        upper = jnp.concatenate(
+        upper = sign * jnp.concatenate(
             [lanes_reversed(cells[:, lane : lane + LANES]) for lane in range(half, width, LANES)][::-1],
             axis=1,
         )
-        store_split(own, (pl.ds(at, TILE),), 0, lower + sign * upper)
-        store_split(other, (pl.ds(at, TILE),), 0, lower - sign * upper)
-
-    for sub in range(count):
-        own, other = scratch[2 * sub : 2 * sub + 2]
+        sums[pl.ds(sums_at, TILE), :] = lower + upper
+        store_split(other, (pl.ds(at, TILE),), 0, lower - upper)
+
+    for sub, other in enumerate(scratch):
+        kept_at = pl.multiple_of(start + sub * piece, piece)
+        sent_at = pl.multiple_of(mirror + (len(scratch) - 1 - sub) * piece, piece)
+        body = piece * steps
+        kept_base = pl.multiple_of(kept_at * steps, body)
         for row in range(0, piece, group):
             at = pl.ds(sub * piece + row, group)
             cells = field[at]
-            force = REACTION_STEP * (cells - cells * cells * cells) + ones * initial[at][:, None, :]
-            put(own, other, row * steps, force.reshape(TILE, width))
+            force = REACTION_STEP * (cells - cells * cells * cells)
+            starts = force[:, :head] + firsts * initial[at][:, None, :]
+            force = jnp.concatenate([starts, force[:, head:]], axis=1) if head < steps else starts
+            put(other, row * steps, kept_base + row * steps, force.reshape(TILE, width))
         for row in range(0, piece, TILE):
             ends = field[pl.ds(sub * piece + row, TILE), steps - 1, :]
-            put(own, other, piece * steps + row, ends)
-        kept = dot(own[...], own_table[0])
-        sent = dot(other[...], other_table[0])
-        body = piece * steps
-        kept_at = pl.multiple_of(start + sub * piece, piece)
-        sent_at = pl.multiple_of(mirror + (count - 1 - sub) * piece, piece)
-        for chunk in range(CHUNKS):
-            keep, send = keeps[chunk], sends[chunk]
+            put(other, body + row, total * steps + kept_at + row, ends)
+        sent = dot(other[...], table[0])
+        base = pl.multiple_of(sent_at * steps, body)
+        for chunk, send in enumerate(sends):
             lanes = slice(chunk * part, (chunk + 1) * part)
-            keep[pl.ds(pl.multiple_of(kept_at * steps, body), body), :] = kept[:body, lanes]
-            keep[pl.ds(total * steps + kept_at, piece), :] = kept[body:, lanes]
-            base = pl.multiple_of(sent_at * steps, body)
             for row in range(piece):
                 line = sent[row * steps : (row + 1) * steps, lanes]
                 send[pl.ds(base + (piece - 1 - row) * steps, steps), :] = line
@@ -181,7 +179,6 @@
     rows, steps, width = field.shape
     half = width // 2
     block, pieces = min(64, rows), 2
-    table = (1, 3 * half, half)
     depth = (steps + 1) * block // pieces
     outs = call(
         forward_second_kernel,
@@ -189,16 +186,48 @@
         [
             pl.BlockSpec((block, steps, width), lambda i, place: (i, 0, 0)),
             pl.BlockSpec((block, width), lambda i, place: (i, 0)),
-            pl.BlockSpec(table, lambda i, place: (place[1], 0, 0)),
-            pl.BlockSpec(table, lambda i, place: (1 - place[1], 0, 0)),
+            pl.BlockSpec((1, 3 * half, half), lambda i, place: (1 - place[1], 0, 0)),
         ],
-        [IN_VMEM] * (2 * CHUNKS),
-        [floats((steps + 1) * rows, half // CHUNKS)] * (2 * CHUNKS),
-        [pltpu.VMEM((depth, 3 * half), jnp.bfloat16)] * (2 * pieces),
+        [IN_VMEM] * (1 + CHUNKS),
+        [floats((steps + 1) * rows, half)]
+        + [floats((steps + 1) * rows, half // CHUNKS)] * CHUNKS,
+        [pltpu.VMEM((depth, 3 * half), jnp.bfloat16)] * pieces,
         1 << 32,
         rows // block,
-    )(place, in_hbm(field), in_hbm(initial), in_hbm(tables), in_hbm(tables))
-    return outs[:CHUNKS], outs[CHUNKS:]
+    )(place, in_hbm(field), in_hbm(initial), in_hbm(tables))
+    return outs[0], outs[1:]
+
+
+def times_table_kernel(inputs, place, tables, *refs):
+    sources, refs = refs[:inputs], refs[inputs:]
+    outs, scratch = refs[:-2], refs[-2:]
+    piece = scratch[0].shape[0]
+    for at in range(0, sources[0].shape[0], piece):
+        split = scratch[at // piece % 2]
+        for row in range(0, piece, TILE):
+            lane = 0
+            for source in sources:
+                store_split(split, (pl.ds(row, TILE),), lane, source[pl.ds(at + row, TILE)])
+                lane += source.shape[1]
+        result = dot(split[...], tables[place[1]])
+        lane = 0
+        for out in outs:
+            out[pl.ds(at, piece)] = result[:, lane : lane + out.shape[1]]
+            lane += out.shape[1]
+
+
+def times_table(place, sources, tables, widths, name):
+    rows = sources[0].shape[0]
+    depth = tables.shape[1]
+    return call(
+        functools.partial(times_table_kernel, len(sources)),
+        name,
+        [IN_VMEM] * (1 + len(sources)),
+        [IN_VMEM] * len(widths),
+        [floats(rows, width) for width in widths],
+        [pltpu.VMEM((rows // 8, depth), jnp.bfloat16)] * 2,
+        1 << 31,
+    )(place, tables, *sources)
 
 
 def ranks(slabs):
@@ -348,9 +377,9 @@
         even, odd = results
         for at in range(block):
             piece = slice(at * part, (at + 1) * part)
-            cells_at = pl.ds(step + at, rows, stride=steps)
-            keep[cells_at, :] = (even[piece] + odd[piece]).T
-            send[cells_at, :] = (even[piece] - odd[piece]).T
+            start = (step + at) * rows
+            keep[pl.ds(start, rows), :] = (even[piece] + odd[piece]).T
+            store_rows_reversed(send, start, (even[piece] - odd[piece]).T)
 
 
 def inverse_first(place, chunk, modes, befores, tables, decays, slabs):
@@ -370,66 +399,60 @@
     )(place, modes, tables, decays, *befores)
 
 
-def inverse_second_kernel(place, tables, *refs):
-    keeps, gots, refs = refs[:CHUNKS], refs[CHUNKS : 2 * CHUNKS], refs[2 * CHUNKS :]
-    out, scratch = refs[0], refs[1:]
+def inverse_second_kernel(place, tables, kept, *refs):
+    gots, out, scratch = refs[:CHUNKS], refs[CHUNKS], refs[CHUNKS + 1 :]
     rows, steps, width = out.shape
-    part = keeps[0].shape[1]
-    half = part * CHUNKS
-    count = len(scratch) // 4
+    half = width // 2
+    part = half // CHUNKS
+    count = len(scratch) // 2
     piece = rows // count
-    group = max(TILE // steps, 1)
+    group = min(SUBLANES, steps)
     strip = place[1]
     sign = 1.0 - 2.0 * strip.astype(jnp.float32)
-    total = rows * pl.num_programs(0)
     start = pl.program_id(0) * rows
-    mirror = total - rows - start
     for sub in range(count):
-        own, other, own_result, other_result = scratch[4 * sub : 4 * sub + 4]
-        kept_at = pl.multiple_of((start + sub * piece) * steps, piece * steps)
-        sent_at = pl.multiple_of((mirror + (count - 1 - sub) * piece) * steps, piece * steps)
-        for row in range(0, piece, group):
-            to = (pl.ds(row * steps, TILE),)
-            for chunk in range(CHUNKS):
-                store_split(own, to, chunk * part, keeps[chunk][pl.ds(kept_at + row * steps, TILE)])
-                lines = [
-                    gots[chunk][pl.ds(sent_at + (piece - 1 - row - at) * steps, steps)]
-                    for at in range(group)
-                ]
-                store_split(other, to, chunk * part, jnp.concatenate(lines, axis=0))
-        own_result[...] = dot(own[...], tables[strip])
-        other_result[...] = dot(other[...], tables[1 - strip])
-        for row in range(0, piece, group):
-            at = pl.ds(row * steps, TILE)
-            first, second = own_result[at], other_result[at]
-            upper = sign * (first - second)
-            parts = [
-                lanes_reversed(upper[:, lane : lane + LANES]) for lane in range(0, half, LANES)
-            ][::-1]
-            whole = jnp.concatenate([first + second, *parts], axis=1)
-            out[pl.ds(sub * piece + row, group)] = whole.reshape(group, TILE // group, width)
-
-
-def inverse_second(place, keeps, gots, tables, steps):
-    part = keeps[0].shape[1]
-    rows = keeps[0].shape[0] // steps
+        split, result = scratch[2 * sub : 2 * sub + 2]
+        base = pl.multiple_of(start + sub * piece, piece)
+        for step in range(steps):
+            for row in range(0, piece, TILE):
+                for chunk, got in enumerate(gots):
+                    cells = got[step, pl.ds(base + row, TILE)]
+                    store_split(split, (step, pl.ds(row, TILE)), chunk * part, cells)
+        product = dot(split[...].reshape(steps * piece, 3 * half), tables[1 - strip])
+        result[...] = product.reshape(result.shape)
+        for row in range(0, piece, SUBLANES):
+            for step in range(0, steps, group):
+                for lane in range(0, half, LANES):
+                    at_steps, at_lanes = pl.ds(step, group), pl.ds(lane, LANES)
+                    first = kept[at_steps, pl.ds(base + row, SUBLANES), at_lanes]
+                    second = result[at_steps, pl.ds(row, SUBLANES), at_lanes]
+                    upper = sign * (first - second)
+                    upper = lanes_reversed(upper.reshape(-1, LANES)).reshape(upper.shape)
+                    to = (pl.ds(sub * piece + row, SUBLANES), at_steps)
+                    out[(*to, at_lanes)] = jnp.swapaxes(first + second, 0, 1)
+                    to_lanes = pl.ds(width - LANES - lane, LANES)
+                    out[(*to, to_lanes)] = jnp.swapaxes(upper, 0, 1)
+
+
+def inverse_second(place, kept, gots, tables):
+    steps, rows, part = gots[0].shape
     half = part * CHUNKS
     block, pieces = min(64, rows), 2
-    depth = steps * block // pieces
+    piece = block // pieces
     return call(
         inverse_second_kernel,
         "inverse_second",
-        [IN_VMEM] * (1 + 2 * CHUNKS),
+        [IN_VMEM] * (2 + CHUNKS),
         pl.BlockSpec((block, steps, 2 * half), lambda i, place: (i, 0, 0)),
         floats(rows, steps, 2 * half),
-        (
-            [pltpu.VMEM((depth, 3 * half), jnp.bfloat16)] * 2
-            + [pltpu.VMEM((depth, half), jnp.float32)] * 2
-        )
+        [
+            pltpu.VMEM((steps, piece, 3 * half), jnp.bfloat16),
+            pltpu.VMEM((steps, piece, half), jnp.float32),
+        ]
         * pieces,
         1 << 32,
         rows // block,
-    )(place, tables, *keeps, *gots)
+    )(place, tables, kept, *gots)
 
 
 def swapped(block):
@@ -466,8 +489,11 @@
         np.stack([by_chunk(table) for table in (slab_decay, half_decay, gain)], axis=2)
     )
     first_table, decays = split_constant(first), constant(decay)
-    keeps, sends = forward_second(place, iterate, initial, split_constant(second))
+    half = width // 2
+    second_table = split_constant(second)
+    sums, sends = forward_second(place, iterate, initial, second_table)
     gots = [swapped(send) for send in sends]
+    keeps = times_table(place, [sums], second_table, [half // CHUNKS] * CHUNKS, "keep_second")
     modes, befores = [], []
     for chunk in range(CHUNKS):
         own_modes, lasts = forward_first(
@@ -484,8 +510,10 @@
             for chunk in range(CHUNKS)
         )
     )
-    gots = [swapped(send) for send in sends]
-    return inverse_second(place, keeps, gots, split_constant(np.swapaxes(second, 1, 2)), steps)
+    gots = [swapped(send).reshape(steps, rows, -1) for send in sends]
+    inverse_table = split_constant(np.swapaxes(second, 1, 2))
+    kept = times_table(place, keeps, inverse_table, [half], "keep_inverse")[0]
+    return inverse_second(place, kept.reshape(steps, rows, half), gots, inverse_table)
 
 
 def solution(mesh):

time: 67 us -> 63.1 us (0.942)
  waiting for transfers between devices: 9.45 us -> 4.26 us
  Pallas kernels: 35.3 us -> 36.9 us
    pallas_call x1 -> x3, Pallas kernels: 6.71 us -> 12.3 us  [the longest x1 6.62 us: inverse_second(): call(inverse_second_kernel, 'inverse_second', [IN_VMEM] * (2 + CHUNKS), p...]
    ppermute x4, waiting for transfers between devices: 7.68 us -> 2.12 us  [swapped(): return lax.ppermute(block, 'space', [(0, 1), (1, 0)])]
    pallas_call x2, Pallas kernels: 9.41 us -> 6.54 us  [inverse_first(): call(functools.partial(inverse_first_kernel, slabs, chunk), 'inverse_firs...]
    pallas_call x1, Pallas kernels: 8.24 us -> 7.07 us  [forward_second(): call(forward_second_kernel, 'forward_second', [pl.BlockSpec((block, steps...]
  transfers between devices with their start and end apart: 18 -> 18, of which waited for: 3 -> 4; matrix products, arithmetic and copies ran while one was open for 0% -> 0% of each run, Pallas kernels for 30% -> 37%
where the time goes in v5:
time: 63.1 us; the launch traced here: 63 us
  Pallas kernels  36.9 us (58%)
  starting transfers between devices  21.5 us (34%)
  waiting for transfers between devices  4.26 us (7%)
    ppermute x14, starting transfers between devices, with_partner(): lax.ppermute(block, 'tm', [(slab, slab ^ distance) for slab in range(slab...  20.2 us
    pallas_call x2, Pallas kernels, forward_first(): call(functools.partial(forward_first_kernel, slabs, chunk), 'forward_firs...  8.61 us
    pallas_call x1, Pallas kernels, forward_second(): call(forward_second_kernel, 'forward_second', [pl.BlockSpec((block, steps...  7.07 us
    pallas_call x1, Pallas kernels, inverse_second(): call(inverse_second_kernel, 'inverse_second', [IN_VMEM] * (2 + CHUNKS), p...  6.62 us
    pallas_call x2, Pallas kernels, inverse_first(): call(functools.partial(inverse_first_kernel, slabs, chunk), 'inverse_firs...  6.54 us
    pallas_call x2, Pallas kernels, times_table(): call(functools.partial(times_table_kernel, len(sources)), name, [IN_VMEM]...  5.7 us
    ppermute x14, waiting for transfers between devices, with_partner(): lax.ppermute(block, 'tm', [(slab, slab ^ distance) for slab in range(slab...  2.14 us
    ppermute x4, waiting for transfers between devices, swapped(): return lax.ppermute(block, 'space', [(0, 1), (1, 0)])  2.12 us
  transfers between devices with their start and end apart: 18, of which 4 were waited for; matrix products, arithmetic and copies ran while one was open for 0% of the time, Pallas kernels for 37%

profile of v5, /device:TPU:0, one launch (start us, length us, event | category | flops | bytes accessed | tf_op | source)
XLA Modules:
  0.0 63.0 jit_solution(5256341195217410976)
XLA Ops:
  0.0 0.1 pad_add_fusion.place
  0.1 7.1 %forward_second.1 = (f32[4352,256]{1,0:T(8,128)S(1)}, f32[4352,128]{1,0:T(8,128)S(1)}, f32[4352,128]{1,0:T(8,128)S(1)}) custom-call(s32[2]{0:T(128)S(1)} %pad_add_fusion.place, f32[256,16,512]{2,1,0:T(8,128)} %field.1, f32[256,512]{1,0:T(8,128)} %initial.1, bf16[2,768,256]{2,1,0:T(8,128)(2,1)} %constant.23.clone.table.tables), custom_call_target="tpu_custom_call" | custom-call | flops 4294967296 | bytes 8388608 | tf_op jit(solution)/shard_map/forward_second/pallas_call | solution.py:183
  7.2 0.9 %collective-permute-start = (f32[4352,128]{1,0:T(8,128)S(1)}, f32[4352,128]{1,0:T(8,128)S(1)}, u32[]{:S(2)}, u32[]{:S(2)}) collective-permute-start(f32[4352,128]{1,0:T(8,128)S(1)} %get-tuple-element.38), channel_id=1, source_target_pairs={{0,1},{1,0},{2,3},{3,2},{4,5},{5,4},{6,7},{7,6},{8,9},{9,8},{10,11... | collective-permute-start | bytes 6684680 | tf_op jit(solution)/shard_map/ppermute | solution.py:459
  8.1 0.1 collective-permute-start.8
  8.1 2.5 %keep_second.1 = (f32[4352,128]{1,0:T(8,128)S(1)}, f32[4352,128]{1,0:T(8,128)S(1)}) custom-call(s32[2]{0:T(128)S(1)} %pad_add_fusion.place, bf16[2,768,256]{2,1,0:T(8,128)(2,1)S(1)} %copy-done.5, f32[4352,256]{1,0:T(8,128)S(1)} %get-tuple-element.36.refs_0_), custom_call_target="tpu_custom_call" | custom-call | flops 2147483648 | bytes 8388608 | tf_op jit(solution)/shard_map/keep_second/pallas_call | solution.py:222
  10.6 1.4 %collective-permute-done.got = f32[4352,128]{1,0:T(8,128)S(1)} collective-permute-done((f32[4352,128]{1,0:T(8,128)S(1)}, f32[4352,128]{1,0:T(8,128)S(1)}, u32[]{:S(2)}, u32[]{:S(2)}) %collective-permute-start) | collective-permute-done | bytes 2228256 | tf_op jit(solution)/shard_map/ppermute | solution.py:459
  12.0 4.3 %forward_first.2 = (f32[16,2,128,256]{3,2,1,0:T(8,128)S(1)}, f32[64,256]{1,0:T(8,128)S(1)}, f32[64,256]{1,0:T(8,128)S(1)}, f32[64,256]{1,0:T(8,128)S(1)}, f32[64,256]{1,0:T(8,128)S(1)}) custom-call(s32[2]{0:T(128)S(1)} %pad_add_fusion.place, f32[4352,128]{1,0:T(8,128)S(1)} %get-tuple-element.37.keep, f32[4352,128]{1,0:T(8,128)S(1)} %collective-permute-done.got, ...), custom_call_target="tpu_custom_call" | custom-call | flops 2147483648 | bytes 8388608 | tf_op jit(solution)/shard_map/forward_first/pallas_call | solution.py:280
  16.3 2.6 %collective-permute-start.1 = (f32[64,256]{1,0:T(8,128)S(1)}, f32[64,256]{1,0:T(8,128)S(1)}, u32[]{:S(2)}, u32[]{:S(2)}) collective-permute-start(f32[64,256]{1,0:T(8,128)S(1)} %get-tuple-element.41), channel_id=1, source_target_pairs={{0,2},{2,0},{4,6},{6,4},{8,10},{10,8},{12,14},{14,12},{1,3},{3,1},... | collective-permute-start | bytes 196616 | tf_op jit(solution)/shard_map/ppermute | solution.py:464
  18.9 1.6 %collective-permute-start.2 = (f32[64,256]{1,0:T(8,128)S(1)}, f32[64,256]{1,0:T(8,128)S(1)}, u32[]{:S(2)}, u32[]{:S(2)}) collective-permute-start(f32[64,256]{1,0:T(8,128)S(1)} %get-tuple-element.42), channel_id=1, source_target_pairs={{0,4},{2,6},{4,0},{6,2},{8,12},{10,14},{12,8},{14,10},{1,5},{3,7},... | collective-permute-start | bytes 196616 | tf_op jit(solution)/shard_map/ppermute | solution.py:464
  20.5 4.3 %forward_first.3 = (f32[16,2,128,256]{3,2,1,0:T(8,128)S(1)}, f32[64,256]{1,0:T(8,128)S(1)}, f32[64,256]{1,0:T(8,128)S(1)}, f32[64,256]{1,0:T(8,128)S(1)}, f32[64,256]{1,0:T(8,128)S(1)}) custom-call(s32[2]{0:T(128)S(1)} %pad_add_fusion.place, f32[4352,128]{1,0:T(8,128)S(1)} %get-tuple-element.51.keep, f32[4352,128]{1,0:T(8,128)S(1)} %collective-permute-done.8.got, ...), custom_call_target="tpu_custom_call" | custom-call | flops 2147483648 | bytes 8388608 | tf_op jit(solution)/shard_map/forward_first/pallas_call | solution.py:280
  24.8 2.0 %collective-permute-start.9 = (f32[64,256]{1,0:T(8,128)S(1)}, f32[64,256]{1,0:T(8,128)S(1)}, u32[]{:S(2)}, u32[]{:S(2)}) collective-permute-start(f32[64,256]{1,0:T(8,128)S(1)} %get-tuple-element.55), channel_id=1, source_target_pairs={{0,2},{2,0},{4,6},{6,4},{8,10},{10,8},{12,14},{14,12},{1,3},{3,1},... | collective-permute-start | bytes 196616 | tf_op jit(solution)/shard_map/ppermute | solution.py:464
  26.8 1.6 %collective-permute-start.10 = (f32[64,256]{1,0:T(8,128)S(1)}, f32[64,256]{1,0:T(8,128)S(1)}, u32[]{:S(2)}, u32[]{:S(2)}) collective-permute-start(f32[64,256]{1,0:T(8,128)S(1)} %get-tuple-element.56), channel_id=1, source_target_pairs={{0,4},{2,6},{4,0},{6,2},{8,12},{10,14},{12,8},{14,10},{1,5},{3,7},... | collective-permute-start | bytes 196616 | tf_op jit(solution)/shard_map/ppermute | solution.py:464
  28.4 0.6 half_sum.2
  29.0 3.0 %collective-permute-start.4 = (f32[64,256]{1,0:T(8,128)S(1)}, f32[64,256]{1,0:T(8,128)S(1)}, u32[]{:S(2)}, u32[]{:S(2)}) collective-permute-start(f32[64,256]{1,0:T(8,128)S(1)} %get-tuple-element.45.near), channel_id=1, source_target_pairs={{0,8},{2,10},{4,12},{6,14},{8,0},{10,2},{12,4},{14,6},{1,9},{3,11}... | collective-permute-start | bytes 196616 | tf_op jit(solution)/shard_map/ppermute | solution.py:464
  32.0 1.8 %collective-permute-done.11.refs_3_ = f32[64,256]{1,0:T(8,128)S(1)} collective-permute-done((f32[64,256]{1,0:T(8,128)S(1)}, f32[64,256]{1,0:T(8,128)S(1)}, u32[]{:S(2)}, u32[]{:S(2)}) %collective-permute-start.11) | collective-permute-done | bytes 65568 | tf_op jit(solution)/shard_map/ppermute | solution.py:464
  33.8 0.6 half_sum.3
  34.4 2.4 %collective-permute-start.12 = (f32[64,256]{1,0:T(8,128)S(1)}, f32[64,256]{1,0:T(8,128)S(1)}, u32[]{:S(2)}, u32[]{:S(2)}) collective-permute-start(f32[64,256]{1,0:T(8,128)S(1)} %get-tuple-element.59.near), channel_id=1, source_target_pairs={{0,8},{2,10},{4,12},{6,14},{8,0},{10,2},{12,4},{14,6},{1,9},{3,11}... | collective-permute-start | bytes 196616 | tf_op jit(solution)/shard_map/ppermute | solution.py:464
  36.8 0.6 close.2
  37.4 0.6 collective-permute-start.5
  38.0 1.6 %collective-permute-start.6 = (f32[64,256]{1,0:T(8,128)S(1)}, f32[64,256]{1,0:T(8,128)S(1)}, u32[]{:S(2)}, u32[]{:S(2)}) collective-permute-start(f32[64,256]{1,0:T(8,128)S(1)} %get-tuple-element.48), channel_id=1, source_target_pairs={{0,4},{2,6},{4,0},{6,2},{8,12},{10,14},{12,8},{14,10},{1,5},{3,7},... | collective-permute-start | bytes 196616 | tf_op jit(solution)/shard_map/ppermute | solution.py:464
  39.6 1.4 %collective-permute-start.7 = (f32[64,256]{1,0:T(8,128)S(1)}, f32[64,256]{1,0:T(8,128)S(1)}, u32[]{:S(2)}, u32[]{:S(2)}) collective-permute-start(f32[64,256]{1,0:T(8,128)S(1)} %get-tuple-element.49), channel_id=1, source_target_pairs={{0,6},{2,4},{4,2},{6,0},{8,14},{10,12},{12,10},{14,8},{1,7},{3,5},... | collective-permute-start | bytes 196616 | tf_op jit(solution)/shard_map/ppermute | solution.py:464
  41.0 0.6 close.3
  41.6 0.6 collective-permute-start.13
  42.1 1.6 %collective-permute-start.14 = (f32[64,256]{1,0:T(8,128)S(1)}, f32[64,256]{1,0:T(8,128)S(1)}, u32[]{:S(2)}, u32[]{:S(2)}) collective-permute-start(f32[64,256]{1,0:T(8,128)S(1)} %get-tuple-element.62), channel_id=1, source_target_pairs={{0,4},{2,6},{4,0},{6,2},{8,12},{10,14},{12,8},{14,10},{1,5},{3,7},... | collective-permute-start | bytes 196616 | tf_op jit(solution)/shard_map/ppermute | solution.py:464
  43.7 1.4 %collective-permute-start.15 = (f32[64,256]{1,0:T(8,128)S(1)}, f32[64,256]{1,0:T(8,128)S(1)}, u32[]{:S(2)}, u32[]{:S(2)}) collective-permute-start(f32[64,256]{1,0:T(8,128)S(1)} %get-tuple-element.63), channel_id=1, source_target_pairs={{0,6},{2,4},{4,2},{6,0},{8,14},{10,12},{12,10},{14,8},{1,7},{3,5},... | collective-permute-start | bytes 196616 | tf_op jit(solution)/shard_map/ppermute | solution.py:464
  45.2 3.4 %inverse_first.2 = (f32[4096,128]{1,0:T(8,128)S(1)}, f32[4096,128]{1,0:T(8,128)S(1)}) custom-call(s32[2]{0:T(128)S(1)} %pad_add_fusion.place, f32[16,2,128,256]{3,2,1,0:T(8,128)S(1)} %get-tuple-element.39.modes, bf16[2,2,768,256]{3,2,1,0:T(8,128)(2,1)S(1)} %copy-done.2, f32[2,2,256,256]{3,2,1,0:T(8,128)S(1)} %copy-done.4, ...), custom_call_target="tpu_custom_call" | custom-call | flops 2147483648 | bytes 8388608 | tf_op jit(solution)/shard_map/inverse_first/pallas_call | solution.py:388
  48.6 0.3 collective-permute-done.15.refs_3_
  48.9 3.2 %inverse_first.3 = (f32[4096,128]{1,0:T(8,128)S(1)}, f32[4096,128]{1,0:T(8,128)S(1)}) custom-call(s32[2]{0:T(128)S(1)} %pad_add_fusion.place, f32[16,2,128,256]{3,2,1,0:T(8,128)S(1)} %get-tuple-element.53.modes, bf16[2,2,768,256]{3,2,1,0:T(8,128)(2,1)S(1)} %copy-done.2, f32[2,2,256,256]{3,2,1,0:T(8,128)S(1)} %copy-done.4, ...), custom_call_target="tpu_custom_call" | custom-call | flops 2147483648 | bytes 8388608 | tf_op jit(solution)/shard_map/inverse_first/pallas_call | solution.py:388
  52.1 0.3 collective-permute-start.17
  52.4 3.2 %keep_inverse.1 = f32[4096,256]{1,0:T(8,128)S(1)} custom-call(s32[2]{0:T(128)S(1)} %pad_add_fusion.place, bf16[2,768,256]{2,1,0:T(8,128)(2,1)S(1)} %copy-done.1, f32[4096,128]{1,0:T(8,128)S(1)} %get-tuple-element.50.refs_0_, f32[4096,128]{1,0:T(8,128)S(1)} %get-tuple-element.64.refs_1_), custom_call_target="tpu_custom_call" | custom-call | flops 2147483648 | bytes 8388608 | tf_op jit(solution)/shard_map/keep_inverse/pallas_call | solution.py:222
  55.6 0.7 %collective-permute-done.17 = f32[4096,128]{1,0:T(8,128)S(1)} collective-permute-done((f32[4096,128]{1,0:T(8,128)S(1)}, f32[4096,128]{1,0:T(8,128)S(1)}, u32[]{:S(2)}, u32[]{:S(2)}) %collective-permute-start.17) | collective-permute-done | bytes 2097184 | tf_op jit(solution)/shard_map/ppermute | solution.py:459
  56.3 6.6 %inverse_second.1 = f32[256,16,512]{2,1,0:T(8,128)} custom-call(s32[2]{0:T(128)S(1)} %pad_add_fusion.place, bf16[2,768,256]{2,1,0:T(8,128)(2,1)S(1)} %copy-done.1, f32[16,256,256]{2,1,0:T(8,128)S(1)} %bitcast.5, f32[16,256,128]{2,1,0:T(8,128)S(1)} %bitcast.6, f32[16,256,128]{2,1,0:T(8,128)S(1)} %bitcast.7), custom_call_target="tpu_custom_call" | custom-call | flops 4294967296 | bytes 8388608 | tf_op jit(solution)/shard_map/inverse_second/pallas_call | solution.py:442
  (29 shorter events, 0.1 us)
Async XLA Ops:
  0.1 8.1 %copy-start.5 = (bf16[2,768,256]{2,1,0:T(8,128)(2,1)S(1)}, bf16[2,768,256]{2,1,0:T(8,128)(2,1)}, u32[]{:S(2)}) copy-start(bf16[2,768,256]{2,1,0:T(8,128)(2,1)} %constant.23.clone.table.tables) | copy-start | bytes 2359300
  7.2 4.9 %collective-permute-start = (f32[4352,128]{1,0:T(8,128)S(1)}, f32[4352,128]{1,0:T(8,128)S(1)}, u32[]{:S(2)}, u32[]{:S(2)}) collective-permute-start(f32[4352,128]{1,0:T(8,128)S(1)} %get-tuple-element.38), channel_id=1, source_target_pairs={{0,1},{1,0},{2,3},{3,2},{4,5},{5,4},{6,7},{7,6},{8,9},{9,8},{10,11... | collective-permute-start | bytes 6684680 | tf_op jit(solution)/shard_map/ppermute | solution.py:459
  8.1 12.4 %collective-permute-start.8 = (f32[4352,128]{1,0:T(8,128)S(1)}, f32[4352,128]{1,0:T(8,128)S(1)}, u32[]{:S(2)}, u32[]{:S(2)}) collective-permute-start(f32[4352,128]{1,0:T(8,128)S(1)} %get-tuple-element.52), channel_id=1, source_target_pairs={{0,1},{1,0},{2,3},{3,2},{4,5},{5,4},{6,7},{7,6},{8,9},{9,8},{10,11... | collective-permute-start | bytes 6684680 | tf_op jit(solution)/shard_map/ppermute | solution.py:459
  8.1 3.9 %copy-start.3 = (bf16[2,2,768,256]{3,2,1,0:T(8,128)(2,1)S(1)}, bf16[2,2,768,256]{3,2,1,0:T(8,128)(2,1)}, u32[]{:S(2)}) copy-start(bf16[2,2,768,256]{3,2,1,0:T(8,128)(2,1)} %constant.21.clone.table) | copy-start | bytes 4718596
  8.1 3.9 %copy-start.4 = (f32[2,2,256,256]{3,2,1,0:T(8,128)S(1)}, f32[2,2,256,256]{3,2,1,0:T(8,128)}, u32[]{:S(2)}) copy-start(f32[2,2,256,256]{3,2,1,0:T(8,128)} %constant.22.clone.decay) | copy-start | bytes 3145732
  16.3 12.1 %collective-permute-start.1 = (f32[64,256]{1,0:T(8,128)S(1)}, f32[64,256]{1,0:T(8,128)S(1)}, u32[]{:S(2)}, u32[]{:S(2)}) collective-permute-start(f32[64,256]{1,0:T(8,128)S(1)} %get-tuple-element.41), channel_id=1, source_target_pairs={{0,2},{2,0},{4,6},{6,4},{8,10},{10,8},{12,14},{14,12},{1,3},{3,1},... | collective-permute-start | bytes 196616 | tf_op jit(solution)/shard_map/ppermute | solution.py:464
  18.9 9.5 %collective-permute-start.2 = (f32[64,256]{1,0:T(8,128)S(1)}, f32[64,256]{1,0:T(8,128)S(1)}, u32[]{:S(2)}, u32[]{:S(2)}) collective-permute-start(f32[64,256]{1,0:T(8,128)S(1)} %get-tuple-element.42), channel_id=1, source_target_pairs={{0,4},{2,6},{4,0},{6,2},{8,12},{10,14},{12,8},{14,10},{1,5},{3,7},... | collective-permute-start | bytes 196616 | tf_op jit(solution)/shard_map/ppermute | solution.py:464
  20.5 7.9 %collective-permute-start.3 = (f32[64,256]{1,0:T(8,128)S(1)}, f32[64,256]{1,0:T(8,128)S(1)}, u32[]{:S(2)}, u32[]{:S(2)}) collective-permute-start(f32[64,256]{1,0:T(8,128)S(1)} %get-tuple-element.43), channel_id=1, source_target_pairs={{0,6},{2,4},{4,2},{6,0},{8,14},{10,12},{12,10},{14,8},{1,7},{3,5},... | collective-permute-start | bytes 196616 | tf_op jit(solution)/shard_map/ppermute | solution.py:464
  20.5 8.0 %copy-start = (f32[2,2,3,256,256]{4,3,2,1,0:T(8,128)S(1)}, f32[2,2,3,256,256]{4,3,2,1,0:T(8,128)}, u32[]{:S(2)}) copy-start(f32[2,2,3,256,256]{4,3,2,1,0:T(8,128)} %constant.20.clone.closing) | copy-start | bytes 9437188
  24.8 7.2 %collective-permute-start.9 = (f32[64,256]{1,0:T(8,128)S(1)}, f32[64,256]{1,0:T(8,128)S(1)}, u32[]{:S(2)}, u32[]{:S(2)}) collective-permute-start(f32[64,256]{1,0:T(8,128)S(1)} %get-tuple-element.55), channel_id=1, source_target_pairs={{0,2},{2,0},{4,6},{6,4},{8,10},{10,8},{12,14},{14,12},{1,3},{3,1},... | collective-permute-start | bytes 196616 | tf_op jit(solution)/shard_map/ppermute | solution.py:464
  26.8 5.2 %collective-permute-start.10 = (f32[64,256]{1,0:T(8,128)S(1)}, f32[64,256]{1,0:T(8,128)S(1)}, u32[]{:S(2)}, u32[]{:S(2)}) collective-permute-start(f32[64,256]{1,0:T(8,128)S(1)} %get-tuple-element.56), channel_id=1, source_target_pairs={{0,4},{2,6},{4,0},{6,2},{8,12},{10,14},{12,8},{14,10},{1,5},{3,7},... | collective-permute-start | bytes 196616 | tf_op jit(solution)/shard_map/ppermute | solution.py:464
  28.4 5.4 %collective-permute-start.11 = (f32[64,256]{1,0:T(8,128)S(1)}, f32[64,256]{1,0:T(8,128)S(1)}, u32[]{:S(2)}, u32[]{:S(2)}) collective-permute-start(f32[64,256]{1,0:T(8,128)S(1)} %get-tuple-element.57), channel_id=1, source_target_pairs={{0,6},{2,4},{4,2},{6,0},{8,14},{10,12},{12,10},{14,8},{1,7},{3,5},... | collective-permute-start | bytes 196616 | tf_op jit(solution)/shard_map/ppermute | solution.py:464
  29.0 7.8 %collective-permute-start.4 = (f32[64,256]{1,0:T(8,128)S(1)}, f32[64,256]{1,0:T(8,128)S(1)}, u32[]{:S(2)}, u32[]{:S(2)}) collective-permute-start(f32[64,256]{1,0:T(8,128)S(1)} %get-tuple-element.45.near), channel_id=1, source_target_pairs={{0,8},{2,10},{4,12},{6,14},{8,0},{10,2},{12,4},{14,6},{1,9},{3,11}... | collective-permute-start | bytes 196616 | tf_op jit(solution)/shard_map/ppermute | solution.py:464
  34.4 6.5 %collective-permute-start.12 = (f32[64,256]{1,0:T(8,128)S(1)}, f32[64,256]{1,0:T(8,128)S(1)}, u32[]{:S(2)}, u32[]{:S(2)}) collective-permute-start(f32[64,256]{1,0:T(8,128)S(1)} %get-tuple-element.59.near), channel_id=1, source_target_pairs={{0,8},{2,10},{4,12},{6,14},{8,0},{10,2},{12,4},{14,6},{1,9},{3,11}... | collective-permute-start | bytes 196616 | tf_op jit(solution)/shard_map/ppermute | solution.py:464
  37.4 7.7 %copy-start.2 = (bf16[2,2,768,256]{3,2,1,0:T(8,128)(2,1)S(1)}, bf16[2,2,768,256]{3,2,1,0:T(8,128)(2,1)}, u32[]{:S(2)}) copy-start(bf16[2,2,768,256]{3,2,1,0:T(8,128)(2,1)} %constant.24.clone.table) | copy-start | bytes 4718596
  37.4 6.3 %collective-permute-start.5 = (f32[64,256]{1,0:T(8,128)S(1)}, f32[64,256]{1,0:T(8,128)S(1)}, u32[]{:S(2)}, u32[]{:S(2)}) collective-permute-start(f32[64,256]{1,0:T(8,128)S(1)} %get-tuple-element.47), channel_id=1, source_target_pairs={{0,2},{2,0},{4,6},{6,4},{8,10},{10,8},{12,14},{14,12},{1,3},{3,1},... | collective-permute-start | bytes 196616 | tf_op jit(solution)/shard_map/ppermute | solution.py:464
  38.0 7.2 %collective-permute-start.6 = (f32[64,256]{1,0:T(8,128)S(1)}, f32[64,256]{1,0:T(8,128)S(1)}, u32[]{:S(2)}, u32[]{:S(2)}) collective-permute-start(f32[64,256]{1,0:T(8,128)S(1)} %get-tuple-element.48), channel_id=1, source_target_pairs={{0,4},{2,6},{4,0},{6,2},{8,12},{10,14},{12,8},{14,10},{1,5},{3,7},... | collective-permute-start | bytes 196616 | tf_op jit(solution)/shard_map/ppermute | solution.py:464
  39.6 5.6 %collective-permute-start.7 = (f32[64,256]{1,0:T(8,128)S(1)}, f32[64,256]{1,0:T(8,128)S(1)}, u32[]{:S(2)}, u32[]{:S(2)}) collective-permute-start(f32[64,256]{1,0:T(8,128)S(1)} %get-tuple-element.49), channel_id=1, source_target_pairs={{0,6},{2,4},{4,2},{6,0},{8,14},{10,12},{12,10},{14,8},{1,7},{3,5},... | collective-permute-start | bytes 196616 | tf_op jit(solution)/shard_map/ppermute | solution.py:464
  41.6 7.0 %collective-permute-start.13 = (f32[64,256]{1,0:T(8,128)S(1)}, f32[64,256]{1,0:T(8,128)S(1)}, u32[]{:S(2)}, u32[]{:S(2)}) collective-permute-start(f32[64,256]{1,0:T(8,128)S(1)} %get-tuple-element.61), channel_id=1, source_target_pairs={{0,2},{2,0},{4,6},{6,4},{8,10},{10,8},{12,14},{14,12},{1,3},{3,1},... | collective-permute-start | bytes 196616 | tf_op jit(solution)/shard_map/ppermute | solution.py:464
  42.1 6.5 %collective-permute-start.14 = (f32[64,256]{1,0:T(8,128)S(1)}, f32[64,256]{1,0:T(8,128)S(1)}, u32[]{:S(2)}, u32[]{:S(2)}) collective-permute-start(f32[64,256]{1,0:T(8,128)S(1)} %get-tuple-element.62), channel_id=1, source_target_pairs={{0,4},{2,6},{4,0},{6,2},{8,12},{10,14},{12,8},{14,10},{1,5},{3,7},... | collective-permute-start | bytes 196616 | tf_op jit(solution)/shard_map/ppermute | solution.py:464
  43.7 5.2 %collective-permute-start.15 = (f32[64,256]{1,0:T(8,128)S(1)}, f32[64,256]{1,0:T(8,128)S(1)}, u32[]{:S(2)}, u32[]{:S(2)}) collective-permute-start(f32[64,256]{1,0:T(8,128)S(1)} %get-tuple-element.63), channel_id=1, source_target_pairs={{0,6},{2,4},{4,2},{6,0},{8,14},{10,12},{12,10},{14,8},{1,7},{3,5},... | collective-permute-start | bytes 196616 | tf_op jit(solution)/shard_map/ppermute | solution.py:464
  48.5 7.1 %collective-permute-start.16 = (f32[4096,128]{1,0:T(8,128)S(1)}, f32[4096,128]{1,0:T(8,128)S(1)}, u32[]{:S(2)}, u32[]{:S(2)}) collective-permute-start(f32[4096,128]{1,0:T(8,128)S(1)} %get-tuple-element.65), channel_id=1, source_target_pairs={{0,1},{1,0},{2,3},{3,2},{4,5},{5,4},{6,7},{7,6},{8,9},{9,8},{10,11... | collective-permute-start | bytes 6291464 | tf_op jit(solution)/shard_map/ppermute | solution.py:459
  48.9 3.5 %copy-start.1 = (bf16[2,768,256]{2,1,0:T(8,128)(2,1)S(1)}, bf16[2,768,256]{2,1,0:T(8,128)(2,1)}, u32[]{:S(2)}) copy-start(bf16[2,768,256]{2,1,0:T(8,128)(2,1)} %constant.25.clone.tables) | copy-start | bytes 2359300
  52.1 4.2 %collective-permute-start.17 = (f32[4096,128]{1,0:T(8,128)S(1)}, f32[4096,128]{1,0:T(8,128)S(1)}, u32[]{:S(2)}, u32[]{:S(2)}) collective-permute-start(f32[4096,128]{1,0:T(8,128)S(1)} %get-tuple-element.66), channel_id=1, source_target_pairs={{0,1},{1,0},{2,3},{3,2},{4,5},{5,4},{6,7},{7,6},{8,9},{9,8},{10,11... | collective-permute-start | bytes 6291464 | tf_op jit(solution)/shard_map/ppermute | solution.py:459

commit v6 on v5

--- a/solution.py
+++ b/solution.py
@@ -178,7 +178,7 @@
 def forward_second(place, field, initial, tables):
     rows, steps, width = field.shape
     half = width // 2
-    block, pieces = min(64, rows), 2
+    block, pieces = min(32, rows), 2
     depth = (steps + 1) * block // pieces
     outs = call(
         forward_second_kernel,
@@ -198,45 +198,43 @@
     return outs[0], outs[1:]
 
 
-def times_table_kernel(inputs, place, tables, *refs):
-    sources, refs = refs[:inputs], refs[inputs:]
-    outs, scratch = refs[:-2], refs[-2:]
-    piece = scratch[0].shape[0]
-    for at in range(0, sources[0].shape[0], piece):
-        split = scratch[at // piece % 2]
-        for row in range(0, piece, TILE):
-            lane = 0
-            for source in sources:
-                store_split(split, (pl.ds(row, TILE),), lane, source[pl.ds(at + row, TILE)])
-                lane += source.shape[1]
+def keep_second_kernel(place, tables, sums, *refs):
+    keeps, scratch = refs[:CHUNKS], refs[CHUNKS:]
+    depth = scratch[0].shape[0]
+    for at in range(0, sums.shape[0], depth):
+        split = scratch[at // depth % 2]
+        for row in range(0, depth, TILE):
+            store_split(split, (pl.ds(row, TILE),), 0, sums[pl.ds(at + row, TILE)])
         result = dot(split[...], tables[place[1]])
-        lane = 0
-        for out in outs:
-            out[pl.ds(at, piece)] = result[:, lane : lane + out.shape[1]]
-            lane += out.shape[1]
-
-
-def times_table(place, sources, tables, widths, name):
-    rows = sources[0].shape[0]
-    depth = tables.shape[1]
+        for chunk, keep in enumerate(keeps):
+            part = keep.shape[1]
+            keep[pl.ds(at, depth)] = result[:, chunk * part : (chunk + 1) * part]
+
+
+def keep_second(place, sums, tables):
+    rows, half = sums.shape
     return call(
-        functools.partial(times_table_kernel, len(sources)),
-        name,
-        [IN_VMEM] * (1 + len(sources)),
-        [IN_VMEM] * len(widths),
-        [floats(rows, width) for width in widths],
-        [pltpu.VMEM((rows // 8, depth), jnp.bfloat16)] * 2,
+        keep_second_kernel,
+        "keep_second",
+        [IN_VMEM] * 2,
+        [IN_VMEM] * CHUNKS,
+        [floats(rows, half // CHUNKS)] * CHUNKS,
+        [pltpu.VMEM((rows // 8, 3 * half), jnp.bfloat16)] * 2,
         1 << 31,
-    )(place, tables, *sources)
+    )(place, tables, sums)
 
 
 def ranks(slabs):
     return slabs // 2
 
 
+def parcels(size):
+    return [(0,), (1,), (2, 3)] if size == 4 else [(partner,) for partner in range(size)]
+
+
 def forward_first_kernel(slabs, chunk, place, keep, got, table, decay, modes, *refs):
     size = ranks(slabs)
-    lasts, (state, split, split_end) = refs[:size], refs[size:]
+    lasts, (state, split, split_end) = refs[:-3], refs[-3:]
     steps, _, part, rows = modes.shape
     block = split.shape[1] // part
     strip = place[1]
@@ -266,9 +264,10 @@
         state[at_state] = state[at_state] - is_last * dot(split_end[c], table[strip, c])
     rank = lax.rem(place[0], size)
     share = 2 * part // size
-    for partner in range(size):
-        at = pl.multiple_of((rank ^ partner) * share, share)
-        lasts[partner][...] = state[pl.ds(at, share)]
+    for parcel, last in zip(parcels(size), lasts):
+        for place_in, partner in enumerate(parcel):
+            at = pl.multiple_of((rank ^ partner) * share, share)
+            last[pl.ds(place_in * share, share)] = state[pl.ds(at, share)]
 
 
 def forward_first(place, chunk, keep, got, tables, decays, slabs):
@@ -281,8 +280,9 @@
         functools.partial(forward_first_kernel, slabs, chunk),
         "forward_first",
         [IN_VMEM] * 4,
-        [IN_VMEM] * (1 + size),
-        [floats(steps, 2, part, rows)] + [floats(share, rows)] * size,
+        [IN_VMEM] * (1 + len(parcels(size))),
+        [floats(steps, 2, part, rows)]
+        + [floats(len(parcel) * share, rows) for parcel in parcels(size)],
         [
             pltpu.VMEM((2 * part, rows), jnp.float32),
             pltpu.VMEM((2, block * part, 3 * rows), jnp.bfloat16),
@@ -300,7 +300,7 @@
     rank = lax.rem(place[0], size)
     decay = closing[place[1], chunk, 0, pl.ds(pl.multiple_of(rank * share, share), share)]
     for partner in range(size):
-        ordered[rank ^ partner] = lasts[partner][...]
+        ordered[rank ^ partner] = lasts[partner][pl.ds(0, share)]
     state = ordered[0]
     for at in range(1, size):
         state = ordered[at] + decay * state
@@ -323,7 +323,7 @@
 
 def close_kernel(slabs, chunk, place, closing, ordered, near, far, *refs):
     size = ranks(slabs)
-    befores, states = refs[:size], refs[size]
+    befores, states = refs[:-1], refs[-1]
     share = near.shape[0]
     rank = lax.rem(place[0], size)
     at_share = pl.ds(pl.multiple_of(rank * share, share), share)
@@ -334,8 +334,9 @@
         states[at] = state
         if at < size - 1:
             state = ordered[at] + decay * state
-    for partner in range(size):
-        befores[partner][...] = states[rank ^ partner]
+    for parcel, before in zip(parcels(size), befores):
+        for place_in, partner in enumerate(parcel):
+            before[pl.ds(place_in * share, share)] = states[rank ^ partner]
 
 
 def close(place, chunk, ordered, near, far, closing, slabs):
@@ -344,8 +345,8 @@
         functools.partial(close_kernel, slabs, chunk),
         "close",
         [IN_VMEM] * 4,
-        [IN_VMEM] * size,
-        [floats(share, rows)] * size,
+        [IN_VMEM] * len(parcels(size)),
+        [floats(len(parcel) * share, rows) for parcel in parcels(size)],
         [pltpu.VMEM((size, share, rows), jnp.float32)],
         1 << 20,
     )(place, closing, ordered, near, far)
@@ -361,7 +362,7 @@
     share = 2 * part // size
     for partner in range(size):
         at = pl.multiple_of((rank ^ partner) * share, share)
-        state[pl.ds(at, share)] = befores[partner][...]
+        state[pl.ds(at, share)] = befores[partner][pl.ds(0, share)]
     for step in range(0, steps, block):
         results = []
         for c in (0, 1):
@@ -379,7 +380,7 @@
             piece = slice(at * part, (at + 1) * part)
             start = (step + at) * rows
             keep[pl.ds(start, rows), :] = (even[piece] + odd[piece]).T
-            store_rows_reversed(send, start, (even[piece] - odd[piece]).T)
+            send[pl.ds(start, rows), :] = (even[piece] - odd[piece]).T
 
 
 def inverse_first(place, chunk, modes, befores, tables, decays, slabs):
@@ -399,6 +400,41 @@
     )(place, modes, tables, decays, *befores)
 
 
+def steps_of(ref, cells, steps):
+    pitch = ref.shape[0] // steps
+    lines = [ref[pl.ds(cell, steps, stride=pitch), :] for cell in cells]
+    return lines[0] if len(lines) == 1 else jnp.concatenate(lines, axis=0)
+
+
+def keep_inverse_kernel(steps, place, tables, *refs):
+    keeps, out, scratch = refs[:CHUNKS], refs[CHUNKS], refs[CHUNKS + 1 :]
+    part = keeps[0].shape[1]
+    depth = scratch[0].shape[0]
+    group = max(TILE // steps, 1)
+    for at in range(0, out.shape[0], depth):
+        split = scratch[at // depth % 2]
+        for row in range(0, depth, TILE):
+            cell = (at + row) // steps
+            for chunk, keep in enumerate(keeps):
+                cells = steps_of(keep, range(cell, cell + group), steps)
+                store_split(split, (pl.ds(row, TILE),), chunk * part, cells)
+        out[pl.ds(at, depth)] = dot(split[...], tables[place[1]])
+
+
+def keep_inverse(place, keeps, tables, steps):
+    rows, part = keeps[0].shape
+    half = part * CHUNKS
+    return call(
+        functools.partial(keep_inverse_kernel, steps),
+        "keep_inverse",
+        [IN_VMEM] * (1 + CHUNKS),
+        IN_VMEM,
+        floats(rows, half),
+        [pltpu.VMEM((rows // 8, 3 * half), jnp.bfloat16)] * 2,
+        1 << 31,
+    )(place, tables, *keeps)
+
+
 def inverse_second_kernel(place, tables, kept, *refs):
     gots, out, scratch = refs[:CHUNKS], refs[CHUNKS], refs[CHUNKS + 1 :]
     rows, steps, width = out.shape
@@ -406,49 +442,43 @@
     part = half // CHUNKS
     count = len(scratch) // 2
     piece = rows // count
-    group = min(SUBLANES, steps)
+    group = max(TILE // steps, 1)
     strip = place[1]
     sign = 1.0 - 2.0 * strip.astype(jnp.float32)
+    total = rows * pl.num_programs(0)
     start = pl.program_id(0) * rows
     for sub in range(count):
         split, result = scratch[2 * sub : 2 * sub + 2]
-        base = pl.multiple_of(start + sub * piece, piece)
-        for step in range(steps):
-            for row in range(0, piece, TILE):
-                for chunk, got in enumerate(gots):
-                    cells = got[step, pl.ds(base + row, TILE)]
-                    store_split(split, (step, pl.ds(row, TILE)), chunk * part, cells)
-        product = dot(split[...].reshape(steps * piece, 3 * half), tables[1 - strip])
-        result[...] = product.reshape(result.shape)
-        for row in range(0, piece, SUBLANES):
-            for step in range(0, steps, group):
-                for lane in range(0, half, LANES):
-                    at_steps, at_lanes = pl.ds(step, group), pl.ds(lane, LANES)
-                    first = kept[at_steps, pl.ds(base + row, SUBLANES), at_lanes]
-                    second = result[at_steps, pl.ds(row, SUBLANES), at_lanes]
-                    upper = sign * (first - second)
-                    upper = lanes_reversed(upper.reshape(-1, LANES)).reshape(upper.shape)
-                    to = (pl.ds(sub * piece + row, SUBLANES), at_steps)
-                    out[(*to, at_lanes)] = jnp.swapaxes(first + second, 0, 1)
-                    to_lanes = pl.ds(width - LANES - lane, LANES)
-                    out[(*to, to_lanes)] = jnp.swapaxes(upper, 0, 1)
-
-
-def inverse_second(place, kept, gots, tables):
-    steps, rows, part = gots[0].shape
-    half = part * CHUNKS
-    block, pieces = min(64, rows), 2
-    piece = block // pieces
+        base = start + sub * piece
+        for row in range(0, piece, group):
+            mirrors = [total - 1 - base - row - at for at in range(group)]
+            for chunk, got in enumerate(gots):
+                cells = steps_of(got, mirrors, steps)
+                store_split(split, (pl.ds(row * steps, TILE),), chunk * part, cells)
+        result[...] = dot(split[...], tables[1 - strip])
+        kept_base = pl.multiple_of(base * steps, piece * steps)
+        for row in range(0, piece, group):
+            first = kept[pl.ds(kept_base + row * steps, TILE)]
+            second = result[pl.ds(row * steps, TILE)]
+            upper = sign * (first - second)
+            parts = [
+                lanes_reversed(upper[:, lane : lane + LANES]) for lane in range(0, half, LANES)
+            ][::-1]
+            whole = jnp.concatenate([first + second, *parts], axis=1)
+            out[pl.ds(sub * piece + row, group)] = whole.reshape(group, TILE // group, width)
+
+
+def inverse_second(place, kept, gots, tables, steps):
+    rows, half = kept.shape[0] // steps, kept.shape[1]
+    block, pieces = min(32, rows), 2
+    depth = steps * block // pieces
     return call(
         inverse_second_kernel,
         "inverse_second",
         [IN_VMEM] * (2 + CHUNKS),
         pl.BlockSpec((block, steps, 2 * half), lambda i, place: (i, 0, 0)),
         floats(rows, steps, 2 * half),
-        [
-            pltpu.VMEM((steps, piece, 3 * half), jnp.bfloat16),
-            pltpu.VMEM((steps, piece, half), jnp.float32),
-        ]
+        [pltpu.VMEM((depth, 3 * half), jnp.bfloat16), pltpu.VMEM((depth, half), jnp.float32)]
         * pieces,
         1 << 32,
         rows // block,
@@ -465,7 +495,12 @@
 
 
 def among_ranks(blocks):
-    return [blocks[0]] + [with_partner(block, at) for at, block in enumerate(blocks) if at]
+    if len(blocks) != 3:
+        return [blocks[0]] + [with_partner(block, at) for at, block in enumerate(blocks) if at]
+    own, near, pair = blocks
+    pair = with_partner(pair, 2)
+    near = with_partner(near, 1)
+    return [own, near, pair, with_partner(pair[own.shape[0] :], 1)]
 
 
 def by_chunk(table):
@@ -489,11 +524,10 @@
         np.stack([by_chunk(table) for table in (slab_decay, half_decay, gain)], axis=2)
     )
     first_table, decays = split_constant(first), constant(decay)
-    half = width // 2
     second_table = split_constant(second)
     sums, sends = forward_second(place, iterate, initial, second_table)
     gots = [swapped(send) for send in sends]
-    keeps = times_table(place, [sums], second_table, [half // CHUNKS] * CHUNKS, "keep_second")
+    keeps = keep_second(place, sums, second_table)
     modes, befores = [], []
     for chunk in range(CHUNKS):
         own_modes, lasts = forward_first(
@@ -510,10 +544,10 @@
             for chunk in range(CHUNKS)
         )
     )
-    gots = [swapped(send).reshape(steps, rows, -1) for send in sends]
+    gots = [swapped(send) for send in sends]
     inverse_table = split_constant(np.swapaxes(second, 1, 2))
-    kept = times_table(place, keeps, inverse_table, [half], "keep_inverse")[0]
-    return inverse_second(place, kept.reshape(steps, rows, half), gots, inverse_table)
+    kept = keep_inverse(place, keeps, inverse_table, steps)
+    return inverse_second(place, kept, gots, inverse_table, steps)
 
 
 def solution(mesh):

time: 63.1 us -> 73.7 us (1.17)
  Pallas kernels: 36.9 us -> 45.2 us
  starting transfers between devices: 21.5 us -> 23 us
  waiting for transfers between devices: 4.26 us -> 5.03 us
    pallas_call x2, Pallas kernels: 5.7 us -> 9.19 us  [the longest x1 6.71 us: keep_inverse(): call(functools.partial(keep_inverse_kernel, steps), 'keep_inverse', [IN_V...]
    pallas_call x1, Pallas kernels: 6.62 us -> 9.73 us  [inverse_second(): call(inverse_second_kernel, 'inverse_second', [IN_VMEM] * (2 + CHUNKS), p...]
    pallas_call x1, Pallas kernels: 7.07 us -> 8.72 us  [forward_second(): call(forward_second_kernel, 'forward_second', [pl.BlockSpec((block, steps...]
    ppermute x14, waiting for transfers between devices: 2.14 us -> 3.61 us  [with_partner(): lax.ppermute(block, 'tm', [(slab, slab ^ distance) for slab in range(slab...]
    ppermute x14, starting transfers between devices: 20.2 us -> 21.6 us  [with_partner(): lax.ppermute(block, 'tm', [(slab, slab ^ distance) for slab in range(slab...]
  transfers between devices with their start and end apart: 18 -> 18, of which waited for: 4 -> 5; matrix products, arithmetic and copies ran while one was open for 0% -> 0% of each run, Pallas kernels for 37% -> 36%
where the time goes in v6:
time: 73.7 us; the launch traced here: 73.5 us
  Pallas kernels  45.2 us (61%)
  starting transfers between devices  23 us (31%)
  waiting for transfers between devices  5.03 us (7%)
    ppermute x14, starting transfers between devices, with_partner(): lax.ppermute(block, 'tm', [(slab, slab ^ distance) for slab in range(slab...  21.6 us
    pallas_call x1, Pallas kernels, inverse_second(): call(inverse_second_kernel, 'inverse_second', [IN_VMEM] * (2 + CHUNKS), p...  9.73 us
    pallas_call x1, Pallas kernels, forward_second(): call(forward_second_kernel, 'forward_second', [pl.BlockSpec((block, steps...  8.72 us
    pallas_call x2, Pallas kernels, forward_first(): call(functools.partial(forward_first_kernel, slabs, chunk), 'forward_firs...  8.68 us
    pallas_call x1, Pallas kernels, keep_inverse(): call(functools.partial(keep_inverse_kernel, steps), 'keep_inverse', [IN_V...  6.71 us
    pallas_call x2, Pallas kernels, inverse_first(): call(functools.partial(inverse_first_kernel, slabs, chunk), 'inverse_firs...  6.54 us
    ppermute x14, waiting for transfers between devices, with_partner(): lax.ppermute(block, 'tm', [(slab, slab ^ distance) for slab in range(slab...  3.61 us
    pallas_call x1, Pallas kernels, keep_second(): call(keep_second_kernel, 'keep_second', [IN_VMEM] * 2, [IN_VMEM] * CHUNKS...  2.48 us
  transfers between devices with their start and end apart: 18, of which 5 were waited for; matrix products, arithmetic and copies ran while one was open for 0% of the time, Pallas kernels for 36%

profile of v6, /device:TPU:0, one launch (start us, length us, event | category | flops | bytes accessed | tf_op | source)
XLA Modules:
  0.0 73.5 jit_solution(7500695110672100132)
XLA Ops:
  0.1 8.7 %forward_second.1 = (f32[4352,256]{1,0:T(8,128)S(1)}, f32[4352,128]{1,0:T(8,128)S(1)}, f32[4352,128]{1,0:T(8,128)S(1)}) custom-call(s32[2]{0:T(128)S(1)} %pad_add_fusion.place, f32[256,16,512]{2,1,0:T(8,128)} %field.1, f32[256,512]{1,0:T(8,128)} %initial.1, bf16[2,768,256]{2,1,0:T(8,128)(2,1)} %constant.23.clone.table.tables), custom_call_target="tpu_custom_call" | custom-call | flops 4294967296 | bytes 8388608 | tf_op jit(solution)/shard_map/forward_second/pallas_call | solution.py:183
  8.8 0.7 collective-permute-start
  9.6 2.5 %keep_second.1 = (f32[4352,128]{1,0:T(8,128)S(1)}, f32[4352,128]{1,0:T(8,128)S(1)}) custom-call(s32[2]{0:T(128)S(1)} %pad_add_fusion.place, bf16[2,768,256]{2,1,0:T(8,128)(2,1)S(1)} %copy-done.5, f32[4352,256]{1,0:T(8,128)S(1)} %get-tuple-element.32.sums), custom_call_target="tpu_custom_call" | custom-call | flops 2147483648 | bytes 8388608 | tf_op jit(solution)/shard_map/keep_second/pallas_call | solution.py:216
  12.0 1.4 %collective-permute-done.got = f32[4352,128]{1,0:T(8,128)S(1)} collective-permute-done((f32[4352,128]{1,0:T(8,128)S(1)}, f32[4352,128]{1,0:T(8,128)S(1)}, u32[]{:S(2)}, u32[]{:S(2)}) %collective-permute-start) | collective-permute-done | bytes 2228256 | tf_op jit(solution)/shard_map/ppermute | solution.py:489
  13.5 4.3 %forward_first.2 = (f32[16,2,128,256]{3,2,1,0:T(8,128)S(1)}, f32[64,256]{1,0:T(8,128)S(1)}, f32[64,256]{1,0:T(8,128)S(1)}, f32[128,256]{1,0:T(8,128)S(1)}) custom-call(s32[2]{0:T(128)S(1)} %pad_add_fusion.place, f32[4352,128]{1,0:T(8,128)S(1)} %get-tuple-element.33.keep, f32[4352,128]{1,0:T(8,128)S(1)} %collective-permute-done.got, ...), custom_call_target="tpu_custom_call" | custom-call | flops 2147483648 | bytes 8388608 | tf_op jit(solution)/shard_map/forward_first/pallas_call | solution.py:279
  17.8 2.9 %collective-permute-start.2 = (f32[128,256]{1,0:T(8,128)S(1)}, f32[128,256]{1,0:T(8,128)S(1)}, u32[]{:S(2)}, u32[]{:S(2)}) collective-permute-start(f32[128,256]{1,0:T(8,128)S(1)} %get-tuple-element.38), channel_id=1, source_target_pairs={{0,4},{2,6},{4,0},{6,2},{8,12},{10,14},{12,8},{14,10},{1,5},{3,7},... | collective-permute-start | bytes 393224 | tf_op jit(solution)/shard_map/ppermute | solution.py:494
  20.7 4.4 %forward_first.3 = (f32[16,2,128,256]{3,2,1,0:T(8,128)S(1)}, f32[64,256]{1,0:T(8,128)S(1)}, f32[64,256]{1,0:T(8,128)S(1)}, f32[128,256]{1,0:T(8,128)S(1)}) custom-call(s32[2]{0:T(128)S(1)} %pad_add_fusion.place, f32[4352,128]{1,0:T(8,128)S(1)} %get-tuple-element.45.keep, f32[4352,128]{1,0:T(8,128)S(1)} %collective-permute-done.8.got, ...), custom_call_target="tpu_custom_call" | custom-call | flops 2147483648 | bytes 8388608 | tf_op jit(solution)/shard_map/forward_first/pallas_call | solution.py:279
  25.1 2.0 %collective-permute-start.1 = (f32[64,256]{1,0:T(8,128)S(1)}, f32[64,256]{1,0:T(8,128)S(1)}, u32[]{:S(2)}, u32[]{:S(2)}) collective-permute-start(f32[64,256]{1,0:T(8,128)S(1)} %get-tuple-element.37), channel_id=1, source_target_pairs={{0,2},{2,0},{4,6},{6,4},{8,10},{10,8},{12,14},{14,12},{1,3},{3,1},... | collective-permute-start | bytes 196616 | tf_op jit(solution)/shard_map/ppermute | solution.py:494
  27.1 0.2 collective-permute-start.3
  27.3 1.9 %collective-permute-start.9 = (f32[64,256]{1,0:T(8,128)S(1)}, f32[64,256]{1,0:T(8,128)S(1)}, u32[]{:S(2)}, u32[]{:S(2)}) collective-permute-start(f32[64,256]{1,0:T(8,128)S(1)} %get-tuple-element.49), channel_id=1, source_target_pairs={{0,2},{2,0},{4,6},{6,4},{8,10},{10,8},{12,14},{14,12},{1,3},{3,1},... | collective-permute-start | bytes 196616 | tf_op jit(solution)/shard_map/ppermute | solution.py:494
  29.2 1.2 %collective-permute-done.10.refs_2_ = f32[128,256]{1,0:T(8,128)S(1)} collective-permute-done((f32[128,256]{1,0:T(8,128)S(1)}, f32[128,256]{1,0:T(8,128)S(1)}, u32[]{:S(2)}, u32[]{:S(2)}) %collective-permute-start.10) | collective-permute-done | bytes 131104 | tf_op jit(solution)/shard_map/ppermute | solution.py:494
  30.3 1.5 %collective-permute-start.11 = (f32[64,256]{1,0:T(8,128)S(1)}, f32[64,256]{1,0:T(8,128)S(1)}, u32[]{:S(2)}, u32[]{:S(2)}) collective-permute-start(f32[64,256]{1,0:T(8,128)S(1)} %slice.18), channel_id=1, source_target_pairs={{0,2},{2,0},{4,6},{6,4},{8,10},{10,8},{12,14},{14,12},{1,3},{3,1},... | collective-permute-start | bytes 196616 | tf_op jit(solution)/shard_map/ppermute | solution.py:494
  31.9 0.6 half_sum.2
  32.5 2.6 %collective-permute-start.4 = (f32[64,256]{1,0:T(8,128)S(1)}, f32[64,256]{1,0:T(8,128)S(1)}, u32[]{:S(2)}, u32[]{:S(2)}) collective-permute-start(f32[64,256]{1,0:T(8,128)S(1)} %get-tuple-element.40.near), channel_id=1, source_target_pairs={{0,8},{2,10},{4,12},{6,14},{8,0},{10,2},{12,4},{14,6},{1,9},{3,11}... | collective-permute-start | bytes 196616 | tf_op jit(solution)/shard_map/ppermute | solution.py:494
  35.1 0.6 half_sum.3
  35.7 2.1 %collective-permute-start.12 = (f32[64,256]{1,0:T(8,128)S(1)}, f32[64,256]{1,0:T(8,128)S(1)}, u32[]{:S(2)}, u32[]{:S(2)}) collective-permute-start(f32[64,256]{1,0:T(8,128)S(1)} %get-tuple-element.52.near), channel_id=1, source_target_pairs={{0,8},{2,10},{4,12},{6,14},{8,0},{10,2},{12,4},{14,6},{1,9},{3,11}... | collective-permute-start | bytes 196616 | tf_op jit(solution)/shard_map/ppermute | solution.py:494
  37.9 0.6 close.2
  38.5 2.8 %collective-permute-start.6 = (f32[128,256]{1,0:T(8,128)S(1)}, f32[128,256]{1,0:T(8,128)S(1)}, u32[]{:S(2)}, u32[]{:S(2)}) collective-permute-start(f32[128,256]{1,0:T(8,128)S(1)} %get-tuple-element.43), channel_id=1, source_target_pairs={{0,4},{2,6},{4,0},{6,2},{8,12},{10,14},{12,8},{14,10},{1,5},{3,7},... | collective-permute-start | bytes 393224 | tf_op jit(solution)/shard_map/ppermute | solution.py:494
  41.3 0.6 close.3
  41.9 2.2 %collective-permute-start.14 = (f32[128,256]{1,0:T(8,128)S(1)}, f32[128,256]{1,0:T(8,128)S(1)}, u32[]{:S(2)}, u32[]{:S(2)}) collective-permute-start(f32[128,256]{1,0:T(8,128)S(1)} %get-tuple-element.55), channel_id=1, source_target_pairs={{0,4},{2,6},{4,0},{6,2},{8,12},{10,14},{12,8},{14,10},{1,5},{3,7},... | collective-permute-start | bytes 393224 | tf_op jit(solution)/shard_map/ppermute | solution.py:494
  44.1 0.5 collective-permute-start.5
  44.6 1.0 %collective-permute-done.6.refs_2_ = f32[128,256]{1,0:T(8,128)S(1)} collective-permute-done((f32[128,256]{1,0:T(8,128)S(1)}, f32[128,256]{1,0:T(8,128)S(1)}, u32[]{:S(2)}, u32[]{:S(2)}) %collective-permute-start.6) | collective-permute-done | bytes 131104 | tf_op jit(solution)/shard_map/ppermute | solution.py:494
  45.6 0.7 collective-permute-start.7
  46.3 1.3 %collective-permute-start.13 = (f32[64,256]{1,0:T(8,128)S(1)}, f32[64,256]{1,0:T(8,128)S(1)}, u32[]{:S(2)}, u32[]{:S(2)}) collective-permute-start(f32[64,256]{1,0:T(8,128)S(1)} %get-tuple-element.54), channel_id=1, source_target_pairs={{0,2},{2,0},{4,6},{6,4},{8,10},{10,8},{12,14},{14,12},{1,3},{3,1},... | collective-permute-start | bytes 196616 | tf_op jit(solution)/shard_map/ppermute | solution.py:494
  47.6 0.8 %collective-permute-start.15 = (f32[64,256]{1,0:T(8,128)S(1)}, f32[64,256]{1,0:T(8,128)S(1)}, u32[]{:S(2)}, u32[]{:S(2)}) collective-permute-start(f32[64,256]{1,0:T(8,128)S(1)} %slice.19), channel_id=1, source_target_pairs={{0,2},{2,0},{4,6},{6,4},{8,10},{10,8},{12,14},{14,12},{1,3},{3,1},... | collective-permute-start | bytes 196616 | tf_op jit(solution)/shard_map/ppermute | solution.py:494
  48.4 0.2 collective-permute-done.5.refs_1_
  48.6 1.3 %collective-permute-done.7.refs_3_ = f32[64,256]{1,0:T(8,128)S(1)} collective-permute-done((f32[64,256]{1,0:T(8,128)S(1)}, f32[64,256]{1,0:T(8,128)S(1)}, u32[]{:S(2)}, u32[]{:S(2)}) %collective-permute-start.7) | collective-permute-done | bytes 65568 | tf_op jit(solution)/shard_map/ppermute | solution.py:494
  49.8 3.4 %inverse_first.2 = (f32[4096,128]{1,0:T(8,128)S(1)}, f32[4096,128]{1,0:T(8,128)S(1)}) custom-call(s32[2]{0:T(128)S(1)} %pad_add_fusion.place, f32[16,2,128,256]{3,2,1,0:T(8,128)S(1)} %get-tuple-element.35.modes, bf16[2,2,768,256]{3,2,1,0:T(8,128)(2,1)S(1)} %copy-done.2, f32[2,2,256,256]{3,2,1,0:T(8,128)S(1)} %copy-done.4, ...), custom_call_target="tpu_custom_call" | custom-call | flops 2147483648 | bytes 8388608 | tf_op jit(solution)/shard_map/inverse_first/pallas_call | solution.py:389
  53.3 3.2 %inverse_first.3 = (f32[4096,128]{1,0:T(8,128)S(1)}, f32[4096,128]{1,0:T(8,128)S(1)}) custom-call(s32[2]{0:T(128)S(1)} %pad_add_fusion.place, f32[16,2,128,256]{3,2,1,0:T(8,128)S(1)} %get-tuple-element.47.modes, bf16[2,2,768,256]{3,2,1,0:T(8,128)(2,1)S(1)} %copy-done.2, f32[2,2,256,256]{3,2,1,0:T(8,128)S(1)} %copy-done.4, ...), custom_call_target="tpu_custom_call" | custom-call | flops 2147483648 | bytes 8388608 | tf_op jit(solution)/shard_map/inverse_first/pallas_call | solution.py:389
  56.5 0.5 collective-permute-start.17
  57.1 6.7 %keep_inverse.1.kept = f32[4096,256]{1,0:T(8,128)S(1)} custom-call(s32[2]{0:T(128)S(1)} %pad_add_fusion.place, bf16[2,768,256]{2,1,0:T(8,128)(2,1)S(1)} %copy-done.1, f32[4096,128]{1,0:T(8,128)S(1)} %get-tuple-element.44.refs_0_, f32[4096,128]{1,0:T(8,128)S(1)} %get-tuple-element.56.refs_1_), custom_call_target="tpu_custom_call" | custom-call | flops 2147483648 | bytes 8388608 | tf_op jit(solution)/shard_map/keep_inverse/pallas_call | solution.py:427
  63.8 9.7 %inverse_second.1 = f32[256,16,512]{2,1,0:T(8,128)} custom-call(s32[2]{0:T(128)S(1)} %pad_add_fusion.place, bf16[2,768,256]{2,1,0:T(8,128)(2,1)S(1)} %copy-done.1, f32[4096,256]{1,0:T(8,128)S(1)} %keep_inverse.1.kept, f32[4096,128]{1,0:T(8,128)S(1)} %collective-permute-done.16.refs_0_, f32[4096,128]{1,0:T(8,128)S(1)} %collective-permute-done.17.refs_1_), custom_call_target="tpu_custom_call" | custom-call | flops 4294967296 | bytes 8388608 | tf_op jit(solution)/shard_map/inverse_second/pallas_call | solution.py:475
  (33 shorter events, 0.4 us)
Async XLA Ops:
  0.1 9.5 %copy-start.5 = (bf16[2,768,256]{2,1,0:T(8,128)(2,1)S(1)}, bf16[2,768,256]{2,1,0:T(8,128)(2,1)}, u32[]{:S(2)}) copy-start(bf16[2,768,256]{2,1,0:T(8,128)(2,1)} %constant.23.clone.table.tables) | copy-start | bytes 2359300
  8.8 4.6 %collective-permute-start = (f32[4352,128]{1,0:T(8,128)S(1)}, f32[4352,128]{1,0:T(8,128)S(1)}, u32[]{:S(2)}, u32[]{:S(2)}) collective-permute-start(f32[4352,128]{1,0:T(8,128)S(1)} %get-tuple-element.34), channel_id=1, source_target_pairs={{0,1},{1,0},{2,3},{3,2},{4,5},{5,4},{6,7},{7,6},{8,9},{9,8},{10,11... | collective-permute-start | bytes 6684680 | tf_op jit(solution)/shard_map/ppermute | solution.py:489
  9.5 11.2 %collective-permute-start.8 = (f32[4352,128]{1,0:T(8,128)S(1)}, f32[4352,128]{1,0:T(8,128)S(1)}, u32[]{:S(2)}, u32[]{:S(2)}) collective-permute-start(f32[4352,128]{1,0:T(8,128)S(1)} %get-tuple-element.46), channel_id=1, source_target_pairs={{0,1},{1,0},{2,3},{3,2},{4,5},{5,4},{6,7},{7,6},{8,9},{9,8},{10,11... | collective-permute-start | bytes 6684680 | tf_op jit(solution)/shard_map/ppermute | solution.py:489
  9.6 3.9 %copy-start.3 = (bf16[2,2,768,256]{3,2,1,0:T(8,128)(2,1)S(1)}, bf16[2,2,768,256]{3,2,1,0:T(8,128)(2,1)}, u32[]{:S(2)}) copy-start(bf16[2,2,768,256]{3,2,1,0:T(8,128)(2,1)} %constant.21.clone.table) | copy-start | bytes 4718596
  9.6 3.9 %copy-start.4 = (f32[2,2,256,256]{3,2,1,0:T(8,128)S(1)}, f32[2,2,256,256]{3,2,1,0:T(8,128)}, u32[]{:S(2)}) copy-start(f32[2,2,256,256]{3,2,1,0:T(8,128)} %constant.22.clone.decay) | copy-start | bytes 3145732
  17.8 9.3 %collective-permute-start.2 = (f32[128,256]{1,0:T(8,128)S(1)}, f32[128,256]{1,0:T(8,128)S(1)}, u32[]{:S(2)}, u32[]{:S(2)}) collective-permute-start(f32[128,256]{1,0:T(8,128)S(1)} %get-tuple-element.38), channel_id=1, source_target_pairs={{0,4},{2,6},{4,0},{6,2},{8,12},{10,14},{12,8},{14,10},{1,5},{3,7},... | collective-permute-start | bytes 393224 | tf_op jit(solution)/shard_map/ppermute | solution.py:494
  20.7 11.2 %copy-start = (f32[2,2,3,256,256]{4,3,2,1,0:T(8,128)S(1)}, f32[2,2,3,256,256]{4,3,2,1,0:T(8,128)}, u32[]{:S(2)}) copy-start(f32[2,2,3,256,256]{4,3,2,1,0:T(8,128)} %constant.20.clone.closing) | copy-start | bytes 9437188
  25.0 5.3 %collective-permute-start.10 = (f32[128,256]{1,0:T(8,128)S(1)}, f32[128,256]{1,0:T(8,128)S(1)}, u32[]{:S(2)}, u32[]{:S(2)}) collective-permute-start(f32[128,256]{1,0:T(8,128)S(1)} %get-tuple-element.50), channel_id=1, source_target_pairs={{0,4},{2,6},{4,0},{6,2},{8,12},{10,14},{12,8},{14,10},{1,5},{3,7},... | collective-permute-start | bytes 393224 | tf_op jit(solution)/shard_map/ppermute | solution.py:494
  25.1 6.8 %collective-permute-start.1 = (f32[64,256]{1,0:T(8,128)S(1)}, f32[64,256]{1,0:T(8,128)S(1)}, u32[]{:S(2)}, u32[]{:S(2)}) collective-permute-start(f32[64,256]{1,0:T(8,128)S(1)} %get-tuple-element.37), channel_id=1, source_target_pairs={{0,2},{2,0},{4,6},{6,4},{8,10},{10,8},{12,14},{14,12},{1,3},{3,1},... | collective-permute-start | bytes 196616 | tf_op jit(solution)/shard_map/ppermute | solution.py:494
  27.1 4.8 %collective-permute-start.3 = (f32[64,256]{1,0:T(8,128)S(1)}, f32[64,256]{1,0:T(8,128)S(1)}, u32[]{:S(2)}, u32[]{:S(2)}) collective-permute-start(f32[64,256]{1,0:T(8,128)S(1)} %slice.16), channel_id=1, source_target_pairs={{0,2},{2,0},{4,6},{6,4},{8,10},{10,8},{12,14},{14,12},{1,3},{3,1},... | collective-permute-start | bytes 196616 | tf_op jit(solution)/shard_map/ppermute | solution.py:494
  27.3 7.9 %collective-permute-start.9 = (f32[64,256]{1,0:T(8,128)S(1)}, f32[64,256]{1,0:T(8,128)S(1)}, u32[]{:S(2)}, u32[]{:S(2)}) collective-permute-start(f32[64,256]{1,0:T(8,128)S(1)} %get-tuple-element.49), channel_id=1, source_target_pairs={{0,2},{2,0},{4,6},{6,4},{8,10},{10,8},{12,14},{14,12},{1,3},{3,1},... | collective-permute-start | bytes 196616 | tf_op jit(solution)/shard_map/ppermute | solution.py:494
  30.3 4.8 %collective-permute-start.11 = (f32[64,256]{1,0:T(8,128)S(1)}, f32[64,256]{1,0:T(8,128)S(1)}, u32[]{:S(2)}, u32[]{:S(2)}) collective-permute-start(f32[64,256]{1,0:T(8,128)S(1)} %slice.18), channel_id=1, source_target_pairs={{0,2},{2,0},{4,6},{6,4},{8,10},{10,8},{12,14},{14,12},{1,3},{3,1},... | collective-permute-start | bytes 196616 | tf_op jit(solution)/shard_map/ppermute | solution.py:494
  32.5 5.4 %collective-permute-start.4 = (f32[64,256]{1,0:T(8,128)S(1)}, f32[64,256]{1,0:T(8,128)S(1)}, u32[]{:S(2)}, u32[]{:S(2)}) collective-permute-start(f32[64,256]{1,0:T(8,128)S(1)} %get-tuple-element.40.near), channel_id=1, source_target_pairs={{0,8},{2,10},{4,12},{6,14},{8,0},{10,2},{12,4},{14,6},{1,9},{3,11}... | collective-permute-start | bytes 196616 | tf_op jit(solution)/shard_map/ppermute | solution.py:494
  35.7 5.6 %collective-permute-start.12 = (f32[64,256]{1,0:T(8,128)S(1)}, f32[64,256]{1,0:T(8,128)S(1)}, u32[]{:S(2)}, u32[]{:S(2)}) collective-permute-start(f32[64,256]{1,0:T(8,128)S(1)} %get-tuple-element.52.near), channel_id=1, source_target_pairs={{0,8},{2,10},{4,12},{6,14},{8,0},{10,2},{12,4},{14,6},{1,9},{3,11}... | collective-permute-start | bytes 196616 | tf_op jit(solution)/shard_map/ppermute | solution.py:494
  38.5 11.4 %copy-start.2 = (bf16[2,2,768,256]{3,2,1,0:T(8,128)(2,1)S(1)}, bf16[2,2,768,256]{3,2,1,0:T(8,128)(2,1)}, u32[]{:S(2)}) copy-start(bf16[2,2,768,256]{3,2,1,0:T(8,128)(2,1)} %constant.24.clone.table) | copy-start | bytes 4718596
  38.5 7.1 %collective-permute-start.6 = (f32[128,256]{1,0:T(8,128)S(1)}, f32[128,256]{1,0:T(8,128)S(1)}, u32[]{:S(2)}, u32[]{:S(2)}) collective-permute-start(f32[128,256]{1,0:T(8,128)S(1)} %get-tuple-element.43), channel_id=1, source_target_pairs={{0,4},{2,6},{4,0},{6,2},{8,12},{10,14},{12,8},{14,10},{1,5},{3,7},... | collective-permute-start | bytes 393224 | tf_op jit(solution)/shard_map/ppermute | solution.py:494
  41.9 5.7 %collective-permute-start.14 = (f32[128,256]{1,0:T(8,128)S(1)}, f32[128,256]{1,0:T(8,128)S(1)}, u32[]{:S(2)}, u32[]{:S(2)}) collective-permute-start(f32[128,256]{1,0:T(8,128)S(1)} %get-tuple-element.55), channel_id=1, source_target_pairs={{0,4},{2,6},{4,0},{6,2},{8,12},{10,14},{12,8},{14,10},{1,5},{3,7},... | collective-permute-start | bytes 393224 | tf_op jit(solution)/shard_map/ppermute | solution.py:494
  44.1 4.4 %collective-permute-start.5 = (f32[64,256]{1,0:T(8,128)S(1)}, f32[64,256]{1,0:T(8,128)S(1)}, u32[]{:S(2)}, u32[]{:S(2)}) collective-permute-start(f32[64,256]{1,0:T(8,128)S(1)} %get-tuple-element.42), channel_id=1, source_target_pairs={{0,2},{2,0},{4,6},{6,4},{8,10},{10,8},{12,14},{14,12},{1,3},{3,1},... | collective-permute-start | bytes 196616 | tf_op jit(solution)/shard_map/ppermute | solution.py:494
  45.6 4.3 %collective-permute-start.7 = (f32[64,256]{1,0:T(8,128)S(1)}, f32[64,256]{1,0:T(8,128)S(1)}, u32[]{:S(2)}, u32[]{:S(2)}) collective-permute-start(f32[64,256]{1,0:T(8,128)S(1)} %slice.17), channel_id=1, source_target_pairs={{0,2},{2,0},{4,6},{6,4},{8,10},{10,8},{12,14},{14,12},{1,3},{3,1},... | collective-permute-start | bytes 196616 | tf_op jit(solution)/shard_map/ppermute | solution.py:494
  46.3 7.0 %collective-permute-start.13 = (f32[64,256]{1,0:T(8,128)S(1)}, f32[64,256]{1,0:T(8,128)S(1)}, u32[]{:S(2)}, u32[]{:S(2)}) collective-permute-start(f32[64,256]{1,0:T(8,128)S(1)} %get-tuple-element.54), channel_id=1, source_target_pairs={{0,2},{2,0},{4,6},{6,4},{8,10},{10,8},{12,14},{14,12},{1,3},{3,1},... | collective-permute-start | bytes 196616 | tf_op jit(solution)/shard_map/ppermute | solution.py:494
  47.6 5.7 %collective-permute-start.15 = (f32[64,256]{1,0:T(8,128)S(1)}, f32[64,256]{1,0:T(8,128)S(1)}, u32[]{:S(2)}, u32[]{:S(2)}) collective-permute-start(f32[64,256]{1,0:T(8,128)S(1)} %slice.19), channel_id=1, source_target_pairs={{0,2},{2,0},{4,6},{6,4},{8,10},{10,8},{12,14},{14,12},{1,3},{3,1},... | collective-permute-start | bytes 196616 | tf_op jit(solution)/shard_map/ppermute | solution.py:494
  53.2 10.6 %collective-permute-start.16 = (f32[4096,128]{1,0:T(8,128)S(1)}, f32[4096,128]{1,0:T(8,128)S(1)}, u32[]{:S(2)}, u32[]{:S(2)}) collective-permute-start(f32[4096,128]{1,0:T(8,128)S(1)} %get-tuple-element.57), channel_id=1, source_target_pairs={{0,1},{1,0},{2,3},{3,2},{4,5},{5,4},{6,7},{7,6},{8,9},{9,8},{10,11... | collective-permute-start | bytes 6291464 | tf_op jit(solution)/shard_map/ppermute | solution.py:489
  53.3 3.7 %copy-start.1 = (bf16[2,768,256]{2,1,0:T(8,128)(2,1)S(1)}, bf16[2,768,256]{2,1,0:T(8,128)(2,1)}, u32[]{:S(2)}) copy-start(bf16[2,768,256]{2,1,0:T(8,128)(2,1)} %constant.25.clone.tables) | copy-start | bytes 2359300
  56.5 7.3 %collective-permute-start.17 = (f32[4096,128]{1,0:T(8,128)S(1)}, f32[4096,128]{1,0:T(8,128)S(1)}, u32[]{:S(2)}, u32[]{:S(2)}) collective-permute-start(f32[4096,128]{1,0:T(8,128)S(1)} %get-tuple-element.58), channel_id=1, source_target_pairs={{0,1},{1,0},{2,3},{3,2},{4,5},{5,4},{6,7},{7,6},{8,9},{9,8},{10,11... | collective-permute-start | bytes 6291464 | tf_op jit(solution)/shard_map/ppermute | solution.py:489

commit v7 on v5

--- a/solution.py
+++ b/solution.py
@@ -235,8 +235,7 @@
 
 
 def forward_first_kernel(slabs, chunk, place, keep, got, table, decay, modes, *refs):
-    size = ranks(slabs)
-    lasts, (state, split, split_end) = refs[:size], refs[size:]
+    lasts, state, split, split_end = refs
     steps, _, part, rows = modes.shape
     block = split.shape[1] // part
     strip = place[1]
@@ -264,11 +263,7 @@
         store_split(split_end, (c, slice(None)), 0, cells.T)
         at_state = pl.ds(c * part, part)
         state[at_state] = state[at_state] - is_last * dot(split_end[c], table[strip, c])
-    rank = lax.rem(place[0], size)
-    share = 2 * part // size
-    for partner in range(size):
-        at = pl.multiple_of((rank ^ partner) * share, share)
-        lasts[partner][...] = state[pl.ds(at, share)]
+    lasts[...] = state[...].reshape(lasts.shape)
 
 
 def forward_first(place, chunk, keep, got, tables, decays, slabs):
@@ -277,12 +272,12 @@
     block = min(8, steps)
     size = ranks(slabs)
     share = 2 * part // size
-    outs = call(
+    return call(
         functools.partial(forward_first_kernel, slabs, chunk),
         "forward_first",
         [IN_VMEM] * 4,
-        [IN_VMEM] * (1 + size),
-        [floats(steps, 2, part, rows)] + [floats(share, rows)] * size,
+        [IN_VMEM] * 2,
+        [floats(steps, 2, part, rows), floats(size, share, rows)],
         [
             pltpu.VMEM((2 * part, rows), jnp.float32),
             pltpu.VMEM((2, block * part, 3 * rows), jnp.bfloat16),
@@ -290,78 +285,61 @@
         ],
         1 << 31,
     )(place, keep, got, tables, decays)
-    return outs[0], outs[1:]
-
-
-def half_sum_kernel(slabs, chunk, place, closing, *refs):
-    size = ranks(slabs)
-    lasts, ordered, total = refs[:size], refs[size], refs[size + 1]
-    share = total.shape[0]
+
+
+def half_sum_kernel(chunk, place, closing, lasts, total):
+    size, share, _ = lasts.shape
     rank = lax.rem(place[0], size)
     decay = closing[place[1], chunk, 0, pl.ds(pl.multiple_of(rank * share, share), share)]
-    for partner in range(size):
-        ordered[rank ^ partner] = lasts[partner][...]
-    state = ordered[0]
+    state = lasts[0]
     for at in range(1, size):
-        state = ordered[at] + decay * state
+        state = lasts[at] + decay * state
     total[...] = state
 
 
-def half_sum(place, chunk, lasts, closing, slabs):
-    size = ranks(slabs)
-    share, rows = lasts[0].shape
+def half_sum(place, chunk, lasts, closing):
+    _, share, rows = lasts.shape
     return call(
-        functools.partial(half_sum_kernel, slabs, chunk),
+        functools.partial(half_sum_kernel, chunk),
         "half_sum",
-        [IN_VMEM] * (1 + size),
         [IN_VMEM] * 2,
-        [floats(size, share, rows), floats(share, rows)],
+        IN_VMEM,
+        floats(share, rows),
         [],
         1 << 20,
-    )(place, closing, *lasts)
-
-
-def close_kernel(slabs, chunk, place, closing, ordered, near, far, *refs):
-    size = ranks(slabs)
-    befores, states = refs[:size], refs[size]
-    share = near.shape[0]
+    )(place, closing, lasts)
+
+
+def close_kernel(chunk, place, closing, lasts, near, far, befores):
+    size, share, _ = lasts.shape
     rank = lax.rem(place[0], size)
     at_share = pl.ds(pl.multiple_of(rank * share, share), share)
     decay, half_decay, gain = (closing[place[1], chunk, at, at_share] for at in range(3))
     entering = jnp.where(place[0] < size, circulant_alpha, 1.0)
     state = gain * (entering * far[...] + circulant_alpha * half_decay * near[...])
     for at in range(size):
-        states[at] = state
+        befores[at] = state
         if at < size - 1:
-            state = ordered[at] + decay * state
-    for partner in range(size):
-        befores[partner][...] = states[rank ^ partner]
-
-
-def close(place, chunk, ordered, near, far, closing, slabs):
-    size, share, rows = ordered.shape
+            state = lasts[at] + decay * state
+
+
+def close(place, chunk, lasts, near, far, closing):
     return call(
-        functools.partial(close_kernel, slabs, chunk),
+        functools.partial(close_kernel, chunk),
         "close",
         [IN_VMEM] * 4,
-        [IN_VMEM] * size,
-        [floats(share, rows)] * size,
-        [pltpu.VMEM((size, share, rows), jnp.float32)],
+        IN_VMEM,
+        floats(*lasts.shape),
+        [],
         1 << 20,
-    )(place, closing, ordered, near, far)
-
-
-def inverse_first_kernel(slabs, chunk, place, modes, table, decay, *refs):
-    size = ranks(slabs)
-    befores, (keep, send, state, split) = refs[:size], refs[size:]
+    )(place, closing, lasts, near, far)
+
+
+def inverse_first_kernel(chunk, place, modes, table, decay, befores, keep, send, state, split):
     steps, _, part, rows = modes.shape
     block = split.shape[1] // part
     strip = place[1]
-    rank = lax.rem(place[0], size)
-    share = 2 * part // size
-    for partner in range(size):
-        at = pl.multiple_of((rank ^ partner) * share, share)
-        state[pl.ds(at, share)] = befores[partner][...]
+    state[...] = befores[...].reshape(state.shape)
     for step in range(0, steps, block):
         results = []
         for c in (0, 1):
@@ -382,13 +360,13 @@
             store_rows_reversed(send, start, (even[piece] - odd[piece]).T)
 
 
-def inverse_first(place, chunk, modes, befores, tables, decays, slabs):
+def inverse_first(place, chunk, modes, befores, tables, decays):
     steps, _, part, rows = modes.shape
     block = min(8, steps)
     return call(
-        functools.partial(inverse_first_kernel, slabs, chunk),
+        functools.partial(inverse_first_kernel, chunk),
         "inverse_first",
-        [IN_VMEM] * (3 + len(befores)),
+        [IN_VMEM] * 4,
         [IN_VMEM] * 2,
         [floats(steps * rows, part)] * 2,
         [
@@ -396,7 +374,7 @@
             pltpu.VMEM((2, block * part, 3 * rows), jnp.bfloat16),
         ],
         1 << 31,
-    )(place, modes, tables, decays, *befores)
+    )(place, modes, tables, decays, befores)
 
 
 def inverse_second_kernel(place, tables, kept, *refs):
@@ -459,13 +437,17 @@
     return lax.ppermute(block, "space", [(0, 1), (1, 0)])
 
 
-def with_partner(block, distance):
+def with_other_half(block):
     slabs = lax.axis_size("tm")
-    return lax.ppermute(block, "tm", [(slab, slab ^ distance) for slab in range(slabs)])
+    size = ranks(slabs)
+    return lax.ppermute(block, "tm", [(slab, (slab + size) % slabs) for slab in range(slabs)])
 
 
 def among_ranks(blocks):
-    return [blocks[0]] + [with_partner(block, at) for at, block in enumerate(blocks) if at]
+    slabs = lax.axis_size("tm")
+    size = ranks(slabs)
+    halves = [list(range(start, start + size)) for start in range(0, slabs, size)]
+    return lax.all_to_all(blocks, "tm", 0, 0, axis_index_groups=halves, tiled=True)
 
 
 def by_chunk(table):
@@ -500,13 +482,14 @@
             place, chunk, keeps[chunk], gots[chunk], first_table, decays, slabs
         )
         modes.append(own_modes)
-        ordered, near = half_sum(place, chunk, among_ranks(lasts), closing, slabs)
-        far = with_partner(near, ranks(slabs))
-        befores.append(among_ranks(close(place, chunk, ordered, near, far, closing, slabs)))
+        lasts = among_ranks(lasts)
+        near = half_sum(place, chunk, lasts, closing)
+        far = with_other_half(near)
+        befores.append(among_ranks(close(place, chunk, lasts, near, far, closing)))
     inverse_table = split_constant(np.swapaxes(first, 2, 3))
     keeps, sends = zip(
         *(
-            inverse_first(place, chunk, modes[chunk], befores[chunk], inverse_table, decays, slabs)
+            inverse_first(place, chunk, modes[chunk], befores[chunk], inverse_table, decays)
             for chunk in range(CHUNKS)
         )
     )

time: 63.1 us -> 99.4 us (1.58)
  local copies, waits for them, and re-layouts: 0.03 us -> 24.8 us
  waiting for transfers between devices: 4.26 us -> 12.4 us
  Pallas kernels: 36.9 us -> 39.5 us
    unnamed x12 -> x52, local copies, waits for them, and re-layouts: 0.03 us -> 24.8 us
    ppermute x14 -> x2, starting transfers between devices: 20.2 us -> 4.07 us  [with_other_half(): lax.ppermute(block, 'tm', [(slab, (slab + size) % slabs) for slab in rang...]
    all_to_all x0 -> x4, starting transfers between devices: none -> 16 us  [among_ranks(): lax.all_to_all(blocks, 'tm', 0, 0, axis_index_groups=halves, tiled=True)]
    ppermute x14 -> x2, waiting for transfers between devices: 2.14 us -> 7.11 us  [with_other_half(): lax.ppermute(block, 'tm', [(slab, (slab + size) % slabs) for slab in rang...]
    ppermute x4, waiting for transfers between devices: 2.12 us -> 5.31 us  [swapped(): return lax.ppermute(block, 'space', [(0, 1), (1, 0)])]
    pallas_call x1, Pallas kernels: 7.07 us -> 8.44 us  [forward_second(): call(forward_second_kernel, 'forward_second', [pl.BlockSpec((block, steps...]
    pallas_call x6, Pallas kernels: 8.9 us -> 9.94 us  [the longest x2 7.66 us: inverse_first(): call(functools.partial(inverse_first_kernel, chunk), 'inverse_first', [IN...]
  transfers between devices with their start and end apart: 18 -> 10, of which waited for: 4 -> 4; matrix products, arithmetic and copies ran while one was open for 0% -> 0% of each run, Pallas kernels for 37% -> 25%
where the time goes in v7:
time: 99.4 us; the launch traced here: 98.6 us
  Pallas kernels  39.5 us (40%)
  local copies, waits for them, and re-layouts  24.8 us (25%)
  starting transfers between devices  21.6 us (22%)
  waiting for transfers between devices  12.4 us (12%)
    unnamed x52, local copies, waits for them, and re-layouts  24.8 us
    all_to_all x4, starting transfers between devices, among_ranks(): lax.all_to_all(blocks, 'tm', 0, 0, axis_index_groups=halves, tiled=True)  16 us
    pallas_call x2, Pallas kernels, forward_first(): call(functools.partial(forward_first_kernel, slabs, chunk), 'forward_firs...  9.03 us
    pallas_call x1, Pallas kernels, forward_second(): call(forward_second_kernel, 'forward_second', [pl.BlockSpec((block, steps...  8.44 us
    pallas_call x2, Pallas kernels, inverse_first(): call(functools.partial(inverse_first_kernel, chunk), 'inverse_first', [IN...  7.66 us
    ppermute x2, waiting for transfers between devices, with_other_half(): lax.ppermute(block, 'tm', [(slab, (slab + size) % slabs) for slab in rang...  7.11 us
    pallas_call x1, Pallas kernels, inverse_second(): call(inverse_second_kernel, 'inverse_second', [IN_VMEM] * (2 + CHUNKS), p...  6.53 us
    pallas_call x2, Pallas kernels, times_table(): call(functools.partial(times_table_kernel, len(sources)), name, [IN_VMEM]...  5.56 us
  transfers between devices with their start and end apart: 10, of which 4 were waited for; matrix products, arithmetic and copies ran while one was open for 0% of the time, Pallas kernels for 25%

profile of v7, /device:TPU:0, one launch (start us, length us, event | category | flops | bytes accessed | tf_op | source)
XLA Modules:
  0.0 98.6 jit_solution(14245650774904364667)
XLA Ops:
  0.1 8.4 %forward_second.1 = (f32[4352,256]{1,0:T(8,128)S(1)}, f32[4352,128]{1,0:T(8,128)S(1)}, f32[4352,128]{1,0:T(8,128)}) custom-call(s32[2]{0:T(128)S(1)} %pad_add_fusion.place, f32[256,16,512]{2,1,0:T(8,128)} %field.1, f32[256,512]{1,0:T(8,128)} %initial.1, bf16[2,768,256]{2,1,0:T(8,128)(2,1)} %constant.23.clone.table.tables), custom_call_target="tpu_custom_call" | custom-call | flops 4294967296 | bytes 8388608 | tf_op jit(solution)/shard_map/forward_second/pallas_call | solution.py:183
  8.5 0.9 collective-permute-start
  9.5 2.4 %keep_second.1 = (f32[4352,128]{1,0:T(8,128)S(1)}, f32[4352,128]{1,0:T(8,128)S(1)}) custom-call(s32[2]{0:T(128)S(1)} %pad_add_fusion.place, bf16[2,768,256]{2,1,0:T(8,128)(2,1)S(1)} %copy-done.19, f32[4352,256]{1,0:T(8,128)S(1)} %get-tuple-element.18.refs_0_), custom_call_target="tpu_custom_call" | custom-call | flops 2147483648 | bytes 8388608 | tf_op jit(solution)/shard_map/keep_second/pallas_call | solution.py:222
  11.9 4.7 %collective-permute-done.got = f32[4352,128]{1,0:T(8,128)S(1)} collective-permute-done((f32[4352,128]{1,0:T(8,128)S(1)}, f32[4352,128]{1,0:T(8,128)S(1)}, u32[]{:S(2)}, u32[]{:S(2)}) %collective-permute-start) | collective-permute-done | bytes 2228256 | tf_op jit(solution)/shard_map/ppermute | solution.py:437
  16.6 4.9 %forward_first.2 = (f32[16,2,128,256]{3,2,1,0:T(8,128)S(1)}, f32[4,64,256]{2,1,0:T(8,128)}) custom-call(s32[2]{0:T(128)S(1)} %pad_add_fusion.place, f32[4352,128]{1,0:T(8,128)S(1)} %get-tuple-element.19.keep, f32[4352,128]{1,0:T(8,128)S(1)} %collective-permute-done.got, bf16[2,2,768,256]{3,2,1,0:T(8,128)(2,1)S(1)} %copy-done.13, ...), custom_call_target="tpu_custom_call" | custom-call | flops 2147483648 | bytes 8388608 | tf_op jit(solution)/shard_map/forward_first/pallas_call | solution.py:275
  21.4 2.0 %copy-done.22 = f32[16,2,128,256]{3,2,1,0:T(8,128)} copy-done((f32[16,2,128,256]{3,2,1,0:T(8,128)}, f32[16,2,128,256]{3,2,1,0:T(8,128)S(1)}, u32[]{:S(2)}) %copy-start.22) | copy-done | bytes 4194328
  23.4 3.4 %all-to-all-start = ((f32[4,64,256]{2,1,0:T(8,128)}), f32[4,64,256]{2,1,0:T(8,128)S(1)}, u32[]{:S(2)}, u32[]{:S(2)}) async-start(f32[4,64,256]{2,1,0:T(8,128)} %get-tuple-element.22), calls=%async_computation | async-start | bytes 524288 | tf_op jit(solution)/shard_map/all_to_all | solution.py:450
  26.9 1.4 %copy-done.9 = f32[4352,128]{1,0:T(8,128)} copy-done((f32[4352,128]{1,0:T(8,128)}, f32[4352,128]{1,0:T(8,128)S(1)}, u32[]{:S(2)}) %copy-start.9) | copy-done | bytes 2228248
  28.3 1.6 %copy-done.10 = f32[4352,128]{1,0:T(8,128)S(1)} copy-done((f32[4352,128]{1,0:T(8,128)S(1)}, f32[4352,128]{1,0:T(8,128)}, u32[]{:S(2)}) %copy-start.10) | copy-done | bytes 2228248
  29.9 1.4 %copy-done.14 = bf16[2,2,768,256]{3,2,1,0:T(8,128)(2,1)S(1)} copy-done((bf16[2,2,768,256]{3,2,1,0:T(8,128)(2,1)S(1)}, bf16[2,2,768,256]{3,2,1,0:T(8,128)(2,1)}, u32[]{:S(2)}) %copy-start.14) | copy-done | bytes 1572888
  31.3 1.2 %copy-done.16 = f32[2,2,256,256]{3,2,1,0:T(8,128)S(1)} copy-done((f32[2,2,256,256]{3,2,1,0:T(8,128)S(1)}, f32[2,2,256,256]{3,2,1,0:T(8,128)}, u32[]{:S(2)}) %copy-start.16) | copy-done | bytes 1048600
  32.5 1.6 %copy-done.25 = f32[4352,128]{1,0:T(8,128)S(1)} copy-done((f32[4352,128]{1,0:T(8,128)S(1)}, f32[4352,128]{1,0:T(8,128)}, u32[]{:S(2)}) %copy-start.25) | copy-done | bytes 2228248
  34.2 4.2 %forward_first.3 = (f32[16,2,128,256]{3,2,1,0:T(8,128)S(1)}, f32[4,64,256]{2,1,0:T(8,128)S(1)}) custom-call(s32[2]{0:T(128)S(1)} %pad_add_fusion.place, f32[4352,128]{1,0:T(8,128)S(1)} %copy-done.25, f32[4352,128]{1,0:T(8,128)S(1)} %copy-done.10, bf16[2,2,768,256]{3,2,1,0:T(8,128)(2,1)S(1)} %copy-done.14, f32[2,2,256,256]{3,2,1,0:T(8,128)S(1)} %copy-done.16), custom_call_target="tpu_custom_call" | custom-call | flops 2147483648 | bytes 8388608 | tf_op jit(solution)/shard_map/forward_first/pallas_call | solution.py:275
  39.1 2.0 %copy-done.20 = f32[16,2,128,256]{3,2,1,0:T(8,128)} copy-done((f32[16,2,128,256]{3,2,1,0:T(8,128)}, f32[16,2,128,256]{3,2,1,0:T(8,128)S(1)}, u32[]{:S(2)}) %copy-start.20) | copy-done | bytes 4194328
  41.7 4.2 %all-to-all-start.2 = ((f32[4,64,256]{2,1,0:T(8,128)}), f32[4,64,256]{2,1,0:T(8,128)S(1)}, u32[]{:S(2)}, u32[]{:S(2)}) async-start(f32[4,64,256]{2,1,0:T(8,128)} %copy-done.8), calls=%async_computation.2 | async-start | bytes 524288 | tf_op jit(solution)/shard_map/all_to_all | solution.py:450
  45.9 0.9 copy-done.3
  47.4 2.0 %collective-permute-start.1 = (f32[64,256]{1,0:T(8,128)S(1)}, f32[64,256]{1,0:T(8,128)S(1)}, u32[]{:S(2)}, u32[]{:S(2)}) collective-permute-start(f32[64,256]{1,0:T(8,128)S(1)} %half_sum.2.near), channel_id=1, source_target_pairs={{0,8},{2,10},{4,12},{6,14},{8,0},{10,2},{12,4},{14,6},{1,9},{3,11}... | collective-permute-start | bytes 196616 | tf_op jit(solution)/shard_map/ppermute | solution.py:443
  49.4 4.0 %collective-permute-done.1.far = f32[64,256]{1,0:T(8,128)S(1)} collective-permute-done((f32[64,256]{1,0:T(8,128)S(1)}, f32[64,256]{1,0:T(8,128)S(1)}, u32[]{:S(2)}, u32[]{:S(2)}) %collective-permute-start.1) | collective-permute-done | bytes 65568 | tf_op jit(solution)/shard_map/ppermute | solution.py:443
  54.7 4.0 %all-to-all-start.1 = ((f32[4,64,256]{2,1,0:T(8,128)}), f32[4,64,256]{2,1,0:T(8,128)}, u32[]{:S(2)}, u32[]{:S(2)}) async-start(f32[4,64,256]{2,1,0:T(8,128)} %copy-done.6), calls=%async_computation.1 | async-start | bytes 524288 | tf_op jit(solution)/shard_map/all_to_all | solution.py:450
  59.3 2.1 %collective-permute-start.3 = (f32[64,256]{1,0:T(8,128)S(1)}, f32[64,256]{1,0:T(8,128)S(1)}, u32[]{:S(2)}, u32[]{:S(2)}) collective-permute-start(f32[64,256]{1,0:T(8,128)S(1)} %half_sum.3.near), channel_id=1, source_target_pairs={{0,8},{2,10},{4,12},{6,14},{8,0},{10,2},{12,4},{14,6},{1,9},{3,11}... | collective-permute-start | bytes 196616 | tf_op jit(solution)/shard_map/ppermute | solution.py:443
  61.4 3.1 %collective-permute-done.3.far = f32[64,256]{1,0:T(8,128)S(1)} collective-permute-done((f32[64,256]{1,0:T(8,128)S(1)}, f32[64,256]{1,0:T(8,128)S(1)}, u32[]{:S(2)}, u32[]{:S(2)}) %collective-permute-start.3) | collective-permute-done | bytes 65568 | tf_op jit(solution)/shard_map/ppermute | solution.py:443
  65.8 4.4 %all-to-all-start.3 = ((f32[4,64,256]{2,1,0:T(8,128)}), f32[4,64,256]{2,1,0:T(8,128)S(1)}, u32[]{:S(2)}, u32[]{:S(2)}) async-start(f32[4,64,256]{2,1,0:T(8,128)} %copy-done.7), calls=%async_computation.3 | async-start | bytes 524288 | tf_op jit(solution)/shard_map/all_to_all | solution.py:450
  70.2 1.4 %copy-done.11 = bf16[2,2,768,256]{3,2,1,0:T(8,128)(2,1)S(1)} copy-done((bf16[2,2,768,256]{3,2,1,0:T(8,128)(2,1)S(1)}, bf16[2,2,768,256]{3,2,1,0:T(8,128)(2,1)}, u32[]{:S(2)}) %copy-start.11) | copy-done | bytes 1572888
  71.6 1.2 %copy-done.17 = f32[2,2,256,256]{3,2,1,0:T(8,128)S(1)} copy-done((f32[2,2,256,256]{3,2,1,0:T(8,128)S(1)}, f32[2,2,256,256]{3,2,1,0:T(8,128)}, u32[]{:S(2)}) %copy-start.17) | copy-done | bytes 1048600
  72.9 2.2 %copy-done.23 = f32[16,2,128,256]{3,2,1,0:T(8,128)S(1)} copy-done((f32[16,2,128,256]{3,2,1,0:T(8,128)S(1)}, f32[16,2,128,256]{3,2,1,0:T(8,128)}, u32[]{:S(2)}) %copy-start.23) | copy-done | bytes 4194328
  75.0 4.7 %inverse_first.2 = (f32[4096,128]{1,0:T(8,128)S(1)}, f32[4096,128]{1,0:T(8,128)}) custom-call(s32[2]{0:T(128)S(1)} %pad_add_fusion.place, f32[16,2,128,256]{3,2,1,0:T(8,128)S(1)} %copy-done.23, bf16[2,2,768,256]{3,2,1,0:T(8,128)(2,1)S(1)} %copy-done.11, f32[2,2,256,256]{3,2,1,0:T(8,128)S(1)} %copy-done.17, f32[4,64,256]{2,1,0:T(8,128)} %all-to-all-done.1.befores), custom_call_target="tpu_custom_call" | custom-call | flops 2147483648 | bytes 8388608 | tf_op jit(solution)/shard_map/inverse_first/pallas_call | solution.py:366
  79.8 1.4 %copy-done.4 = f32[4096,128]{1,0:T(8,128)} copy-done((f32[4096,128]{1,0:T(8,128)}, f32[4096,128]{1,0:T(8,128)S(1)}, u32[]{:S(2)}) %copy-start.4) | copy-done | bytes 2097176
  81.2 1.4 %copy-done.12 = bf16[2,2,768,256]{3,2,1,0:T(8,128)(2,1)S(1)} copy-done((bf16[2,2,768,256]{3,2,1,0:T(8,128)(2,1)S(1)}, bf16[2,2,768,256]{3,2,1,0:T(8,128)(2,1)}, u32[]{:S(2)}) %copy-start.12) | copy-done | bytes 1572888
  82.6 2.2 %copy-done.21 = f32[16,2,128,256]{3,2,1,0:T(8,128)S(1)} copy-done((f32[16,2,128,256]{3,2,1,0:T(8,128)S(1)}, f32[16,2,128,256]{3,2,1,0:T(8,128)}, u32[]{:S(2)}) %copy-start.21) | copy-done | bytes 4194328
  84.8 2.9 %inverse_first.3 = (f32[4096,128]{1,0:T(8,128)S(1)}, f32[4096,128]{1,0:T(8,128)S(1)}) custom-call(s32[2]{0:T(128)S(1)} %pad_add_fusion.place, f32[16,2,128,256]{3,2,1,0:T(8,128)S(1)} %copy-done.21, bf16[2,2,768,256]{3,2,1,0:T(8,128)(2,1)S(1)} %copy-done.12, f32[2,2,256,256]{3,2,1,0:T(8,128)S(1)} %copy-done.18, f32[4,64,256]{2,1,0:T(8,128)S(1)} %all-to-all-done.3.befores), custom_call_target="tpu_custom_call" | custom-call | flops 2147483648 | bytes 8388608 | tf_op jit(solution)/shard_map/inverse_first/pallas_call | solution.py:366
  88.3 3.1 %keep_inverse.1 = f32[4096,256]{1,0:T(8,128)S(1)} custom-call(s32[2]{0:T(128)S(1)} %pad_add_fusion.place, bf16[2,768,256]{2,1,0:T(8,128)(2,1)S(1)} %copy-done.1, f32[4096,128]{1,0:T(8,128)S(1)} %copy-done.5, f32[4096,128]{1,0:T(8,128)S(1)} %get-tuple-element.28.refs_1_), custom_call_target="tpu_custom_call" | custom-call | flops 2147483648 | bytes 8388608 | tf_op jit(solution)/shard_map/keep_inverse/pallas_call | solution.py:222
  92.1 6.5 %inverse_second.1 = f32[256,16,512]{2,1,0:T(8,128)} custom-call(s32[2]{0:T(128)S(1)} %pad_add_fusion.place, bf16[2,768,256]{2,1,0:T(8,128)(2,1)S(1)} %copy-done.1, f32[16,256,256]{2,1,0:T(8,128)S(1)} %bitcast.5, f32[16,256,128]{2,1,0:T(8,128)S(1)} %bitcast.6, f32[16,256,128]{2,1,0:T(8,128)S(1)} %bitcast.7), custom_call_target="tpu_custom_call" | custom-call | flops 4294967296 | bytes 8388608 | tf_op jit(solution)/shard_map/inverse_second/pallas_call | solution.py:420
  (53 shorter events, 6.5 us)
Async XLA Ops:
  0.1 9.4 %copy-start.19 = (bf16[2,768,256]{2,1,0:T(8,128)(2,1)S(1)}, bf16[2,768,256]{2,1,0:T(8,128)(2,1)}, u32[]{:S(2)}) copy-start(bf16[2,768,256]{2,1,0:T(8,128)(2,1)} %constant.23.clone.table.tables) | copy-start | bytes 2359300
  8.5 8.1 %collective-permute-start = (f32[4352,128]{1,0:T(8,128)S(1)}, f32[4352,128]{1,0:T(8,128)S(1)}, u32[]{:S(2)}, u32[]{:S(2)}) collective-permute-start(f32[4352,128]{1,0:T(8,128)S(1)} %get-tuple-element.20), channel_id=1, source_target_pairs={{0,1},{1,0},{2,3},{3,2},{4,5},{5,4},{6,7},{7,6},{8,9},{9,8},{10,11... | collective-permute-start | bytes 6684680 | tf_op jit(solution)/shard_map/ppermute | solution.py:437
  9.4 17.4 %collective-permute-start.2 = (f32[4352,128]{1,0:T(8,128)}, f32[4352,128]{1,0:T(8,128)S(1)}, u32[]{:S(2)}, u32[]{:S(2)}) collective-permute-start(f32[4352,128]{1,0:T(8,128)} %get-tuple-element.25), channel_id=1, source_target_pairs={{0,1},{1,0},{2,3},{3,2},{4,5},{5,4},{6,7},{7,6},{8,9},{9,8},{10,11... | collective-permute-start | bytes 6684680 | tf_op jit(solution)/shard_map/ppermute | solution.py:437
  9.4 7.1 %copy-start.13 = (bf16[2,2,768,256]{3,2,1,0:T(8,128)(2,1)S(1)}, bf16[2,2,768,256]{3,2,1,0:T(8,128)(2,1)}, u32[]{:S(2)}) copy-start(bf16[2,2,768,256]{3,2,1,0:T(8,128)(2,1)} %constant.21.clone.table) | copy-start | bytes 4718596
  9.5 7.1 %copy-start.15 = (f32[2,2,256,256]{3,2,1,0:T(8,128)S(1)}, f32[2,2,256,256]{3,2,1,0:T(8,128)}, u32[]{:S(2)}) copy-start(f32[2,2,256,256]{3,2,1,0:T(8,128)} %constant.22.clone.decay) | copy-start | bytes 3145732
  11.9 9.5 %copy-start.24 = (f32[4352,128]{1,0:T(8,128)}, f32[4352,128]{1,0:T(8,128)S(1)}, u32[]{:S(2)}) copy-start(f32[4352,128]{1,0:T(8,128)S(1)} %get-tuple-element.24.keep) | copy-start | bytes 6684676
  21.4 2.0 %copy-start.22 = (f32[16,2,128,256]{3,2,1,0:T(8,128)}, f32[16,2,128,256]{3,2,1,0:T(8,128)S(1)}, u32[]{:S(2)}) copy-start(f32[16,2,128,256]{3,2,1,0:T(8,128)S(1)} %get-tuple-element.21.modes) | copy-start | bytes 12582916
  23.4 17.6 %all-to-all-start = ((f32[4,64,256]{2,1,0:T(8,128)}), f32[4,64,256]{2,1,0:T(8,128)S(1)}, u32[]{:S(2)}, u32[]{:S(2)}) async-start(f32[4,64,256]{2,1,0:T(8,128)} %get-tuple-element.22), calls=%async_computation | async-start | bytes 524288 | tf_op jit(solution)/shard_map/all_to_all | solution.py:450
  26.9 1.4 %copy-start.9 = (f32[4352,128]{1,0:T(8,128)}, f32[4352,128]{1,0:T(8,128)S(1)}, u32[]{:S(2)}) copy-start(f32[4352,128]{1,0:T(8,128)S(1)} %collective-permute-done.2.got) | copy-start | bytes 6684676
  28.3 1.6 %copy-start.10 = (f32[4352,128]{1,0:T(8,128)S(1)}, f32[4352,128]{1,0:T(8,128)}, u32[]{:S(2)}) copy-start(f32[4352,128]{1,0:T(8,128)} %copy-done.9) | copy-start | bytes 6684676
  29.9 1.4 %copy-start.14 = (bf16[2,2,768,256]{3,2,1,0:T(8,128)(2,1)S(1)}, bf16[2,2,768,256]{3,2,1,0:T(8,128)(2,1)}, u32[]{:S(2)}) copy-start(bf16[2,2,768,256]{3,2,1,0:T(8,128)(2,1)} %constant.21.clone.table) | copy-start | bytes 4718596
  31.3 1.2 %copy-start.16 = (f32[2,2,256,256]{3,2,1,0:T(8,128)S(1)}, f32[2,2,256,256]{3,2,1,0:T(8,128)}, u32[]{:S(2)}) copy-start(f32[2,2,256,256]{3,2,1,0:T(8,128)} %constant.22.clone.decay) | copy-start | bytes 3145732
  32.5 1.6 %copy-start.25 = (f32[4352,128]{1,0:T(8,128)S(1)}, f32[4352,128]{1,0:T(8,128)}, u32[]{:S(2)}) copy-start(f32[4352,128]{1,0:T(8,128)} %copy-done.24) | copy-start | bytes 6684676
  34.2 11.7 %copy-start = (f32[2,2,3,256,256]{4,3,2,1,0:T(8,128)S(1)}, f32[2,2,3,256,256]{4,3,2,1,0:T(8,128)}, u32[]{:S(2)}) copy-start(f32[2,2,3,256,256]{4,3,2,1,0:T(8,128)} %constant.20.clone.closing) | copy-start | bytes 9437188
  39.1 2.0 %copy-start.20 = (f32[16,2,128,256]{3,2,1,0:T(8,128)}, f32[16,2,128,256]{3,2,1,0:T(8,128)S(1)}, u32[]{:S(2)}) copy-start(f32[16,2,128,256]{3,2,1,0:T(8,128)S(1)} %get-tuple-element.26.modes) | copy-start | bytes 12582916
  41.7 12.9 %all-to-all-start.2 = ((f32[4,64,256]{2,1,0:T(8,128)}), f32[4,64,256]{2,1,0:T(8,128)S(1)}, u32[]{:S(2)}, u32[]{:S(2)}) async-start(f32[4,64,256]{2,1,0:T(8,128)} %copy-done.8), calls=%async_computation.2 | async-start | bytes 524288 | tf_op jit(solution)/shard_map/all_to_all | solution.py:450
  45.9 1.0 copy-start.3
  47.4 5.9 %collective-permute-start.1 = (f32[64,256]{1,0:T(8,128)S(1)}, f32[64,256]{1,0:T(8,128)S(1)}, u32[]{:S(2)}, u32[]{:S(2)}) collective-permute-start(f32[64,256]{1,0:T(8,128)S(1)} %half_sum.2.near), channel_id=1, source_target_pairs={{0,8},{2,10},{4,12},{6,14},{8,0},{10,2},{12,4},{14,6},{1,9},{3,11}... | collective-permute-start | bytes 196616 | tf_op jit(solution)/shard_map/ppermute | solution.py:443
  54.7 11.2 %all-to-all-start.1 = ((f32[4,64,256]{2,1,0:T(8,128)}), f32[4,64,256]{2,1,0:T(8,128)}, u32[]{:S(2)}, u32[]{:S(2)}) async-start(f32[4,64,256]{2,1,0:T(8,128)} %copy-done.6), calls=%async_computation.1 | async-start | bytes 524288 | tf_op jit(solution)/shard_map/all_to_all | solution.py:450
  59.3 5.3 %collective-permute-start.3 = (f32[64,256]{1,0:T(8,128)S(1)}, f32[64,256]{1,0:T(8,128)S(1)}, u32[]{:S(2)}, u32[]{:S(2)}) collective-permute-start(f32[64,256]{1,0:T(8,128)S(1)} %half_sum.3.near), channel_id=1, source_target_pairs={{0,8},{2,10},{4,12},{6,14},{8,0},{10,2},{12,4},{14,6},{1,9},{3,11}... | collective-permute-start | bytes 196616 | tf_op jit(solution)/shard_map/ppermute | solution.py:443
  65.8 15.3 %all-to-all-start.3 = ((f32[4,64,256]{2,1,0:T(8,128)}), f32[4,64,256]{2,1,0:T(8,128)S(1)}, u32[]{:S(2)}, u32[]{:S(2)}) async-start(f32[4,64,256]{2,1,0:T(8,128)} %copy-done.7), calls=%async_computation.3 | async-start | bytes 524288 | tf_op jit(solution)/shard_map/all_to_all | solution.py:450
  70.2 1.4 %copy-start.11 = (bf16[2,2,768,256]{3,2,1,0:T(8,128)(2,1)S(1)}, bf16[2,2,768,256]{3,2,1,0:T(8,128)(2,1)}, u32[]{:S(2)}) copy-start(bf16[2,2,768,256]{3,2,1,0:T(8,128)(2,1)} %constant.24.clone.table) | copy-start | bytes 4718596
  71.6 1.2 %copy-start.17 = (f32[2,2,256,256]{3,2,1,0:T(8,128)S(1)}, f32[2,2,256,256]{3,2,1,0:T(8,128)}, u32[]{:S(2)}) copy-start(f32[2,2,256,256]{3,2,1,0:T(8,128)} %constant.22.clone.decay) | copy-start | bytes 3145732
  72.9 2.2 %copy-start.23 = (f32[16,2,128,256]{3,2,1,0:T(8,128)S(1)}, f32[16,2,128,256]{3,2,1,0:T(8,128)}, u32[]{:S(2)}) copy-start(f32[16,2,128,256]{3,2,1,0:T(8,128)} %copy-done.22) | copy-start | bytes 12582916
  75.0 6.1 %copy-start.18 = (f32[2,2,256,256]{3,2,1,0:T(8,128)S(1)}, f32[2,2,256,256]{3,2,1,0:T(8,128)}, u32[]{:S(2)}) copy-start(f32[2,2,256,256]{3,2,1,0:T(8,128)} %constant.22.clone.decay) | copy-start | bytes 3145732
  79.8 1.4 %copy-start.4 = (f32[4096,128]{1,0:T(8,128)}, f32[4096,128]{1,0:T(8,128)S(1)}, u32[]{:S(2)}) copy-start(f32[4096,128]{1,0:T(8,128)S(1)} %get-tuple-element.23.refs_0_) | copy-start | bytes 6291460
  81.2 10.2 %collective-permute-start.4 = (f32[4096,128]{1,0:T(8,128)}, f32[4096,128]{1,0:T(8,128)S(1)}, u32[]{:S(2)}, u32[]{:S(2)}) collective-permute-start(f32[4096,128]{1,0:T(8,128)} %get-tuple-element.29), channel_id=1, source_target_pairs={{0,1},{1,0},{2,3},{3,2},{4,5},{5,4},{6,7},{7,6},{8,9},{9,8},{10,11... | collective-permute-start | bytes 6291464 | tf_op jit(solution)/shard_map/ppermute | solution.py:437
  81.2 1.4 %copy-start.12 = (bf16[2,2,768,256]{3,2,1,0:T(8,128)(2,1)S(1)}, bf16[2,2,768,256]{3,2,1,0:T(8,128)(2,1)}, u32[]{:S(2)}) copy-start(bf16[2,2,768,256]{3,2,1,0:T(8,128)(2,1)} %constant.24.clone.table) | copy-start | bytes 4718596
  82.6 2.2 %copy-start.21 = (f32[16,2,128,256]{3,2,1,0:T(8,128)S(1)}, f32[16,2,128,256]{3,2,1,0:T(8,128)}, u32[]{:S(2)}) copy-start(f32[16,2,128,256]{3,2,1,0:T(8,128)} %copy-done.20) | copy-start | bytes 12582916
  84.8 3.5 %copy-start.1 = (bf16[2,768,256]{2,1,0:T(8,128)(2,1)S(1)}, bf16[2,768,256]{2,1,0:T(8,128)(2,1)}, u32[]{:S(2)}) copy-start(bf16[2,768,256]{2,1,0:T(8,128)(2,1)} %constant.25.clone.tables) | copy-start | bytes 2359300
  84.8 3.5 %copy-start.5 = (f32[4096,128]{1,0:T(8,128)S(1)}, f32[4096,128]{1,0:T(8,128)}, u32[]{:S(2)}) copy-start(f32[4096,128]{1,0:T(8,128)} %copy-done.4) | copy-start | bytes 6291460
  87.7 4.4 %collective-permute-start.5 = (f32[4096,128]{1,0:T(8,128)S(1)}, f32[4096,128]{1,0:T(8,128)S(1)}, u32[]{:S(2)}, u32[]{:S(2)}) collective-permute-start(f32[4096,128]{1,0:T(8,128)S(1)} %get-tuple-element.30), channel_id=1, source_target_pairs={{0,1},{1,0},{2,3},{3,2},{4,5},{5,4},{6,7},{7,6},{8,9},{9,8},{10,11... | collective-permute-start | bytes 6291464 | tf_op jit(solution)/shard_map/ppermute | solution.py:437
  (4 other events, 2.8 us)

commit v8 on v6

--- a/solution.py
+++ b/solution.py
@@ -88,6 +88,15 @@
         ref[pl.ds(to, SUBLANES), :] = jnp.take_along_axis(
             block[row : row + SUBLANES], index, axis=0, mode="promise_in_bounds"
         )
+
+
+def pitch_of(cells):
+    return cells + SUBLANES * (1 - cells // SUBLANES % 2)
+
+
+def steps_of(ref, cells, steps, pitch):
+    lines = [ref[pl.ds(cell, steps, stride=pitch), :] for cell in cells]
+    return lines[0] if len(lines) == 1 else jnp.concatenate(lines, axis=0)
 
 
 IN_VMEM = pl.BlockSpec(memory_space=pltpu.VMEM)
@@ -134,6 +143,7 @@
     group = max(TILE // steps, 1)
     head = min(steps, SUBLANES)
     total = rows * pl.num_programs(0)
+    pitch = sends[0].shape[0] // (steps + 1)
     start = pl.program_id(0) * rows
     mirror = total - rows - start
     is_first = (place[0] == 0).astype(jnp.float32)
@@ -166,19 +176,18 @@
             ends = field[pl.ds(sub * piece + row, TILE), steps - 1, :]
             put(other, body + row, total * steps + kept_at + row, ends)
         sent = dot(other[...], table[0])
-        base = pl.multiple_of(sent_at * steps, body)
         for chunk, send in enumerate(sends):
             lanes = slice(chunk * part, (chunk + 1) * part)
             for row in range(piece):
                 line = sent[row * steps : (row + 1) * steps, lanes]
-                send[pl.ds(base + (piece - 1 - row) * steps, steps), :] = line
-            store_rows_reversed(send, total * steps + sent_at, sent[body:, lanes])
+                send[pl.ds(sent_at + piece - 1 - row, steps, stride=pitch), :] = line
+            store_rows_reversed(send, pitch * steps + sent_at, sent[body:, lanes])
 
 
 def forward_second(place, field, initial, tables):
     rows, steps, width = field.shape
     half = width // 2
-    block, pieces = min(32, rows), 2
+    block, pieces = min(64, rows), 2
     depth = (steps + 1) * block // pieces
     outs = call(
         forward_second_kernel,
@@ -190,7 +199,7 @@
         ],
         [IN_VMEM] * (1 + CHUNKS),
         [floats((steps + 1) * rows, half)]
-        + [floats((steps + 1) * rows, half // CHUNKS)] * CHUNKS,
+        + [floats((steps + 1) * pitch_of(rows), half // CHUNKS)] * CHUNKS,
         [pltpu.VMEM((depth, 3 * half), jnp.bfloat16)] * pieces,
         1 << 32,
         rows // block,
@@ -198,9 +207,11 @@
     return outs[0], outs[1:]
 
 
-def keep_second_kernel(place, tables, sums, *refs):
+def keep_second_kernel(steps, place, tables, sums, *refs):
     keeps, scratch = refs[:CHUNKS], refs[CHUNKS:]
     depth = scratch[0].shape[0]
+    cells = sums.shape[0] // (steps + 1)
+    pitch = keeps[0].shape[0] // (steps + 1)
     for at in range(0, sums.shape[0], depth):
         split = scratch[at // depth % 2]
         for row in range(0, depth, TILE):
@@ -208,17 +219,25 @@
         result = dot(split[...], tables[place[1]])
         for chunk, keep in enumerate(keeps):
             part = keep.shape[1]
-            keep[pl.ds(at, depth)] = result[:, chunk * part : (chunk + 1) * part]
-
-
-def keep_second(place, sums, tables):
+            lanes = slice(chunk * part, (chunk + 1) * part)
+            body = max(0, min(depth, cells * steps - at))
+            for row in range(0, body, steps):
+                line = result[row : row + steps, lanes]
+                keep[pl.ds((at + row) // steps, steps, stride=pitch), :] = line
+            if body < depth:
+                ends = pl.ds(pitch * steps + at + body - cells * steps, depth - body)
+                keep[ends, :] = result[body:, lanes]
+
+
+def keep_second(place, sums, tables, steps):
     rows, half = sums.shape
+    shape = ((steps + 1) * pitch_of(rows // (steps + 1)), half // CHUNKS)
     return call(
-        keep_second_kernel,
+        functools.partial(keep_second_kernel, steps),
         "keep_second",
         [IN_VMEM] * 2,
         [IN_VMEM] * CHUNKS,
-        [floats(rows, half // CHUNKS)] * CHUNKS,
+        [floats(*shape)] * CHUNKS,
         [pltpu.VMEM((rows // 8, 3 * half), jnp.bfloat16)] * 2,
         1 << 31,
     )(place, tables, sums)
@@ -228,22 +247,19 @@
     return slabs // 2
 
 
-def parcels(size):
-    return [(0,), (1,), (2, 3)] if size == 4 else [(partner,) for partner in range(size)]
-
-
 def forward_first_kernel(slabs, chunk, place, keep, got, table, decay, modes, *refs):
     size = ranks(slabs)
-    lasts, (state, split, split_end) = refs[:-3], refs[-3:]
+    lasts, (state, split, split_end) = refs[:size], refs[size:]
     steps, _, part, rows = modes.shape
+    pitch = keep.shape[0] // (steps + 1)
     block = split.shape[1] // part
     strip = place[1]
     state[...] = jnp.zeros_like(state)
     for step in range(0, steps, block):
         for c in (0, 1):
             for at in range(block):
-                cells_at = pl.ds(step + at, rows, stride=steps)
-                near, far = keep[cells_at, :], got[cells_at, :]
+                cells_at = pl.ds((step + at) * pitch, rows)
+                near, far = keep[cells_at], got[cells_at]
                 cells = near - far if c else near + far
                 store_split(split, (c, pl.ds(at * part, part)), 0, cells.T)
             result = dot(split[c], table[strip, c])
@@ -257,22 +273,21 @@
                     value = rate * (value + modes[step + at, c, tile])
                 state[at_state] = value
     is_last = (place[0] == slabs - 1).astype(jnp.float32)
-    near, far = keep[pl.ds(rows * steps, rows)], got[pl.ds(rows * steps, rows)]
+    near, far = keep[pl.ds(pitch * steps, rows)], got[pl.ds(pitch * steps, rows)]
     for c, cells in enumerate((near + far, near - far)):
         store_split(split_end, (c, slice(None)), 0, cells.T)
         at_state = pl.ds(c * part, part)
         state[at_state] = state[at_state] - is_last * dot(split_end[c], table[strip, c])
     rank = lax.rem(place[0], size)
     share = 2 * part // size
-    for parcel, last in zip(parcels(size), lasts):
-        for place_in, partner in enumerate(parcel):
-            at = pl.multiple_of((rank ^ partner) * share, share)
-            last[pl.ds(place_in * share, share)] = state[pl.ds(at, share)]
+    for partner in range(size):
+        at = pl.multiple_of((rank ^ partner) * share, share)
+        lasts[partner][...] = state[pl.ds(at, share)]
 
 
 def forward_first(place, chunk, keep, got, tables, decays, slabs):
     rows, part = tables.shape[-1], keep.shape[1]
-    steps = keep.shape[0] // rows - 1
+    steps = keep.shape[0] // pitch_of(rows) - 1
     block = min(8, steps)
     size = ranks(slabs)
     share = 2 * part // size
@@ -280,9 +295,8 @@
         functools.partial(forward_first_kernel, slabs, chunk),
         "forward_first",
         [IN_VMEM] * 4,
-        [IN_VMEM] * (1 + len(parcels(size))),
-        [floats(steps, 2, part, rows)]
-        + [floats(len(parcel) * share, rows) for parcel in parcels(size)],
+        [IN_VMEM] * (1 + size),
+        [floats(steps, 2, part, rows)] + [floats(share, rows)] * size,
         [
             pltpu.VMEM((2 * part, rows), jnp.float32),
             pltpu.VMEM((2, block * part, 3 * rows), jnp.bfloat16),
@@ -300,7 +314,7 @@
     rank = lax.rem(place[0], size)
     decay = closing[place[1], chunk, 0, pl.ds(pl.multiple_of(rank * share, share), share)]
     for partner in range(size):
-        ordered[rank ^ partner] = lasts[partner][pl.ds(0, share)]
+        ordered[rank ^ partner] = lasts[partner][...]
     state = ordered[0]
     for at in range(1, size):
         state = ordered[at] + decay * state
@@ -323,7 +337,7 @@
 
 def close_kernel(slabs, chunk, place, closing, ordered, near, far, *refs):
     size = ranks(slabs)
-    befores, states = refs[:-1], refs[-1]
+    befores, states = refs[:size], refs[size]
     share = near.shape[0]
     rank = lax.rem(place[0], size)
     at_share = pl.ds(pl.multiple_of(rank * share, share), share)
@@ -334,9 +348,8 @@
         states[at] = state
         if at < size - 1:
             state = ordered[at] + decay * state
-    for parcel, before in zip(parcels(size), befores):
-        for place_in, partner in enumerate(parcel):
-            before[pl.ds(place_in * share, share)] = states[rank ^ partner]
+    for partner in range(size):
+        befores[partner][...] = states[rank ^ partner]
 
 
 def close(place, chunk, ordered, near, far, closing, slabs):
@@ -345,8 +358,8 @@
         functools.partial(close_kernel, slabs, chunk),
         "close",
         [IN_VMEM] * 4,
-        [IN_VMEM] * len(parcels(size)),
-        [floats(len(parcel) * share, rows) for parcel in parcels(size)],
+        [IN_VMEM] * size,
+        [floats(share, rows)] * size,
         [pltpu.VMEM((size, share, rows), jnp.float32)],
         1 << 20,
     )(place, closing, ordered, near, far)
@@ -356,13 +369,14 @@
     size = ranks(slabs)
     befores, (keep, send, state, split) = refs[:size], refs[size:]
     steps, _, part, rows = modes.shape
+    pitch = keep.shape[0] // steps
     block = split.shape[1] // part
     strip = place[1]
     rank = lax.rem(place[0], size)
     share = 2 * part // size
     for partner in range(size):
         at = pl.multiple_of((rank ^ partner) * share, share)
-        state[pl.ds(at, share)] = befores[partner][pl.ds(0, share)]
+        state[pl.ds(at, share)] = befores[partner][...]
     for step in range(0, steps, block):
         results = []
         for c in (0, 1):
@@ -378,9 +392,9 @@
         even, odd = results
         for at in range(block):
             piece = slice(at * part, (at + 1) * part)
-            start = (step + at) * rows
-            keep[pl.ds(start, rows), :] = (even[piece] + odd[piece]).T
-            send[pl.ds(start, rows), :] = (even[piece] - odd[piece]).T
+            cells_at = pl.ds((step + at) * pitch, rows)
+            keep[cells_at, :] = (even[piece] + odd[piece]).T
+            send[cells_at, :] = (even[piece] - odd[piece]).T
 
 
 def inverse_first(place, chunk, modes, befores, tables, decays, slabs):
@@ -391,7 +405,7 @@
         "inverse_first",
         [IN_VMEM] * (3 + len(befores)),
         [IN_VMEM] * 2,
-        [floats(steps * rows, part)] * 2,
+        [floats(steps * pitch_of(rows), part)] * 2,
         [
             pltpu.VMEM((2 * part, rows), jnp.float32),
             pltpu.VMEM((2, block * part, 3 * rows), jnp.bfloat16),
@@ -400,15 +414,10 @@
     )(place, modes, tables, decays, *befores)
 
 
-def steps_of(ref, cells, steps):
-    pitch = ref.shape[0] // steps
-    lines = [ref[pl.ds(cell, steps, stride=pitch), :] for cell in cells]
-    return lines[0] if len(lines) == 1 else jnp.concatenate(lines, axis=0)
-
-
 def keep_inverse_kernel(steps, place, tables, *refs):
     keeps, out, scratch = refs[:CHUNKS], refs[CHUNKS], refs[CHUNKS + 1 :]
     part = keeps[0].shape[1]
+    pitch = keeps[0].shape[0] // steps
     depth = scratch[0].shape[0]
     group = max(TILE // steps, 1)
     for at in range(0, out.shape[0], depth):
@@ -416,21 +425,20 @@
         for row in range(0, depth, TILE):
             cell = (at + row) // steps
             for chunk, keep in enumerate(keeps):
-                cells = steps_of(keep, range(cell, cell + group), steps)
+                cells = steps_of(keep, range(cell, cell + group), steps, pitch)
                 store_split(split, (pl.ds(row, TILE),), chunk * part, cells)
         out[pl.ds(at, depth)] = dot(split[...], tables[place[1]])
 
 
-def keep_inverse(place, keeps, tables, steps):
-    rows, part = keeps[0].shape
-    half = part * CHUNKS
+def keep_inverse(place, keeps, tables, rows, steps):
+    half = keeps[0].shape[1] * CHUNKS
     return call(
         functools.partial(keep_inverse_kernel, steps),
         "keep_inverse",
         [IN_VMEM] * (1 + CHUNKS),
         IN_VMEM,
-        floats(rows, half),
-        [pltpu.VMEM((rows // 8, 3 * half), jnp.bfloat16)] * 2,
+        floats(rows * steps, half),
+        [pltpu.VMEM((rows * steps // 8, 3 * half), jnp.bfloat16)] * 2,
         1 << 31,
     )(place, tables, *keeps)
 
@@ -440,6 +448,7 @@
     rows, steps, width = out.shape
     half = width // 2
     part = half // CHUNKS
+    pitch = gots[0].shape[0] // steps
     count = len(scratch) // 2
     piece = rows // count
     group = max(TILE // steps, 1)
@@ -453,7 +462,7 @@
         for row in range(0, piece, group):
             mirrors = [total - 1 - base - row - at for at in range(group)]
             for chunk, got in enumerate(gots):
-                cells = steps_of(got, mirrors, steps)
+                cells = steps_of(got, mirrors, steps, pitch)
                 store_split(split, (pl.ds(row * steps, TILE),), chunk * part, cells)
         result[...] = dot(split[...], tables[1 - strip])
         kept_base = pl.multiple_of(base * steps, piece * steps)
@@ -470,7 +479,7 @@
 
 def inverse_second(place, kept, gots, tables, steps):
     rows, half = kept.shape[0] // steps, kept.shape[1]
-    block, pieces = min(32, rows), 2
+    block, pieces = min(64, rows), 2
     depth = steps * block // pieces
     return call(
         inverse_second_kernel,
@@ -495,12 +504,7 @@
 
 
 def among_ranks(blocks):
-    if len(blocks) != 3:
-        return [blocks[0]] + [with_partner(block, at) for at, block in enumerate(blocks) if at]
-    own, near, pair = blocks
-    pair = with_partner(pair, 2)
-    near = with_partner(near, 1)
-    return [own, near, pair, with_partner(pair[own.shape[0] :], 1)]
+    return [blocks[0]] + [with_partner(block, at) for at, block in enumerate(blocks) if at]
 
 
 def by_chunk(table):
@@ -527,7 +531,7 @@
     second_table = split_constant(second)
     sums, sends = forward_second(place, iterate, initial, second_table)
     gots = [swapped(send) for send in sends]
-    keeps = keep_second(place, sums, second_table)
+    keeps = keep_second(place, sums, second_table, steps)
     modes, befores = [], []
     for chunk in range(CHUNKS):
         own_modes, lasts = forward_first(
@@ -546,7 +550,7 @@
     )
     gots = [swapped(send) for send in sends]
     inverse_table = split_constant(np.swapaxes(second, 1, 2))
-    kept = keep_inverse(place, keeps, inverse_table, steps)
+    kept = keep_inverse(place, keeps, inverse_table, rows, steps)
     return inverse_second(place, kept, gots, inverse_table, steps)
 
 

time: 73.7 us -> 61 us (0.83)
  Pallas kernels: 45.2 us -> 34.9 us
  starting transfers between devices: 23 us -> 21.3 us
    pallas_call x1, Pallas kernels: 9.73 us -> 6.27 us  [inverse_second(): call(inverse_second_kernel, 'inverse_second', [IN_VMEM] * (2 + CHUNKS), p...]
    pallas_call x1, Pallas kernels: 6.71 us -> 3.64 us  [keep_inverse(): call(functools.partial(keep_inverse_kernel, steps), 'keep_inverse', [IN_V...]
    pallas_call x2, Pallas kernels: 8.68 us -> 6.4 us  [forward_first(): call(functools.partial(forward_first_kernel, slabs, chunk), 'forward_firs...]
    pallas_call x1, Pallas kernels: 8.72 us -> 7.15 us  [forward_second(): call(forward_second_kernel, 'forward_second', [pl.BlockSpec((block, steps...]
    ppermute x14, starting transfers between devices: 21.6 us -> 20.2 us  [with_partner(): lax.ppermute(block, 'tm', [(slab, slab ^ distance) for slab in range(slab...]
    ppermute x14, waiting for transfers between devices: 3.61 us -> 2.46 us  [with_partner(): lax.ppermute(block, 'tm', [(slab, slab ^ distance) for slab in range(slab...]
  transfers between devices with their start and end apart: 18 -> 18, of which waited for: 5 -> 4; matrix products, arithmetic and copies ran while one was open for 0% -> 0% of each run, Pallas kernels for 36% -> 35%
where the time goes in v8:
time: 61 us; the launch traced here: 60.8 us
  Pallas kernels  34.9 us (57%)
  starting transfers between devices  21.3 us (35%)
  waiting for transfers between devices  4.34 us (7%)
    ppermute x14, starting transfers between devices, with_partner(): lax.ppermute(block, 'tm', [(slab, slab ^ distance) for slab in range(slab...  20.2 us
    pallas_call x1, Pallas kernels, forward_second(): call(forward_second_kernel, 'forward_second', [pl.BlockSpec((block, steps...  7.15 us
    pallas_call x2, Pallas kernels, forward_first(): call(functools.partial(forward_first_kernel, slabs, chunk), 'forward_firs...  6.4 us
    pallas_call x2, Pallas kernels, inverse_first(): call(functools.partial(inverse_first_kernel, slabs, chunk), 'inverse_firs...  6.35 us
    pallas_call x1, Pallas kernels, inverse_second(): call(inverse_second_kernel, 'inverse_second', [IN_VMEM] * (2 + CHUNKS), p...  6.27 us
    pallas_call x1, Pallas kernels, keep_inverse(): call(functools.partial(keep_inverse_kernel, steps), 'keep_inverse', [IN_V...  3.64 us
    pallas_call x1, Pallas kernels, keep_second(): call(functools.partial(keep_second_kernel, steps), 'keep_second', [IN_VME...  2.68 us
    ppermute x14, waiting for transfers between devices, with_partner(): lax.ppermute(block, 'tm', [(slab, slab ^ distance) for slab in range(slab...  2.46 us
  transfers between devices with their start and end apart: 18, of which 4 were waited for; matrix products, arithmetic and copies ran while one was open for 0% of the time, Pallas kernels for 35%

profile of v8, /device:TPU:0, one launch (start us, length us, event | category | flops | bytes accessed | tf_op | source)
XLA Modules:
  0.0 60.8 jit_solution(12404925854476269542)
XLA Ops:
  0.0 0.1 pad_add_fusion.place
  0.1 7.2 %forward_second.1 = (f32[4352,256]{1,0:T(8,128)S(1)}, f32[4488,128]{1,0:T(8,128)S(1)}, f32[4488,128]{1,0:T(8,128)S(1)}) custom-call(s32[2]{0:T(128)S(1)} %pad_add_fusion.place, f32[256,16,512]{2,1,0:T(8,128)} %field.1, f32[256,512]{1,0:T(8,128)} %initial.1, bf16[2,768,256]{2,1,0:T(8,128)(2,1)} %constant.23.clone.table.tables), custom_call_target="tpu_custom_call" | custom-call | flops 4294967296 | bytes 8388608 | tf_op jit(solution)/shard_map/forward_second/pallas_call | solution.py:192
  7.2 0.9 %collective-permute-start = (f32[4488,128]{1,0:T(8,128)S(1)}, f32[4488,128]{1,0:T(8,128)S(1)}, u32[]{:S(2)}, u32[]{:S(2)}) collective-permute-start(f32[4488,128]{1,0:T(8,128)S(1)} %get-tuple-element.38), channel_id=1, source_target_pairs={{0,1},{1,0},{2,3},{3,2},{4,5},{5,4},{6,7},{7,6},{8,9},{9,8},{10,11... | collective-permute-start | bytes 6893576 | tf_op jit(solution)/shard_map/ppermute | solution.py:498
  8.2 0.1 collective-permute-start.8
  8.2 2.7 %keep_second.1 = (f32[4488,128]{1,0:T(8,128)S(1)}, f32[4488,128]{1,0:T(8,128)S(1)}) custom-call(s32[2]{0:T(128)S(1)} %pad_add_fusion.place, bf16[2,768,256]{2,1,0:T(8,128)(2,1)S(1)} %copy-done.5, f32[4352,256]{1,0:T(8,128)S(1)} %get-tuple-element.36.sums), custom_call_target="tpu_custom_call" | custom-call | flops 2147483648 | bytes 8388608 | tf_op jit(solution)/shard_map/keep_second/pallas_call | solution.py:235
  10.9 1.3 %collective-permute-done.got = f32[4488,128]{1,0:T(8,128)S(1)} collective-permute-done((f32[4488,128]{1,0:T(8,128)S(1)}, f32[4488,128]{1,0:T(8,128)S(1)}, u32[]{:S(2)}, u32[]{:S(2)}) %collective-permute-start) | collective-permute-done | bytes 2297888 | tf_op jit(solution)/shard_map/ppermute | solution.py:498
  12.2 3.2 %forward_first.2 = (f32[16,2,128,256]{3,2,1,0:T(8,128)S(1)}, f32[64,256]{1,0:T(8,128)S(1)}, f32[64,256]{1,0:T(8,128)S(1)}, f32[64,256]{1,0:T(8,128)S(1)}, f32[64,256]{1,0:T(8,128)S(1)}) custom-call(s32[2]{0:T(128)S(1)} %pad_add_fusion.place, f32[4488,128]{1,0:T(8,128)S(1)} %get-tuple-element.37.keep, f32[4488,128]{1,0:T(8,128)S(1)} %collective-permute-done.got, ...), custom_call_target="tpu_custom_call" | custom-call | flops 2147483648 | bytes 8388608 | tf_op jit(solution)/shard_map/forward_first/pallas_call | solution.py:294
  15.4 2.6 %collective-permute-start.1 = (f32[64,256]{1,0:T(8,128)S(1)}, f32[64,256]{1,0:T(8,128)S(1)}, u32[]{:S(2)}, u32[]{:S(2)}) collective-permute-start(f32[64,256]{1,0:T(8,128)S(1)} %get-tuple-element.41), channel_id=1, source_target_pairs={{0,2},{2,0},{4,6},{6,4},{8,10},{10,8},{12,14},{14,12},{1,3},{3,1},... | collective-permute-start | bytes 196616 | tf_op jit(solution)/shard_map/ppermute | solution.py:503
  18.0 1.6 %collective-permute-start.2 = (f32[64,256]{1,0:T(8,128)S(1)}, f32[64,256]{1,0:T(8,128)S(1)}, u32[]{:S(2)}, u32[]{:S(2)}) collective-permute-start(f32[64,256]{1,0:T(8,128)S(1)} %get-tuple-element.42), channel_id=1, source_target_pairs={{0,4},{2,6},{4,0},{6,2},{8,12},{10,14},{12,8},{14,10},{1,5},{3,7},... | collective-permute-start | bytes 196616 | tf_op jit(solution)/shard_map/ppermute | solution.py:503
  19.6 3.2 %forward_first.3 = (f32[16,2,128,256]{3,2,1,0:T(8,128)S(1)}, f32[64,256]{1,0:T(8,128)S(1)}, f32[64,256]{1,0:T(8,128)S(1)}, f32[64,256]{1,0:T(8,128)S(1)}, f32[64,256]{1,0:T(8,128)S(1)}) custom-call(s32[2]{0:T(128)S(1)} %pad_add_fusion.place, f32[4488,128]{1,0:T(8,128)S(1)} %get-tuple-element.51.keep, f32[4488,128]{1,0:T(8,128)S(1)} %collective-permute-done.8.got, ...), custom_call_target="tpu_custom_call" | custom-call | flops 2147483648 | bytes 8388608 | tf_op jit(solution)/shard_map/forward_first/pallas_call | solution.py:294
  22.8 2.0 %collective-permute-start.9 = (f32[64,256]{1,0:T(8,128)S(1)}, f32[64,256]{1,0:T(8,128)S(1)}, u32[]{:S(2)}, u32[]{:S(2)}) collective-permute-start(f32[64,256]{1,0:T(8,128)S(1)} %get-tuple-element.55), channel_id=1, source_target_pairs={{0,2},{2,0},{4,6},{6,4},{8,10},{10,8},{12,14},{14,12},{1,3},{3,1},... | collective-permute-start | bytes 196616 | tf_op jit(solution)/shard_map/ppermute | solution.py:503
  24.8 1.6 %collective-permute-start.10 = (f32[64,256]{1,0:T(8,128)S(1)}, f32[64,256]{1,0:T(8,128)S(1)}, u32[]{:S(2)}, u32[]{:S(2)}) collective-permute-start(f32[64,256]{1,0:T(8,128)S(1)} %get-tuple-element.56), channel_id=1, source_target_pairs={{0,4},{2,6},{4,0},{6,2},{8,12},{10,14},{12,8},{14,10},{1,5},{3,7},... | collective-permute-start | bytes 196616 | tf_op jit(solution)/shard_map/ppermute | solution.py:503
  26.4 0.6 half_sum.2
  27.0 3.0 %collective-permute-start.4 = (f32[64,256]{1,0:T(8,128)S(1)}, f32[64,256]{1,0:T(8,128)S(1)}, u32[]{:S(2)}, u32[]{:S(2)}) collective-permute-start(f32[64,256]{1,0:T(8,128)S(1)} %get-tuple-element.45.near), channel_id=1, source_target_pairs={{0,8},{2,10},{4,12},{6,14},{8,0},{10,2},{12,4},{14,6},{1,9},{3,11}... | collective-permute-start | bytes 196616 | tf_op jit(solution)/shard_map/ppermute | solution.py:503
  30.0 1.8 %collective-permute-done.11.refs_3_ = f32[64,256]{1,0:T(8,128)S(1)} collective-permute-done((f32[64,256]{1,0:T(8,128)S(1)}, f32[64,256]{1,0:T(8,128)S(1)}, u32[]{:S(2)}, u32[]{:S(2)}) %collective-permute-start.11) | collective-permute-done | bytes 65568 | tf_op jit(solution)/shard_map/ppermute | solution.py:503
  31.8 0.6 half_sum.3
  32.4 2.4 %collective-permute-start.12 = (f32[64,256]{1,0:T(8,128)S(1)}, f32[64,256]{1,0:T(8,128)S(1)}, u32[]{:S(2)}, u32[]{:S(2)}) collective-permute-start(f32[64,256]{1,0:T(8,128)S(1)} %get-tuple-element.59.near), channel_id=1, source_target_pairs={{0,8},{2,10},{4,12},{6,14},{8,0},{10,2},{12,4},{14,6},{1,9},{3,11}... | collective-permute-start | bytes 196616 | tf_op jit(solution)/shard_map/ppermute | solution.py:503
  34.8 0.6 close.2
  35.4 0.5 collective-permute-start.5
  36.0 1.7 %collective-permute-start.6 = (f32[64,256]{1,0:T(8,128)S(1)}, f32[64,256]{1,0:T(8,128)S(1)}, u32[]{:S(2)}, u32[]{:S(2)}) collective-permute-start(f32[64,256]{1,0:T(8,128)S(1)} %get-tuple-element.48), channel_id=1, source_target_pairs={{0,4},{2,6},{4,0},{6,2},{8,12},{10,14},{12,8},{14,10},{1,5},{3,7},... | collective-permute-start | bytes 196616 | tf_op jit(solution)/shard_map/ppermute | solution.py:503
  37.6 1.4 %collective-permute-start.7 = (f32[64,256]{1,0:T(8,128)S(1)}, f32[64,256]{1,0:T(8,128)S(1)}, u32[]{:S(2)}, u32[]{:S(2)}) collective-permute-start(f32[64,256]{1,0:T(8,128)S(1)} %get-tuple-element.49), channel_id=1, source_target_pairs={{0,6},{2,4},{4,2},{6,0},{8,14},{10,12},{12,10},{14,8},{1,7},{3,5},... | collective-permute-start | bytes 196616 | tf_op jit(solution)/shard_map/ppermute | solution.py:503
  39.0 0.6 close.3
  39.6 0.5 collective-permute-start.13
  40.1 1.7 %collective-permute-start.14 = (f32[64,256]{1,0:T(8,128)S(1)}, f32[64,256]{1,0:T(8,128)S(1)}, u32[]{:S(2)}, u32[]{:S(2)}) collective-permute-start(f32[64,256]{1,0:T(8,128)S(1)} %get-tuple-element.62), channel_id=1, source_target_pairs={{0,4},{2,6},{4,0},{6,2},{8,12},{10,14},{12,8},{14,10},{1,5},{3,7},... | collective-permute-start | bytes 196616 | tf_op jit(solution)/shard_map/ppermute | solution.py:503
  41.8 1.4 %collective-permute-start.15 = (f32[64,256]{1,0:T(8,128)S(1)}, f32[64,256]{1,0:T(8,128)S(1)}, u32[]{:S(2)}, u32[]{:S(2)}) collective-permute-start(f32[64,256]{1,0:T(8,128)S(1)} %get-tuple-element.63), channel_id=1, source_target_pairs={{0,6},{2,4},{4,2},{6,0},{8,14},{10,12},{12,10},{14,8},{1,7},{3,5},... | collective-permute-start | bytes 196616 | tf_op jit(solution)/shard_map/ppermute | solution.py:503
  43.1 3.1 %inverse_first.2 = (f32[4224,128]{1,0:T(8,128)S(1)}, f32[4224,128]{1,0:T(8,128)S(1)}) custom-call(s32[2]{0:T(128)S(1)} %pad_add_fusion.place, f32[16,2,128,256]{3,2,1,0:T(8,128)S(1)} %get-tuple-element.39.modes, bf16[2,2,768,256]{3,2,1,0:T(8,128)(2,1)S(1)} %copy-done.2, f32[2,2,256,256]{3,2,1,0:T(8,128)S(1)} %copy-done.4, ...), custom_call_target="tpu_custom_call" | custom-call | flops 2147483648 | bytes 8388608 | tf_op jit(solution)/shard_map/inverse_first/pallas_call | solution.py:403
  46.3 0.6 %collective-permute-done.15.refs_3_ = f32[64,256]{1,0:T(8,128)S(1)} collective-permute-done((f32[64,256]{1,0:T(8,128)S(1)}, f32[64,256]{1,0:T(8,128)S(1)}, u32[]{:S(2)}, u32[]{:S(2)}) %collective-permute-start.15) | collective-permute-done | bytes 65568 | tf_op jit(solution)/shard_map/ppermute | solution.py:503
  46.9 3.3 %inverse_first.3 = (f32[4224,128]{1,0:T(8,128)S(1)}, f32[4224,128]{1,0:T(8,128)S(1)}) custom-call(s32[2]{0:T(128)S(1)} %pad_add_fusion.place, f32[16,2,128,256]{3,2,1,0:T(8,128)S(1)} %get-tuple-element.53.modes, bf16[2,2,768,256]{3,2,1,0:T(8,128)(2,1)S(1)} %copy-done.2, f32[2,2,256,256]{3,2,1,0:T(8,128)S(1)} %copy-done.4, ...), custom_call_target="tpu_custom_call" | custom-call | flops 2147483648 | bytes 8388608 | tf_op jit(solution)/shard_map/inverse_first/pallas_call | solution.py:403
  50.2 0.1 collective-permute-start.17
  50.3 3.6 %keep_inverse.1.kept = f32[4096,256]{1,0:T(8,128)S(1)} custom-call(s32[2]{0:T(128)S(1)} %pad_add_fusion.place, bf16[2,768,256]{2,1,0:T(8,128)(2,1)S(1)} %copy-done.1, f32[4224,128]{1,0:T(8,128)S(1)} %get-tuple-element.50.refs_0_, f32[4224,128]{1,0:T(8,128)S(1)} %get-tuple-element.64.refs_1_), custom_call_target="tpu_custom_call" | custom-call | flops 2147483648 | bytes 8388608 | tf_op jit(solution)/shard_map/keep_inverse/pallas_call | solution.py:435
  54.0 0.6 collective-permute-done.17.refs_1_
  54.5 6.3 %inverse_second.1 = f32[256,16,512]{2,1,0:T(8,128)} custom-call(s32[2]{0:T(128)S(1)} %pad_add_fusion.place, bf16[2,768,256]{2,1,0:T(8,128)(2,1)S(1)} %copy-done.1, f32[4096,256]{1,0:T(8,128)S(1)} %keep_inverse.1.kept, f32[4224,128]{1,0:T(8,128)S(1)} %collective-permute-done.16.refs_0_, f32[4224,128]{1,0:T(8,128)S(1)} %collective-permute-done.17.refs_1_), custom_call_target="tpu_custom_call" | custom-call | flops 4294967296 | bytes 8388608 | tf_op jit(solution)/shard_map/inverse_second/pallas_call | solution.py:484
  (29 shorter events, 0.1 us)
Async XLA Ops:
  0.1 8.2 %copy-start.5 = (bf16[2,768,256]{2,1,0:T(8,128)(2,1)S(1)}, bf16[2,768,256]{2,1,0:T(8,128)(2,1)}, u32[]{:S(2)}) copy-start(bf16[2,768,256]{2,1,0:T(8,128)(2,1)} %constant.23.clone.table.tables) | copy-start | bytes 2359300
  7.2 5.0 %collective-permute-start = (f32[4488,128]{1,0:T(8,128)S(1)}, f32[4488,128]{1,0:T(8,128)S(1)}, u32[]{:S(2)}, u32[]{:S(2)}) collective-permute-start(f32[4488,128]{1,0:T(8,128)S(1)} %get-tuple-element.38), channel_id=1, source_target_pairs={{0,1},{1,0},{2,3},{3,2},{4,5},{5,4},{6,7},{7,6},{8,9},{9,8},{10,11... | collective-permute-start | bytes 6893576 | tf_op jit(solution)/shard_map/ppermute | solution.py:498
  8.2 11.4 %collective-permute-start.8 = (f32[4488,128]{1,0:T(8,128)S(1)}, f32[4488,128]{1,0:T(8,128)S(1)}, u32[]{:S(2)}, u32[]{:S(2)}) collective-permute-start(f32[4488,128]{1,0:T(8,128)S(1)} %get-tuple-element.52), channel_id=1, source_target_pairs={{0,1},{1,0},{2,3},{3,2},{4,5},{5,4},{6,7},{7,6},{8,9},{9,8},{10,11... | collective-permute-start | bytes 6893576 | tf_op jit(solution)/shard_map/ppermute | solution.py:498
  8.2 4.0 %copy-start.3 = (bf16[2,2,768,256]{3,2,1,0:T(8,128)(2,1)S(1)}, bf16[2,2,768,256]{3,2,1,0:T(8,128)(2,1)}, u32[]{:S(2)}) copy-start(bf16[2,2,768,256]{3,2,1,0:T(8,128)(2,1)} %constant.21.clone.table) | copy-start | bytes 4718596
  8.2 4.0 %copy-start.4 = (f32[2,2,256,256]{3,2,1,0:T(8,128)S(1)}, f32[2,2,256,256]{3,2,1,0:T(8,128)}, u32[]{:S(2)}) copy-start(f32[2,2,256,256]{3,2,1,0:T(8,128)} %constant.22.clone.decay) | copy-start | bytes 3145732
  15.4 10.9 %collective-permute-start.1 = (f32[64,256]{1,0:T(8,128)S(1)}, f32[64,256]{1,0:T(8,128)S(1)}, u32[]{:S(2)}, u32[]{:S(2)}) collective-permute-start(f32[64,256]{1,0:T(8,128)S(1)} %get-tuple-element.41), channel_id=1, source_target_pairs={{0,2},{2,0},{4,6},{6,4},{8,10},{10,8},{12,14},{14,12},{1,3},{3,1},... | collective-permute-start | bytes 196616 | tf_op jit(solution)/shard_map/ppermute | solution.py:503
  18.0 8.4 %collective-permute-start.2 = (f32[64,256]{1,0:T(8,128)S(1)}, f32[64,256]{1,0:T(8,128)S(1)}, u32[]{:S(2)}, u32[]{:S(2)}) collective-permute-start(f32[64,256]{1,0:T(8,128)S(1)} %get-tuple-element.42), channel_id=1, source_target_pairs={{0,4},{2,6},{4,0},{6,2},{8,12},{10,14},{12,8},{14,10},{1,5},{3,7},... | collective-permute-start | bytes 196616 | tf_op jit(solution)/shard_map/ppermute | solution.py:503
  19.6 6.8 %collective-permute-start.3 = (f32[64,256]{1,0:T(8,128)S(1)}, f32[64,256]{1,0:T(8,128)S(1)}, u32[]{:S(2)}, u32[]{:S(2)}) collective-permute-start(f32[64,256]{1,0:T(8,128)S(1)} %get-tuple-element.43), channel_id=1, source_target_pairs={{0,6},{2,4},{4,2},{6,0},{8,14},{10,12},{12,10},{14,8},{1,7},{3,5},... | collective-permute-start | bytes 196616 | tf_op jit(solution)/shard_map/ppermute | solution.py:503
  19.6 6.8 %copy-start = (f32[2,2,3,256,256]{4,3,2,1,0:T(8,128)S(1)}, f32[2,2,3,256,256]{4,3,2,1,0:T(8,128)}, u32[]{:S(2)}) copy-start(f32[2,2,3,256,256]{4,3,2,1,0:T(8,128)} %constant.20.clone.closing) | copy-start | bytes 9437188
  22.8 7.2 %collective-permute-start.9 = (f32[64,256]{1,0:T(8,128)S(1)}, f32[64,256]{1,0:T(8,128)S(1)}, u32[]{:S(2)}, u32[]{:S(2)}) collective-permute-start(f32[64,256]{1,0:T(8,128)S(1)} %get-tuple-element.55), channel_id=1, source_target_pairs={{0,2},{2,0},{4,6},{6,4},{8,10},{10,8},{12,14},{14,12},{1,3},{3,1},... | collective-permute-start | bytes 196616 | tf_op jit(solution)/shard_map/ppermute | solution.py:503
  24.8 5.2 %collective-permute-start.10 = (f32[64,256]{1,0:T(8,128)S(1)}, f32[64,256]{1,0:T(8,128)S(1)}, u32[]{:S(2)}, u32[]{:S(2)}) collective-permute-start(f32[64,256]{1,0:T(8,128)S(1)} %get-tuple-element.56), channel_id=1, source_target_pairs={{0,4},{2,6},{4,0},{6,2},{8,12},{10,14},{12,8},{14,10},{1,5},{3,7},... | collective-permute-start | bytes 196616 | tf_op jit(solution)/shard_map/ppermute | solution.py:503
  26.4 5.4 %collective-permute-start.11 = (f32[64,256]{1,0:T(8,128)S(1)}, f32[64,256]{1,0:T(8,128)S(1)}, u32[]{:S(2)}, u32[]{:S(2)}) collective-permute-start(f32[64,256]{1,0:T(8,128)S(1)} %get-tuple-element.57), channel_id=1, source_target_pairs={{0,6},{2,4},{4,2},{6,0},{8,14},{10,12},{12,10},{14,8},{1,7},{3,5},... | collective-permute-start | bytes 196616 | tf_op jit(solution)/shard_map/ppermute | solution.py:503
  27.0 7.8 %collective-permute-start.4 = (f32[64,256]{1,0:T(8,128)S(1)}, f32[64,256]{1,0:T(8,128)S(1)}, u32[]{:S(2)}, u32[]{:S(2)}) collective-permute-start(f32[64,256]{1,0:T(8,128)S(1)} %get-tuple-element.45.near), channel_id=1, source_target_pairs={{0,8},{2,10},{4,12},{6,14},{8,0},{10,2},{12,4},{14,6},{1,9},{3,11}... | collective-permute-start | bytes 196616 | tf_op jit(solution)/shard_map/ppermute | solution.py:503
  32.4 6.6 %collective-permute-start.12 = (f32[64,256]{1,0:T(8,128)S(1)}, f32[64,256]{1,0:T(8,128)S(1)}, u32[]{:S(2)}, u32[]{:S(2)}) collective-permute-start(f32[64,256]{1,0:T(8,128)S(1)} %get-tuple-element.59.near), channel_id=1, source_target_pairs={{0,8},{2,10},{4,12},{6,14},{8,0},{10,2},{12,4},{14,6},{1,9},{3,11}... | collective-permute-start | bytes 196616 | tf_op jit(solution)/shard_map/ppermute | solution.py:503
  35.4 7.7 %copy-start.2 = (bf16[2,2,768,256]{3,2,1,0:T(8,128)(2,1)S(1)}, bf16[2,2,768,256]{3,2,1,0:T(8,128)(2,1)}, u32[]{:S(2)}) copy-start(bf16[2,2,768,256]{3,2,1,0:T(8,128)(2,1)} %constant.24.clone.table) | copy-start | bytes 4718596
  35.4 6.4 %collective-permute-start.5 = (f32[64,256]{1,0:T(8,128)S(1)}, f32[64,256]{1,0:T(8,128)S(1)}, u32[]{:S(2)}, u32[]{:S(2)}) collective-permute-start(f32[64,256]{1,0:T(8,128)S(1)} %get-tuple-element.47), channel_id=1, source_target_pairs={{0,2},{2,0},{4,6},{6,4},{8,10},{10,8},{12,14},{14,12},{1,3},{3,1},... | collective-permute-start | bytes 196616 | tf_op jit(solution)/shard_map/ppermute | solution.py:503
  36.0 7.2 %collective-permute-start.6 = (f32[64,256]{1,0:T(8,128)S(1)}, f32[64,256]{1,0:T(8,128)S(1)}, u32[]{:S(2)}, u32[]{:S(2)}) collective-permute-start(f32[64,256]{1,0:T(8,128)S(1)} %get-tuple-element.48), channel_id=1, source_target_pairs={{0,4},{2,6},{4,0},{6,2},{8,12},{10,14},{12,8},{14,10},{1,5},{3,7},... | collective-permute-start | bytes 196616 | tf_op jit(solution)/shard_map/ppermute | solution.py:503
  37.6 5.5 %collective-permute-start.7 = (f32[64,256]{1,0:T(8,128)S(1)}, f32[64,256]{1,0:T(8,128)S(1)}, u32[]{:S(2)}, u32[]{:S(2)}) collective-permute-start(f32[64,256]{1,0:T(8,128)S(1)} %get-tuple-element.49), channel_id=1, source_target_pairs={{0,6},{2,4},{4,2},{6,0},{8,14},{10,12},{12,10},{14,8},{1,7},{3,5},... | collective-permute-start | bytes 196616 | tf_op jit(solution)/shard_map/ppermute | solution.py:503
  39.6 6.7 %collective-permute-start.13 = (f32[64,256]{1,0:T(8,128)S(1)}, f32[64,256]{1,0:T(8,128)S(1)}, u32[]{:S(2)}, u32[]{:S(2)}) collective-permute-start(f32[64,256]{1,0:T(8,128)S(1)} %get-tuple-element.61), channel_id=1, source_target_pairs={{0,2},{2,0},{4,6},{6,4},{8,10},{10,8},{12,14},{14,12},{1,3},{3,1},... | collective-permute-start | bytes 196616 | tf_op jit(solution)/shard_map/ppermute | solution.py:503
  40.1 6.2 %collective-permute-start.14 = (f32[64,256]{1,0:T(8,128)S(1)}, f32[64,256]{1,0:T(8,128)S(1)}, u32[]{:S(2)}, u32[]{:S(2)}) collective-permute-start(f32[64,256]{1,0:T(8,128)S(1)} %get-tuple-element.62), channel_id=1, source_target_pairs={{0,4},{2,6},{4,0},{6,2},{8,12},{10,14},{12,8},{14,10},{1,5},{3,7},... | collective-permute-start | bytes 196616 | tf_op jit(solution)/shard_map/ppermute | solution.py:503
  41.8 5.2 %collective-permute-start.15 = (f32[64,256]{1,0:T(8,128)S(1)}, f32[64,256]{1,0:T(8,128)S(1)}, u32[]{:S(2)}, u32[]{:S(2)}) collective-permute-start(f32[64,256]{1,0:T(8,128)S(1)} %get-tuple-element.63), channel_id=1, source_target_pairs={{0,6},{2,4},{4,2},{6,0},{8,14},{10,12},{12,10},{14,8},{1,7},{3,5},... | collective-permute-start | bytes 196616 | tf_op jit(solution)/shard_map/ppermute | solution.py:503
  46.2 7.7 %collective-permute-start.16 = (f32[4224,128]{1,0:T(8,128)S(1)}, f32[4224,128]{1,0:T(8,128)S(1)}, u32[]{:S(2)}, u32[]{:S(2)}) collective-permute-start(f32[4224,128]{1,0:T(8,128)S(1)} %get-tuple-element.65), channel_id=1, source_target_pairs={{0,1},{1,0},{2,3},{3,2},{4,5},{5,4},{6,7},{7,6},{8,9},{9,8},{10,11... | collective-permute-start | bytes 6488072 | tf_op jit(solution)/shard_map/ppermute | solution.py:498
  46.9 3.4 %copy-start.1 = (bf16[2,768,256]{2,1,0:T(8,128)(2,1)S(1)}, bf16[2,768,256]{2,1,0:T(8,128)(2,1)}, u32[]{:S(2)}) copy-start(bf16[2,768,256]{2,1,0:T(8,128)(2,1)} %constant.25.clone.tables) | copy-start | bytes 2359300
  50.2 4.3 %collective-permute-start.17 = (f32[4224,128]{1,0:T(8,128)S(1)}, f32[4224,128]{1,0:T(8,128)S(1)}, u32[]{:S(2)}, u32[]{:S(2)}) collective-permute-start(f32[4224,128]{1,0:T(8,128)S(1)} %get-tuple-element.66), channel_id=1, source_target_pairs={{0,1},{1,0},{2,3},{3,2},{4,5},{5,4},{6,7},{7,6},{8,9},{9,8},{10,11... | collective-permute-start | bytes 6488072 | tf_op jit(solution)/shard_map/ppermute | solution.py:498

commit v9 on v8

--- a/solution.py
+++ b/solution.py
@@ -141,15 +141,12 @@
     part = half // CHUNKS
     piece = rows // len(scratch)
     group = max(TILE // steps, 1)
-    head = min(steps, SUBLANES)
-    total = rows * pl.num_programs(0)
+    block, blocks = pl.program_id(0), pl.num_programs(0)
+    total = rows * blocks
     pitch = sends[0].shape[0] // (steps + 1)
-    start = pl.program_id(0) * rows
-    mirror = total - rows - start
-    is_first = (place[0] == 0).astype(jnp.float32)
+    body = piece * steps
+    is_first = place[0] == 0
     sign = 1.0 - 2.0 * place[1].astype(jnp.float32)
-    firsts = lax.broadcasted_iota(jnp.int32, (group, head, width), 1) == 0
-    firsts = jnp.where(firsts, is_first, 0.0)
 
     def put(other, at, sums_at, cells):
         lower = cells[:, :half]
@@ -160,28 +157,38 @@
         sums[pl.ds(sums_at, TILE), :] = lower + upper
         store_split(other, (pl.ds(at, TILE),), 0, lower - upper)
 
-    for sub, other in enumerate(scratch):
-        kept_at = pl.multiple_of(start + sub * piece, piece)
-        sent_at = pl.multiple_of(mirror + (len(scratch) - 1 - sub) * piece, piece)
-        body = piece * steps
+    def prepare(sub):
+        kept_at = pl.multiple_of(block * rows + sub * piece, piece)
         kept_base = pl.multiple_of(kept_at * steps, body)
         for row in range(0, piece, group):
-            at = pl.ds(sub * piece + row, group)
-            cells = field[at]
-            force = REACTION_STEP * (cells - cells * cells * cells)
-            starts = force[:, :head] + firsts * initial[at][:, None, :]
-            force = jnp.concatenate([starts, force[:, head:]], axis=1) if head < steps else starts
-            put(other, row * steps, kept_base + row * steps, force.reshape(TILE, width))
+            cells = field[pl.ds(sub * piece + row, group)]
+            force = cells - cells * cells * cells
+            put(scratch[sub], row * steps, kept_base + row * steps, force.reshape(TILE, width))
         for row in range(0, piece, TILE):
-            ends = field[pl.ds(sub * piece + row, TILE), steps - 1, :]
-            put(other, body + row, total * steps + kept_at + row, ends)
-        sent = dot(other[...], table[0])
+            at = pl.ds(sub * piece + row, TILE)
+            ends = jnp.where(is_first, initial[at], field[at, steps - 1, :])
+            put(scratch[sub], body + row, total * steps + kept_at + row, ends)
+
+    def transform(sub, block):
+        sent = dot(scratch[sub][...], table[0])
+        sent_at = pl.multiple_of(total - block * rows - (sub + 1) * piece, piece)
         for chunk, send in enumerate(sends):
             lanes = slice(chunk * part, (chunk + 1) * part)
             for row in range(piece):
                 line = sent[row * steps : (row + 1) * steps, lanes]
                 send[pl.ds(sent_at + piece - 1 - row, steps, stride=pitch), :] = line
             store_rows_reversed(send, pitch * steps + sent_at, sent[body:, lanes])
+
+    last = len(scratch) - 1
+    transform(last, jnp.maximum(block - 1, 0))
+    for sub in range(last):
+        prepare(sub)
+        transform(sub, block)
+    prepare(last)
+
+    @pl.when(block == blocks - 1)
+    def _():
+        transform(last, block)
 
 
 def forward_second(place, field, initial, tables):
@@ -249,11 +256,17 @@
 
 def forward_first_kernel(slabs, chunk, place, keep, got, table, decay, modes, *refs):
     size = ranks(slabs)
-    lasts, (state, split, split_end) = refs[:size], refs[size:]
+    lasts, (state, split, split_end, extra) = refs[:size], refs[size:]
     steps, _, part, rows = modes.shape
     pitch = keep.shape[0] // (steps + 1)
     block = split.shape[1] // part
     strip = place[1]
+    near, far = keep[pl.ds(pitch * steps, rows)], got[pl.ds(pitch * steps, rows)]
+    for c, cells in enumerate((near + far, near - far)):
+        store_split(split_end, (c, slice(None)), 0, cells.T)
+        extra[c] = dot(split_end[c], table[strip, c])
+    is_first = jnp.where(place[0] == 0, 1.0 / REACTION_STEP, 0.0)
+    is_last = jnp.where(place[0] == slabs - 1, 1.0 / REACTION_STEP, 0.0)
     state[...] = jnp.zeros_like(state)
     for step in range(0, steps, block):
         for c in (0, 1):
@@ -264,6 +277,8 @@
                 store_split(split, (c, pl.ds(at * part, part)), 0, cells.T)
             result = dot(split[c], table[strip, c])
             modes[pl.ds(step, block), c] = result.reshape(block, part, rows)
+            if step == 0:
+                modes[0, c] = result[:part] + is_first * extra[c]
         for c in (0, 1):
             for row in range(0, part, TILE):
                 tile, at_state = pl.ds(row, TILE), pl.ds(c * part + row, TILE)
@@ -272,12 +287,9 @@
                 for at in range(block):
                     value = rate * (value + modes[step + at, c, tile])
                 state[at_state] = value
-    is_last = (place[0] == slabs - 1).astype(jnp.float32)
-    near, far = keep[pl.ds(pitch * steps, rows)], got[pl.ds(pitch * steps, rows)]
-    for c, cells in enumerate((near + far, near - far)):
-        store_split(split_end, (c, slice(None)), 0, cells.T)
+    for c in (0, 1):
         at_state = pl.ds(c * part, part)
-        state[at_state] = state[at_state] - is_last * dot(split_end[c], table[strip, c])
+        state[at_state] = state[at_state] - is_last * extra[c]
     rank = lax.rem(place[0], size)
     share = 2 * part // size
     for partner in range(size):
@@ -301,6 +313,7 @@
             pltpu.VMEM((2 * part, rows), jnp.float32),
             pltpu.VMEM((2, block * part, 3 * rows), jnp.bfloat16),
             pltpu.VMEM((2, part, 3 * rows), jnp.bfloat16),
+            pltpu.VMEM((2, part, rows), jnp.float32),
         ],
         1 << 31,
     )(place, keep, got, tables, decays)
@@ -465,7 +478,9 @@
                 cells = steps_of(got, mirrors, steps, pitch)
                 store_split(split, (pl.ds(row * steps, TILE),), chunk * part, cells)
         result[...] = dot(split[...], tables[1 - strip])
-        kept_base = pl.multiple_of(base * steps, piece * steps)
+    for sub in range(count):
+        result = scratch[2 * sub + 1]
+        kept_base = pl.multiple_of((start + sub * piece) * steps, piece * steps)
         for row in range(0, piece, group):
             first = kept[pl.ds(kept_base + row * steps, TILE)]
             second = result[pl.ds(row * steps, TILE)]
@@ -528,7 +543,7 @@
         np.stack([by_chunk(table) for table in (slab_decay, half_decay, gain)], axis=2)
     )
     first_table, decays = split_constant(first), constant(decay)
-    second_table = split_constant(second)
+    second_table = split_constant(REACTION_STEP * second)
     sums, sends = forward_second(place, iterate, initial, second_table)
     gots = [swapped(send) for send in sends]
     keeps = keep_second(place, sums, second_table, steps)

time: 61 us -> 60.5 us (level)
  no operation moved by 1% of the time
where the time goes in v9:
time: 60.5 us; the launch traced here: 60.4 us
  Pallas kernels  34.5 us (57%)
  starting transfers between devices  21.3 us (35%)
  waiting for transfers between devices  4.32 us (7%)
    ppermute x14, starting transfers between devices, with_partner(): lax.ppermute(block, 'tm', [(slab, slab ^ distance) for slab in range(slab...  20.2 us
    pallas_call x1, Pallas kernels, forward_second(): call(forward_second_kernel, 'forward_second', [pl.BlockSpec((block, steps...  6.95 us
    pallas_call x2, Pallas kernels, inverse_first(): call(functools.partial(inverse_first_kernel, slabs, chunk), 'inverse_firs...  6.34 us
    pallas_call x1, Pallas kernels, inverse_second(): call(inverse_second_kernel, 'inverse_second', [IN_VMEM] * (2 + CHUNKS), p...  6.27 us
    pallas_call x2, Pallas kernels, forward_first(): call(functools.partial(forward_first_kernel, slabs, chunk), 'forward_firs...  6.23 us
    pallas_call x1, Pallas kernels, keep_inverse(): call(functools.partial(keep_inverse_kernel, steps), 'keep_inverse', [IN_V...  3.64 us
    pallas_call x1, Pallas kernels, keep_second(): call(functools.partial(keep_second_kernel, steps), 'keep_second', [IN_VME...  2.68 us
    ppermute x14, waiting for transfers between devices, with_partner(): lax.ppermute(block, 'tm', [(slab, slab ^ distance) for slab in range(slab...  2.44 us
  transfers between devices with their start and end apart: 18, of which 4 were waited for; matrix products, arithmetic and copies ran while one was open for 0% of the time, Pallas kernels for 35%

profile of v9, /device:TPU:0, one launch (start us, length us, event | category | flops | bytes accessed | tf_op | source)
XLA Modules:
  0.0 60.4 jit_solution(13267931271306162823)
XLA Ops:
  0.0 0.1 pad_add_fusion.place
  0.1 6.9 %forward_second.1 = (f32[4352,256]{1,0:T(8,128)S(1)}, f32[4488,128]{1,0:T(8,128)S(1)}, f32[4488,128]{1,0:T(8,128)S(1)}) custom-call(s32[2]{0:T(128)S(1)} %pad_add_fusion.place, f32[256,16,512]{2,1,0:T(8,128)} %field.1, f32[256,512]{1,0:T(8,128)} %initial.1, bf16[2,768,256]{2,1,0:T(8,128)(2,1)} %constant.23.clone.table.tables), custom_call_target="tpu_custom_call" | custom-call | flops 4294967296 | bytes 8388608 | tf_op jit(solution)/shard_map/forward_second/pallas_call | solution.py:199
  7.0 0.9 %collective-permute-start = (f32[4488,128]{1,0:T(8,128)S(1)}, f32[4488,128]{1,0:T(8,128)S(1)}, u32[]{:S(2)}, u32[]{:S(2)}) collective-permute-start(f32[4488,128]{1,0:T(8,128)S(1)} %get-tuple-element.38), channel_id=1, source_target_pairs={{0,1},{1,0},{2,3},{3,2},{4,5},{5,4},{6,7},{7,6},{8,9},{9,8},{10,11... | collective-permute-start | bytes 6893576 | tf_op jit(solution)/shard_map/ppermute | solution.py:513
  7.9 0.1 collective-permute-start.8
  8.0 2.7 %keep_second.1 = (f32[4488,128]{1,0:T(8,128)S(1)}, f32[4488,128]{1,0:T(8,128)S(1)}) custom-call(s32[2]{0:T(128)S(1)} %pad_add_fusion.place, bf16[2,768,256]{2,1,0:T(8,128)(2,1)S(1)} %copy-done.5, f32[4352,256]{1,0:T(8,128)S(1)} %get-tuple-element.36.sums), custom_call_target="tpu_custom_call" | custom-call | flops 2147483648 | bytes 8388608 | tf_op jit(solution)/shard_map/keep_second/pallas_call | solution.py:242
  10.7 1.3 %collective-permute-done.got = f32[4488,128]{1,0:T(8,128)S(1)} collective-permute-done((f32[4488,128]{1,0:T(8,128)S(1)}, f32[4488,128]{1,0:T(8,128)S(1)}, u32[]{:S(2)}, u32[]{:S(2)}) %collective-permute-start) | collective-permute-done | bytes 2297888 | tf_op jit(solution)/shard_map/ppermute | solution.py:513
  12.0 3.1 %forward_first.2 = (f32[16,2,128,256]{3,2,1,0:T(8,128)S(1)}, f32[64,256]{1,0:T(8,128)S(1)}, f32[64,256]{1,0:T(8,128)S(1)}, f32[64,256]{1,0:T(8,128)S(1)}, f32[64,256]{1,0:T(8,128)S(1)}) custom-call(s32[2]{0:T(128)S(1)} %pad_add_fusion.place, f32[4488,128]{1,0:T(8,128)S(1)} %get-tuple-element.37.keep, f32[4488,128]{1,0:T(8,128)S(1)} %collective-permute-done.got, ...), custom_call_target="tpu_custom_call" | custom-call | flops 2147483648 | bytes 8388608 | tf_op jit(solution)/shard_map/forward_first/pallas_call | solution.py:306
  15.1 2.6 %collective-permute-start.1 = (f32[64,256]{1,0:T(8,128)S(1)}, f32[64,256]{1,0:T(8,128)S(1)}, u32[]{:S(2)}, u32[]{:S(2)}) collective-permute-start(f32[64,256]{1,0:T(8,128)S(1)} %get-tuple-element.41), channel_id=1, source_target_pairs={{0,2},{2,0},{4,6},{6,4},{8,10},{10,8},{12,14},{14,12},{1,3},{3,1},... | collective-permute-start | bytes 196616 | tf_op jit(solution)/shard_map/ppermute | solution.py:518
  17.7 1.6 %collective-permute-start.2 = (f32[64,256]{1,0:T(8,128)S(1)}, f32[64,256]{1,0:T(8,128)S(1)}, u32[]{:S(2)}, u32[]{:S(2)}) collective-permute-start(f32[64,256]{1,0:T(8,128)S(1)} %get-tuple-element.42), channel_id=1, source_target_pairs={{0,4},{2,6},{4,0},{6,2},{8,12},{10,14},{12,8},{14,10},{1,5},{3,7},... | collective-permute-start | bytes 196616 | tf_op jit(solution)/shard_map/ppermute | solution.py:518
  19.3 3.1 %forward_first.3 = (f32[16,2,128,256]{3,2,1,0:T(8,128)S(1)}, f32[64,256]{1,0:T(8,128)S(1)}, f32[64,256]{1,0:T(8,128)S(1)}, f32[64,256]{1,0:T(8,128)S(1)}, f32[64,256]{1,0:T(8,128)S(1)}) custom-call(s32[2]{0:T(128)S(1)} %pad_add_fusion.place, f32[4488,128]{1,0:T(8,128)S(1)} %get-tuple-element.51.keep, f32[4488,128]{1,0:T(8,128)S(1)} %collective-permute-done.8.got, ...), custom_call_target="tpu_custom_call" | custom-call | flops 2147483648 | bytes 8388608 | tf_op jit(solution)/shard_map/forward_first/pallas_call | solution.py:306
  22.4 2.0 %collective-permute-start.9 = (f32[64,256]{1,0:T(8,128)S(1)}, f32[64,256]{1,0:T(8,128)S(1)}, u32[]{:S(2)}, u32[]{:S(2)}) collective-permute-start(f32[64,256]{1,0:T(8,128)S(1)} %get-tuple-element.55), channel_id=1, source_target_pairs={{0,2},{2,0},{4,6},{6,4},{8,10},{10,8},{12,14},{14,12},{1,3},{3,1},... | collective-permute-start | bytes 196616 | tf_op jit(solution)/shard_map/ppermute | solution.py:518
  24.4 1.6 %collective-permute-start.10 = (f32[64,256]{1,0:T(8,128)S(1)}, f32[64,256]{1,0:T(8,128)S(1)}, u32[]{:S(2)}, u32[]{:S(2)}) collective-permute-start(f32[64,256]{1,0:T(8,128)S(1)} %get-tuple-element.56), channel_id=1, source_target_pairs={{0,4},{2,6},{4,0},{6,2},{8,12},{10,14},{12,8},{14,10},{1,5},{3,7},... | collective-permute-start | bytes 196616 | tf_op jit(solution)/shard_map/ppermute | solution.py:518
  26.0 0.6 half_sum.2
  26.6 3.0 %collective-permute-start.4 = (f32[64,256]{1,0:T(8,128)S(1)}, f32[64,256]{1,0:T(8,128)S(1)}, u32[]{:S(2)}, u32[]{:S(2)}) collective-permute-start(f32[64,256]{1,0:T(8,128)S(1)} %get-tuple-element.45.near), channel_id=1, source_target_pairs={{0,8},{2,10},{4,12},{6,14},{8,0},{10,2},{12,4},{14,6},{1,9},{3,11}... | collective-permute-start | bytes 196616 | tf_op jit(solution)/shard_map/ppermute | solution.py:518
  29.6 1.8 %collective-permute-done.11.refs_3_ = f32[64,256]{1,0:T(8,128)S(1)} collective-permute-done((f32[64,256]{1,0:T(8,128)S(1)}, f32[64,256]{1,0:T(8,128)S(1)}, u32[]{:S(2)}, u32[]{:S(2)}) %collective-permute-start.11) | collective-permute-done | bytes 65568 | tf_op jit(solution)/shard_map/ppermute | solution.py:518
  31.4 0.6 half_sum.3
  32.0 2.4 %collective-permute-start.12 = (f32[64,256]{1,0:T(8,128)S(1)}, f32[64,256]{1,0:T(8,128)S(1)}, u32[]{:S(2)}, u32[]{:S(2)}) collective-permute-start(f32[64,256]{1,0:T(8,128)S(1)} %get-tuple-element.59.near), channel_id=1, source_target_pairs={{0,8},{2,10},{4,12},{6,14},{8,0},{10,2},{12,4},{14,6},{1,9},{3,11}... | collective-permute-start | bytes 196616 | tf_op jit(solution)/shard_map/ppermute | solution.py:518
  34.4 0.6 close.2
  35.0 0.6 collective-permute-start.5
  35.6 1.6 %collective-permute-start.6 = (f32[64,256]{1,0:T(8,128)S(1)}, f32[64,256]{1,0:T(8,128)S(1)}, u32[]{:S(2)}, u32[]{:S(2)}) collective-permute-start(f32[64,256]{1,0:T(8,128)S(1)} %get-tuple-element.48), channel_id=1, source_target_pairs={{0,4},{2,6},{4,0},{6,2},{8,12},{10,14},{12,8},{14,10},{1,5},{3,7},... | collective-permute-start | bytes 196616 | tf_op jit(solution)/shard_map/ppermute | solution.py:518
  37.2 1.4 %collective-permute-start.7 = (f32[64,256]{1,0:T(8,128)S(1)}, f32[64,256]{1,0:T(8,128)S(1)}, u32[]{:S(2)}, u32[]{:S(2)}) collective-permute-start(f32[64,256]{1,0:T(8,128)S(1)} %get-tuple-element.49), channel_id=1, source_target_pairs={{0,6},{2,4},{4,2},{6,0},{8,14},{10,12},{12,10},{14,8},{1,7},{3,5},... | collective-permute-start | bytes 196616 | tf_op jit(solution)/shard_map/ppermute | solution.py:518
  38.6 0.6 close.3
  39.2 0.6 collective-permute-start.13
  39.7 1.6 %collective-permute-start.14 = (f32[64,256]{1,0:T(8,128)S(1)}, f32[64,256]{1,0:T(8,128)S(1)}, u32[]{:S(2)}, u32[]{:S(2)}) collective-permute-start(f32[64,256]{1,0:T(8,128)S(1)} %get-tuple-element.62), channel_id=1, source_target_pairs={{0,4},{2,6},{4,0},{6,2},{8,12},{10,14},{12,8},{14,10},{1,5},{3,7},... | collective-permute-start | bytes 196616 | tf_op jit(solution)/shard_map/ppermute | solution.py:518
  41.4 1.4 %collective-permute-start.15 = (f32[64,256]{1,0:T(8,128)S(1)}, f32[64,256]{1,0:T(8,128)S(1)}, u32[]{:S(2)}, u32[]{:S(2)}) collective-permute-start(f32[64,256]{1,0:T(8,128)S(1)} %get-tuple-element.63), channel_id=1, source_target_pairs={{0,6},{2,4},{4,2},{6,0},{8,14},{10,12},{12,10},{14,8},{1,7},{3,5},... | collective-permute-start | bytes 196616 | tf_op jit(solution)/shard_map/ppermute | solution.py:518
  42.7 3.1 %inverse_first.2 = (f32[4224,128]{1,0:T(8,128)S(1)}, f32[4224,128]{1,0:T(8,128)S(1)}) custom-call(s32[2]{0:T(128)S(1)} %pad_add_fusion.place, f32[16,2,128,256]{3,2,1,0:T(8,128)S(1)} %get-tuple-element.39.modes, bf16[2,2,768,256]{3,2,1,0:T(8,128)(2,1)S(1)} %copy-done.2, f32[2,2,256,256]{3,2,1,0:T(8,128)S(1)} %copy-done.4, ...), custom_call_target="tpu_custom_call" | custom-call | flops 2147483648 | bytes 8388608 | tf_op jit(solution)/shard_map/inverse_first/pallas_call | solution.py:416
  45.8 0.1 collective-permute-start.16
  45.9 0.6 collective-permute-done.15.refs_3_
  46.5 3.3 %inverse_first.3 = (f32[4224,128]{1,0:T(8,128)S(1)}, f32[4224,128]{1,0:T(8,128)S(1)}) custom-call(s32[2]{0:T(128)S(1)} %pad_add_fusion.place, f32[16,2,128,256]{3,2,1,0:T(8,128)S(1)} %get-tuple-element.53.modes, bf16[2,2,768,256]{3,2,1,0:T(8,128)(2,1)S(1)} %copy-done.2, f32[2,2,256,256]{3,2,1,0:T(8,128)S(1)} %copy-done.4, ...), custom_call_target="tpu_custom_call" | custom-call | flops 2147483648 | bytes 8388608 | tf_op jit(solution)/shard_map/inverse_first/pallas_call | solution.py:416
  49.9 3.6 %keep_inverse.1.kept = f32[4096,256]{1,0:T(8,128)S(1)} custom-call(s32[2]{0:T(128)S(1)} %pad_add_fusion.place, bf16[2,768,256]{2,1,0:T(8,128)(2,1)S(1)} %copy-done.1, f32[4224,128]{1,0:T(8,128)S(1)} %get-tuple-element.50.refs_0_, f32[4224,128]{1,0:T(8,128)S(1)} %get-tuple-element.64.refs_1_), custom_call_target="tpu_custom_call" | custom-call | flops 2147483648 | bytes 8388608 | tf_op jit(solution)/shard_map/keep_inverse/pallas_call | solution.py:448
  53.5 0.6 collective-permute-done.17.refs_1_
  54.1 6.3 %inverse_second.1 = f32[256,16,512]{2,1,0:T(8,128)} custom-call(s32[2]{0:T(128)S(1)} %pad_add_fusion.place, bf16[2,768,256]{2,1,0:T(8,128)(2,1)S(1)} %copy-done.1, f32[4096,256]{1,0:T(8,128)S(1)} %keep_inverse.1.kept, f32[4224,128]{1,0:T(8,128)S(1)} %collective-permute-done.16.refs_0_, f32[4224,128]{1,0:T(8,128)S(1)} %collective-permute-done.17.refs_1_), custom_call_target="tpu_custom_call" | custom-call | flops 4294967296 | bytes 8388608 | tf_op jit(solution)/shard_map/inverse_second/pallas_call | solution.py:499
  (29 shorter events, 0.1 us)
Async XLA Ops:
  0.1 7.9 %copy-start.5 = (bf16[2,768,256]{2,1,0:T(8,128)(2,1)S(1)}, bf16[2,768,256]{2,1,0:T(8,128)(2,1)}, u32[]{:S(2)}) copy-start(bf16[2,768,256]{2,1,0:T(8,128)(2,1)} %constant.23.clone.table.tables) | copy-start | bytes 2359300
  7.0 5.0 %collective-permute-start = (f32[4488,128]{1,0:T(8,128)S(1)}, f32[4488,128]{1,0:T(8,128)S(1)}, u32[]{:S(2)}, u32[]{:S(2)}) collective-permute-start(f32[4488,128]{1,0:T(8,128)S(1)} %get-tuple-element.38), channel_id=1, source_target_pairs={{0,1},{1,0},{2,3},{3,2},{4,5},{5,4},{6,7},{7,6},{8,9},{9,8},{10,11... | collective-permute-start | bytes 6893576 | tf_op jit(solution)/shard_map/ppermute | solution.py:513
  7.9 11.4 %collective-permute-start.8 = (f32[4488,128]{1,0:T(8,128)S(1)}, f32[4488,128]{1,0:T(8,128)S(1)}, u32[]{:S(2)}, u32[]{:S(2)}) collective-permute-start(f32[4488,128]{1,0:T(8,128)S(1)} %get-tuple-element.52), channel_id=1, source_target_pairs={{0,1},{1,0},{2,3},{3,2},{4,5},{5,4},{6,7},{7,6},{8,9},{9,8},{10,11... | collective-permute-start | bytes 6893576 | tf_op jit(solution)/shard_map/ppermute | solution.py:513
  8.0 4.0 %copy-start.3 = (bf16[2,2,768,256]{3,2,1,0:T(8,128)(2,1)S(1)}, bf16[2,2,768,256]{3,2,1,0:T(8,128)(2,1)}, u32[]{:S(2)}) copy-start(bf16[2,2,768,256]{3,2,1,0:T(8,128)(2,1)} %constant.21.clone.table) | copy-start | bytes 4718596
  8.0 4.0 %copy-start.4 = (f32[2,2,256,256]{3,2,1,0:T(8,128)S(1)}, f32[2,2,256,256]{3,2,1,0:T(8,128)}, u32[]{:S(2)}) copy-start(f32[2,2,256,256]{3,2,1,0:T(8,128)} %constant.22.clone.decay) | copy-start | bytes 3145732
  15.1 10.8 %collective-permute-start.1 = (f32[64,256]{1,0:T(8,128)S(1)}, f32[64,256]{1,0:T(8,128)S(1)}, u32[]{:S(2)}, u32[]{:S(2)}) collective-permute-start(f32[64,256]{1,0:T(8,128)S(1)} %get-tuple-element.41), channel_id=1, source_target_pairs={{0,2},{2,0},{4,6},{6,4},{8,10},{10,8},{12,14},{14,12},{1,3},{3,1},... | collective-permute-start | bytes 196616 | tf_op jit(solution)/shard_map/ppermute | solution.py:518
  17.7 8.3 %collective-permute-start.2 = (f32[64,256]{1,0:T(8,128)S(1)}, f32[64,256]{1,0:T(8,128)S(1)}, u32[]{:S(2)}, u32[]{:S(2)}) collective-permute-start(f32[64,256]{1,0:T(8,128)S(1)} %get-tuple-element.42), channel_id=1, source_target_pairs={{0,4},{2,6},{4,0},{6,2},{8,12},{10,14},{12,8},{14,10},{1,5},{3,7},... | collective-permute-start | bytes 196616 | tf_op jit(solution)/shard_map/ppermute | solution.py:518
  19.3 6.7 %collective-permute-start.3 = (f32[64,256]{1,0:T(8,128)S(1)}, f32[64,256]{1,0:T(8,128)S(1)}, u32[]{:S(2)}, u32[]{:S(2)}) collective-permute-start(f32[64,256]{1,0:T(8,128)S(1)} %get-tuple-element.43), channel_id=1, source_target_pairs={{0,6},{2,4},{4,2},{6,0},{8,14},{10,12},{12,10},{14,8},{1,7},{3,5},... | collective-permute-start | bytes 196616 | tf_op jit(solution)/shard_map/ppermute | solution.py:518
  19.3 6.7 %copy-start = (f32[2,2,3,256,256]{4,3,2,1,0:T(8,128)S(1)}, f32[2,2,3,256,256]{4,3,2,1,0:T(8,128)}, u32[]{:S(2)}) copy-start(f32[2,2,3,256,256]{4,3,2,1,0:T(8,128)} %constant.20.clone.closing) | copy-start | bytes 9437188
  22.4 7.2 %collective-permute-start.9 = (f32[64,256]{1,0:T(8,128)S(1)}, f32[64,256]{1,0:T(8,128)S(1)}, u32[]{:S(2)}, u32[]{:S(2)}) collective-permute-start(f32[64,256]{1,0:T(8,128)S(1)} %get-tuple-element.55), channel_id=1, source_target_pairs={{0,2},{2,0},{4,6},{6,4},{8,10},{10,8},{12,14},{14,12},{1,3},{3,1},... | collective-permute-start | bytes 196616 | tf_op jit(solution)/shard_map/ppermute | solution.py:518
  24.4 5.2 %collective-permute-start.10 = (f32[64,256]{1,0:T(8,128)S(1)}, f32[64,256]{1,0:T(8,128)S(1)}, u32[]{:S(2)}, u32[]{:S(2)}) collective-permute-start(f32[64,256]{1,0:T(8,128)S(1)} %get-tuple-element.56), channel_id=1, source_target_pairs={{0,4},{2,6},{4,0},{6,2},{8,12},{10,14},{12,8},{14,10},{1,5},{3,7},... | collective-permute-start | bytes 196616 | tf_op jit(solution)/shard_map/ppermute | solution.py:518
  26.0 5.5 %collective-permute-start.11 = (f32[64,256]{1,0:T(8,128)S(1)}, f32[64,256]{1,0:T(8,128)S(1)}, u32[]{:S(2)}, u32[]{:S(2)}) collective-permute-start(f32[64,256]{1,0:T(8,128)S(1)} %get-tuple-element.57), channel_id=1, source_target_pairs={{0,6},{2,4},{4,2},{6,0},{8,14},{10,12},{12,10},{14,8},{1,7},{3,5},... | collective-permute-start | bytes 196616 | tf_op jit(solution)/shard_map/ppermute | solution.py:518
  26.6 7.8 %collective-permute-start.4 = (f32[64,256]{1,0:T(8,128)S(1)}, f32[64,256]{1,0:T(8,128)S(1)}, u32[]{:S(2)}, u32[]{:S(2)}) collective-permute-start(f32[64,256]{1,0:T(8,128)S(1)} %get-tuple-element.45.near), channel_id=1, source_target_pairs={{0,8},{2,10},{4,12},{6,14},{8,0},{10,2},{12,4},{14,6},{1,9},{3,11}... | collective-permute-start | bytes 196616 | tf_op jit(solution)/shard_map/ppermute | solution.py:518
  32.0 6.5 %collective-permute-start.12 = (f32[64,256]{1,0:T(8,128)S(1)}, f32[64,256]{1,0:T(8,128)S(1)}, u32[]{:S(2)}, u32[]{:S(2)}) collective-permute-start(f32[64,256]{1,0:T(8,128)S(1)} %get-tuple-element.59.near), channel_id=1, source_target_pairs={{0,8},{2,10},{4,12},{6,14},{8,0},{10,2},{12,4},{14,6},{1,9},{3,11}... | collective-permute-start | bytes 196616 | tf_op jit(solution)/shard_map/ppermute | solution.py:518
  35.0 7.7 %copy-start.2 = (bf16[2,2,768,256]{3,2,1,0:T(8,128)(2,1)S(1)}, bf16[2,2,768,256]{3,2,1,0:T(8,128)(2,1)}, u32[]{:S(2)}) copy-start(bf16[2,2,768,256]{3,2,1,0:T(8,128)(2,1)} %constant.24.clone.table) | copy-start | bytes 4718596
  35.0 6.3 %collective-permute-start.5 = (f32[64,256]{1,0:T(8,128)S(1)}, f32[64,256]{1,0:T(8,128)S(1)}, u32[]{:S(2)}, u32[]{:S(2)}) collective-permute-start(f32[64,256]{1,0:T(8,128)S(1)} %get-tuple-element.47), channel_id=1, source_target_pairs={{0,2},{2,0},{4,6},{6,4},{8,10},{10,8},{12,14},{14,12},{1,3},{3,1},... | collective-permute-start | bytes 196616 | tf_op jit(solution)/shard_map/ppermute | solution.py:518
  35.6 7.2 %collective-permute-start.6 = (f32[64,256]{1,0:T(8,128)S(1)}, f32[64,256]{1,0:T(8,128)S(1)}, u32[]{:S(2)}, u32[]{:S(2)}) collective-permute-start(f32[64,256]{1,0:T(8,128)S(1)} %get-tuple-element.48), channel_id=1, source_target_pairs={{0,4},{2,6},{4,0},{6,2},{8,12},{10,14},{12,8},{14,10},{1,5},{3,7},... | collective-permute-start | bytes 196616 | tf_op jit(solution)/shard_map/ppermute | solution.py:518
  37.2 5.5 %collective-permute-start.7 = (f32[64,256]{1,0:T(8,128)S(1)}, f32[64,256]{1,0:T(8,128)S(1)}, u32[]{:S(2)}, u32[]{:S(2)}) collective-permute-start(f32[64,256]{1,0:T(8,128)S(1)} %get-tuple-element.49), channel_id=1, source_target_pairs={{0,6},{2,4},{4,2},{6,0},{8,14},{10,12},{12,10},{14,8},{1,7},{3,5},... | collective-permute-start | bytes 196616 | tf_op jit(solution)/shard_map/ppermute | solution.py:518
  39.2 6.7 %collective-permute-start.13 = (f32[64,256]{1,0:T(8,128)S(1)}, f32[64,256]{1,0:T(8,128)S(1)}, u32[]{:S(2)}, u32[]{:S(2)}) collective-permute-start(f32[64,256]{1,0:T(8,128)S(1)} %get-tuple-element.61), channel_id=1, source_target_pairs={{0,2},{2,0},{4,6},{6,4},{8,10},{10,8},{12,14},{14,12},{1,3},{3,1},... | collective-permute-start | bytes 196616 | tf_op jit(solution)/shard_map/ppermute | solution.py:518
  39.7 6.2 %collective-permute-start.14 = (f32[64,256]{1,0:T(8,128)S(1)}, f32[64,256]{1,0:T(8,128)S(1)}, u32[]{:S(2)}, u32[]{:S(2)}) collective-permute-start(f32[64,256]{1,0:T(8,128)S(1)} %get-tuple-element.62), channel_id=1, source_target_pairs={{0,4},{2,6},{4,0},{6,2},{8,12},{10,14},{12,8},{14,10},{1,5},{3,7},... | collective-permute-start | bytes 196616 | tf_op jit(solution)/shard_map/ppermute | solution.py:518
  41.4 5.2 %collective-permute-start.15 = (f32[64,256]{1,0:T(8,128)S(1)}, f32[64,256]{1,0:T(8,128)S(1)}, u32[]{:S(2)}, u32[]{:S(2)}) collective-permute-start(f32[64,256]{1,0:T(8,128)S(1)} %get-tuple-element.63), channel_id=1, source_target_pairs={{0,6},{2,4},{4,2},{6,0},{8,14},{10,12},{12,10},{14,8},{1,7},{3,5},... | collective-permute-start | bytes 196616 | tf_op jit(solution)/shard_map/ppermute | solution.py:518
  45.8 7.7 %collective-permute-start.16 = (f32[4224,128]{1,0:T(8,128)S(1)}, f32[4224,128]{1,0:T(8,128)S(1)}, u32[]{:S(2)}, u32[]{:S(2)}) collective-permute-start(f32[4224,128]{1,0:T(8,128)S(1)} %get-tuple-element.65), channel_id=1, source_target_pairs={{0,1},{1,0},{2,3},{3,2},{4,5},{5,4},{6,7},{7,6},{8,9},{9,8},{10,11... | collective-permute-start | bytes 6488072 | tf_op jit(solution)/shard_map/ppermute | solution.py:513
  46.5 3.4 %copy-start.1 = (bf16[2,768,256]{2,1,0:T(8,128)(2,1)S(1)}, bf16[2,768,256]{2,1,0:T(8,128)(2,1)}, u32[]{:S(2)}) copy-start(bf16[2,768,256]{2,1,0:T(8,128)(2,1)} %constant.25.clone.tables) | copy-start | bytes 2359300
  49.8 4.3 %collective-permute-start.17 = (f32[4224,128]{1,0:T(8,128)S(1)}, f32[4224,128]{1,0:T(8,128)S(1)}, u32[]{:S(2)}, u32[]{:S(2)}) collective-permute-start(f32[4224,128]{1,0:T(8,128)S(1)} %get-tuple-element.66), channel_id=1, source_target_pairs={{0,1},{1,0},{2,3},{3,2},{4,5},{5,4},{6,7},{7,6},{8,9},{9,8},{10,11... | collective-permute-start | bytes 6488072 | tf_op jit(solution)/shard_map/ppermute | solution.py:513

commit v10 on v9

--- a/solution.py
+++ b/solution.py
@@ -100,6 +100,7 @@
 
 
 IN_VMEM = pl.BlockSpec(memory_space=pltpu.VMEM)
+IN_HBM = pl.BlockSpec(memory_space=pltpu.HBM)
 IN_SMEM = pl.BlockSpec(memory_space=pltpu.SMEM)
 
 
@@ -111,22 +112,12 @@
     return jax.ShapeDtypeStruct(shape, jnp.float32)
 
 
-def call(kernel, name, in_specs, out_specs, out_shape, scratch, flops, grid=None):
-    if grid is None:
-        spec = pl.GridSpec(
-            in_specs=[IN_SMEM, *in_specs], out_specs=out_specs, scratch_shapes=scratch
-        )
-    else:
-        spec = pltpu.PrefetchScalarGridSpec(
-            num_scalar_prefetch=1,
-            grid=(grid,),
-            in_specs=in_specs,
-            out_specs=out_specs,
-            scratch_shapes=scratch,
-        )
+def call(kernel, name, in_specs, out_specs, out_shape, scratch, flops):
     return pl.pallas_call(
         kernel,
-        grid_spec=spec,
+        in_specs=[IN_SMEM, *in_specs],
+        out_specs=out_specs,
+        scratch_shapes=scratch,
         out_shape=out_shape,
         compiler_params=pltpu.CompilerParams(vmem_limit_bytes=VMEM_BYTES),
         cost_estimate=pl.CostEstimate(flops=flops, bytes_accessed=1 << 23, transcendentals=0),
@@ -134,19 +125,44 @@
     )
 
 
-def forward_second_kernel(place, field, initial, table, sums, *refs):
-    sends, scratch = refs[:CHUNKS], refs[CHUNKS:]
-    rows, steps, width = field.shape
+def forward_second_kernel(place, field_in, initial_in, tables, sums, *refs):
+    sends, refs = refs[:CHUNKS], refs[CHUNKS:]
+    field, initial, table, sems, table_sem, *scratch = refs
+    cells, steps, width = field.shape
     half = width // 2
     part = half // CHUNKS
-    piece = rows // len(scratch)
+    pieces = sems.shape[0]
+    piece = cells // pieces
+    rows = piece * len(scratch)
+    blocks = cells // rows
     group = max(TILE // steps, 1)
-    block, blocks = pl.program_id(0), pl.num_programs(0)
-    total = rows * blocks
     pitch = sends[0].shape[0] // (steps + 1)
     body = piece * steps
     is_first = place[0] == 0
     sign = 1.0 - 2.0 * place[1].astype(jnp.float32)
+
+    def copies(at):
+        here = pl.ds(at * piece, piece)
+        return [
+            pltpu.make_async_copy(source.at[here], to.at[here], sems.at[at, which])
+            for which, (source, to) in enumerate(((field_in, field), (initial_in, initial)))
+        ]
+
+    def wait(block):
+        for sub in range(len(scratch)):
+            for copy in copies(block * len(scratch) + sub):
+                copy.wait()
+
+    table_copy = pltpu.make_async_copy(tables.at[1 - place[1]], table, table_sem)
+    for at in range(len(scratch)):
+        for copy in copies(at):
+            copy.start()
+    table_copy.start()
+    wait(0)
+    table_copy.wait()
+    for at in range(len(scratch), pieces):
+        for copy in copies(at):
+            copy.start()
 
     def put(other, at, sums_at, cells):
         lower = cells[:, :half]
@@ -157,21 +173,21 @@
         sums[pl.ds(sums_at, TILE), :] = lower + upper
         store_split(other, (pl.ds(at, TILE),), 0, lower - upper)
 
-    def prepare(sub):
+    def prepare(sub, block):
         kept_at = pl.multiple_of(block * rows + sub * piece, piece)
         kept_base = pl.multiple_of(kept_at * steps, body)
         for row in range(0, piece, group):
-            cells = field[pl.ds(sub * piece + row, group)]
-            force = cells - cells * cells * cells
+            values = field[pl.ds(kept_at + row, group)]
+            force = values - values * values * values
             put(scratch[sub], row * steps, kept_base + row * steps, force.reshape(TILE, width))
         for row in range(0, piece, TILE):
-            at = pl.ds(sub * piece + row, TILE)
+            at = pl.ds(pl.multiple_of(kept_at + row, TILE), TILE)
             ends = jnp.where(is_first, initial[at], field[at, steps - 1, :])
-            put(scratch[sub], body + row, total * steps + kept_at + row, ends)
+            put(scratch[sub], body + row, cells * steps + kept_at + row, ends)
 
     def transform(sub, block):
-        sent = dot(scratch[sub][...], table[0])
-        sent_at = pl.multiple_of(total - block * rows - (sub + 1) * piece, piece)
+        sent = dot(scratch[sub][...], table[...])
+        sent_at = pl.multiple_of(cells - block * rows - (sub + 1) * piece, piece)
         for chunk, send in enumerate(sends):
             lanes = slice(chunk * part, (chunk + 1) * part)
             for row in range(piece):
@@ -180,36 +196,44 @@
             store_rows_reversed(send, pitch * steps + sent_at, sent[body:, lanes])
 
     last = len(scratch) - 1
-    transform(last, jnp.maximum(block - 1, 0))
-    for sub in range(last):
-        prepare(sub)
-        transform(sub, block)
-    prepare(last)
-
-    @pl.when(block == blocks - 1)
-    def _():
-        transform(last, block)
+
+    def prepare_block(block):
+        for sub in range(last):
+            prepare(sub, block)
+            transform(sub, block)
+        prepare(last, block)
+
+    prepare_block(0)
+
+    @pl.loop(1, blocks)
+    def _(block):
+        wait(block)
+        transform(last, block - 1)
+        prepare_block(block)
+
+    transform(last, blocks - 1)
 
 
 def forward_second(place, field, initial, tables):
     rows, steps, width = field.shape
     half = width // 2
-    block, pieces = min(64, rows), 2
-    depth = (steps + 1) * block // pieces
+    piece, pieces = min(32, rows // 2), 2
     outs = call(
         forward_second_kernel,
         "forward_second",
-        [
-            pl.BlockSpec((block, steps, width), lambda i, place: (i, 0, 0)),
-            pl.BlockSpec((block, width), lambda i, place: (i, 0)),
-            pl.BlockSpec((1, 3 * half, half), lambda i, place: (1 - place[1], 0, 0)),
-        ],
+        [IN_HBM] * 3,
         [IN_VMEM] * (1 + CHUNKS),
         [floats((steps + 1) * rows, half)]
         + [floats((steps + 1) * pitch_of(rows), half // CHUNKS)] * CHUNKS,
-        [pltpu.VMEM((depth, 3 * half), jnp.bfloat16)] * pieces,
+        [
+            pltpu.VMEM(field.shape, jnp.float32),
+            pltpu.VMEM(initial.shape, jnp.float32),
+            pltpu.VMEM(tables.shape[1:], jnp.bfloat16),
+            pltpu.SemaphoreType.DMA((rows // piece, 2)),
+            pltpu.SemaphoreType.DMA,
+        ]
+        + [pltpu.VMEM(((steps + 1) * piece, 3 * half), jnp.bfloat16)] * pieces,
         1 << 32,
-        rows // block,
     )(place, in_hbm(field), in_hbm(initial), in_hbm(tables))
     return outs[0], outs[1:]
 
@@ -457,55 +481,68 @@
 
 
 def inverse_second_kernel(place, tables, kept, *refs):
-    gots, out, scratch = refs[:CHUNKS], refs[CHUNKS], refs[CHUNKS + 1 :]
-    rows, steps, width = out.shape
+    gots, target, out, sems, scratch = (
+        refs[:CHUNKS], refs[CHUNKS], refs[CHUNKS + 1], refs[CHUNKS + 2], refs[CHUNKS + 3 :]
+    )
+    cells, steps, width = out.shape
     half = width // 2
     part = half // CHUNKS
     pitch = gots[0].shape[0] // steps
     count = len(scratch) // 2
-    piece = rows // count
+    pieces = sems.shape[0]
+    piece = cells // pieces
     group = max(TILE // steps, 1)
     strip = place[1]
     sign = 1.0 - 2.0 * strip.astype(jnp.float32)
-    total = rows * pl.num_programs(0)
-    start = pl.program_id(0) * rows
-    for sub in range(count):
-        split, result = scratch[2 * sub : 2 * sub + 2]
-        base = start + sub * piece
-        for row in range(0, piece, group):
-            mirrors = [total - 1 - base - row - at for at in range(group)]
-            for chunk, got in enumerate(gots):
-                cells = steps_of(got, mirrors, steps, pitch)
-                store_split(split, (pl.ds(row * steps, TILE),), chunk * part, cells)
-        result[...] = dot(split[...], tables[1 - strip])
-    for sub in range(count):
-        result = scratch[2 * sub + 1]
-        kept_base = pl.multiple_of((start + sub * piece) * steps, piece * steps)
-        for row in range(0, piece, group):
-            first = kept[pl.ds(kept_base + row * steps, TILE)]
-            second = result[pl.ds(row * steps, TILE)]
-            upper = sign * (first - second)
-            parts = [
-                lanes_reversed(upper[:, lane : lane + LANES]) for lane in range(0, half, LANES)
-            ][::-1]
-            whole = jnp.concatenate([first + second, *parts], axis=1)
-            out[pl.ds(sub * piece + row, group)] = whole.reshape(group, TILE // group, width)
+
+    def copy(at):
+        here = pl.ds(at * piece, piece)
+        return pltpu.make_async_copy(out.at[here], target.at[here], sems.at[at])
+
+    @pl.loop(0, pieces, step=count)
+    def _(first_piece):
+        for sub in range(count):
+            split, result = scratch[2 * sub : 2 * sub + 2]
+            base = (first_piece + sub) * piece
+            for row in range(0, piece, group):
+                mirrors = [cells - 1 - base - row - at for at in range(group)]
+                for chunk, got in enumerate(gots):
+                    values = steps_of(got, mirrors, steps, pitch)
+                    store_split(split, (pl.ds(row * steps, TILE),), chunk * part, values)
+            result[...] = dot(split[...], tables[1 - strip])
+        for sub in range(count):
+            result = scratch[2 * sub + 1]
+            base = pl.multiple_of((first_piece + sub) * piece, piece)
+            kept_base = pl.multiple_of(base * steps, piece * steps)
+            for row in range(0, piece, group):
+                first = kept[pl.ds(kept_base + row * steps, TILE)]
+                second = result[pl.ds(row * steps, TILE)]
+                upper = sign * (first - second)
+                parts = [
+                    lanes_reversed(upper[:, lane : lane + LANES]) for lane in range(0, half, LANES)
+                ][::-1]
+                whole = jnp.concatenate([first + second, *parts], axis=1)
+                out[pl.ds(base + row, group)] = whole.reshape(group, TILE // group, width)
+            copy(first_piece + sub).start()
+
+    for at in range(pieces):
+        copy(at).wait()
 
 
 def inverse_second(place, kept, gots, tables, steps):
     rows, half = kept.shape[0] // steps, kept.shape[1]
-    block, pieces = min(64, rows), 2
-    depth = steps * block // pieces
+    piece, pieces = min(32, rows // 2), 2
+    depth = steps * piece
     return call(
         inverse_second_kernel,
         "inverse_second",
         [IN_VMEM] * (2 + CHUNKS),
-        pl.BlockSpec((block, steps, 2 * half), lambda i, place: (i, 0, 0)),
+        IN_HBM,
         floats(rows, steps, 2 * half),
-        [pltpu.VMEM((depth, 3 * half), jnp.bfloat16), pltpu.VMEM((depth, half), jnp.float32)]
+        [pltpu.VMEM((rows, steps, 2 * half), jnp.float32), pltpu.SemaphoreType.DMA((rows // piece,))]
+        + [pltpu.VMEM((depth, 3 * half), jnp.bfloat16), pltpu.VMEM((depth, half), jnp.float32)]
         * pieces,
         1 << 32,
-        rows // block,
     )(place, tables, kept, *gots)
 
 

time: 60.5 us -> 60.4 us (level)
  no operation moved by 1% of the time
where the time goes in v10:
time: 60.4 us; the launch traced here: 60.3 us
  Pallas kernels  34.2 us (57%)
  starting transfers between devices  21.4 us (35%)
  waiting for transfers between devices  4.23 us (7%)
    ppermute x14, starting transfers between devices, with_partner(): lax.ppermute(block, 'tm', [(slab, slab ^ distance) for slab in range(slab...  20.7 us
    pallas_call x1, Pallas kernels, forward_second(): call(forward_second_kernel, 'forward_second', [IN_HBM] * 3, [IN_VMEM] * (...  6.81 us
    pallas_call x2, Pallas kernels, inverse_first(): call(functools.partial(inverse_first_kernel, slabs, chunk), 'inverse_firs...  6.33 us
    pallas_call x2, Pallas kernels, forward_first(): call(functools.partial(forward_first_kernel, slabs, chunk), 'forward_firs...  6.23 us
    pallas_call x1, Pallas kernels, inverse_second(): call(inverse_second_kernel, 'inverse_second', [IN_VMEM] * (2 + CHUNKS), I...  6.15 us
    pallas_call x1, Pallas kernels, keep_inverse(): call(functools.partial(keep_inverse_kernel, steps), 'keep_inverse', [IN_V...  3.64 us
    pallas_call x1, Pallas kernels, keep_second(): call(functools.partial(keep_second_kernel, steps), 'keep_second', [IN_VME...  2.68 us
    ppermute x14, waiting for transfers between devices, with_partner(): lax.ppermute(block, 'tm', [(slab, slab ^ distance) for slab in range(slab...  2.34 us
  transfers between devices with their start and end apart: 18, of which 4 were waited for; matrix products, arithmetic and copies ran while one was open for 0% of the time, Pallas kernels for 35%

profile of v10, /device:TPU:0, one launch (start us, length us, event | category | flops | bytes accessed | tf_op | source)
XLA Modules:
  0.0 60.3 jit_solution(1199758763403460902)
XLA Ops:
  0.0 0.1 pad_add_fusion.place
  0.1 6.8 %forward_second.1 = (f32[4352,256]{1,0:T(8,128)S(1)}, f32[4488,128]{1,0:T(8,128)S(1)}, f32[4488,128]{1,0:T(8,128)S(1)}) custom-call(s32[2]{0:T(128)S(1)} %pad_add_fusion.place, f32[256,16,512]{2,1,0:T(8,128)} %field_in.1, f32[256,512]{1,0:T(8,128)} %initial_in.1, bf16[2,768,256]{2,1,0:T(8,128)(2,1)} %constant.23.clone.tables), custom_call_target="tpu_custom_call" | custom-call | flops 4294967296 | bytes 8388608 | tf_op jit(solution)/shard_map/forward_second/pallas_call | solution.py:221
  6.9 0.5 collective-permute-start
  7.4 0.1 collective-permute-start.8
  7.5 2.7 %keep_second.1 = (f32[4488,128]{1,0:T(8,128)S(1)}, f32[4488,128]{1,0:T(8,128)S(1)}) custom-call(s32[2]{0:T(128)S(1)} %pad_add_fusion.place, bf16[2,768,256]{2,1,0:T(8,128)(2,1)S(1)} %copy-done.5, f32[4352,256]{1,0:T(8,128)S(1)} %get-tuple-element.36.sums), custom_call_target="tpu_custom_call" | custom-call | flops 2147483648 | bytes 8388608 | tf_op jit(solution)/shard_map/keep_second/pallas_call | solution.py:266
  10.2 1.3 %collective-permute-done.got = f32[4488,128]{1,0:T(8,128)S(1)} collective-permute-done((f32[4488,128]{1,0:T(8,128)S(1)}, f32[4488,128]{1,0:T(8,128)S(1)}, u32[]{:S(2)}, u32[]{:S(2)}) %collective-permute-start) | collective-permute-done | bytes 2297888 | tf_op jit(solution)/shard_map/ppermute | solution.py:550
  11.5 3.1 %forward_first.2 = (f32[16,2,128,256]{3,2,1,0:T(8,128)S(1)}, f32[64,256]{1,0:T(8,128)S(1)}, f32[64,256]{1,0:T(8,128)S(1)}, f32[64,256]{1,0:T(8,128)S(1)}, f32[64,256]{1,0:T(8,128)S(1)}) custom-call(s32[2]{0:T(128)S(1)} %pad_add_fusion.place, f32[4488,128]{1,0:T(8,128)S(1)} %get-tuple-element.37.keep, f32[4488,128]{1,0:T(8,128)S(1)} %collective-permute-done.got, ...), custom_call_target="tpu_custom_call" | custom-call | flops 2147483648 | bytes 8388608 | tf_op jit(solution)/shard_map/forward_first/pallas_call | solution.py:330
  14.6 3.0 %collective-permute-start.1 = (f32[64,256]{1,0:T(8,128)S(1)}, f32[64,256]{1,0:T(8,128)S(1)}, u32[]{:S(2)}, u32[]{:S(2)}) collective-permute-start(f32[64,256]{1,0:T(8,128)S(1)} %get-tuple-element.41), channel_id=1, source_target_pairs={{0,2},{2,0},{4,6},{6,4},{8,10},{10,8},{12,14},{14,12},{1,3},{3,1},... | collective-permute-start | bytes 196616 | tf_op jit(solution)/shard_map/ppermute | solution.py:555
  17.6 1.6 %collective-permute-start.2 = (f32[64,256]{1,0:T(8,128)S(1)}, f32[64,256]{1,0:T(8,128)S(1)}, u32[]{:S(2)}, u32[]{:S(2)}) collective-permute-start(f32[64,256]{1,0:T(8,128)S(1)} %get-tuple-element.42), channel_id=1, source_target_pairs={{0,4},{2,6},{4,0},{6,2},{8,12},{10,14},{12,8},{14,10},{1,5},{3,7},... | collective-permute-start | bytes 196616 | tf_op jit(solution)/shard_map/ppermute | solution.py:555
  19.2 3.1 %forward_first.3 = (f32[16,2,128,256]{3,2,1,0:T(8,128)S(1)}, f32[64,256]{1,0:T(8,128)S(1)}, f32[64,256]{1,0:T(8,128)S(1)}, f32[64,256]{1,0:T(8,128)S(1)}, f32[64,256]{1,0:T(8,128)S(1)}) custom-call(s32[2]{0:T(128)S(1)} %pad_add_fusion.place, f32[4488,128]{1,0:T(8,128)S(1)} %get-tuple-element.51.keep, f32[4488,128]{1,0:T(8,128)S(1)} %collective-permute-done.8.got, ...), custom_call_target="tpu_custom_call" | custom-call | flops 2147483648 | bytes 8388608 | tf_op jit(solution)/shard_map/forward_first/pallas_call | solution.py:330
  22.3 2.0 %collective-permute-start.9 = (f32[64,256]{1,0:T(8,128)S(1)}, f32[64,256]{1,0:T(8,128)S(1)}, u32[]{:S(2)}, u32[]{:S(2)}) collective-permute-start(f32[64,256]{1,0:T(8,128)S(1)} %get-tuple-element.55), channel_id=1, source_target_pairs={{0,2},{2,0},{4,6},{6,4},{8,10},{10,8},{12,14},{14,12},{1,3},{3,1},... | collective-permute-start | bytes 196616 | tf_op jit(solution)/shard_map/ppermute | solution.py:555
  24.3 1.6 %collective-permute-start.10 = (f32[64,256]{1,0:T(8,128)S(1)}, f32[64,256]{1,0:T(8,128)S(1)}, u32[]{:S(2)}, u32[]{:S(2)}) collective-permute-start(f32[64,256]{1,0:T(8,128)S(1)} %get-tuple-element.56), channel_id=1, source_target_pairs={{0,4},{2,6},{4,0},{6,2},{8,12},{10,14},{12,8},{14,10},{1,5},{3,7},... | collective-permute-start | bytes 196616 | tf_op jit(solution)/shard_map/ppermute | solution.py:555
  25.9 0.6 half_sum.2
  26.5 3.0 %collective-permute-start.4 = (f32[64,256]{1,0:T(8,128)S(1)}, f32[64,256]{1,0:T(8,128)S(1)}, u32[]{:S(2)}, u32[]{:S(2)}) collective-permute-start(f32[64,256]{1,0:T(8,128)S(1)} %get-tuple-element.45.near), channel_id=1, source_target_pairs={{0,8},{2,10},{4,12},{6,14},{8,0},{10,2},{12,4},{14,6},{1,9},{3,11}... | collective-permute-start | bytes 196616 | tf_op jit(solution)/shard_map/ppermute | solution.py:555
  29.5 1.7 %collective-permute-done.11.refs_3_ = f32[64,256]{1,0:T(8,128)S(1)} collective-permute-done((f32[64,256]{1,0:T(8,128)S(1)}, f32[64,256]{1,0:T(8,128)S(1)}, u32[]{:S(2)}, u32[]{:S(2)}) %collective-permute-start.11) | collective-permute-done | bytes 65568 | tf_op jit(solution)/shard_map/ppermute | solution.py:555
  31.2 0.6 half_sum.3
  31.8 2.5 %collective-permute-start.12 = (f32[64,256]{1,0:T(8,128)S(1)}, f32[64,256]{1,0:T(8,128)S(1)}, u32[]{:S(2)}, u32[]{:S(2)}) collective-permute-start(f32[64,256]{1,0:T(8,128)S(1)} %get-tuple-element.59.near), channel_id=1, source_target_pairs={{0,8},{2,10},{4,12},{6,14},{8,0},{10,2},{12,4},{14,6},{1,9},{3,11}... | collective-permute-start | bytes 196616 | tf_op jit(solution)/shard_map/ppermute | solution.py:555
  34.3 0.6 close.2
  34.9 0.6 collective-permute-start.5
  35.4 1.6 %collective-permute-start.6 = (f32[64,256]{1,0:T(8,128)S(1)}, f32[64,256]{1,0:T(8,128)S(1)}, u32[]{:S(2)}, u32[]{:S(2)}) collective-permute-start(f32[64,256]{1,0:T(8,128)S(1)} %get-tuple-element.48), channel_id=1, source_target_pairs={{0,4},{2,6},{4,0},{6,2},{8,12},{10,14},{12,8},{14,10},{1,5},{3,7},... | collective-permute-start | bytes 196616 | tf_op jit(solution)/shard_map/ppermute | solution.py:555
  37.1 1.4 %collective-permute-start.7 = (f32[64,256]{1,0:T(8,128)S(1)}, f32[64,256]{1,0:T(8,128)S(1)}, u32[]{:S(2)}, u32[]{:S(2)}) collective-permute-start(f32[64,256]{1,0:T(8,128)S(1)} %get-tuple-element.49), channel_id=1, source_target_pairs={{0,6},{2,4},{4,2},{6,0},{8,14},{10,12},{12,10},{14,8},{1,7},{3,5},... | collective-permute-start | bytes 196616 | tf_op jit(solution)/shard_map/ppermute | solution.py:555
  38.4 0.6 close.3
  39.0 0.6 collective-permute-start.13
  39.6 1.6 %collective-permute-start.14 = (f32[64,256]{1,0:T(8,128)S(1)}, f32[64,256]{1,0:T(8,128)S(1)}, u32[]{:S(2)}, u32[]{:S(2)}) collective-permute-start(f32[64,256]{1,0:T(8,128)S(1)} %get-tuple-element.62), channel_id=1, source_target_pairs={{0,4},{2,6},{4,0},{6,2},{8,12},{10,14},{12,8},{14,10},{1,5},{3,7},... | collective-permute-start | bytes 196616 | tf_op jit(solution)/shard_map/ppermute | solution.py:555
  41.2 1.4 %collective-permute-start.15 = (f32[64,256]{1,0:T(8,128)S(1)}, f32[64,256]{1,0:T(8,128)S(1)}, u32[]{:S(2)}, u32[]{:S(2)}) collective-permute-start(f32[64,256]{1,0:T(8,128)S(1)} %get-tuple-element.63), channel_id=1, source_target_pairs={{0,6},{2,4},{4,2},{6,0},{8,14},{10,12},{12,10},{14,8},{1,7},{3,5},... | collective-permute-start | bytes 196616 | tf_op jit(solution)/shard_map/ppermute | solution.py:555
  42.6 3.1 %inverse_first.2 = (f32[4224,128]{1,0:T(8,128)S(1)}, f32[4224,128]{1,0:T(8,128)S(1)}) custom-call(s32[2]{0:T(128)S(1)} %pad_add_fusion.place, f32[16,2,128,256]{3,2,1,0:T(8,128)S(1)} %get-tuple-element.39.modes, bf16[2,2,768,256]{3,2,1,0:T(8,128)(2,1)S(1)} %copy-done.2, f32[2,2,256,256]{3,2,1,0:T(8,128)S(1)} %copy-done.4, ...), custom_call_target="tpu_custom_call" | custom-call | flops 2147483648 | bytes 8388608 | tf_op jit(solution)/shard_map/inverse_first/pallas_call | solution.py:440
  45.7 0.1 collective-permute-start.16
  45.8 0.6 collective-permute-done.15.refs_3_
  46.4 3.3 %inverse_first.3 = (f32[4224,128]{1,0:T(8,128)S(1)}, f32[4224,128]{1,0:T(8,128)S(1)}) custom-call(s32[2]{0:T(128)S(1)} %pad_add_fusion.place, f32[16,2,128,256]{3,2,1,0:T(8,128)S(1)} %get-tuple-element.53.modes, bf16[2,2,768,256]{3,2,1,0:T(8,128)(2,1)S(1)} %copy-done.2, f32[2,2,256,256]{3,2,1,0:T(8,128)S(1)} %copy-done.4, ...), custom_call_target="tpu_custom_call" | custom-call | flops 2147483648 | bytes 8388608 | tf_op jit(solution)/shard_map/inverse_first/pallas_call | solution.py:440
  49.7 3.6 %keep_inverse.1.kept = f32[4096,256]{1,0:T(8,128)S(1)} custom-call(s32[2]{0:T(128)S(1)} %pad_add_fusion.place, bf16[2,768,256]{2,1,0:T(8,128)(2,1)S(1)} %copy-done.1, f32[4224,128]{1,0:T(8,128)S(1)} %get-tuple-element.50.refs_0_, f32[4224,128]{1,0:T(8,128)S(1)} %get-tuple-element.64.refs_1_), custom_call_target="tpu_custom_call" | custom-call | flops 2147483648 | bytes 8388608 | tf_op jit(solution)/shard_map/keep_inverse/pallas_call | solution.py:472
  53.4 0.6 collective-permute-done.17.refs_1_
  54.0 6.1 %inverse_second.1 = f32[256,16,512]{2,1,0:T(8,128)} custom-call(s32[2]{0:T(128)S(1)} %pad_add_fusion.place, bf16[2,768,256]{2,1,0:T(8,128)(2,1)S(1)} %copy-done.1, f32[4096,256]{1,0:T(8,128)S(1)} %keep_inverse.1.kept, f32[4224,128]{1,0:T(8,128)S(1)} %collective-permute-done.16.refs_0_, f32[4224,128]{1,0:T(8,128)S(1)} %collective-permute-done.17.refs_1_), custom_call_target="tpu_custom_call" | custom-call | flops 4294967296 | bytes 8388608 | tf_op jit(solution)/shard_map/inverse_second/pallas_call | solution.py:536
  (29 shorter events, 0.1 us)
Async XLA Ops:
  0.1 7.4 %copy-start.5 = (bf16[2,768,256]{2,1,0:T(8,128)(2,1)S(1)}, bf16[2,768,256]{2,1,0:T(8,128)(2,1)}, u32[]{:S(2)}) copy-start(bf16[2,768,256]{2,1,0:T(8,128)(2,1)} %constant.23.clone.tables) | copy-start | bytes 2359300
  6.9 4.6 %collective-permute-start = (f32[4488,128]{1,0:T(8,128)S(1)}, f32[4488,128]{1,0:T(8,128)S(1)}, u32[]{:S(2)}, u32[]{:S(2)}) collective-permute-start(f32[4488,128]{1,0:T(8,128)S(1)} %get-tuple-element.38), channel_id=1, source_target_pairs={{0,1},{1,0},{2,3},{3,2},{4,5},{5,4},{6,7},{7,6},{8,9},{9,8},{10,11... | collective-permute-start | bytes 6893576 | tf_op jit(solution)/shard_map/ppermute | solution.py:550
  7.4 11.7 %collective-permute-start.8 = (f32[4488,128]{1,0:T(8,128)S(1)}, f32[4488,128]{1,0:T(8,128)S(1)}, u32[]{:S(2)}, u32[]{:S(2)}) collective-permute-start(f32[4488,128]{1,0:T(8,128)S(1)} %get-tuple-element.52), channel_id=1, source_target_pairs={{0,1},{1,0},{2,3},{3,2},{4,5},{5,4},{6,7},{7,6},{8,9},{9,8},{10,11... | collective-permute-start | bytes 6893576 | tf_op jit(solution)/shard_map/ppermute | solution.py:550
  7.5 4.0 %copy-start.3 = (bf16[2,2,768,256]{3,2,1,0:T(8,128)(2,1)S(1)}, bf16[2,2,768,256]{3,2,1,0:T(8,128)(2,1)}, u32[]{:S(2)}) copy-start(bf16[2,2,768,256]{3,2,1,0:T(8,128)(2,1)} %constant.21.clone.table) | copy-start | bytes 4718596
  7.5 4.0 %copy-start.4 = (f32[2,2,256,256]{3,2,1,0:T(8,128)S(1)}, f32[2,2,256,256]{3,2,1,0:T(8,128)}, u32[]{:S(2)}) copy-start(f32[2,2,256,256]{3,2,1,0:T(8,128)} %constant.22.clone.decay) | copy-start | bytes 3145732
  14.6 11.2 %collective-permute-start.1 = (f32[64,256]{1,0:T(8,128)S(1)}, f32[64,256]{1,0:T(8,128)S(1)}, u32[]{:S(2)}, u32[]{:S(2)}) collective-permute-start(f32[64,256]{1,0:T(8,128)S(1)} %get-tuple-element.41), channel_id=1, source_target_pairs={{0,2},{2,0},{4,6},{6,4},{8,10},{10,8},{12,14},{14,12},{1,3},{3,1},... | collective-permute-start | bytes 196616 | tf_op jit(solution)/shard_map/ppermute | solution.py:555
  17.6 8.3 %collective-permute-start.2 = (f32[64,256]{1,0:T(8,128)S(1)}, f32[64,256]{1,0:T(8,128)S(1)}, u32[]{:S(2)}, u32[]{:S(2)}) collective-permute-start(f32[64,256]{1,0:T(8,128)S(1)} %get-tuple-element.42), channel_id=1, source_target_pairs={{0,4},{2,6},{4,0},{6,2},{8,12},{10,14},{12,8},{14,10},{1,5},{3,7},... | collective-permute-start | bytes 196616 | tf_op jit(solution)/shard_map/ppermute | solution.py:555
  19.2 6.7 %collective-permute-start.3 = (f32[64,256]{1,0:T(8,128)S(1)}, f32[64,256]{1,0:T(8,128)S(1)}, u32[]{:S(2)}, u32[]{:S(2)}) collective-permute-start(f32[64,256]{1,0:T(8,128)S(1)} %get-tuple-element.43), channel_id=1, source_target_pairs={{0,6},{2,4},{4,2},{6,0},{8,14},{10,12},{12,10},{14,8},{1,7},{3,5},... | collective-permute-start | bytes 196616 | tf_op jit(solution)/shard_map/ppermute | solution.py:555
  19.2 6.7 %copy-start = (f32[2,2,3,256,256]{4,3,2,1,0:T(8,128)S(1)}, f32[2,2,3,256,256]{4,3,2,1,0:T(8,128)}, u32[]{:S(2)}) copy-start(f32[2,2,3,256,256]{4,3,2,1,0:T(8,128)} %constant.20.clone.closing) | copy-start | bytes 9437188
  22.3 7.2 %collective-permute-start.9 = (f32[64,256]{1,0:T(8,128)S(1)}, f32[64,256]{1,0:T(8,128)S(1)}, u32[]{:S(2)}, u32[]{:S(2)}) collective-permute-start(f32[64,256]{1,0:T(8,128)S(1)} %get-tuple-element.55), channel_id=1, source_target_pairs={{0,2},{2,0},{4,6},{6,4},{8,10},{10,8},{12,14},{14,12},{1,3},{3,1},... | collective-permute-start | bytes 196616 | tf_op jit(solution)/shard_map/ppermute | solution.py:555
  24.3 5.2 %collective-permute-start.10 = (f32[64,256]{1,0:T(8,128)S(1)}, f32[64,256]{1,0:T(8,128)S(1)}, u32[]{:S(2)}, u32[]{:S(2)}) collective-permute-start(f32[64,256]{1,0:T(8,128)S(1)} %get-tuple-element.56), channel_id=1, source_target_pairs={{0,4},{2,6},{4,0},{6,2},{8,12},{10,14},{12,8},{14,10},{1,5},{3,7},... | collective-permute-start | bytes 196616 | tf_op jit(solution)/shard_map/ppermute | solution.py:555
  25.8 5.4 %collective-permute-start.11 = (f32[64,256]{1,0:T(8,128)S(1)}, f32[64,256]{1,0:T(8,128)S(1)}, u32[]{:S(2)}, u32[]{:S(2)}) collective-permute-start(f32[64,256]{1,0:T(8,128)S(1)} %get-tuple-element.57), channel_id=1, source_target_pairs={{0,6},{2,4},{4,2},{6,0},{8,14},{10,12},{12,10},{14,8},{1,7},{3,5},... | collective-permute-start | bytes 196616 | tf_op jit(solution)/shard_map/ppermute | solution.py:555
  26.5 7.8 %collective-permute-start.4 = (f32[64,256]{1,0:T(8,128)S(1)}, f32[64,256]{1,0:T(8,128)S(1)}, u32[]{:S(2)}, u32[]{:S(2)}) collective-permute-start(f32[64,256]{1,0:T(8,128)S(1)} %get-tuple-element.45.near), channel_id=1, source_target_pairs={{0,8},{2,10},{4,12},{6,14},{8,0},{10,2},{12,4},{14,6},{1,9},{3,11}... | collective-permute-start | bytes 196616 | tf_op jit(solution)/shard_map/ppermute | solution.py:555
  31.8 6.6 %collective-permute-start.12 = (f32[64,256]{1,0:T(8,128)S(1)}, f32[64,256]{1,0:T(8,128)S(1)}, u32[]{:S(2)}, u32[]{:S(2)}) collective-permute-start(f32[64,256]{1,0:T(8,128)S(1)} %get-tuple-element.59.near), channel_id=1, source_target_pairs={{0,8},{2,10},{4,12},{6,14},{8,0},{10,2},{12,4},{14,6},{1,9},{3,11}... | collective-permute-start | bytes 196616 | tf_op jit(solution)/shard_map/ppermute | solution.py:555
  34.9 7.7 %copy-start.2 = (bf16[2,2,768,256]{3,2,1,0:T(8,128)(2,1)S(1)}, bf16[2,2,768,256]{3,2,1,0:T(8,128)(2,1)}, u32[]{:S(2)}) copy-start(bf16[2,2,768,256]{3,2,1,0:T(8,128)(2,1)} %constant.24.clone.table) | copy-start | bytes 4718596
  34.9 6.3 %collective-permute-start.5 = (f32[64,256]{1,0:T(8,128)S(1)}, f32[64,256]{1,0:T(8,128)S(1)}, u32[]{:S(2)}, u32[]{:S(2)}) collective-permute-start(f32[64,256]{1,0:T(8,128)S(1)} %get-tuple-element.47), channel_id=1, source_target_pairs={{0,2},{2,0},{4,6},{6,4},{8,10},{10,8},{12,14},{14,12},{1,3},{3,1},... | collective-permute-start | bytes 196616 | tf_op jit(solution)/shard_map/ppermute | solution.py:555
  35.4 7.2 %collective-permute-start.6 = (f32[64,256]{1,0:T(8,128)S(1)}, f32[64,256]{1,0:T(8,128)S(1)}, u32[]{:S(2)}, u32[]{:S(2)}) collective-permute-start(f32[64,256]{1,0:T(8,128)S(1)} %get-tuple-element.48), channel_id=1, source_target_pairs={{0,4},{2,6},{4,0},{6,2},{8,12},{10,14},{12,8},{14,10},{1,5},{3,7},... | collective-permute-start | bytes 196616 | tf_op jit(solution)/shard_map/ppermute | solution.py:555
  37.1 5.5 %collective-permute-start.7 = (f32[64,256]{1,0:T(8,128)S(1)}, f32[64,256]{1,0:T(8,128)S(1)}, u32[]{:S(2)}, u32[]{:S(2)}) collective-permute-start(f32[64,256]{1,0:T(8,128)S(1)} %get-tuple-element.49), channel_id=1, source_target_pairs={{0,6},{2,4},{4,2},{6,0},{8,14},{10,12},{12,10},{14,8},{1,7},{3,5},... | collective-permute-start | bytes 196616 | tf_op jit(solution)/shard_map/ppermute | solution.py:555
  39.0 6.7 %collective-permute-start.13 = (f32[64,256]{1,0:T(8,128)S(1)}, f32[64,256]{1,0:T(8,128)S(1)}, u32[]{:S(2)}, u32[]{:S(2)}) collective-permute-start(f32[64,256]{1,0:T(8,128)S(1)} %get-tuple-element.61), channel_id=1, source_target_pairs={{0,2},{2,0},{4,6},{6,4},{8,10},{10,8},{12,14},{14,12},{1,3},{3,1},... | collective-permute-start | bytes 196616 | tf_op jit(solution)/shard_map/ppermute | solution.py:555
  39.6 6.2 %collective-permute-start.14 = (f32[64,256]{1,0:T(8,128)S(1)}, f32[64,256]{1,0:T(8,128)S(1)}, u32[]{:S(2)}, u32[]{:S(2)}) collective-permute-start(f32[64,256]{1,0:T(8,128)S(1)} %get-tuple-element.62), channel_id=1, source_target_pairs={{0,4},{2,6},{4,0},{6,2},{8,12},{10,14},{12,8},{14,10},{1,5},{3,7},... | collective-permute-start | bytes 196616 | tf_op jit(solution)/shard_map/ppermute | solution.py:555
  41.2 5.2 %collective-permute-start.15 = (f32[64,256]{1,0:T(8,128)S(1)}, f32[64,256]{1,0:T(8,128)S(1)}, u32[]{:S(2)}, u32[]{:S(2)}) collective-permute-start(f32[64,256]{1,0:T(8,128)S(1)} %get-tuple-element.63), channel_id=1, source_target_pairs={{0,6},{2,4},{4,2},{6,0},{8,14},{10,12},{12,10},{14,8},{1,7},{3,5},... | collective-permute-start | bytes 196616 | tf_op jit(solution)/shard_map/ppermute | solution.py:555
  45.7 7.7 %collective-permute-start.16 = (f32[4224,128]{1,0:T(8,128)S(1)}, f32[4224,128]{1,0:T(8,128)S(1)}, u32[]{:S(2)}, u32[]{:S(2)}) collective-permute-start(f32[4224,128]{1,0:T(8,128)S(1)} %get-tuple-element.65), channel_id=1, source_target_pairs={{0,1},{1,0},{2,3},{3,2},{4,5},{5,4},{6,7},{7,6},{8,9},{9,8},{10,11... | collective-permute-start | bytes 6488072 | tf_op jit(solution)/shard_map/ppermute | solution.py:550
  46.4 3.4 %copy-start.1 = (bf16[2,768,256]{2,1,0:T(8,128)(2,1)S(1)}, bf16[2,768,256]{2,1,0:T(8,128)(2,1)}, u32[]{:S(2)}) copy-start(bf16[2,768,256]{2,1,0:T(8,128)(2,1)} %constant.25.clone.tables) | copy-start | bytes 2359300
  49.7 4.3 %collective-permute-start.17 = (f32[4224,128]{1,0:T(8,128)S(1)}, f32[4224,128]{1,0:T(8,128)S(1)}, u32[]{:S(2)}, u32[]{:S(2)}) collective-permute-start(f32[4224,128]{1,0:T(8,128)S(1)} %get-tuple-element.66), channel_id=1, source_target_pairs={{0,1},{1,0},{2,3},{3,2},{4,5},{5,4},{6,7},{7,6},{8,9},{9,8},{10,11... | collective-permute-start | bytes 6488072 | tf_op jit(solution)/shard_map/ppermute | solution.py:550

commit v11 on v10

--- a/solution.py
+++ b/solution.py
@@ -63,16 +63,17 @@
 
 
 def store_split(ref, at, lane, block):
-    depth = ref.shape[-1] // 3
+    depth = ref.shape[-1] // 2
     width = block.shape[-1]
     high = block.astype(jnp.bfloat16)
     low = (block - high.astype(jnp.float32)).astype(jnp.bfloat16)
-    for part, value in enumerate((high, low, high)):
-        ref[(*at, pl.ds(part * depth + lane, width))] = value
-
-
-def dot(first, second):
-    return jnp.dot(first, second, preferred_element_type=jnp.float32)
+    ref[(*at, pl.ds(lane, width))] = high
+    ref[(*at, pl.ds(depth + lane, width))] = low
+
+
+def dot(split, table):
+    rows = jnp.concatenate([split, split[:, : split.shape[1] // 2]], axis=1)
+    return jnp.dot(rows, table, preferred_element_type=jnp.float32)
 
 
 def lanes_reversed(block):
@@ -148,21 +149,12 @@
             for which, (source, to) in enumerate(((field_in, field), (initial_in, initial)))
         ]
 
-    def wait(block):
-        for sub in range(len(scratch)):
-            for copy in copies(block * len(scratch) + sub):
-                copy.wait()
-
     table_copy = pltpu.make_async_copy(tables.at[1 - place[1]], table, table_sem)
-    for at in range(len(scratch)):
+    for at in range(pieces):
         for copy in copies(at):
             copy.start()
-    table_copy.start()
-    wait(0)
-    table_copy.wait()
-    for at in range(len(scratch), pieces):
-        for copy in copies(at):
-            copy.start()
+        if at == 0:
+            table_copy.start()
 
     def put(other, at, sums_at, cells):
         lower = cells[:, :half]
@@ -195,23 +187,25 @@
                 send[pl.ds(sent_at + piece - 1 - row, steps, stride=pitch), :] = line
             store_rows_reversed(send, pitch * steps + sent_at, sent[body:, lanes])
 
-    last = len(scratch) - 1
-
-    def prepare_block(block):
-        for sub in range(last):
-            prepare(sub, block)
-            transform(sub, block)
-        prepare(last, block)
-
-    prepare_block(0)
-
-    @pl.loop(1, blocks)
+    count = len(scratch)
+
+    def piece_of(block, sub):
+        for copy in copies(block * count + sub):
+            copy.wait()
+        if sub:
+            transform(sub - 1, block)
+        else:
+            transform(count - 1, jnp.maximum(block - 1, 0))
+        prepare(sub, block)
+
+    table_copy.wait()
+
+    @pl.loop(0, blocks)
     def _(block):
-        wait(block)
-        transform(last, block - 1)
-        prepare_block(block)
-
-    transform(last, blocks - 1)
+        for sub in range(count):
+            piece_of(block, sub)
+
+    transform(count - 1, blocks - 1)
 
 
 def forward_second(place, field, initial, tables):
@@ -232,7 +226,7 @@
             pltpu.SemaphoreType.DMA((rows // piece, 2)),
             pltpu.SemaphoreType.DMA,
         ]
-        + [pltpu.VMEM(((steps + 1) * piece, 3 * half), jnp.bfloat16)] * pieces,
+        + [pltpu.VMEM(((steps + 1) * piece, 2 * half), jnp.bfloat16)] * pieces,
         1 << 32,
     )(place, in_hbm(field), in_hbm(initial), in_hbm(tables))
     return outs[0], outs[1:]
@@ -269,7 +263,7 @@
         [IN_VMEM] * 2,
         [IN_VMEM] * CHUNKS,
         [floats(*shape)] * CHUNKS,
-        [pltpu.VMEM((rows // 8, 3 * half), jnp.bfloat16)] * 2,
+        [pltpu.VMEM((rows // 8, 2 * half), jnp.bfloat16)] * 2,
         1 << 31,
     )(place, tables, sums)
 
@@ -335,8 +329,8 @@
         [floats(steps, 2, part, rows)] + [floats(share, rows)] * size,
         [
             pltpu.VMEM((2 * part, rows), jnp.float32),
-            pltpu.VMEM((2, block * part, 3 * rows), jnp.bfloat16),
-            pltpu.VMEM((2, part, 3 * rows), jnp.bfloat16),
+            pltpu.VMEM((2, block * part, 2 * rows), jnp.bfloat16),
+            pltpu.VMEM((2, part, 2 * rows), jnp.bfloat16),
             pltpu.VMEM((2, part, rows), jnp.float32),
         ],
         1 << 31,
@@ -445,7 +439,7 @@
         [floats(steps * pitch_of(rows), part)] * 2,
         [
             pltpu.VMEM((2 * part, rows), jnp.float32),
-            pltpu.VMEM((2, block * part, 3 * rows), jnp.bfloat16),
+            pltpu.VMEM((2, block * part, 2 * rows), jnp.bfloat16),
         ],
         1 << 31,
     )(place, modes, tables, decays, *befores)
@@ -475,7 +469,7 @@
         [IN_VMEM] * (1 + CHUNKS),
         IN_VMEM,
         floats(rows * steps, half),
-        [pltpu.VMEM((rows * steps // 8, 3 * half), jnp.bfloat16)] * 2,
+        [pltpu.VMEM((rows * steps // 8, 2 * half), jnp.bfloat16)] * 2,
         1 << 31,
     )(place, tables, *keeps)
 
@@ -540,7 +534,7 @@
         IN_HBM,
         floats(rows, steps, 2 * half),
         [pltpu.VMEM((rows, steps, 2 * half), jnp.float32), pltpu.SemaphoreType.DMA((rows // piece,))]
-        + [pltpu.VMEM((depth, 3 * half), jnp.bfloat16), pltpu.VMEM((depth, half), jnp.float32)]
+        + [pltpu.VMEM((depth, 2 * half), jnp.bfloat16), pltpu.VMEM((depth, half), jnp.float32)]
         * pieces,
         1 << 32,
     )(place, tables, kept, *gots)

time: 60.4 us -> 63 us (1.043)
  Pallas kernels: 34.2 us -> 36.7 us
    pallas_call x1, Pallas kernels: 6.81 us -> 9.37 us  [forward_second(): call(forward_second_kernel, 'forward_second', [IN_HBM] * 3, [IN_VMEM] * (...]
  transfers between devices with their start and end apart: 18 -> 18, of which waited for: 4 -> 4; matrix products, arithmetic and copies ran while one was open for 0% -> 0% of each run, Pallas kernels for 35% -> 34%
where the time goes in v11:
time: 63 us; the launch traced here: 62.9 us
  Pallas kernels  36.7 us (58%)
  starting transfers between devices  21.4 us (34%)
  waiting for transfers between devices  4.33 us (7%)
    ppermute x14, starting transfers between devices, with_partner(): lax.ppermute(block, 'tm', [(slab, slab ^ distance) for slab in range(slab...  20.7 us
    pallas_call x1, Pallas kernels, forward_second(): call(forward_second_kernel, 'forward_second', [IN_HBM] * 3, [IN_VMEM] * (...  9.37 us
    pallas_call x2, Pallas kernels, inverse_first(): call(functools.partial(inverse_first_kernel, slabs, chunk), 'inverse_firs...  6.34 us
    pallas_call x2, Pallas kernels, forward_first(): call(functools.partial(forward_first_kernel, slabs, chunk), 'forward_firs...  6.24 us
    pallas_call x1, Pallas kernels, inverse_second(): call(inverse_second_kernel, 'inverse_second', [IN_VMEM] * (2 + CHUNKS), I...  6.19 us
    pallas_call x1, Pallas kernels, keep_inverse(): call(functools.partial(keep_inverse_kernel, steps), 'keep_inverse', [IN_V...  3.55 us
    pallas_call x1, Pallas kernels, keep_second(): call(functools.partial(keep_second_kernel, steps), 'keep_second', [IN_VME...  2.68 us
    ppermute x14, waiting for transfers between devices, with_partner(): lax.ppermute(block, 'tm', [(slab, slab ^ distance) for slab in range(slab...  2.35 us
  transfers between devices with their start and end apart: 18, of which 4 were waited for; matrix products, arithmetic and copies ran while one was open for 0% of the time, Pallas kernels for 34%

profile of v11, /device:TPU:0, one launch (start us, length us, event | category | flops | bytes accessed | tf_op | source)
XLA Modules:
  0.0 62.9 jit_solution(13518989647413937797)
XLA Ops:
  0.0 0.1 pad_add_fusion.place
  0.1 9.4 %forward_second.1 = (f32[4352,256]{1,0:T(8,128)S(1)}, f32[4488,128]{1,0:T(8,128)S(1)}, f32[4488,128]{1,0:T(8,128)S(1)}) custom-call(s32[2]{0:T(128)S(1)} %pad_add_fusion.place, f32[256,16,512]{2,1,0:T(8,128)} %field_in.1, f32[256,512]{1,0:T(8,128)} %initial_in.1, bf16[2,768,256]{2,1,0:T(8,128)(2,1)} %constant.23.clone.tables), custom_call_target="tpu_custom_call" | custom-call | flops 4294967296 | bytes 8388608 | tf_op jit(solution)/shard_map/forward_second/pallas_call | solution.py:215
  9.5 0.5 collective-permute-start
  10.0 0.1 collective-permute-start.8
  10.1 2.7 %keep_second.1 = (f32[4488,128]{1,0:T(8,128)S(1)}, f32[4488,128]{1,0:T(8,128)S(1)}) custom-call(s32[2]{0:T(128)S(1)} %pad_add_fusion.place, bf16[2,768,256]{2,1,0:T(8,128)(2,1)S(1)} %copy-done.5, f32[4352,256]{1,0:T(8,128)S(1)} %get-tuple-element.36.sums), custom_call_target="tpu_custom_call" | custom-call | flops 2147483648 | bytes 8388608 | tf_op jit(solution)/shard_map/keep_second/pallas_call | solution.py:260
  12.8 1.3 %collective-permute-done.got = f32[4488,128]{1,0:T(8,128)S(1)} collective-permute-done((f32[4488,128]{1,0:T(8,128)S(1)}, f32[4488,128]{1,0:T(8,128)S(1)}, u32[]{:S(2)}, u32[]{:S(2)}) %collective-permute-start) | collective-permute-done | bytes 2297888 | tf_op jit(solution)/shard_map/ppermute | solution.py:544
  14.1 3.1 %forward_first.2 = (f32[16,2,128,256]{3,2,1,0:T(8,128)S(1)}, f32[64,256]{1,0:T(8,128)S(1)}, f32[64,256]{1,0:T(8,128)S(1)}, f32[64,256]{1,0:T(8,128)S(1)}, f32[64,256]{1,0:T(8,128)S(1)}) custom-call(s32[2]{0:T(128)S(1)} %pad_add_fusion.place, f32[4488,128]{1,0:T(8,128)S(1)} %get-tuple-element.37.keep, f32[4488,128]{1,0:T(8,128)S(1)} %collective-permute-done.got, ...), custom_call_target="tpu_custom_call" | custom-call | flops 2147483648 | bytes 8388608 | tf_op jit(solution)/shard_map/forward_first/pallas_call | solution.py:324
  17.2 3.0 %collective-permute-start.1 = (f32[64,256]{1,0:T(8,128)S(1)}, f32[64,256]{1,0:T(8,128)S(1)}, u32[]{:S(2)}, u32[]{:S(2)}) collective-permute-start(f32[64,256]{1,0:T(8,128)S(1)} %get-tuple-element.41), channel_id=1, source_target_pairs={{0,2},{2,0},{4,6},{6,4},{8,10},{10,8},{12,14},{14,12},{1,3},{3,1},... | collective-permute-start | bytes 196616 | tf_op jit(solution)/shard_map/ppermute | solution.py:549
  20.1 1.6 %collective-permute-start.2 = (f32[64,256]{1,0:T(8,128)S(1)}, f32[64,256]{1,0:T(8,128)S(1)}, u32[]{:S(2)}, u32[]{:S(2)}) collective-permute-start(f32[64,256]{1,0:T(8,128)S(1)} %get-tuple-element.42), channel_id=1, source_target_pairs={{0,4},{2,6},{4,0},{6,2},{8,12},{10,14},{12,8},{14,10},{1,5},{3,7},... | collective-permute-start | bytes 196616 | tf_op jit(solution)/shard_map/ppermute | solution.py:549
  21.7 3.1 %forward_first.3 = (f32[16,2,128,256]{3,2,1,0:T(8,128)S(1)}, f32[64,256]{1,0:T(8,128)S(1)}, f32[64,256]{1,0:T(8,128)S(1)}, f32[64,256]{1,0:T(8,128)S(1)}, f32[64,256]{1,0:T(8,128)S(1)}) custom-call(s32[2]{0:T(128)S(1)} %pad_add_fusion.place, f32[4488,128]{1,0:T(8,128)S(1)} %get-tuple-element.51.keep, f32[4488,128]{1,0:T(8,128)S(1)} %collective-permute-done.8.got, ...), custom_call_target="tpu_custom_call" | custom-call | flops 2147483648 | bytes 8388608 | tf_op jit(solution)/shard_map/forward_first/pallas_call | solution.py:324
  24.9 2.0 %collective-permute-start.9 = (f32[64,256]{1,0:T(8,128)S(1)}, f32[64,256]{1,0:T(8,128)S(1)}, u32[]{:S(2)}, u32[]{:S(2)}) collective-permute-start(f32[64,256]{1,0:T(8,128)S(1)} %get-tuple-element.55), channel_id=1, source_target_pairs={{0,2},{2,0},{4,6},{6,4},{8,10},{10,8},{12,14},{14,12},{1,3},{3,1},... | collective-permute-start | bytes 196616 | tf_op jit(solution)/shard_map/ppermute | solution.py:549
  26.8 1.6 %collective-permute-start.10 = (f32[64,256]{1,0:T(8,128)S(1)}, f32[64,256]{1,0:T(8,128)S(1)}, u32[]{:S(2)}, u32[]{:S(2)}) collective-permute-start(f32[64,256]{1,0:T(8,128)S(1)} %get-tuple-element.56), channel_id=1, source_target_pairs={{0,4},{2,6},{4,0},{6,2},{8,12},{10,14},{12,8},{14,10},{1,5},{3,7},... | collective-permute-start | bytes 196616 | tf_op jit(solution)/shard_map/ppermute | solution.py:549
  28.4 0.6 half_sum.2
  29.0 3.0 %collective-permute-start.4 = (f32[64,256]{1,0:T(8,128)S(1)}, f32[64,256]{1,0:T(8,128)S(1)}, u32[]{:S(2)}, u32[]{:S(2)}) collective-permute-start(f32[64,256]{1,0:T(8,128)S(1)} %get-tuple-element.45.near), channel_id=1, source_target_pairs={{0,8},{2,10},{4,12},{6,14},{8,0},{10,2},{12,4},{14,6},{1,9},{3,11}... | collective-permute-start | bytes 196616 | tf_op jit(solution)/shard_map/ppermute | solution.py:549
  32.1 1.7 %collective-permute-done.11.refs_3_ = f32[64,256]{1,0:T(8,128)S(1)} collective-permute-done((f32[64,256]{1,0:T(8,128)S(1)}, f32[64,256]{1,0:T(8,128)S(1)}, u32[]{:S(2)}, u32[]{:S(2)}) %collective-permute-start.11) | collective-permute-done | bytes 65568 | tf_op jit(solution)/shard_map/ppermute | solution.py:549
  33.8 0.6 half_sum.3
  34.4 2.4 %collective-permute-start.12 = (f32[64,256]{1,0:T(8,128)S(1)}, f32[64,256]{1,0:T(8,128)S(1)}, u32[]{:S(2)}, u32[]{:S(2)}) collective-permute-start(f32[64,256]{1,0:T(8,128)S(1)} %get-tuple-element.59.near), channel_id=1, source_target_pairs={{0,8},{2,10},{4,12},{6,14},{8,0},{10,2},{12,4},{14,6},{1,9},{3,11}... | collective-permute-start | bytes 196616 | tf_op jit(solution)/shard_map/ppermute | solution.py:549
  36.8 0.6 close.2
  37.4 0.6 collective-permute-start.5
  38.0 1.6 %collective-permute-start.6 = (f32[64,256]{1,0:T(8,128)S(1)}, f32[64,256]{1,0:T(8,128)S(1)}, u32[]{:S(2)}, u32[]{:S(2)}) collective-permute-start(f32[64,256]{1,0:T(8,128)S(1)} %get-tuple-element.48), channel_id=1, source_target_pairs={{0,4},{2,6},{4,0},{6,2},{8,12},{10,14},{12,8},{14,10},{1,5},{3,7},... | collective-permute-start | bytes 196616 | tf_op jit(solution)/shard_map/ppermute | solution.py:549
  39.6 1.4 %collective-permute-start.7 = (f32[64,256]{1,0:T(8,128)S(1)}, f32[64,256]{1,0:T(8,128)S(1)}, u32[]{:S(2)}, u32[]{:S(2)}) collective-permute-start(f32[64,256]{1,0:T(8,128)S(1)} %get-tuple-element.49), channel_id=1, source_target_pairs={{0,6},{2,4},{4,2},{6,0},{8,14},{10,12},{12,10},{14,8},{1,7},{3,5},... | collective-permute-start | bytes 196616 | tf_op jit(solution)/shard_map/ppermute | solution.py:549
  41.0 0.6 close.3
  41.6 0.6 collective-permute-start.13
  42.2 1.6 %collective-permute-start.14 = (f32[64,256]{1,0:T(8,128)S(1)}, f32[64,256]{1,0:T(8,128)S(1)}, u32[]{:S(2)}, u32[]{:S(2)}) collective-permute-start(f32[64,256]{1,0:T(8,128)S(1)} %get-tuple-element.62), channel_id=1, source_target_pairs={{0,4},{2,6},{4,0},{6,2},{8,12},{10,14},{12,8},{14,10},{1,5},{3,7},... | collective-permute-start | bytes 196616 | tf_op jit(solution)/shard_map/ppermute | solution.py:549
  43.8 1.4 %collective-permute-start.15 = (f32[64,256]{1,0:T(8,128)S(1)}, f32[64,256]{1,0:T(8,128)S(1)}, u32[]{:S(2)}, u32[]{:S(2)}) collective-permute-start(f32[64,256]{1,0:T(8,128)S(1)} %get-tuple-element.63), channel_id=1, source_target_pairs={{0,6},{2,4},{4,2},{6,0},{8,14},{10,12},{12,10},{14,8},{1,7},{3,5},... | collective-permute-start | bytes 196616 | tf_op jit(solution)/shard_map/ppermute | solution.py:549
  45.2 3.1 %inverse_first.2 = (f32[4224,128]{1,0:T(8,128)S(1)}, f32[4224,128]{1,0:T(8,128)S(1)}) custom-call(s32[2]{0:T(128)S(1)} %pad_add_fusion.place, f32[16,2,128,256]{3,2,1,0:T(8,128)S(1)} %get-tuple-element.39.modes, bf16[2,2,768,256]{3,2,1,0:T(8,128)(2,1)S(1)} %copy-done.2, f32[2,2,256,256]{3,2,1,0:T(8,128)S(1)} %copy-done.4, ...), custom_call_target="tpu_custom_call" | custom-call | flops 2147483648 | bytes 8388608 | tf_op jit(solution)/shard_map/inverse_first/pallas_call | solution.py:434
  48.2 0.1 collective-permute-start.16
  48.3 0.6 collective-permute-done.15.refs_3_
  49.0 3.3 %inverse_first.3 = (f32[4224,128]{1,0:T(8,128)S(1)}, f32[4224,128]{1,0:T(8,128)S(1)}) custom-call(s32[2]{0:T(128)S(1)} %pad_add_fusion.place, f32[16,2,128,256]{3,2,1,0:T(8,128)S(1)} %get-tuple-element.53.modes, bf16[2,2,768,256]{3,2,1,0:T(8,128)(2,1)S(1)} %copy-done.2, f32[2,2,256,256]{3,2,1,0:T(8,128)S(1)} %copy-done.4, ...), custom_call_target="tpu_custom_call" | custom-call | flops 2147483648 | bytes 8388608 | tf_op jit(solution)/shard_map/inverse_first/pallas_call | solution.py:434
  52.3 3.5 %keep_inverse.1.kept = f32[4096,256]{1,0:T(8,128)S(1)} custom-call(s32[2]{0:T(128)S(1)} %pad_add_fusion.place, bf16[2,768,256]{2,1,0:T(8,128)(2,1)S(1)} %copy-done.1, f32[4224,128]{1,0:T(8,128)S(1)} %get-tuple-element.50.refs_0_, f32[4224,128]{1,0:T(8,128)S(1)} %get-tuple-element.64.refs_1_), custom_call_target="tpu_custom_call" | custom-call | flops 2147483648 | bytes 8388608 | tf_op jit(solution)/shard_map/keep_inverse/pallas_call | solution.py:466
  55.9 0.7 %collective-permute-done.17.refs_1_ = f32[4224,128]{1,0:T(8,128)S(1)} collective-permute-done((f32[4224,128]{1,0:T(8,128)S(1)}, f32[4224,128]{1,0:T(8,128)S(1)}, u32[]{:S(2)}, u32[]{:S(2)}) %collective-permute-start.17) | collective-permute-done | bytes 2162720 | tf_op jit(solution)/shard_map/ppermute | solution.py:544
  56.5 6.2 %inverse_second.1 = f32[256,16,512]{2,1,0:T(8,128)} custom-call(s32[2]{0:T(128)S(1)} %pad_add_fusion.place, bf16[2,768,256]{2,1,0:T(8,128)(2,1)S(1)} %copy-done.1, f32[4096,256]{1,0:T(8,128)S(1)} %keep_inverse.1.kept, f32[4224,128]{1,0:T(8,128)S(1)} %collective-permute-done.16.refs_0_, f32[4224,128]{1,0:T(8,128)S(1)} %collective-permute-done.17.refs_1_), custom_call_target="tpu_custom_call" | custom-call | flops 4294967296 | bytes 8388608 | tf_op jit(solution)/shard_map/inverse_second/pallas_call | solution.py:530
  (29 shorter events, 0.1 us)
Async XLA Ops:
  0.1 10.0 %copy-start.5 = (bf16[2,768,256]{2,1,0:T(8,128)(2,1)S(1)}, bf16[2,768,256]{2,1,0:T(8,128)(2,1)}, u32[]{:S(2)}) copy-start(bf16[2,768,256]{2,1,0:T(8,128)(2,1)} %constant.23.clone.tables) | copy-start | bytes 2359300
  9.5 4.6 %collective-permute-start = (f32[4488,128]{1,0:T(8,128)S(1)}, f32[4488,128]{1,0:T(8,128)S(1)}, u32[]{:S(2)}, u32[]{:S(2)}) collective-permute-start(f32[4488,128]{1,0:T(8,128)S(1)} %get-tuple-element.38), channel_id=1, source_target_pairs={{0,1},{1,0},{2,3},{3,2},{4,5},{5,4},{6,7},{7,6},{8,9},{9,8},{10,11... | collective-permute-start | bytes 6893576 | tf_op jit(solution)/shard_map/ppermute | solution.py:544
  10.0 11.7 %collective-permute-start.8 = (f32[4488,128]{1,0:T(8,128)S(1)}, f32[4488,128]{1,0:T(8,128)S(1)}, u32[]{:S(2)}, u32[]{:S(2)}) collective-permute-start(f32[4488,128]{1,0:T(8,128)S(1)} %get-tuple-element.52), channel_id=1, source_target_pairs={{0,1},{1,0},{2,3},{3,2},{4,5},{5,4},{6,7},{7,6},{8,9},{9,8},{10,11... | collective-permute-start | bytes 6893576 | tf_op jit(solution)/shard_map/ppermute | solution.py:544
  10.1 4.0 %copy-start.3 = (bf16[2,2,768,256]{3,2,1,0:T(8,128)(2,1)S(1)}, bf16[2,2,768,256]{3,2,1,0:T(8,128)(2,1)}, u32[]{:S(2)}) copy-start(bf16[2,2,768,256]{3,2,1,0:T(8,128)(2,1)} %constant.21.clone.table) | copy-start | bytes 4718596
  10.1 4.0 %copy-start.4 = (f32[2,2,256,256]{3,2,1,0:T(8,128)S(1)}, f32[2,2,256,256]{3,2,1,0:T(8,128)}, u32[]{:S(2)}) copy-start(f32[2,2,256,256]{3,2,1,0:T(8,128)} %constant.22.clone.decay) | copy-start | bytes 3145732
  17.2 11.2 %collective-permute-start.1 = (f32[64,256]{1,0:T(8,128)S(1)}, f32[64,256]{1,0:T(8,128)S(1)}, u32[]{:S(2)}, u32[]{:S(2)}) collective-permute-start(f32[64,256]{1,0:T(8,128)S(1)} %get-tuple-element.41), channel_id=1, source_target_pairs={{0,2},{2,0},{4,6},{6,4},{8,10},{10,8},{12,14},{14,12},{1,3},{3,1},... | collective-permute-start | bytes 196616 | tf_op jit(solution)/shard_map/ppermute | solution.py:549
  20.1 8.3 %collective-permute-start.2 = (f32[64,256]{1,0:T(8,128)S(1)}, f32[64,256]{1,0:T(8,128)S(1)}, u32[]{:S(2)}, u32[]{:S(2)}) collective-permute-start(f32[64,256]{1,0:T(8,128)S(1)} %get-tuple-element.42), channel_id=1, source_target_pairs={{0,4},{2,6},{4,0},{6,2},{8,12},{10,14},{12,8},{14,10},{1,5},{3,7},... | collective-permute-start | bytes 196616 | tf_op jit(solution)/shard_map/ppermute | solution.py:549
  21.7 6.7 %collective-permute-start.3 = (f32[64,256]{1,0:T(8,128)S(1)}, f32[64,256]{1,0:T(8,128)S(1)}, u32[]{:S(2)}, u32[]{:S(2)}) collective-permute-start(f32[64,256]{1,0:T(8,128)S(1)} %get-tuple-element.43), channel_id=1, source_target_pairs={{0,6},{2,4},{4,2},{6,0},{8,14},{10,12},{12,10},{14,8},{1,7},{3,5},... | collective-permute-start | bytes 196616 | tf_op jit(solution)/shard_map/ppermute | solution.py:549
  21.7 6.7 %copy-start = (f32[2,2,3,256,256]{4,3,2,1,0:T(8,128)S(1)}, f32[2,2,3,256,256]{4,3,2,1,0:T(8,128)}, u32[]{:S(2)}) copy-start(f32[2,2,3,256,256]{4,3,2,1,0:T(8,128)} %constant.20.clone.closing) | copy-start | bytes 9437188
  24.9 7.2 %collective-permute-start.9 = (f32[64,256]{1,0:T(8,128)S(1)}, f32[64,256]{1,0:T(8,128)S(1)}, u32[]{:S(2)}, u32[]{:S(2)}) collective-permute-start(f32[64,256]{1,0:T(8,128)S(1)} %get-tuple-element.55), channel_id=1, source_target_pairs={{0,2},{2,0},{4,6},{6,4},{8,10},{10,8},{12,14},{14,12},{1,3},{3,1},... | collective-permute-start | bytes 196616 | tf_op jit(solution)/shard_map/ppermute | solution.py:549
  26.8 5.2 %collective-permute-start.10 = (f32[64,256]{1,0:T(8,128)S(1)}, f32[64,256]{1,0:T(8,128)S(1)}, u32[]{:S(2)}, u32[]{:S(2)}) collective-permute-start(f32[64,256]{1,0:T(8,128)S(1)} %get-tuple-element.56), channel_id=1, source_target_pairs={{0,4},{2,6},{4,0},{6,2},{8,12},{10,14},{12,8},{14,10},{1,5},{3,7},... | collective-permute-start | bytes 196616 | tf_op jit(solution)/shard_map/ppermute | solution.py:549
  28.4 5.4 %collective-permute-start.11 = (f32[64,256]{1,0:T(8,128)S(1)}, f32[64,256]{1,0:T(8,128)S(1)}, u32[]{:S(2)}, u32[]{:S(2)}) collective-permute-start(f32[64,256]{1,0:T(8,128)S(1)} %get-tuple-element.57), channel_id=1, source_target_pairs={{0,6},{2,4},{4,2},{6,0},{8,14},{10,12},{12,10},{14,8},{1,7},{3,5},... | collective-permute-start | bytes 196616 | tf_op jit(solution)/shard_map/ppermute | solution.py:549
  29.0 7.8 %collective-permute-start.4 = (f32[64,256]{1,0:T(8,128)S(1)}, f32[64,256]{1,0:T(8,128)S(1)}, u32[]{:S(2)}, u32[]{:S(2)}) collective-permute-start(f32[64,256]{1,0:T(8,128)S(1)} %get-tuple-element.45.near), channel_id=1, source_target_pairs={{0,8},{2,10},{4,12},{6,14},{8,0},{10,2},{12,4},{14,6},{1,9},{3,11}... | collective-permute-start | bytes 196616 | tf_op jit(solution)/shard_map/ppermute | solution.py:549
  34.4 6.6 %collective-permute-start.12 = (f32[64,256]{1,0:T(8,128)S(1)}, f32[64,256]{1,0:T(8,128)S(1)}, u32[]{:S(2)}, u32[]{:S(2)}) collective-permute-start(f32[64,256]{1,0:T(8,128)S(1)} %get-tuple-element.59.near), channel_id=1, source_target_pairs={{0,8},{2,10},{4,12},{6,14},{8,0},{10,2},{12,4},{14,6},{1,9},{3,11}... | collective-permute-start | bytes 196616 | tf_op jit(solution)/shard_map/ppermute | solution.py:549
  37.4 7.7 %copy-start.2 = (bf16[2,2,768,256]{3,2,1,0:T(8,128)(2,1)S(1)}, bf16[2,2,768,256]{3,2,1,0:T(8,128)(2,1)}, u32[]{:S(2)}) copy-start(bf16[2,2,768,256]{3,2,1,0:T(8,128)(2,1)} %constant.24.clone.table) | copy-start | bytes 4718596
  37.4 6.3 %collective-permute-start.5 = (f32[64,256]{1,0:T(8,128)S(1)}, f32[64,256]{1,0:T(8,128)S(1)}, u32[]{:S(2)}, u32[]{:S(2)}) collective-permute-start(f32[64,256]{1,0:T(8,128)S(1)} %get-tuple-element.47), channel_id=1, source_target_pairs={{0,2},{2,0},{4,6},{6,4},{8,10},{10,8},{12,14},{14,12},{1,3},{3,1},... | collective-permute-start | bytes 196616 | tf_op jit(solution)/shard_map/ppermute | solution.py:549
  38.0 7.2 %collective-permute-start.6 = (f32[64,256]{1,0:T(8,128)S(1)}, f32[64,256]{1,0:T(8,128)S(1)}, u32[]{:S(2)}, u32[]{:S(2)}) collective-permute-start(f32[64,256]{1,0:T(8,128)S(1)} %get-tuple-element.48), channel_id=1, source_target_pairs={{0,4},{2,6},{4,0},{6,2},{8,12},{10,14},{12,8},{14,10},{1,5},{3,7},... | collective-permute-start | bytes 196616 | tf_op jit(solution)/shard_map/ppermute | solution.py:549
  39.6 5.5 %collective-permute-start.7 = (f32[64,256]{1,0:T(8,128)S(1)}, f32[64,256]{1,0:T(8,128)S(1)}, u32[]{:S(2)}, u32[]{:S(2)}) collective-permute-start(f32[64,256]{1,0:T(8,128)S(1)} %get-tuple-element.49), channel_id=1, source_target_pairs={{0,6},{2,4},{4,2},{6,0},{8,14},{10,12},{12,10},{14,8},{1,7},{3,5},... | collective-permute-start | bytes 196616 | tf_op jit(solution)/shard_map/ppermute | solution.py:549
  41.6 6.7 %collective-permute-start.13 = (f32[64,256]{1,0:T(8,128)S(1)}, f32[64,256]{1,0:T(8,128)S(1)}, u32[]{:S(2)}, u32[]{:S(2)}) collective-permute-start(f32[64,256]{1,0:T(8,128)S(1)} %get-tuple-element.61), channel_id=1, source_target_pairs={{0,2},{2,0},{4,6},{6,4},{8,10},{10,8},{12,14},{14,12},{1,3},{3,1},... | collective-permute-start | bytes 196616 | tf_op jit(solution)/shard_map/ppermute | solution.py:549
  42.2 6.2 %collective-permute-start.14 = (f32[64,256]{1,0:T(8,128)S(1)}, f32[64,256]{1,0:T(8,128)S(1)}, u32[]{:S(2)}, u32[]{:S(2)}) collective-permute-start(f32[64,256]{1,0:T(8,128)S(1)} %get-tuple-element.62), channel_id=1, source_target_pairs={{0,4},{2,6},{4,0},{6,2},{8,12},{10,14},{12,8},{14,10},{1,5},{3,7},... | collective-permute-start | bytes 196616 | tf_op jit(solution)/shard_map/ppermute | solution.py:549
  43.8 5.2 %collective-permute-start.15 = (f32[64,256]{1,0:T(8,128)S(1)}, f32[64,256]{1,0:T(8,128)S(1)}, u32[]{:S(2)}, u32[]{:S(2)}) collective-permute-start(f32[64,256]{1,0:T(8,128)S(1)} %get-tuple-element.63), channel_id=1, source_target_pairs={{0,6},{2,4},{4,2},{6,0},{8,14},{10,12},{12,10},{14,8},{1,7},{3,5},... | collective-permute-start | bytes 196616 | tf_op jit(solution)/shard_map/ppermute | solution.py:549
  48.2 7.6 %collective-permute-start.16 = (f32[4224,128]{1,0:T(8,128)S(1)}, f32[4224,128]{1,0:T(8,128)S(1)}, u32[]{:S(2)}, u32[]{:S(2)}) collective-permute-start(f32[4224,128]{1,0:T(8,128)S(1)} %get-tuple-element.65), channel_id=1, source_target_pairs={{0,1},{1,0},{2,3},{3,2},{4,5},{5,4},{6,7},{7,6},{8,9},{9,8},{10,11... | collective-permute-start | bytes 6488072 | tf_op jit(solution)/shard_map/ppermute | solution.py:544
  48.9 3.4 %copy-start.1 = (bf16[2,768,256]{2,1,0:T(8,128)(2,1)S(1)}, bf16[2,768,256]{2,1,0:T(8,128)(2,1)}, u32[]{:S(2)}) copy-start(bf16[2,768,256]{2,1,0:T(8,128)(2,1)} %constant.25.clone.tables) | copy-start | bytes 2359300
  52.2 4.3 %collective-permute-start.17 = (f32[4224,128]{1,0:T(8,128)S(1)}, f32[4224,128]{1,0:T(8,128)S(1)}, u32[]{:S(2)}, u32[]{:S(2)}) collective-permute-start(f32[4224,128]{1,0:T(8,128)S(1)} %get-tuple-element.66), channel_id=1, source_target_pairs={{0,1},{1,0},{2,3},{3,2},{4,5},{5,4},{6,7},{7,6},{8,9},{9,8},{10,11... | collective-permute-start | bytes 6488072 | tf_op jit(solution)/shard_map/ppermute | solution.py:544

commit v12 on v11

--- a/solution.py
+++ b/solution.py
@@ -150,11 +150,11 @@
         ]
 
     table_copy = pltpu.make_async_copy(tables.at[1 - place[1]], table, table_sem)
-    for at in range(pieces):
-        for copy in copies(at):
-            copy.start()
-        if at == 0:
-            table_copy.start()
+    for copy in copies(0):
+        copy.start()
+    table_copy.start()
+    for copy in copies(1):
+        copy.start()
 
     def put(other, at, sums_at, cells):
         lower = cells[:, :half]
@@ -190,8 +190,15 @@
     count = len(scratch)
 
     def piece_of(block, sub):
-        for copy in copies(block * count + sub):
+        at = block * count + sub
+        for copy in copies(at):
             copy.wait()
+
+        @pl.when(at + 2 < pieces)
+        def _():
+            for copy in copies(at + 2):
+                copy.start()
+
         if sub:
             transform(sub - 1, block)
         else:
@@ -550,7 +557,8 @@
 
 
 def among_ranks(blocks):
-    return [blocks[0]] + [with_partner(block, at) for at, block in enumerate(blocks) if at]
+    arrived = [with_partner(blocks[at], at) for at in range(len(blocks) - 1, 0, -1)]
+    return [blocks[0]] + arrived[::-1]
 
 
 def by_chunk(table):

time: 63 us -> 61.6 us (0.978)
  Pallas kernels: 36.7 us -> 35.2 us
    pallas_call x1, Pallas kernels: 9.37 us -> 7.82 us  [forward_second(): call(forward_second_kernel, 'forward_second', [IN_HBM] * 3, [IN_VMEM] * (...]
where the time goes in v12:
time: 61.6 us; the launch traced here: 61.4 us
  Pallas kernels  35.2 us (57%)
  starting transfers between devices  21.4 us (35%)
  waiting for transfers between devices  4.35 us (7%)
    ppermute x14, starting transfers between devices, with_partner(): lax.ppermute(block, 'tm', [(slab, slab ^ distance) for slab in range(slab...  20.7 us
    pallas_call x1, Pallas kernels, forward_second(): call(forward_second_kernel, 'forward_second', [IN_HBM] * 3, [IN_VMEM] * (...  7.82 us
    pallas_call x2, Pallas kernels, inverse_first(): call(functools.partial(inverse_first_kernel, slabs, chunk), 'inverse_firs...  6.34 us
    pallas_call x2, Pallas kernels, forward_first(): call(functools.partial(forward_first_kernel, slabs, chunk), 'forward_firs...  6.23 us
    pallas_call x1, Pallas kernels, inverse_second(): call(inverse_second_kernel, 'inverse_second', [IN_VMEM] * (2 + CHUNKS), I...  6.19 us
    pallas_call x1, Pallas kernels, keep_inverse(): call(functools.partial(keep_inverse_kernel, steps), 'keep_inverse', [IN_V...  3.55 us
    pallas_call x1, Pallas kernels, keep_second(): call(functools.partial(keep_second_kernel, steps), 'keep_second', [IN_VME...  2.68 us
    ppermute x14, waiting for transfers between devices, with_partner(): lax.ppermute(block, 'tm', [(slab, slab ^ distance) for slab in range(slab...  2.37 us
  transfers between devices with their start and end apart: 18, of which 4 were waited for; matrix products, arithmetic and copies ran while one was open for 0% of the time, Pallas kernels for 34%

profile of v12, /device:TPU:0, one launch (start us, length us, event | category | flops | bytes accessed | tf_op | source)
XLA Modules:
  0.0 61.4 jit_solution(17322872601896193725)
XLA Ops:
  0.0 0.1 pad_add_fusion.place
  0.1 7.8 %forward_second.1 = (f32[4352,256]{1,0:T(8,128)S(1)}, f32[4488,128]{1,0:T(8,128)S(1)}, f32[4488,128]{1,0:T(8,128)S(1)}) custom-call(s32[2]{0:T(128)S(1)} %pad_add_fusion.place, f32[256,16,512]{2,1,0:T(8,128)} %field_in.1, f32[256,512]{1,0:T(8,128)} %initial_in.1, bf16[2,768,256]{2,1,0:T(8,128)(2,1)} %constant.23.clone.tables), custom_call_target="tpu_custom_call" | custom-call | flops 4294967296 | bytes 8388608 | tf_op jit(solution)/shard_map/forward_second/pallas_call | solution.py:222
  7.9 0.5 collective-permute-start
  8.4 0.1 collective-permute-start.8
  8.5 2.7 %keep_second.1 = (f32[4488,128]{1,0:T(8,128)S(1)}, f32[4488,128]{1,0:T(8,128)S(1)}) custom-call(s32[2]{0:T(128)S(1)} %pad_add_fusion.place, bf16[2,768,256]{2,1,0:T(8,128)(2,1)S(1)} %copy-done.5, f32[4352,256]{1,0:T(8,128)S(1)} %get-tuple-element.36.sums), custom_call_target="tpu_custom_call" | custom-call | flops 2147483648 | bytes 8388608 | tf_op jit(solution)/shard_map/keep_second/pallas_call | solution.py:267
  11.2 1.3 %collective-permute-done.got = f32[4488,128]{1,0:T(8,128)S(1)} collective-permute-done((f32[4488,128]{1,0:T(8,128)S(1)}, f32[4488,128]{1,0:T(8,128)S(1)}, u32[]{:S(2)}, u32[]{:S(2)}) %collective-permute-start) | collective-permute-done | bytes 2297888 | tf_op jit(solution)/shard_map/ppermute | solution.py:551
  12.5 3.1 %forward_first.2 = (f32[16,2,128,256]{3,2,1,0:T(8,128)S(1)}, f32[64,256]{1,0:T(8,128)S(1)}, f32[64,256]{1,0:T(8,128)S(1)}, f32[64,256]{1,0:T(8,128)S(1)}, f32[64,256]{1,0:T(8,128)S(1)}) custom-call(s32[2]{0:T(128)S(1)} %pad_add_fusion.place, f32[4488,128]{1,0:T(8,128)S(1)} %get-tuple-element.37.keep, f32[4488,128]{1,0:T(8,128)S(1)} %collective-permute-done.got, ...), custom_call_target="tpu_custom_call" | custom-call | flops 2147483648 | bytes 8388608 | tf_op jit(solution)/shard_map/forward_first/pallas_call | solution.py:331
  15.6 3.0 %collective-permute-start.1 = (f32[64,256]{1,0:T(8,128)S(1)}, f32[64,256]{1,0:T(8,128)S(1)}, u32[]{:S(2)}, u32[]{:S(2)}) collective-permute-start(f32[64,256]{1,0:T(8,128)S(1)} %get-tuple-element.41), channel_id=1, source_target_pairs={{0,2},{2,0},{4,6},{6,4},{8,10},{10,8},{12,14},{14,12},{1,3},{3,1},... | collective-permute-start | bytes 196616 | tf_op jit(solution)/shard_map/ppermute | solution.py:556
  18.6 1.6 %collective-permute-start.2 = (f32[64,256]{1,0:T(8,128)S(1)}, f32[64,256]{1,0:T(8,128)S(1)}, u32[]{:S(2)}, u32[]{:S(2)}) collective-permute-start(f32[64,256]{1,0:T(8,128)S(1)} %get-tuple-element.42), channel_id=1, source_target_pairs={{0,4},{2,6},{4,0},{6,2},{8,12},{10,14},{12,8},{14,10},{1,5},{3,7},... | collective-permute-start | bytes 196616 | tf_op jit(solution)/shard_map/ppermute | solution.py:556
  20.2 3.1 %forward_first.3 = (f32[16,2,128,256]{3,2,1,0:T(8,128)S(1)}, f32[64,256]{1,0:T(8,128)S(1)}, f32[64,256]{1,0:T(8,128)S(1)}, f32[64,256]{1,0:T(8,128)S(1)}, f32[64,256]{1,0:T(8,128)S(1)}) custom-call(s32[2]{0:T(128)S(1)} %pad_add_fusion.place, f32[4488,128]{1,0:T(8,128)S(1)} %get-tuple-element.51.keep, f32[4488,128]{1,0:T(8,128)S(1)} %collective-permute-done.8.got, ...), custom_call_target="tpu_custom_call" | custom-call | flops 2147483648 | bytes 8388608 | tf_op jit(solution)/shard_map/forward_first/pallas_call | solution.py:331
  23.3 2.0 %collective-permute-start.9 = (f32[64,256]{1,0:T(8,128)S(1)}, f32[64,256]{1,0:T(8,128)S(1)}, u32[]{:S(2)}, u32[]{:S(2)}) collective-permute-start(f32[64,256]{1,0:T(8,128)S(1)} %get-tuple-element.55), channel_id=1, source_target_pairs={{0,2},{2,0},{4,6},{6,4},{8,10},{10,8},{12,14},{14,12},{1,3},{3,1},... | collective-permute-start | bytes 196616 | tf_op jit(solution)/shard_map/ppermute | solution.py:556
  25.3 1.6 %collective-permute-start.10 = (f32[64,256]{1,0:T(8,128)S(1)}, f32[64,256]{1,0:T(8,128)S(1)}, u32[]{:S(2)}, u32[]{:S(2)}) collective-permute-start(f32[64,256]{1,0:T(8,128)S(1)} %get-tuple-element.56), channel_id=1, source_target_pairs={{0,4},{2,6},{4,0},{6,2},{8,12},{10,14},{12,8},{14,10},{1,5},{3,7},... | collective-permute-start | bytes 196616 | tf_op jit(solution)/shard_map/ppermute | solution.py:556
  26.9 0.6 half_sum.2
  27.5 3.0 %collective-permute-start.4 = (f32[64,256]{1,0:T(8,128)S(1)}, f32[64,256]{1,0:T(8,128)S(1)}, u32[]{:S(2)}, u32[]{:S(2)}) collective-permute-start(f32[64,256]{1,0:T(8,128)S(1)} %get-tuple-element.45.near), channel_id=1, source_target_pairs={{0,8},{2,10},{4,12},{6,14},{8,0},{10,2},{12,4},{14,6},{1,9},{3,11}... | collective-permute-start | bytes 196616 | tf_op jit(solution)/shard_map/ppermute | solution.py:556
  30.5 1.7 %collective-permute-done.11.refs_3_ = f32[64,256]{1,0:T(8,128)S(1)} collective-permute-done((f32[64,256]{1,0:T(8,128)S(1)}, f32[64,256]{1,0:T(8,128)S(1)}, u32[]{:S(2)}, u32[]{:S(2)}) %collective-permute-start.11) | collective-permute-done | bytes 65568 | tf_op jit(solution)/shard_map/ppermute | solution.py:556
  32.2 0.6 half_sum.3
  32.8 2.4 %collective-permute-start.12 = (f32[64,256]{1,0:T(8,128)S(1)}, f32[64,256]{1,0:T(8,128)S(1)}, u32[]{:S(2)}, u32[]{:S(2)}) collective-permute-start(f32[64,256]{1,0:T(8,128)S(1)} %get-tuple-element.59.near), channel_id=1, source_target_pairs={{0,8},{2,10},{4,12},{6,14},{8,0},{10,2},{12,4},{14,6},{1,9},{3,11}... | collective-permute-start | bytes 196616 | tf_op jit(solution)/shard_map/ppermute | solution.py:556
  35.3 0.6 close.2
  35.9 0.6 collective-permute-start.5
  36.4 1.6 %collective-permute-start.6 = (f32[64,256]{1,0:T(8,128)S(1)}, f32[64,256]{1,0:T(8,128)S(1)}, u32[]{:S(2)}, u32[]{:S(2)}) collective-permute-start(f32[64,256]{1,0:T(8,128)S(1)} %get-tuple-element.48), channel_id=1, source_target_pairs={{0,4},{2,6},{4,0},{6,2},{8,12},{10,14},{12,8},{14,10},{1,5},{3,7},... | collective-permute-start | bytes 196616 | tf_op jit(solution)/shard_map/ppermute | solution.py:556
  38.1 1.4 %collective-permute-start.7 = (f32[64,256]{1,0:T(8,128)S(1)}, f32[64,256]{1,0:T(8,128)S(1)}, u32[]{:S(2)}, u32[]{:S(2)}) collective-permute-start(f32[64,256]{1,0:T(8,128)S(1)} %get-tuple-element.49), channel_id=1, source_target_pairs={{0,6},{2,4},{4,2},{6,0},{8,14},{10,12},{12,10},{14,8},{1,7},{3,5},... | collective-permute-start | bytes 196616 | tf_op jit(solution)/shard_map/ppermute | solution.py:556
  39.4 0.6 close.3
  40.0 0.6 collective-permute-start.13
  40.6 1.6 %collective-permute-start.14 = (f32[64,256]{1,0:T(8,128)S(1)}, f32[64,256]{1,0:T(8,128)S(1)}, u32[]{:S(2)}, u32[]{:S(2)}) collective-permute-start(f32[64,256]{1,0:T(8,128)S(1)} %get-tuple-element.62), channel_id=1, source_target_pairs={{0,4},{2,6},{4,0},{6,2},{8,12},{10,14},{12,8},{14,10},{1,5},{3,7},... | collective-permute-start | bytes 196616 | tf_op jit(solution)/shard_map/ppermute | solution.py:556
  42.2 1.4 %collective-permute-start.15 = (f32[64,256]{1,0:T(8,128)S(1)}, f32[64,256]{1,0:T(8,128)S(1)}, u32[]{:S(2)}, u32[]{:S(2)}) collective-permute-start(f32[64,256]{1,0:T(8,128)S(1)} %get-tuple-element.63), channel_id=1, source_target_pairs={{0,6},{2,4},{4,2},{6,0},{8,14},{10,12},{12,10},{14,8},{1,7},{3,5},... | collective-permute-start | bytes 196616 | tf_op jit(solution)/shard_map/ppermute | solution.py:556
  43.6 3.1 %inverse_first.2 = (f32[4224,128]{1,0:T(8,128)S(1)}, f32[4224,128]{1,0:T(8,128)S(1)}) custom-call(s32[2]{0:T(128)S(1)} %pad_add_fusion.place, f32[16,2,128,256]{3,2,1,0:T(8,128)S(1)} %get-tuple-element.39.modes, bf16[2,2,768,256]{3,2,1,0:T(8,128)(2,1)S(1)} %copy-done.2, f32[2,2,256,256]{3,2,1,0:T(8,128)S(1)} %copy-done.4, ...), custom_call_target="tpu_custom_call" | custom-call | flops 2147483648 | bytes 8388608 | tf_op jit(solution)/shard_map/inverse_first/pallas_call | solution.py:441
  46.7 0.1 collective-permute-start.16
  46.8 0.6 collective-permute-done.15.refs_3_
  47.4 3.3 %inverse_first.3 = (f32[4224,128]{1,0:T(8,128)S(1)}, f32[4224,128]{1,0:T(8,128)S(1)}) custom-call(s32[2]{0:T(128)S(1)} %pad_add_fusion.place, f32[16,2,128,256]{3,2,1,0:T(8,128)S(1)} %get-tuple-element.53.modes, bf16[2,2,768,256]{3,2,1,0:T(8,128)(2,1)S(1)} %copy-done.2, f32[2,2,256,256]{3,2,1,0:T(8,128)S(1)} %copy-done.4, ...), custom_call_target="tpu_custom_call" | custom-call | flops 2147483648 | bytes 8388608 | tf_op jit(solution)/shard_map/inverse_first/pallas_call | solution.py:441
  50.8 3.5 %keep_inverse.1.kept = f32[4096,256]{1,0:T(8,128)S(1)} custom-call(s32[2]{0:T(128)S(1)} %pad_add_fusion.place, bf16[2,768,256]{2,1,0:T(8,128)(2,1)S(1)} %copy-done.1, f32[4224,128]{1,0:T(8,128)S(1)} %get-tuple-element.50.refs_0_, f32[4224,128]{1,0:T(8,128)S(1)} %get-tuple-element.64.refs_1_), custom_call_target="tpu_custom_call" | custom-call | flops 2147483648 | bytes 8388608 | tf_op jit(solution)/shard_map/keep_inverse/pallas_call | solution.py:473
  54.3 0.7 %collective-permute-done.17.refs_1_ = f32[4224,128]{1,0:T(8,128)S(1)} collective-permute-done((f32[4224,128]{1,0:T(8,128)S(1)}, f32[4224,128]{1,0:T(8,128)S(1)}, u32[]{:S(2)}, u32[]{:S(2)}) %collective-permute-start.17) | collective-permute-done | bytes 2162720 | tf_op jit(solution)/shard_map/ppermute | solution.py:551
  55.0 6.2 %inverse_second.1 = f32[256,16,512]{2,1,0:T(8,128)} custom-call(s32[2]{0:T(128)S(1)} %pad_add_fusion.place, bf16[2,768,256]{2,1,0:T(8,128)(2,1)S(1)} %copy-done.1, f32[4096,256]{1,0:T(8,128)S(1)} %keep_inverse.1.kept, f32[4224,128]{1,0:T(8,128)S(1)} %collective-permute-done.16.refs_0_, f32[4224,128]{1,0:T(8,128)S(1)} %collective-permute-done.17.refs_1_), custom_call_target="tpu_custom_call" | custom-call | flops 4294967296 | bytes 8388608 | tf_op jit(solution)/shard_map/inverse_second/pallas_call | solution.py:537
  (29 shorter events, 0.1 us)
Async XLA Ops:
  0.1 8.4 %copy-start.5 = (bf16[2,768,256]{2,1,0:T(8,128)(2,1)S(1)}, bf16[2,768,256]{2,1,0:T(8,128)(2,1)}, u32[]{:S(2)}) copy-start(bf16[2,768,256]{2,1,0:T(8,128)(2,1)} %constant.23.clone.tables) | copy-start | bytes 2359300
  7.9 4.6 %collective-permute-start = (f32[4488,128]{1,0:T(8,128)S(1)}, f32[4488,128]{1,0:T(8,128)S(1)}, u32[]{:S(2)}, u32[]{:S(2)}) collective-permute-start(f32[4488,128]{1,0:T(8,128)S(1)} %get-tuple-element.38), channel_id=1, source_target_pairs={{0,1},{1,0},{2,3},{3,2},{4,5},{5,4},{6,7},{7,6},{8,9},{9,8},{10,11... | collective-permute-start | bytes 6893576 | tf_op jit(solution)/shard_map/ppermute | solution.py:551
  8.4 11.7 %collective-permute-start.8 = (f32[4488,128]{1,0:T(8,128)S(1)}, f32[4488,128]{1,0:T(8,128)S(1)}, u32[]{:S(2)}, u32[]{:S(2)}) collective-permute-start(f32[4488,128]{1,0:T(8,128)S(1)} %get-tuple-element.52), channel_id=1, source_target_pairs={{0,1},{1,0},{2,3},{3,2},{4,5},{5,4},{6,7},{7,6},{8,9},{9,8},{10,11... | collective-permute-start | bytes 6893576 | tf_op jit(solution)/shard_map/ppermute | solution.py:551
  8.5 4.0 %copy-start.3 = (bf16[2,2,768,256]{3,2,1,0:T(8,128)(2,1)S(1)}, bf16[2,2,768,256]{3,2,1,0:T(8,128)(2,1)}, u32[]{:S(2)}) copy-start(bf16[2,2,768,256]{3,2,1,0:T(8,128)(2,1)} %constant.21.clone.table) | copy-start | bytes 4718596
  8.5 4.0 %copy-start.4 = (f32[2,2,256,256]{3,2,1,0:T(8,128)S(1)}, f32[2,2,256,256]{3,2,1,0:T(8,128)}, u32[]{:S(2)}) copy-start(f32[2,2,256,256]{3,2,1,0:T(8,128)} %constant.22.clone.decay) | copy-start | bytes 3145732
  15.6 11.2 %collective-permute-start.1 = (f32[64,256]{1,0:T(8,128)S(1)}, f32[64,256]{1,0:T(8,128)S(1)}, u32[]{:S(2)}, u32[]{:S(2)}) collective-permute-start(f32[64,256]{1,0:T(8,128)S(1)} %get-tuple-element.41), channel_id=1, source_target_pairs={{0,2},{2,0},{4,6},{6,4},{8,10},{10,8},{12,14},{14,12},{1,3},{3,1},... | collective-permute-start | bytes 196616 | tf_op jit(solution)/shard_map/ppermute | solution.py:556
  18.6 8.3 %collective-permute-start.2 = (f32[64,256]{1,0:T(8,128)S(1)}, f32[64,256]{1,0:T(8,128)S(1)}, u32[]{:S(2)}, u32[]{:S(2)}) collective-permute-start(f32[64,256]{1,0:T(8,128)S(1)} %get-tuple-element.42), channel_id=1, source_target_pairs={{0,4},{2,6},{4,0},{6,2},{8,12},{10,14},{12,8},{14,10},{1,5},{3,7},... | collective-permute-start | bytes 196616 | tf_op jit(solution)/shard_map/ppermute | solution.py:556
  20.2 6.7 %collective-permute-start.3 = (f32[64,256]{1,0:T(8,128)S(1)}, f32[64,256]{1,0:T(8,128)S(1)}, u32[]{:S(2)}, u32[]{:S(2)}) collective-permute-start(f32[64,256]{1,0:T(8,128)S(1)} %get-tuple-element.43), channel_id=1, source_target_pairs={{0,6},{2,4},{4,2},{6,0},{8,14},{10,12},{12,10},{14,8},{1,7},{3,5},... | collective-permute-start | bytes 196616 | tf_op jit(solution)/shard_map/ppermute | solution.py:556
  20.2 6.7 %copy-start = (f32[2,2,3,256,256]{4,3,2,1,0:T(8,128)S(1)}, f32[2,2,3,256,256]{4,3,2,1,0:T(8,128)}, u32[]{:S(2)}) copy-start(f32[2,2,3,256,256]{4,3,2,1,0:T(8,128)} %constant.20.clone.closing) | copy-start | bytes 9437188
  23.3 7.2 %collective-permute-start.9 = (f32[64,256]{1,0:T(8,128)S(1)}, f32[64,256]{1,0:T(8,128)S(1)}, u32[]{:S(2)}, u32[]{:S(2)}) collective-permute-start(f32[64,256]{1,0:T(8,128)S(1)} %get-tuple-element.55), channel_id=1, source_target_pairs={{0,2},{2,0},{4,6},{6,4},{8,10},{10,8},{12,14},{14,12},{1,3},{3,1},... | collective-permute-start | bytes 196616 | tf_op jit(solution)/shard_map/ppermute | solution.py:556
  25.3 5.2 %collective-permute-start.10 = (f32[64,256]{1,0:T(8,128)S(1)}, f32[64,256]{1,0:T(8,128)S(1)}, u32[]{:S(2)}, u32[]{:S(2)}) collective-permute-start(f32[64,256]{1,0:T(8,128)S(1)} %get-tuple-element.56), channel_id=1, source_target_pairs={{0,4},{2,6},{4,0},{6,2},{8,12},{10,14},{12,8},{14,10},{1,5},{3,7},... | collective-permute-start | bytes 196616 | tf_op jit(solution)/shard_map/ppermute | solution.py:556
  26.9 5.4 %collective-permute-start.11 = (f32[64,256]{1,0:T(8,128)S(1)}, f32[64,256]{1,0:T(8,128)S(1)}, u32[]{:S(2)}, u32[]{:S(2)}) collective-permute-start(f32[64,256]{1,0:T(8,128)S(1)} %get-tuple-element.57), channel_id=1, source_target_pairs={{0,6},{2,4},{4,2},{6,0},{8,14},{10,12},{12,10},{14,8},{1,7},{3,5},... | collective-permute-start | bytes 196616 | tf_op jit(solution)/shard_map/ppermute | solution.py:556
  27.5 7.8 %collective-permute-start.4 = (f32[64,256]{1,0:T(8,128)S(1)}, f32[64,256]{1,0:T(8,128)S(1)}, u32[]{:S(2)}, u32[]{:S(2)}) collective-permute-start(f32[64,256]{1,0:T(8,128)S(1)} %get-tuple-element.45.near), channel_id=1, source_target_pairs={{0,8},{2,10},{4,12},{6,14},{8,0},{10,2},{12,4},{14,6},{1,9},{3,11}... | collective-permute-start | bytes 196616 | tf_op jit(solution)/shard_map/ppermute | solution.py:556
  32.8 6.6 %collective-permute-start.12 = (f32[64,256]{1,0:T(8,128)S(1)}, f32[64,256]{1,0:T(8,128)S(1)}, u32[]{:S(2)}, u32[]{:S(2)}) collective-permute-start(f32[64,256]{1,0:T(8,128)S(1)} %get-tuple-element.59.near), channel_id=1, source_target_pairs={{0,8},{2,10},{4,12},{6,14},{8,0},{10,2},{12,4},{14,6},{1,9},{3,11}... | collective-permute-start | bytes 196616 | tf_op jit(solution)/shard_map/ppermute | solution.py:556
  35.9 7.7 %copy-start.2 = (bf16[2,2,768,256]{3,2,1,0:T(8,128)(2,1)S(1)}, bf16[2,2,768,256]{3,2,1,0:T(8,128)(2,1)}, u32[]{:S(2)}) copy-start(bf16[2,2,768,256]{3,2,1,0:T(8,128)(2,1)} %constant.24.clone.table) | copy-start | bytes 4718596
  35.9 6.4 %collective-permute-start.5 = (f32[64,256]{1,0:T(8,128)S(1)}, f32[64,256]{1,0:T(8,128)S(1)}, u32[]{:S(2)}, u32[]{:S(2)}) collective-permute-start(f32[64,256]{1,0:T(8,128)S(1)} %get-tuple-element.47), channel_id=1, source_target_pairs={{0,2},{2,0},{4,6},{6,4},{8,10},{10,8},{12,14},{14,12},{1,3},{3,1},... | collective-permute-start | bytes 196616 | tf_op jit(solution)/shard_map/ppermute | solution.py:556
  36.4 7.2 %collective-permute-start.6 = (f32[64,256]{1,0:T(8,128)S(1)}, f32[64,256]{1,0:T(8,128)S(1)}, u32[]{:S(2)}, u32[]{:S(2)}) collective-permute-start(f32[64,256]{1,0:T(8,128)S(1)} %get-tuple-element.48), channel_id=1, source_target_pairs={{0,4},{2,6},{4,0},{6,2},{8,12},{10,14},{12,8},{14,10},{1,5},{3,7},... | collective-permute-start | bytes 196616 | tf_op jit(solution)/shard_map/ppermute | solution.py:556
  38.1 5.5 %collective-permute-start.7 = (f32[64,256]{1,0:T(8,128)S(1)}, f32[64,256]{1,0:T(8,128)S(1)}, u32[]{:S(2)}, u32[]{:S(2)}) collective-permute-start(f32[64,256]{1,0:T(8,128)S(1)} %get-tuple-element.49), channel_id=1, source_target_pairs={{0,6},{2,4},{4,2},{6,0},{8,14},{10,12},{12,10},{14,8},{1,7},{3,5},... | collective-permute-start | bytes 196616 | tf_op jit(solution)/shard_map/ppermute | solution.py:556
  40.0 6.7 %collective-permute-start.13 = (f32[64,256]{1,0:T(8,128)S(1)}, f32[64,256]{1,0:T(8,128)S(1)}, u32[]{:S(2)}, u32[]{:S(2)}) collective-permute-start(f32[64,256]{1,0:T(8,128)S(1)} %get-tuple-element.61), channel_id=1, source_target_pairs={{0,2},{2,0},{4,6},{6,4},{8,10},{10,8},{12,14},{14,12},{1,3},{3,1},... | collective-permute-start | bytes 196616 | tf_op jit(solution)/shard_map/ppermute | solution.py:556
  40.6 6.2 %collective-permute-start.14 = (f32[64,256]{1,0:T(8,128)S(1)}, f32[64,256]{1,0:T(8,128)S(1)}, u32[]{:S(2)}, u32[]{:S(2)}) collective-permute-start(f32[64,256]{1,0:T(8,128)S(1)} %get-tuple-element.62), channel_id=1, source_target_pairs={{0,4},{2,6},{4,0},{6,2},{8,12},{10,14},{12,8},{14,10},{1,5},{3,7},... | collective-permute-start | bytes 196616 | tf_op jit(solution)/shard_map/ppermute | solution.py:556
  42.2 5.2 %collective-permute-start.15 = (f32[64,256]{1,0:T(8,128)S(1)}, f32[64,256]{1,0:T(8,128)S(1)}, u32[]{:S(2)}, u32[]{:S(2)}) collective-permute-start(f32[64,256]{1,0:T(8,128)S(1)} %get-tuple-element.63), channel_id=1, source_target_pairs={{0,6},{2,4},{4,2},{6,0},{8,14},{10,12},{12,10},{14,8},{1,7},{3,5},... | collective-permute-start | bytes 196616 | tf_op jit(solution)/shard_map/ppermute | solution.py:556
  46.7 7.6 %collective-permute-start.16 = (f32[4224,128]{1,0:T(8,128)S(1)}, f32[4224,128]{1,0:T(8,128)S(1)}, u32[]{:S(2)}, u32[]{:S(2)}) collective-permute-start(f32[4224,128]{1,0:T(8,128)S(1)} %get-tuple-element.65), channel_id=1, source_target_pairs={{0,1},{1,0},{2,3},{3,2},{4,5},{5,4},{6,7},{7,6},{8,9},{9,8},{10,11... | collective-permute-start | bytes 6488072 | tf_op jit(solution)/shard_map/ppermute | solution.py:551
  47.4 3.4 %copy-start.1 = (bf16[2,768,256]{2,1,0:T(8,128)(2,1)S(1)}, bf16[2,768,256]{2,1,0:T(8,128)(2,1)}, u32[]{:S(2)}) copy-start(bf16[2,768,256]{2,1,0:T(8,128)(2,1)} %constant.25.clone.tables) | copy-start | bytes 2359300
  50.7 4.3 %collective-permute-start.17 = (f32[4224,128]{1,0:T(8,128)S(1)}, f32[4224,128]{1,0:T(8,128)S(1)}, u32[]{:S(2)}, u32[]{:S(2)}) collective-permute-start(f32[4224,128]{1,0:T(8,128)S(1)} %get-tuple-element.66), channel_id=1, source_target_pairs={{0,1},{1,0},{2,3},{3,2},{4,5},{5,4},{6,7},{7,6},{8,9},{9,8},{10,11... | collective-permute-start | bytes 6488072 | tf_op jit(solution)/shard_map/ppermute | solution.py:551

commit v13 on v9

--- a/solution.py
+++ b/solution.py
@@ -13,7 +13,6 @@
 DIFFUSION = 2.0
 REACTION_STEP = 0.5
 VMEM_BYTES = 24 * 1024 * 1024
-LANES = 128
 SUBLANES = 8
 TILE = 16
 CHUNKS = 2
@@ -29,8 +28,8 @@
 
 
 def second_tables(width):
-    half = width // 2
-    return np.stack([sine_table(np.arange(half), np.arange(s, width, 2), width) for s in (0, 1)])
+    cells = np.arange(width)
+    return np.stack([sine_table(cells, np.arange(s, width, 2), width) for s in (0, 1)])
 
 
 def first_tables(total):
@@ -63,21 +62,17 @@
 
 
 def store_split(ref, at, lane, block):
-    depth = ref.shape[-1] // 3
+    depth = ref.shape[-1] // 2
     width = block.shape[-1]
     high = block.astype(jnp.bfloat16)
     low = (block - high.astype(jnp.float32)).astype(jnp.bfloat16)
-    for part, value in enumerate((high, low, high)):
-        ref[(*at, pl.ds(part * depth + lane, width))] = value
-
-
-def dot(first, second):
-    return jnp.dot(first, second, preferred_element_type=jnp.float32)
-
-
-def lanes_reversed(block):
-    index = LANES - 1 - lax.broadcasted_iota(jnp.int32, (block.shape[0], LANES), 1)
-    return jnp.take_along_axis(block, index, axis=1, mode="promise_in_bounds")
+    ref[(*at, pl.ds(lane, width))] = high
+    ref[(*at, pl.ds(depth + lane, width))] = low
+
+
+def dot(split, table):
+    rows = jnp.concatenate([split, split[:, : split.shape[1] // 2]], axis=1)
+    return jnp.dot(rows, table, preferred_element_type=jnp.float32)
 
 
 def store_rows_reversed(ref, start, block):
@@ -134,96 +129,73 @@
     )
 
 
-def forward_second_kernel(place, field, initial, table, sums, *refs):
-    sends, scratch = refs[:CHUNKS], refs[CHUNKS:]
+def forward_second_kernel(place, field, initial, table, split, *sends):
     rows, steps, width = field.shape
-    half = width // 2
-    part = half // CHUNKS
-    piece = rows // len(scratch)
+    part = width // 2 // CHUNKS
+    piece = rows // 2
     group = max(TILE // steps, 1)
     block, blocks = pl.program_id(0), pl.num_programs(0)
     total = rows * blocks
     pitch = sends[0].shape[0] // (steps + 1)
     body = piece * steps
     is_first = place[0] == 0
-    sign = 1.0 - 2.0 * place[1].astype(jnp.float32)
-
-    def put(other, at, sums_at, cells):
-        lower = cells[:, :half]
-        upper = sign * jnp.concatenate(
-            [lanes_reversed(cells[:, lane : lane + LANES]) for lane in range(half, width, LANES)][::-1],
-            axis=1,
-        )
-        sums[pl.ds(sums_at, TILE), :] = lower + upper
-        store_split(other, (pl.ds(at, TILE),), 0, lower - upper)
-
-    def prepare(sub):
-        kept_at = pl.multiple_of(block * rows + sub * piece, piece)
-        kept_base = pl.multiple_of(kept_at * steps, body)
+
+    def send_ends():
+        sent = dot(split[pl.ds(total * steps, total)], table[0])
+        for chunk, send in enumerate(sends):
+            lanes = slice(chunk * part, (chunk + 1) * part)
+            store_rows_reversed(send, pitch * steps, sent[:, lanes])
+
+    for sub in range(2):
+        cell = pl.multiple_of(block * rows + sub * piece, piece)
+        start = pl.multiple_of(cell * steps, body)
         for row in range(0, piece, group):
             cells = field[pl.ds(sub * piece + row, group)]
             force = cells - cells * cells * cells
-            put(scratch[sub], row * steps, kept_base + row * steps, force.reshape(TILE, width))
+            store_split(split, (pl.ds(start + row * steps, TILE),), 0, force.reshape(TILE, width))
         for row in range(0, piece, TILE):
             at = pl.ds(sub * piece + row, TILE)
             ends = jnp.where(is_first, initial[at], field[at, steps - 1, :])
-            put(scratch[sub], body + row, total * steps + kept_at + row, ends)
-
-    def transform(sub, block):
-        sent = dot(scratch[sub][...], table[0])
-        sent_at = pl.multiple_of(total - block * rows - (sub + 1) * piece, piece)
+            store_split(split, (pl.ds(total * steps + cell + row, TILE),), 0, ends)
+        sent = dot(split[pl.ds(start, body)], table[0])
         for chunk, send in enumerate(sends):
             lanes = slice(chunk * part, (chunk + 1) * part)
             for row in range(piece):
                 line = sent[row * steps : (row + 1) * steps, lanes]
-                send[pl.ds(sent_at + piece - 1 - row, steps, stride=pitch), :] = line
-            store_rows_reversed(send, pitch * steps + sent_at, sent[body:, lanes])
-
-    last = len(scratch) - 1
-    transform(last, jnp.maximum(block - 1, 0))
-    for sub in range(last):
-        prepare(sub)
-        transform(sub, block)
-    prepare(last)
-
-    @pl.when(block == blocks - 1)
-    def _():
-        transform(last, block)
+                send[pl.ds(total - 1 - cell - row, steps, stride=pitch), :] = line
+
+    pl.when(block == blocks - 1)(send_ends)
 
 
 def forward_second(place, field, initial, tables):
     rows, steps, width = field.shape
     half = width // 2
-    block, pieces = min(64, rows), 2
-    depth = (steps + 1) * block // pieces
+    block = min(64, rows)
     outs = call(
         forward_second_kernel,
         "forward_second",
         [
             pl.BlockSpec((block, steps, width), lambda i, place: (i, 0, 0)),
             pl.BlockSpec((block, width), lambda i, place: (i, 0)),
-            pl.BlockSpec((1, 3 * half, half), lambda i, place: (1 - place[1], 0, 0)),
+            pl.BlockSpec((1, 3 * width, half), lambda i, place: (1 - place[1], 0, 0)),
         ],
         [IN_VMEM] * (1 + CHUNKS),
-        [floats((steps + 1) * rows, half)]
+        [jax.ShapeDtypeStruct(((steps + 1) * rows, 2 * width), jnp.bfloat16)]
         + [floats((steps + 1) * pitch_of(rows), half // CHUNKS)] * CHUNKS,
-        [pltpu.VMEM((depth, 3 * half), jnp.bfloat16)] * pieces,
+        [],
         1 << 32,
         rows // block,
     )(place, in_hbm(field), in_hbm(initial), in_hbm(tables))
     return outs[0], outs[1:]
 
 
-def keep_second_kernel(steps, place, tables, sums, *refs):
-    keeps, scratch = refs[:CHUNKS], refs[CHUNKS:]
-    depth = scratch[0].shape[0]
-    cells = sums.shape[0] // (steps + 1)
+def keep_second_kernel(steps, place, tables, split, *keeps):
+    rows = split.shape[0]
+    depth = rows // 8
+    cells = rows // (steps + 1)
     pitch = keeps[0].shape[0] // (steps + 1)
-    for at in range(0, sums.shape[0], depth):
-        split = scratch[at // depth % 2]
-        for row in range(0, depth, TILE):
-            store_split(split, (pl.ds(row, TILE),), 0, sums[pl.ds(at + row, TILE)])
-        result = dot(split[...], tables[place[1]])
+    for at in range(0, rows, depth):
+        result = dot(split[pl.ds(at, depth)], tables[place[1]])
         for chunk, keep in enumerate(keeps):
             part = keep.shape[1]
             lanes = slice(chunk * part, (chunk + 1) * part)
@@ -236,18 +208,18 @@
                 keep[ends, :] = result[body:, lanes]
 
 
-def keep_second(place, sums, tables, steps):
-    rows, half = sums.shape
-    shape = ((steps + 1) * pitch_of(rows // (steps + 1)), half // CHUNKS)
+def keep_second(place, split, tables, steps):
+    rows = split.shape[0]
+    shape = ((steps + 1) * pitch_of(rows // (steps + 1)), tables.shape[2] // CHUNKS)
     return call(
         functools.partial(keep_second_kernel, steps),
         "keep_second",
         [IN_VMEM] * 2,
         [IN_VMEM] * CHUNKS,
         [floats(*shape)] * CHUNKS,
-        [pltpu.VMEM((rows // 8, 3 * half), jnp.bfloat16)] * 2,
+        [],
         1 << 31,
-    )(place, tables, sums)
+    )(place, tables, split)
 
 
 def ranks(slabs):
@@ -311,8 +283,8 @@
         [floats(steps, 2, part, rows)] + [floats(share, rows)] * size,
         [
             pltpu.VMEM((2 * part, rows), jnp.float32),
-            pltpu.VMEM((2, block * part, 3 * rows), jnp.bfloat16),
-            pltpu.VMEM((2, part, 3 * rows), jnp.bfloat16),
+            pltpu.VMEM((2, block * part, 2 * rows), jnp.bfloat16),
+            pltpu.VMEM((2, part, 2 * rows), jnp.bfloat16),
             pltpu.VMEM((2, part, rows), jnp.float32),
         ],
         1 << 31,
@@ -421,7 +393,7 @@
         [floats(steps * pitch_of(rows), part)] * 2,
         [
             pltpu.VMEM((2 * part, rows), jnp.float32),
-            pltpu.VMEM((2, block * part, 3 * rows), jnp.bfloat16),
+            pltpu.VMEM((2, block * part, 2 * rows), jnp.bfloat16),
         ],
         1 << 31,
     )(place, modes, tables, decays, *befores)
@@ -450,8 +422,8 @@
         "keep_inverse",
         [IN_VMEM] * (1 + CHUNKS),
         IN_VMEM,
-        floats(rows * steps, half),
-        [pltpu.VMEM((rows * steps // 8, 3 * half), jnp.bfloat16)] * 2,
+        floats(rows * steps, 2 * half),
+        [pltpu.VMEM((rows * steps // 8, 2 * half), jnp.bfloat16)] * 2,
         1 << 31,
     )(place, tables, *keeps)
 
@@ -459,51 +431,34 @@
 def inverse_second_kernel(place, tables, kept, *refs):
     gots, out, scratch = refs[:CHUNKS], refs[CHUNKS], refs[CHUNKS + 1 :]
     rows, steps, width = out.shape
-    half = width // 2
-    part = half // CHUNKS
+    part = width // 2 // CHUNKS
     pitch = gots[0].shape[0] // steps
-    count = len(scratch) // 2
-    piece = rows // count
+    piece = rows // len(scratch)
     group = max(TILE // steps, 1)
-    strip = place[1]
-    sign = 1.0 - 2.0 * strip.astype(jnp.float32)
     total = rows * pl.num_programs(0)
     start = pl.program_id(0) * rows
-    for sub in range(count):
-        split, result = scratch[2 * sub : 2 * sub + 2]
+    for sub, split in enumerate(scratch):
         base = start + sub * piece
         for row in range(0, piece, group):
             mirrors = [total - 1 - base - row - at for at in range(group)]
             for chunk, got in enumerate(gots):
                 cells = steps_of(got, mirrors, steps, pitch)
                 store_split(split, (pl.ds(row * steps, TILE),), chunk * part, cells)
-        result[...] = dot(split[...], tables[1 - strip])
-    for sub in range(count):
-        result = scratch[2 * sub + 1]
-        kept_base = pl.multiple_of((start + sub * piece) * steps, piece * steps)
-        for row in range(0, piece, group):
-            first = kept[pl.ds(kept_base + row * steps, TILE)]
-            second = result[pl.ds(row * steps, TILE)]
-            upper = sign * (first - second)
-            parts = [
-                lanes_reversed(upper[:, lane : lane + LANES]) for lane in range(0, half, LANES)
-            ][::-1]
-            whole = jnp.concatenate([first + second, *parts], axis=1)
-            out[pl.ds(sub * piece + row, group)] = whole.reshape(group, TILE // group, width)
+        kept_at = pl.ds(pl.multiple_of(base * steps, piece * steps), piece * steps)
+        whole = kept[kept_at] + dot(split[...], tables[1 - place[1]])
+        out[pl.ds(sub * piece, piece)] = whole.reshape(piece, steps, width)
 
 
 def inverse_second(place, kept, gots, tables, steps):
-    rows, half = kept.shape[0] // steps, kept.shape[1]
+    rows, width = kept.shape[0] // steps, kept.shape[1]
     block, pieces = min(64, rows), 2
-    depth = steps * block // pieces
     return call(
         inverse_second_kernel,
         "inverse_second",
         [IN_VMEM] * (2 + CHUNKS),
-        pl.BlockSpec((block, steps, 2 * half), lambda i, place: (i, 0, 0)),
-        floats(rows, steps, 2 * half),
-        [pltpu.VMEM((depth, 3 * half), jnp.bfloat16), pltpu.VMEM((depth, half), jnp.float32)]
-        * pieces,
+        pl.BlockSpec((block, steps, width), lambda i, place: (i, 0, 0)),
+        floats(rows, steps, width),
+        [pltpu.VMEM((steps * block // pieces, width), jnp.bfloat16)] * pieces,
         1 << 32,
         rows // block,
     )(place, tables, kept, *gots)
@@ -544,9 +499,9 @@
     )
     first_table, decays = split_constant(first), constant(decay)
     second_table = split_constant(REACTION_STEP * second)
-    sums, sends = forward_second(place, iterate, initial, second_table)
+    split, sends = forward_second(place, iterate, initial, second_table)
     gots = [swapped(send) for send in sends]
-    keeps = keep_second(place, sums, second_table, steps)
+    keeps = keep_second(place, split, second_table, steps)
     modes, befores = [], []
     for chunk in range(CHUNKS):
         own_modes, lasts = forward_first(

time: 60.5 us -> 64.5 us (1.066)
  Pallas kernels: 34.5 us -> 40.3 us
  waiting for transfers between devices: 4.32 us -> 2.34 us
    pallas_call x1, Pallas kernels: 6.95 us -> 9.17 us  [forward_second(): call(forward_second_kernel, 'forward_second', [pl.BlockSpec((block, steps...]
    ppermute x4, waiting for transfers between devices: 1.88 us -> 0.01 us  [swapped(): return lax.ppermute(block, 'space', [(0, 1), (1, 0)])]
    pallas_call x1, Pallas kernels: 2.68 us -> 4.5 us  [keep_second(): call(functools.partial(keep_second_kernel, steps), 'keep_second', [IN_VME...]
    pallas_call x1, Pallas kernels: 3.64 us -> 4.73 us  [keep_inverse(): call(functools.partial(keep_inverse_kernel, steps), 'keep_inverse', [IN_V...]
  transfers between devices with their start and end apart: 18 -> 18, of which waited for: 4 -> 2; matrix products, arithmetic and copies ran while one was open for 0% -> 0% of each run, Pallas kernels for 35% -> 38%
where the time goes in v13:
time: 64.5 us; the launch traced here: 64.4 us
  Pallas kernels  40.3 us (62%)
  starting transfers between devices  21.4 us (33%)
  waiting for transfers between devices  2.34 us (4%)
    ppermute x14, starting transfers between devices, with_partner(): lax.ppermute(block, 'tm', [(slab, slab ^ distance) for slab in range(slab...  20.2 us
    pallas_call x1, Pallas kernels, forward_second(): call(forward_second_kernel, 'forward_second', [pl.BlockSpec((block, steps...  9.17 us
    pallas_call x2, Pallas kernels, inverse_first(): call(functools.partial(inverse_first_kernel, slabs, chunk), 'inverse_firs...  6.62 us
    pallas_call x1, Pallas kernels, inverse_second(): call(inverse_second_kernel, 'inverse_second', [IN_VMEM] * (2 + CHUNKS), p...  6.61 us
    pallas_call x2, Pallas kernels, forward_first(): call(functools.partial(forward_first_kernel, slabs, chunk), 'forward_firs...  6.34 us
    pallas_call x1, Pallas kernels, keep_inverse(): call(functools.partial(keep_inverse_kernel, steps), 'keep_inverse', [IN_V...  4.73 us
    pallas_call x1, Pallas kernels, keep_second(): call(functools.partial(keep_second_kernel, steps), 'keep_second', [IN_VME...  4.5 us
    ppermute x14, waiting for transfers between devices, with_partner(): lax.ppermute(block, 'tm', [(slab, slab ^ distance) for slab in range(slab...  2.33 us
  transfers between devices with their start and end apart: 18, of which 2 were waited for; matrix products, arithmetic and copies ran while one was open for 0% of the time, Pallas kernels for 38%

profile of v13, /device:TPU:0, one launch (start us, length us, event | category | flops | bytes accessed | tf_op | source)
XLA Modules:
  0.0 64.4 jit_solution(17165560771598434171)
XLA Ops:
  0.0 0.1 pad_add_fusion.place
  0.1 9.2 %forward_second.1 = (bf16[4352,1024]{1,0:T(8,128)(2,1)S(1)}, f32[4488,128]{1,0:T(8,128)S(1)}, f32[4488,128]{1,0:T(8,128)S(1)}) custom-call(s32[2]{0:T(128)S(1)} %pad_add_fusion.place, f32[256,16,512]{2,1,0:T(8,128)} %field.1, f32[256,512]{1,0:T(8,128)} %initial.1, bf16[2,1536,256]{2,1,0:T(8,128)(2,1)} %constant.23.clone.table.tables), custom_call_target="tpu_custom_call" | custom-call | flops 4294967296 | bytes 8388608 | tf_op jit(solution)/shard_map/forward_second/pallas_call | solution.py:174
  9.3 0.9 %collective-permute-start = (f32[4488,128]{1,0:T(8,128)S(1)}, f32[4488,128]{1,0:T(8,128)S(1)}, u32[]{:S(2)}, u32[]{:S(2)}) collective-permute-start(f32[4488,128]{1,0:T(8,128)S(1)} %get-tuple-element.38), channel_id=1, source_target_pairs={{0,1},{1,0},{2,3},{3,2},{4,5},{5,4},{6,7},{7,6},{8,9},{9,8},{10,11... | collective-permute-start | bytes 6893576 | tf_op jit(solution)/shard_map/ppermute | solution.py:468
  10.2 0.1 collective-permute-start.8
  10.3 4.5 %keep_second.1 = (f32[4488,128]{1,0:T(8,128)S(1)}, f32[4488,128]{1,0:T(8,128)S(1)}) custom-call(s32[2]{0:T(128)S(1)} %pad_add_fusion.place, bf16[2,1536,256]{2,1,0:T(8,128)(2,1)S(1)} %copy-done.2, bf16[4352,1024]{1,0:T(8,128)(2,1)S(1)} %get-tuple-element.36.split), custom_call_target="tpu_custom_call" | custom-call | flops 2147483648 | bytes 8388608 | tf_op jit(solution)/shard_map/keep_second/pallas_call | solution.py:214
  14.8 3.1 %forward_first.2 = (f32[16,2,128,256]{3,2,1,0:T(8,128)S(1)}, f32[64,256]{1,0:T(8,128)S(1)}, f32[64,256]{1,0:T(8,128)S(1)}, f32[64,256]{1,0:T(8,128)S(1)}, f32[64,256]{1,0:T(8,128)S(1)}) custom-call(s32[2]{0:T(128)S(1)} %pad_add_fusion.place, f32[4488,128]{1,0:T(8,128)S(1)} %get-tuple-element.37.keep, f32[4488,128]{1,0:T(8,128)S(1)} %collective-permute-done.got, ...), custom_call_target="tpu_custom_call" | custom-call | flops 2147483648 | bytes 8388608 | tf_op jit(solution)/shard_map/forward_first/pallas_call | solution.py:278
  18.0 2.6 %collective-permute-start.1 = (f32[64,256]{1,0:T(8,128)S(1)}, f32[64,256]{1,0:T(8,128)S(1)}, u32[]{:S(2)}, u32[]{:S(2)}) collective-permute-start(f32[64,256]{1,0:T(8,128)S(1)} %get-tuple-element.41), channel_id=1, source_target_pairs={{0,2},{2,0},{4,6},{6,4},{8,10},{10,8},{12,14},{14,12},{1,3},{3,1},... | collective-permute-start | bytes 196616 | tf_op jit(solution)/shard_map/ppermute | solution.py:473
  20.6 1.6 %collective-permute-start.2 = (f32[64,256]{1,0:T(8,128)S(1)}, f32[64,256]{1,0:T(8,128)S(1)}, u32[]{:S(2)}, u32[]{:S(2)}) collective-permute-start(f32[64,256]{1,0:T(8,128)S(1)} %get-tuple-element.42), channel_id=1, source_target_pairs={{0,4},{2,6},{4,0},{6,2},{8,12},{10,14},{12,8},{14,10},{1,5},{3,7},... | collective-permute-start | bytes 196616 | tf_op jit(solution)/shard_map/ppermute | solution.py:473
  22.2 3.2 %forward_first.3 = (f32[16,2,128,256]{3,2,1,0:T(8,128)S(1)}, f32[64,256]{1,0:T(8,128)S(1)}, f32[64,256]{1,0:T(8,128)S(1)}, f32[64,256]{1,0:T(8,128)S(1)}, f32[64,256]{1,0:T(8,128)S(1)}) custom-call(s32[2]{0:T(128)S(1)} %pad_add_fusion.place, f32[4488,128]{1,0:T(8,128)S(1)} %get-tuple-element.51.keep, f32[4488,128]{1,0:T(8,128)S(1)} %collective-permute-done.8.got, ...), custom_call_target="tpu_custom_call" | custom-call | flops 2147483648 | bytes 8388608 | tf_op jit(solution)/shard_map/forward_first/pallas_call | solution.py:278
  25.4 2.0 %collective-permute-start.9 = (f32[64,256]{1,0:T(8,128)S(1)}, f32[64,256]{1,0:T(8,128)S(1)}, u32[]{:S(2)}, u32[]{:S(2)}) collective-permute-start(f32[64,256]{1,0:T(8,128)S(1)} %get-tuple-element.55), channel_id=1, source_target_pairs={{0,2},{2,0},{4,6},{6,4},{8,10},{10,8},{12,14},{14,12},{1,3},{3,1},... | collective-permute-start | bytes 196616 | tf_op jit(solution)/shard_map/ppermute | solution.py:473
  27.3 1.6 %collective-permute-start.10 = (f32[64,256]{1,0:T(8,128)S(1)}, f32[64,256]{1,0:T(8,128)S(1)}, u32[]{:S(2)}, u32[]{:S(2)}) collective-permute-start(f32[64,256]{1,0:T(8,128)S(1)} %get-tuple-element.56), channel_id=1, source_target_pairs={{0,4},{2,6},{4,0},{6,2},{8,12},{10,14},{12,8},{14,10},{1,5},{3,7},... | collective-permute-start | bytes 196616 | tf_op jit(solution)/shard_map/ppermute | solution.py:473
  28.9 0.0 collective-permute-start.11
  28.9 0.6 half_sum.2
  29.5 3.0 %collective-permute-start.4 = (f32[64,256]{1,0:T(8,128)S(1)}, f32[64,256]{1,0:T(8,128)S(1)}, u32[]{:S(2)}, u32[]{:S(2)}) collective-permute-start(f32[64,256]{1,0:T(8,128)S(1)} %get-tuple-element.45.near), channel_id=1, source_target_pairs={{0,8},{2,10},{4,12},{6,14},{8,0},{10,2},{12,4},{14,6},{1,9},{3,11}... | collective-permute-start | bytes 196616 | tf_op jit(solution)/shard_map/ppermute | solution.py:473
  32.6 1.8 %collective-permute-done.11.refs_3_ = f32[64,256]{1,0:T(8,128)S(1)} collective-permute-done((f32[64,256]{1,0:T(8,128)S(1)}, f32[64,256]{1,0:T(8,128)S(1)}, u32[]{:S(2)}, u32[]{:S(2)}) %collective-permute-start.11) | collective-permute-done | bytes 65568 | tf_op jit(solution)/shard_map/ppermute | solution.py:473
  34.4 0.6 half_sum.3
  35.0 2.3 %collective-permute-start.12 = (f32[64,256]{1,0:T(8,128)S(1)}, f32[64,256]{1,0:T(8,128)S(1)}, u32[]{:S(2)}, u32[]{:S(2)}) collective-permute-start(f32[64,256]{1,0:T(8,128)S(1)} %get-tuple-element.59.near), channel_id=1, source_target_pairs={{0,8},{2,10},{4,12},{6,14},{8,0},{10,2},{12,4},{14,6},{1,9},{3,11}... | collective-permute-start | bytes 196616 | tf_op jit(solution)/shard_map/ppermute | solution.py:473
  37.3 0.6 close.2
  38.0 0.6 collective-permute-start.5
  38.5 1.6 %collective-permute-start.6 = (f32[64,256]{1,0:T(8,128)S(1)}, f32[64,256]{1,0:T(8,128)S(1)}, u32[]{:S(2)}, u32[]{:S(2)}) collective-permute-start(f32[64,256]{1,0:T(8,128)S(1)} %get-tuple-element.48), channel_id=1, source_target_pairs={{0,4},{2,6},{4,0},{6,2},{8,12},{10,14},{12,8},{14,10},{1,5},{3,7},... | collective-permute-start | bytes 196616 | tf_op jit(solution)/shard_map/ppermute | solution.py:473
  40.1 1.4 %collective-permute-start.7 = (f32[64,256]{1,0:T(8,128)S(1)}, f32[64,256]{1,0:T(8,128)S(1)}, u32[]{:S(2)}, u32[]{:S(2)}) collective-permute-start(f32[64,256]{1,0:T(8,128)S(1)} %get-tuple-element.49), channel_id=1, source_target_pairs={{0,6},{2,4},{4,2},{6,0},{8,14},{10,12},{12,10},{14,8},{1,7},{3,5},... | collective-permute-start | bytes 196616 | tf_op jit(solution)/shard_map/ppermute | solution.py:473
  41.5 0.6 close.3
  42.1 0.6 collective-permute-start.13
  42.7 1.6 %collective-permute-start.14 = (f32[64,256]{1,0:T(8,128)S(1)}, f32[64,256]{1,0:T(8,128)S(1)}, u32[]{:S(2)}, u32[]{:S(2)}) collective-permute-start(f32[64,256]{1,0:T(8,128)S(1)} %get-tuple-element.62), channel_id=1, source_target_pairs={{0,4},{2,6},{4,0},{6,2},{8,12},{10,14},{12,8},{14,10},{1,5},{3,7},... | collective-permute-start | bytes 196616 | tf_op jit(solution)/shard_map/ppermute | solution.py:473
  44.3 1.4 %collective-permute-start.15 = (f32[64,256]{1,0:T(8,128)S(1)}, f32[64,256]{1,0:T(8,128)S(1)}, u32[]{:S(2)}, u32[]{:S(2)}) collective-permute-start(f32[64,256]{1,0:T(8,128)S(1)} %get-tuple-element.63), channel_id=1, source_target_pairs={{0,6},{2,4},{4,2},{6,0},{8,14},{10,12},{12,10},{14,8},{1,7},{3,5},... | collective-permute-start | bytes 196616 | tf_op jit(solution)/shard_map/ppermute | solution.py:473
  45.7 3.2 %inverse_first.2 = (f32[4224,128]{1,0:T(8,128)S(1)}, f32[4224,128]{1,0:T(8,128)S(1)}) custom-call(s32[2]{0:T(128)S(1)} %pad_add_fusion.place, f32[16,2,128,256]{3,2,1,0:T(8,128)S(1)} %get-tuple-element.39.modes, bf16[2,2,768,256]{3,2,1,0:T(8,128)(2,1)S(1)} %copy-done.3, f32[2,2,256,256]{3,2,1,0:T(8,128)S(1)} %copy-done.5, ...), custom_call_target="tpu_custom_call" | custom-call | flops 2147483648 | bytes 8388608 | tf_op jit(solution)/shard_map/inverse_first/pallas_call | solution.py:388
  48.9 0.1 collective-permute-start.16
  49.0 0.5 collective-permute-done.15.refs_3_
  49.5 3.4 %inverse_first.3 = (f32[4224,128]{1,0:T(8,128)S(1)}, f32[4224,128]{1,0:T(8,128)S(1)}) custom-call(s32[2]{0:T(128)S(1)} %pad_add_fusion.place, f32[16,2,128,256]{3,2,1,0:T(8,128)S(1)} %get-tuple-element.53.modes, bf16[2,2,768,256]{3,2,1,0:T(8,128)(2,1)S(1)} %copy-done.3, f32[2,2,256,256]{3,2,1,0:T(8,128)S(1)} %copy-done.5, ...), custom_call_target="tpu_custom_call" | custom-call | flops 2147483648 | bytes 8388608 | tf_op jit(solution)/shard_map/inverse_first/pallas_call | solution.py:388
  52.9 0.1 collective-permute-start.17
  53.0 4.7 %keep_inverse.1.kept = f32[4096,512]{1,0:T(8,128)S(1)} custom-call(s32[2]{0:T(128)S(1)} %pad_add_fusion.place, bf16[2,768,512]{2,1,0:T(8,128)(2,1)S(1)} %copy-done.1, f32[4224,128]{1,0:T(8,128)S(1)} %get-tuple-element.50.refs_0_, f32[4224,128]{1,0:T(8,128)S(1)} %get-tuple-element.64.refs_1_), custom_call_target="tpu_custom_call" | custom-call | flops 2147483648 | bytes 8388608 | tf_op jit(solution)/shard_map/keep_inverse/pallas_call | solution.py:420
  57.7 6.6 %inverse_second.1 = f32[256,16,512]{2,1,0:T(8,128)} custom-call(s32[2]{0:T(128)S(1)} %pad_add_fusion.place, bf16[2,768,512]{2,1,0:T(8,128)(2,1)S(1)} %copy-done.1, f32[4096,512]{1,0:T(8,128)S(1)} %keep_inverse.1.kept, f32[4224,128]{1,0:T(8,128)S(1)} %collective-permute-done.16.refs_0_, f32[4224,128]{1,0:T(8,128)S(1)} %collective-permute-done.17.refs_1_), custom_call_target="tpu_custom_call" | custom-call | flops 4294967296 | bytes 8388608 | tf_op jit(solution)/shard_map/inverse_second/pallas_call | solution.py:455
  (29 shorter events, 0.1 us)
Async XLA Ops:
  0.1 10.2 %copy-start.2 = (bf16[2,1536,256]{2,1,0:T(8,128)(2,1)S(1)}, bf16[2,1536,256]{2,1,0:T(8,128)(2,1)}, u32[]{:S(2)}) copy-start(bf16[2,1536,256]{2,1,0:T(8,128)(2,1)} %constant.23.clone.table.tables) | copy-start | bytes 4718596
  9.3 5.5 %collective-permute-start = (f32[4488,128]{1,0:T(8,128)S(1)}, f32[4488,128]{1,0:T(8,128)S(1)}, u32[]{:S(2)}, u32[]{:S(2)}) collective-permute-start(f32[4488,128]{1,0:T(8,128)S(1)} %get-tuple-element.38), channel_id=1, source_target_pairs={{0,1},{1,0},{2,3},{3,2},{4,5},{5,4},{6,7},{7,6},{8,9},{9,8},{10,11... | collective-permute-start | bytes 6893576 | tf_op jit(solution)/shard_map/ppermute | solution.py:468
  10.2 12.0 %collective-permute-start.8 = (f32[4488,128]{1,0:T(8,128)S(1)}, f32[4488,128]{1,0:T(8,128)S(1)}, u32[]{:S(2)}, u32[]{:S(2)}) collective-permute-start(f32[4488,128]{1,0:T(8,128)S(1)} %get-tuple-element.52), channel_id=1, source_target_pairs={{0,1},{1,0},{2,3},{3,2},{4,5},{5,4},{6,7},{7,6},{8,9},{9,8},{10,11... | collective-permute-start | bytes 6893576 | tf_op jit(solution)/shard_map/ppermute | solution.py:468
  10.3 4.5 %copy-start.4 = (bf16[2,2,768,256]{3,2,1,0:T(8,128)(2,1)S(1)}, bf16[2,2,768,256]{3,2,1,0:T(8,128)(2,1)}, u32[]{:S(2)}) copy-start(bf16[2,2,768,256]{3,2,1,0:T(8,128)(2,1)} %constant.21.clone.table) | copy-start | bytes 4718596
  10.3 4.5 %copy-start.5 = (f32[2,2,256,256]{3,2,1,0:T(8,128)S(1)}, f32[2,2,256,256]{3,2,1,0:T(8,128)}, u32[]{:S(2)}) copy-start(f32[2,2,256,256]{3,2,1,0:T(8,128)} %constant.22.clone.decay) | copy-start | bytes 3145732
  18.0 10.9 %collective-permute-start.1 = (f32[64,256]{1,0:T(8,128)S(1)}, f32[64,256]{1,0:T(8,128)S(1)}, u32[]{:S(2)}, u32[]{:S(2)}) collective-permute-start(f32[64,256]{1,0:T(8,128)S(1)} %get-tuple-element.41), channel_id=1, source_target_pairs={{0,2},{2,0},{4,6},{6,4},{8,10},{10,8},{12,14},{14,12},{1,3},{3,1},... | collective-permute-start | bytes 196616 | tf_op jit(solution)/shard_map/ppermute | solution.py:473
  20.6 8.3 %collective-permute-start.2 = (f32[64,256]{1,0:T(8,128)S(1)}, f32[64,256]{1,0:T(8,128)S(1)}, u32[]{:S(2)}, u32[]{:S(2)}) collective-permute-start(f32[64,256]{1,0:T(8,128)S(1)} %get-tuple-element.42), channel_id=1, source_target_pairs={{0,4},{2,6},{4,0},{6,2},{8,12},{10,14},{12,8},{14,10},{1,5},{3,7},... | collective-permute-start | bytes 196616 | tf_op jit(solution)/shard_map/ppermute | solution.py:473
  22.2 6.8 %collective-permute-start.3 = (f32[64,256]{1,0:T(8,128)S(1)}, f32[64,256]{1,0:T(8,128)S(1)}, u32[]{:S(2)}, u32[]{:S(2)}) collective-permute-start(f32[64,256]{1,0:T(8,128)S(1)} %get-tuple-element.43), channel_id=1, source_target_pairs={{0,6},{2,4},{4,2},{6,0},{8,14},{10,12},{12,10},{14,8},{1,7},{3,5},... | collective-permute-start | bytes 196616 | tf_op jit(solution)/shard_map/ppermute | solution.py:473
  22.2 6.8 %copy-start = (f32[2,2,3,256,256]{4,3,2,1,0:T(8,128)S(1)}, f32[2,2,3,256,256]{4,3,2,1,0:T(8,128)}, u32[]{:S(2)}) copy-start(f32[2,2,3,256,256]{4,3,2,1,0:T(8,128)} %constant.20.clone.closing) | copy-start | bytes 9437188
  25.4 7.2 %collective-permute-start.9 = (f32[64,256]{1,0:T(8,128)S(1)}, f32[64,256]{1,0:T(8,128)S(1)}, u32[]{:S(2)}, u32[]{:S(2)}) collective-permute-start(f32[64,256]{1,0:T(8,128)S(1)} %get-tuple-element.55), channel_id=1, source_target_pairs={{0,2},{2,0},{4,6},{6,4},{8,10},{10,8},{12,14},{14,12},{1,3},{3,1},... | collective-permute-start | bytes 196616 | tf_op jit(solution)/shard_map/ppermute | solution.py:473
  27.3 5.2 %collective-permute-start.10 = (f32[64,256]{1,0:T(8,128)S(1)}, f32[64,256]{1,0:T(8,128)S(1)}, u32[]{:S(2)}, u32[]{:S(2)}) collective-permute-start(f32[64,256]{1,0:T(8,128)S(1)} %get-tuple-element.56), channel_id=1, source_target_pairs={{0,4},{2,6},{4,0},{6,2},{8,12},{10,14},{12,8},{14,10},{1,5},{3,7},... | collective-permute-start | bytes 196616 | tf_op jit(solution)/shard_map/ppermute | solution.py:473
  28.9 5.5 %collective-permute-start.11 = (f32[64,256]{1,0:T(8,128)S(1)}, f32[64,256]{1,0:T(8,128)S(1)}, u32[]{:S(2)}, u32[]{:S(2)}) collective-permute-start(f32[64,256]{1,0:T(8,128)S(1)} %get-tuple-element.57), channel_id=1, source_target_pairs={{0,6},{2,4},{4,2},{6,0},{8,14},{10,12},{12,10},{14,8},{1,7},{3,5},... | collective-permute-start | bytes 196616 | tf_op jit(solution)/shard_map/ppermute | solution.py:473
  29.5 7.8 %collective-permute-start.4 = (f32[64,256]{1,0:T(8,128)S(1)}, f32[64,256]{1,0:T(8,128)S(1)}, u32[]{:S(2)}, u32[]{:S(2)}) collective-permute-start(f32[64,256]{1,0:T(8,128)S(1)} %get-tuple-element.45.near), channel_id=1, source_target_pairs={{0,8},{2,10},{4,12},{6,14},{8,0},{10,2},{12,4},{14,6},{1,9},{3,11}... | collective-permute-start | bytes 196616 | tf_op jit(solution)/shard_map/ppermute | solution.py:473
  35.0 6.5 %collective-permute-start.12 = (f32[64,256]{1,0:T(8,128)S(1)}, f32[64,256]{1,0:T(8,128)S(1)}, u32[]{:S(2)}, u32[]{:S(2)}) collective-permute-start(f32[64,256]{1,0:T(8,128)S(1)} %get-tuple-element.59.near), channel_id=1, source_target_pairs={{0,8},{2,10},{4,12},{6,14},{8,0},{10,2},{12,4},{14,6},{1,9},{3,11}... | collective-permute-start | bytes 196616 | tf_op jit(solution)/shard_map/ppermute | solution.py:473
  37.9 7.7 %copy-start.3 = (bf16[2,2,768,256]{3,2,1,0:T(8,128)(2,1)S(1)}, bf16[2,2,768,256]{3,2,1,0:T(8,128)(2,1)}, u32[]{:S(2)}) copy-start(bf16[2,2,768,256]{3,2,1,0:T(8,128)(2,1)} %constant.24.clone.table) | copy-start | bytes 4718596
  38.0 6.3 %collective-permute-start.5 = (f32[64,256]{1,0:T(8,128)S(1)}, f32[64,256]{1,0:T(8,128)S(1)}, u32[]{:S(2)}, u32[]{:S(2)}) collective-permute-start(f32[64,256]{1,0:T(8,128)S(1)} %get-tuple-element.47), channel_id=1, source_target_pairs={{0,2},{2,0},{4,6},{6,4},{8,10},{10,8},{12,14},{14,12},{1,3},{3,1},... | collective-permute-start | bytes 196616 | tf_op jit(solution)/shard_map/ppermute | solution.py:473
  38.5 7.2 %collective-permute-start.6 = (f32[64,256]{1,0:T(8,128)S(1)}, f32[64,256]{1,0:T(8,128)S(1)}, u32[]{:S(2)}, u32[]{:S(2)}) collective-permute-start(f32[64,256]{1,0:T(8,128)S(1)} %get-tuple-element.48), channel_id=1, source_target_pairs={{0,4},{2,6},{4,0},{6,2},{8,12},{10,14},{12,8},{14,10},{1,5},{3,7},... | collective-permute-start | bytes 196616 | tf_op jit(solution)/shard_map/ppermute | solution.py:473
  40.1 5.5 %collective-permute-start.7 = (f32[64,256]{1,0:T(8,128)S(1)}, f32[64,256]{1,0:T(8,128)S(1)}, u32[]{:S(2)}, u32[]{:S(2)}) collective-permute-start(f32[64,256]{1,0:T(8,128)S(1)} %get-tuple-element.49), channel_id=1, source_target_pairs={{0,6},{2,4},{4,2},{6,0},{8,14},{10,12},{12,10},{14,8},{1,7},{3,5},... | collective-permute-start | bytes 196616 | tf_op jit(solution)/shard_map/ppermute | solution.py:473
  42.1 6.9 %collective-permute-start.13 = (f32[64,256]{1,0:T(8,128)S(1)}, f32[64,256]{1,0:T(8,128)S(1)}, u32[]{:S(2)}, u32[]{:S(2)}) collective-permute-start(f32[64,256]{1,0:T(8,128)S(1)} %get-tuple-element.61), channel_id=1, source_target_pairs={{0,2},{2,0},{4,6},{6,4},{8,10},{10,8},{12,14},{14,12},{1,3},{3,1},... | collective-permute-start | bytes 196616 | tf_op jit(solution)/shard_map/ppermute | solution.py:473
  42.7 6.3 %collective-permute-start.14 = (f32[64,256]{1,0:T(8,128)S(1)}, f32[64,256]{1,0:T(8,128)S(1)}, u32[]{:S(2)}, u32[]{:S(2)}) collective-permute-start(f32[64,256]{1,0:T(8,128)S(1)} %get-tuple-element.62), channel_id=1, source_target_pairs={{0,4},{2,6},{4,0},{6,2},{8,12},{10,14},{12,8},{14,10},{1,5},{3,7},... | collective-permute-start | bytes 196616 | tf_op jit(solution)/shard_map/ppermute | solution.py:473
  44.3 5.2 %collective-permute-start.15 = (f32[64,256]{1,0:T(8,128)S(1)}, f32[64,256]{1,0:T(8,128)S(1)}, u32[]{:S(2)}, u32[]{:S(2)}) collective-permute-start(f32[64,256]{1,0:T(8,128)S(1)} %get-tuple-element.63), channel_id=1, source_target_pairs={{0,6},{2,4},{4,2},{6,0},{8,14},{10,12},{12,10},{14,8},{1,7},{3,5},... | collective-permute-start | bytes 196616 | tf_op jit(solution)/shard_map/ppermute | solution.py:473
  48.9 8.8 %collective-permute-start.16 = (f32[4224,128]{1,0:T(8,128)S(1)}, f32[4224,128]{1,0:T(8,128)S(1)}, u32[]{:S(2)}, u32[]{:S(2)}) collective-permute-start(f32[4224,128]{1,0:T(8,128)S(1)} %get-tuple-element.65), channel_id=1, source_target_pairs={{0,1},{1,0},{2,3},{3,2},{4,5},{5,4},{6,7},{7,6},{8,9},{9,8},{10,11... | collective-permute-start | bytes 6488072 | tf_op jit(solution)/shard_map/ppermute | solution.py:468
  49.5 3.5 %copy-start.1 = (bf16[2,768,512]{2,1,0:T(8,128)(2,1)S(1)}, bf16[2,768,512]{2,1,0:T(8,128)(2,1)}, u32[]{:S(2)}) copy-start(bf16[2,768,512]{2,1,0:T(8,128)(2,1)} %constant.25.clone.tables) | copy-start | bytes 4718596
  52.9 4.8 %collective-permute-start.17 = (f32[4224,128]{1,0:T(8,128)S(1)}, f32[4224,128]{1,0:T(8,128)S(1)}, u32[]{:S(2)}, u32[]{:S(2)}) collective-permute-start(f32[4224,128]{1,0:T(8,128)S(1)} %get-tuple-element.66), channel_id=1, source_target_pairs={{0,1},{1,0},{2,3},{3,2},{4,5},{5,4},{6,7},{7,6},{8,9},{9,8},{10,11... | collective-permute-start | bytes 6488072 | tf_op jit(solution)/shard_map/ppermute | solution.py:468

commit v14 on v11

--- a/solution.py
+++ b/solution.py
@@ -134,8 +134,6 @@
     part = half // CHUNKS
     pieces = sems.shape[0]
     piece = cells // pieces
-    rows = piece * len(scratch)
-    blocks = cells // rows
     group = max(TILE // steps, 1)
     pitch = sends[0].shape[0] // (steps + 1)
     body = piece * steps
@@ -150,11 +148,11 @@
         ]
 
     table_copy = pltpu.make_async_copy(tables.at[1 - place[1]], table, table_sem)
-    for at in range(pieces):
-        for copy in copies(at):
-            copy.start()
-        if at == 0:
-            table_copy.start()
+
+    def start(first, last):
+        for at in range(first, min(last, pieces)):
+            for copy in copies(at):
+                copy.start()
 
     def put(other, at, sums_at, cells):
         lower = cells[:, :half]
@@ -165,47 +163,41 @@
         sums[pl.ds(sums_at, TILE), :] = lower + upper
         store_split(other, (pl.ds(at, TILE),), 0, lower - upper)
 
-    def prepare(sub, block):
-        kept_at = pl.multiple_of(block * rows + sub * piece, piece)
-        kept_base = pl.multiple_of(kept_at * steps, body)
+    def prepare(at):
+        split = scratch[at % len(scratch)]
+        cell = at * piece
         for row in range(0, piece, group):
-            values = field[pl.ds(kept_at + row, group)]
+            values = field[pl.ds(cell + row, group)]
             force = values - values * values * values
-            put(scratch[sub], row * steps, kept_base + row * steps, force.reshape(TILE, width))
+            put(split, row * steps, (cell + row) * steps, force.reshape(TILE, width))
         for row in range(0, piece, TILE):
-            at = pl.ds(pl.multiple_of(kept_at + row, TILE), TILE)
-            ends = jnp.where(is_first, initial[at], field[at, steps - 1, :])
-            put(scratch[sub], body + row, cells * steps + kept_at + row, ends)
-
-    def transform(sub, block):
-        sent = dot(scratch[sub][...], table[...])
-        sent_at = pl.multiple_of(cells - block * rows - (sub + 1) * piece, piece)
+            here = pl.ds(cell + row, TILE)
+            ends = jnp.where(is_first, initial[here], field[here, steps - 1, :])
+            put(split, body + row, cells * steps + cell + row, ends)
+
+    def transform(at):
+        sent = dot(scratch[at % len(scratch)][...], table[...])
+        first = cells - (at + 1) * piece
         for chunk, send in enumerate(sends):
             lanes = slice(chunk * part, (chunk + 1) * part)
             for row in range(piece):
                 line = sent[row * steps : (row + 1) * steps, lanes]
-                send[pl.ds(sent_at + piece - 1 - row, steps, stride=pitch), :] = line
-            store_rows_reversed(send, pitch * steps + sent_at, sent[body:, lanes])
-
-    count = len(scratch)
-
-    def piece_of(block, sub):
-        for copy in copies(block * count + sub):
+                send[pl.ds(first + piece - 1 - row, steps, stride=pitch), :] = line
+            store_rows_reversed(send, pitch * steps + first, sent[body:, lanes])
+
+    start(0, 1)
+    table_copy.start()
+    start(1, 2)
+    for at in range(pieces):
+        for copy in copies(at):
             copy.wait()
-        if sub:
-            transform(sub - 1, block)
-        else:
-            transform(count - 1, jnp.maximum(block - 1, 0))
-        prepare(sub, block)
-
-    table_copy.wait()
-
-    @pl.loop(0, blocks)
-    def _(block):
-        for sub in range(count):
-            piece_of(block, sub)
-
-    transform(count - 1, blocks - 1)
+        start(2 * at + 2, 2 * at + 4)
+        if at == 1:
+            table_copy.wait()
+        if at:
+            transform(at - 1)
+        prepare(at)
+    transform(pieces - 1)
 
 
 def forward_second(place, field, initial, tables):
@@ -274,29 +266,30 @@
 
 def forward_first_kernel(slabs, chunk, place, keep, got, table, decay, modes, *refs):
     size = ranks(slabs)
-    lasts, (state, split, split_end, extra) = refs[:size], refs[size:]
+    lasts, (state, split, extra) = refs[:size], refs[size:]
     steps, _, part, rows = modes.shape
     pitch = keep.shape[0] // (steps + 1)
-    block = split.shape[1] // part
+    block = split.shape[1] // part - 1
     strip = place[1]
-    near, far = keep[pl.ds(pitch * steps, rows)], got[pl.ds(pitch * steps, rows)]
-    for c, cells in enumerate((near + far, near - far)):
-        store_split(split_end, (c, slice(None)), 0, cells.T)
-        extra[c] = dot(split_end[c], table[strip, c])
     is_first = jnp.where(place[0] == 0, 1.0 / REACTION_STEP, 0.0)
     is_last = jnp.where(place[0] == slabs - 1, 1.0 / REACTION_STEP, 0.0)
     state[...] = jnp.zeros_like(state)
     for step in range(0, steps, block):
+        count = block if step else block + 1
         for c in (0, 1):
-            for at in range(block):
-                cells_at = pl.ds((step + at) * pitch, rows)
+            for at in range(count):
+                from_step = steps if at == block else step + at
+                cells_at = pl.ds(from_step * pitch, rows)
                 near, far = keep[cells_at], got[cells_at]
                 cells = near - far if c else near + far
                 store_split(split, (c, pl.ds(at * part, part)), 0, cells.T)
-            result = dot(split[c], table[strip, c])
-            modes[pl.ds(step, block), c] = result.reshape(block, part, rows)
+            result = dot(split[c, pl.ds(0, count * part)], table[strip, c])
             if step == 0:
-                modes[0, c] = result[:part] + is_first * extra[c]
+                extra[c] = result[block * part :]
+                modes[0, c] = result[:part] + is_first * result[block * part :]
+                modes[pl.ds(1, block - 1), c] = result[part : block * part].reshape(block - 1, part, rows)
+            else:
+                modes[pl.ds(step, block), c] = result.reshape(block, part, rows)
         for c in (0, 1):
             for row in range(0, part, TILE):
                 tile, at_state = pl.ds(row, TILE), pl.ds(c * part + row, TILE)
@@ -329,8 +322,7 @@
         [floats(steps, 2, part, rows)] + [floats(share, rows)] * size,
         [
             pltpu.VMEM((2 * part, rows), jnp.float32),
-            pltpu.VMEM((2, block * part, 2 * rows), jnp.bfloat16),
-            pltpu.VMEM((2, part, 2 * rows), jnp.bfloat16),
+            pltpu.VMEM((2, (block + 1) * part, 2 * rows), jnp.bfloat16),
             pltpu.VMEM((2, part, rows), jnp.float32),
         ],
         1 << 31,
@@ -493,32 +485,33 @@
         here = pl.ds(at * piece, piece)
         return pltpu.make_async_copy(out.at[here], target.at[here], sems.at[at])
 
-    @pl.loop(0, pieces, step=count)
-    def _(first_piece):
-        for sub in range(count):
-            split, result = scratch[2 * sub : 2 * sub + 2]
-            base = (first_piece + sub) * piece
-            for row in range(0, piece, group):
-                mirrors = [cells - 1 - base - row - at for at in range(group)]
-                for chunk, got in enumerate(gots):
-                    values = steps_of(got, mirrors, steps, pitch)
-                    store_split(split, (pl.ds(row * steps, TILE),), chunk * part, values)
-            result[...] = dot(split[...], tables[1 - strip])
-        for sub in range(count):
-            result = scratch[2 * sub + 1]
-            base = pl.multiple_of((first_piece + sub) * piece, piece)
-            kept_base = pl.multiple_of(base * steps, piece * steps)
-            for row in range(0, piece, group):
-                first = kept[pl.ds(kept_base + row * steps, TILE)]
-                second = result[pl.ds(row * steps, TILE)]
-                upper = sign * (first - second)
-                parts = [
-                    lanes_reversed(upper[:, lane : lane + LANES]) for lane in range(0, half, LANES)
-                ][::-1]
-                whole = jnp.concatenate([first + second, *parts], axis=1)
-                out[pl.ds(base + row, group)] = whole.reshape(group, TILE // group, width)
-            copy(first_piece + sub).start()
-
+    def product(at):
+        split, result = scratch[2 * (at % count) : 2 * (at % count) + 2]
+        for row in range(0, piece, group):
+            mirrors = [cells - 1 - at * piece - row - cell for cell in range(group)]
+            for chunk, got in enumerate(gots):
+                values = steps_of(got, mirrors, steps, pitch)
+                store_split(split, (pl.ds(row * steps, TILE),), chunk * part, values)
+        result[...] = dot(split[...], tables[1 - strip])
+
+    def finish(at):
+        result = scratch[2 * (at % count) + 1]
+        for row in range(0, piece, group):
+            first = kept[pl.ds((at * piece + row) * steps, TILE)]
+            second = result[pl.ds(row * steps, TILE)]
+            upper = sign * (first - second)
+            parts = [
+                lanes_reversed(upper[:, lane : lane + LANES]) for lane in range(0, half, LANES)
+            ][::-1]
+            whole = jnp.concatenate([first + second, *parts], axis=1)
+            out[pl.ds(at * piece + row, group)] = whole.reshape(group, TILE // group, width)
+        copy(at).start()
+
+    for at in range(pieces):
+        product(at)
+        if at:
+            finish(at - 1)
+    finish(pieces - 1)
     for at in range(pieces):
         copy(at).wait()
 

time: 63 us -> 60.4 us (0.959)
  Pallas kernels: 36.7 us -> 34.2 us
    pallas_call x1, Pallas kernels: 9.37 us -> 6.92 us  [forward_second(): call(forward_second_kernel, 'forward_second', [IN_HBM] * 3, [IN_VMEM] * (...]
  transfers between devices with their start and end apart: 18 -> 18, of which waited for: 4 -> 4; matrix products, arithmetic and copies ran while one was open for 0% -> 0% of each run, Pallas kernels for 34% -> 36%
where the time goes in v14:
time: 60.4 us; the launch traced here: 60.2 us
  Pallas kernels  34.2 us (57%)
  starting transfers between devices  21.5 us (36%)
  waiting for transfers between devices  4.07 us (7%)
    ppermute x14, starting transfers between devices, with_partner(): lax.ppermute(block, 'tm', [(slab, slab ^ distance) for slab in range(slab...  20.6 us
    pallas_call x1, Pallas kernels, forward_second(): call(forward_second_kernel, 'forward_second', [IN_HBM] * 3, [IN_VMEM] * (...  6.92 us
    pallas_call x2, Pallas kernels, forward_first(): call(functools.partial(forward_first_kernel, slabs, chunk), 'forward_firs...  6.49 us
    pallas_call x2, Pallas kernels, inverse_first(): call(functools.partial(inverse_first_kernel, slabs, chunk), 'inverse_firs...  6.33 us
    pallas_call x1, Pallas kernels, inverse_second(): call(inverse_second_kernel, 'inverse_second', [IN_VMEM] * (2 + CHUNKS), I...  5.9 us
    pallas_call x1, Pallas kernels, keep_inverse(): call(functools.partial(keep_inverse_kernel, steps), 'keep_inverse', [IN_V...  3.54 us
    pallas_call x1, Pallas kernels, keep_second(): call(functools.partial(keep_second_kernel, steps), 'keep_second', [IN_VME...  2.68 us
    ppermute x14, waiting for transfers between devices, with_partner(): lax.ppermute(block, 'tm', [(slab, slab ^ distance) for slab in range(slab...  2.16 us
  transfers between devices with their start and end apart: 18, of which 4 were waited for; matrix products, arithmetic and copies ran while one was open for 0% of the time, Pallas kernels for 36%

profile of v14, /device:TPU:0, one launch (start us, length us, event | category | flops | bytes accessed | tf_op | source)
XLA Modules:
  0.0 60.2 jit_solution(17206433030196911105)
XLA Ops:
  0.0 0.1 pad_add_fusion.place
  0.1 6.9 %forward_second.1 = (f32[4352,256]{1,0:T(8,128)S(1)}, f32[4488,128]{1,0:T(8,128)S(1)}, f32[4488,128]{1,0:T(8,128)S(1)}) custom-call(s32[2]{0:T(128)S(1)} %pad_add_fusion.place, f32[256,16,512]{2,1,0:T(8,128)} %field_in.1, f32[256,512]{1,0:T(8,128)} %initial_in.1, bf16[2,768,256]{2,1,0:T(8,128)(2,1)} %constant.23.clone.tables), custom_call_target="tpu_custom_call" | custom-call | flops 4294967296 | bytes 8388608 | tf_op jit(solution)/shard_map/forward_second/pallas_call | solution.py:207
  7.0 0.6 collective-permute-start
  7.6 0.1 collective-permute-start.8
  7.7 2.7 %keep_second.1 = (f32[4488,128]{1,0:T(8,128)S(1)}, f32[4488,128]{1,0:T(8,128)S(1)}) custom-call(s32[2]{0:T(128)S(1)} %pad_add_fusion.place, bf16[2,768,256]{2,1,0:T(8,128)(2,1)S(1)} %copy-done.5, f32[4352,256]{1,0:T(8,128)S(1)} %get-tuple-element.36.sums), custom_call_target="tpu_custom_call" | custom-call | flops 2147483648 | bytes 8388608 | tf_op jit(solution)/shard_map/keep_second/pallas_call | solution.py:252
  10.3 1.3 %collective-permute-done.got = f32[4488,128]{1,0:T(8,128)S(1)} collective-permute-done((f32[4488,128]{1,0:T(8,128)S(1)}, f32[4488,128]{1,0:T(8,128)S(1)}, u32[]{:S(2)}, u32[]{:S(2)}) %collective-permute-start) | collective-permute-done | bytes 2297888 | tf_op jit(solution)/shard_map/ppermute | solution.py:537
  11.6 3.2 %forward_first.2 = (f32[16,2,128,256]{3,2,1,0:T(8,128)S(1)}, f32[64,256]{1,0:T(8,128)S(1)}, f32[64,256]{1,0:T(8,128)S(1)}, f32[64,256]{1,0:T(8,128)S(1)}, f32[64,256]{1,0:T(8,128)S(1)}) custom-call(s32[2]{0:T(128)S(1)} %pad_add_fusion.place, f32[4488,128]{1,0:T(8,128)S(1)} %get-tuple-element.37.keep, f32[4488,128]{1,0:T(8,128)S(1)} %collective-permute-done.got, ...), custom_call_target="tpu_custom_call" | custom-call | flops 2147483648 | bytes 8388608 | tf_op jit(solution)/shard_map/forward_first/pallas_call | solution.py:317
  14.9 2.9 %collective-permute-start.1 = (f32[64,256]{1,0:T(8,128)S(1)}, f32[64,256]{1,0:T(8,128)S(1)}, u32[]{:S(2)}, u32[]{:S(2)}) collective-permute-start(f32[64,256]{1,0:T(8,128)S(1)} %get-tuple-element.41), channel_id=1, source_target_pairs={{0,2},{2,0},{4,6},{6,4},{8,10},{10,8},{12,14},{14,12},{1,3},{3,1},... | collective-permute-start | bytes 196616 | tf_op jit(solution)/shard_map/ppermute | solution.py:542
  17.8 1.6 %collective-permute-start.2 = (f32[64,256]{1,0:T(8,128)S(1)}, f32[64,256]{1,0:T(8,128)S(1)}, u32[]{:S(2)}, u32[]{:S(2)}) collective-permute-start(f32[64,256]{1,0:T(8,128)S(1)} %get-tuple-element.42), channel_id=1, source_target_pairs={{0,4},{2,6},{4,0},{6,2},{8,12},{10,14},{12,8},{14,10},{1,5},{3,7},... | collective-permute-start | bytes 196616 | tf_op jit(solution)/shard_map/ppermute | solution.py:542
  19.4 3.2 %forward_first.3 = (f32[16,2,128,256]{3,2,1,0:T(8,128)S(1)}, f32[64,256]{1,0:T(8,128)S(1)}, f32[64,256]{1,0:T(8,128)S(1)}, f32[64,256]{1,0:T(8,128)S(1)}, f32[64,256]{1,0:T(8,128)S(1)}) custom-call(s32[2]{0:T(128)S(1)} %pad_add_fusion.place, f32[4488,128]{1,0:T(8,128)S(1)} %get-tuple-element.51.keep, f32[4488,128]{1,0:T(8,128)S(1)} %collective-permute-done.8.got, ...), custom_call_target="tpu_custom_call" | custom-call | flops 2147483648 | bytes 8388608 | tf_op jit(solution)/shard_map/forward_first/pallas_call | solution.py:317
  22.7 2.0 %collective-permute-start.9 = (f32[64,256]{1,0:T(8,128)S(1)}, f32[64,256]{1,0:T(8,128)S(1)}, u32[]{:S(2)}, u32[]{:S(2)}) collective-permute-start(f32[64,256]{1,0:T(8,128)S(1)} %get-tuple-element.55), channel_id=1, source_target_pairs={{0,2},{2,0},{4,6},{6,4},{8,10},{10,8},{12,14},{14,12},{1,3},{3,1},... | collective-permute-start | bytes 196616 | tf_op jit(solution)/shard_map/ppermute | solution.py:542
  24.6 1.6 %collective-permute-start.10 = (f32[64,256]{1,0:T(8,128)S(1)}, f32[64,256]{1,0:T(8,128)S(1)}, u32[]{:S(2)}, u32[]{:S(2)}) collective-permute-start(f32[64,256]{1,0:T(8,128)S(1)} %get-tuple-element.56), channel_id=1, source_target_pairs={{0,4},{2,6},{4,0},{6,2},{8,12},{10,14},{12,8},{14,10},{1,5},{3,7},... | collective-permute-start | bytes 196616 | tf_op jit(solution)/shard_map/ppermute | solution.py:542
  26.2 0.6 half_sum.2
  26.8 3.0 %collective-permute-start.4 = (f32[64,256]{1,0:T(8,128)S(1)}, f32[64,256]{1,0:T(8,128)S(1)}, u32[]{:S(2)}, u32[]{:S(2)}) collective-permute-start(f32[64,256]{1,0:T(8,128)S(1)} %get-tuple-element.45.near), channel_id=1, source_target_pairs={{0,8},{2,10},{4,12},{6,14},{8,0},{10,2},{12,4},{14,6},{1,9},{3,11}... | collective-permute-start | bytes 196616 | tf_op jit(solution)/shard_map/ppermute | solution.py:542
  29.9 1.7 %collective-permute-done.11.refs_3_ = f32[64,256]{1,0:T(8,128)S(1)} collective-permute-done((f32[64,256]{1,0:T(8,128)S(1)}, f32[64,256]{1,0:T(8,128)S(1)}, u32[]{:S(2)}, u32[]{:S(2)}) %collective-permute-start.11) | collective-permute-done | bytes 65568 | tf_op jit(solution)/shard_map/ppermute | solution.py:542
  31.6 0.6 half_sum.3
  32.2 2.4 %collective-permute-start.12 = (f32[64,256]{1,0:T(8,128)S(1)}, f32[64,256]{1,0:T(8,128)S(1)}, u32[]{:S(2)}, u32[]{:S(2)}) collective-permute-start(f32[64,256]{1,0:T(8,128)S(1)} %get-tuple-element.59.near), channel_id=1, source_target_pairs={{0,8},{2,10},{4,12},{6,14},{8,0},{10,2},{12,4},{14,6},{1,9},{3,11}... | collective-permute-start | bytes 196616 | tf_op jit(solution)/shard_map/ppermute | solution.py:542
  34.6 0.6 close.2
  35.2 0.6 collective-permute-start.5
  35.8 1.6 %collective-permute-start.6 = (f32[64,256]{1,0:T(8,128)S(1)}, f32[64,256]{1,0:T(8,128)S(1)}, u32[]{:S(2)}, u32[]{:S(2)}) collective-permute-start(f32[64,256]{1,0:T(8,128)S(1)} %get-tuple-element.48), channel_id=1, source_target_pairs={{0,4},{2,6},{4,0},{6,2},{8,12},{10,14},{12,8},{14,10},{1,5},{3,7},... | collective-permute-start | bytes 196616 | tf_op jit(solution)/shard_map/ppermute | solution.py:542
  37.4 1.4 %collective-permute-start.7 = (f32[64,256]{1,0:T(8,128)S(1)}, f32[64,256]{1,0:T(8,128)S(1)}, u32[]{:S(2)}, u32[]{:S(2)}) collective-permute-start(f32[64,256]{1,0:T(8,128)S(1)} %get-tuple-element.49), channel_id=1, source_target_pairs={{0,6},{2,4},{4,2},{6,0},{8,14},{10,12},{12,10},{14,8},{1,7},{3,5},... | collective-permute-start | bytes 196616 | tf_op jit(solution)/shard_map/ppermute | solution.py:542
  38.8 0.6 close.3
  39.4 0.6 collective-permute-start.13
  40.0 1.6 %collective-permute-start.14 = (f32[64,256]{1,0:T(8,128)S(1)}, f32[64,256]{1,0:T(8,128)S(1)}, u32[]{:S(2)}, u32[]{:S(2)}) collective-permute-start(f32[64,256]{1,0:T(8,128)S(1)} %get-tuple-element.62), channel_id=1, source_target_pairs={{0,4},{2,6},{4,0},{6,2},{8,12},{10,14},{12,8},{14,10},{1,5},{3,7},... | collective-permute-start | bytes 196616 | tf_op jit(solution)/shard_map/ppermute | solution.py:542
  41.6 1.4 %collective-permute-start.15 = (f32[64,256]{1,0:T(8,128)S(1)}, f32[64,256]{1,0:T(8,128)S(1)}, u32[]{:S(2)}, u32[]{:S(2)}) collective-permute-start(f32[64,256]{1,0:T(8,128)S(1)} %get-tuple-element.63), channel_id=1, source_target_pairs={{0,6},{2,4},{4,2},{6,0},{8,14},{10,12},{12,10},{14,8},{1,7},{3,5},... | collective-permute-start | bytes 196616 | tf_op jit(solution)/shard_map/ppermute | solution.py:542
  43.0 3.3 %inverse_first.2 = (f32[4224,128]{1,0:T(8,128)S(1)}, f32[4224,128]{1,0:T(8,128)S(1)}) custom-call(s32[2]{0:T(128)S(1)} %pad_add_fusion.place, f32[16,2,128,256]{3,2,1,0:T(8,128)S(1)} %get-tuple-element.39.modes, bf16[2,2,768,256]{3,2,1,0:T(8,128)(2,1)S(1)} %copy-done.2, f32[2,2,256,256]{3,2,1,0:T(8,128)S(1)} %copy-done.4, ...), custom_call_target="tpu_custom_call" | custom-call | flops 2147483648 | bytes 8388608 | tf_op jit(solution)/shard_map/inverse_first/pallas_call | solution.py:426
  46.3 0.4 collective-permute-done.15.refs_3_
  46.8 3.1 %inverse_first.3 = (f32[4224,128]{1,0:T(8,128)S(1)}, f32[4224,128]{1,0:T(8,128)S(1)}) custom-call(s32[2]{0:T(128)S(1)} %pad_add_fusion.place, f32[16,2,128,256]{3,2,1,0:T(8,128)S(1)} %get-tuple-element.53.modes, bf16[2,2,768,256]{3,2,1,0:T(8,128)(2,1)S(1)} %copy-done.2, f32[2,2,256,256]{3,2,1,0:T(8,128)S(1)} %copy-done.4, ...), custom_call_target="tpu_custom_call" | custom-call | flops 2147483648 | bytes 8388608 | tf_op jit(solution)/shard_map/inverse_first/pallas_call | solution.py:426
  49.8 0.2 collective-permute-start.17
  50.0 3.5 %keep_inverse.1.kept = f32[4096,256]{1,0:T(8,128)S(1)} custom-call(s32[2]{0:T(128)S(1)} %pad_add_fusion.place, bf16[2,768,256]{2,1,0:T(8,128)(2,1)S(1)} %copy-done.1, f32[4224,128]{1,0:T(8,128)S(1)} %get-tuple-element.50.refs_0_, f32[4224,128]{1,0:T(8,128)S(1)} %get-tuple-element.64.refs_1_), custom_call_target="tpu_custom_call" | custom-call | flops 2147483648 | bytes 8388608 | tf_op jit(solution)/shard_map/keep_inverse/pallas_call | solution.py:458
  53.6 0.6 collective-permute-done.17.refs_1_
  54.2 5.9 %inverse_second.1 = f32[256,16,512]{2,1,0:T(8,128)} custom-call(s32[2]{0:T(128)S(1)} %pad_add_fusion.place, bf16[2,768,256]{2,1,0:T(8,128)(2,1)S(1)} %copy-done.1, f32[4096,256]{1,0:T(8,128)S(1)} %keep_inverse.1.kept, f32[4224,128]{1,0:T(8,128)S(1)} %collective-permute-done.16.refs_0_, f32[4224,128]{1,0:T(8,128)S(1)} %collective-permute-done.17.refs_1_), custom_call_target="tpu_custom_call" | custom-call | flops 4294967296 | bytes 8388608 | tf_op jit(solution)/shard_map/inverse_second/pallas_call | solution.py:523
  (29 shorter events, 0.1 us)
Async XLA Ops:
  0.1 7.6 %copy-start.5 = (bf16[2,768,256]{2,1,0:T(8,128)(2,1)S(1)}, bf16[2,768,256]{2,1,0:T(8,128)(2,1)}, u32[]{:S(2)}) copy-start(bf16[2,768,256]{2,1,0:T(8,128)(2,1)} %constant.23.clone.tables) | copy-start | bytes 2359300
  7.0 4.6 %collective-permute-start = (f32[4488,128]{1,0:T(8,128)S(1)}, f32[4488,128]{1,0:T(8,128)S(1)}, u32[]{:S(2)}, u32[]{:S(2)}) collective-permute-start(f32[4488,128]{1,0:T(8,128)S(1)} %get-tuple-element.38), channel_id=1, source_target_pairs={{0,1},{1,0},{2,3},{3,2},{4,5},{5,4},{6,7},{7,6},{8,9},{9,8},{10,11... | collective-permute-start | bytes 6893576 | tf_op jit(solution)/shard_map/ppermute | solution.py:537
  7.6 11.8 %collective-permute-start.8 = (f32[4488,128]{1,0:T(8,128)S(1)}, f32[4488,128]{1,0:T(8,128)S(1)}, u32[]{:S(2)}, u32[]{:S(2)}) collective-permute-start(f32[4488,128]{1,0:T(8,128)S(1)} %get-tuple-element.52), channel_id=1, source_target_pairs={{0,1},{1,0},{2,3},{3,2},{4,5},{5,4},{6,7},{7,6},{8,9},{9,8},{10,11... | collective-permute-start | bytes 6893576 | tf_op jit(solution)/shard_map/ppermute | solution.py:537
  7.6 4.0 %copy-start.3 = (bf16[2,2,768,256]{3,2,1,0:T(8,128)(2,1)S(1)}, bf16[2,2,768,256]{3,2,1,0:T(8,128)(2,1)}, u32[]{:S(2)}) copy-start(bf16[2,2,768,256]{3,2,1,0:T(8,128)(2,1)} %constant.21.clone.table) | copy-start | bytes 4718596
  7.6 4.0 %copy-start.4 = (f32[2,2,256,256]{3,2,1,0:T(8,128)S(1)}, f32[2,2,256,256]{3,2,1,0:T(8,128)}, u32[]{:S(2)}) copy-start(f32[2,2,256,256]{3,2,1,0:T(8,128)} %constant.22.clone.decay) | copy-start | bytes 3145732
  14.9 11.3 %collective-permute-start.1 = (f32[64,256]{1,0:T(8,128)S(1)}, f32[64,256]{1,0:T(8,128)S(1)}, u32[]{:S(2)}, u32[]{:S(2)}) collective-permute-start(f32[64,256]{1,0:T(8,128)S(1)} %get-tuple-element.41), channel_id=1, source_target_pairs={{0,2},{2,0},{4,6},{6,4},{8,10},{10,8},{12,14},{14,12},{1,3},{3,1},... | collective-permute-start | bytes 196616 | tf_op jit(solution)/shard_map/ppermute | solution.py:542
  17.8 8.4 %collective-permute-start.2 = (f32[64,256]{1,0:T(8,128)S(1)}, f32[64,256]{1,0:T(8,128)S(1)}, u32[]{:S(2)}, u32[]{:S(2)}) collective-permute-start(f32[64,256]{1,0:T(8,128)S(1)} %get-tuple-element.42), channel_id=1, source_target_pairs={{0,4},{2,6},{4,0},{6,2},{8,12},{10,14},{12,8},{14,10},{1,5},{3,7},... | collective-permute-start | bytes 196616 | tf_op jit(solution)/shard_map/ppermute | solution.py:542
  19.4 6.8 %collective-permute-start.3 = (f32[64,256]{1,0:T(8,128)S(1)}, f32[64,256]{1,0:T(8,128)S(1)}, u32[]{:S(2)}, u32[]{:S(2)}) collective-permute-start(f32[64,256]{1,0:T(8,128)S(1)} %get-tuple-element.43), channel_id=1, source_target_pairs={{0,6},{2,4},{4,2},{6,0},{8,14},{10,12},{12,10},{14,8},{1,7},{3,5},... | collective-permute-start | bytes 196616 | tf_op jit(solution)/shard_map/ppermute | solution.py:542
  19.4 6.8 %copy-start = (f32[2,2,3,256,256]{4,3,2,1,0:T(8,128)S(1)}, f32[2,2,3,256,256]{4,3,2,1,0:T(8,128)}, u32[]{:S(2)}) copy-start(f32[2,2,3,256,256]{4,3,2,1,0:T(8,128)} %constant.20.clone.closing) | copy-start | bytes 9437188
  22.7 7.2 %collective-permute-start.9 = (f32[64,256]{1,0:T(8,128)S(1)}, f32[64,256]{1,0:T(8,128)S(1)}, u32[]{:S(2)}, u32[]{:S(2)}) collective-permute-start(f32[64,256]{1,0:T(8,128)S(1)} %get-tuple-element.55), channel_id=1, source_target_pairs={{0,2},{2,0},{4,6},{6,4},{8,10},{10,8},{12,14},{14,12},{1,3},{3,1},... | collective-permute-start | bytes 196616 | tf_op jit(solution)/shard_map/ppermute | solution.py:542
  24.6 5.2 %collective-permute-start.10 = (f32[64,256]{1,0:T(8,128)S(1)}, f32[64,256]{1,0:T(8,128)S(1)}, u32[]{:S(2)}, u32[]{:S(2)}) collective-permute-start(f32[64,256]{1,0:T(8,128)S(1)} %get-tuple-element.56), channel_id=1, source_target_pairs={{0,4},{2,6},{4,0},{6,2},{8,12},{10,14},{12,8},{14,10},{1,5},{3,7},... | collective-permute-start | bytes 196616 | tf_op jit(solution)/shard_map/ppermute | solution.py:542
  26.2 5.4 %collective-permute-start.11 = (f32[64,256]{1,0:T(8,128)S(1)}, f32[64,256]{1,0:T(8,128)S(1)}, u32[]{:S(2)}, u32[]{:S(2)}) collective-permute-start(f32[64,256]{1,0:T(8,128)S(1)} %get-tuple-element.57), channel_id=1, source_target_pairs={{0,6},{2,4},{4,2},{6,0},{8,14},{10,12},{12,10},{14,8},{1,7},{3,5},... | collective-permute-start | bytes 196616 | tf_op jit(solution)/shard_map/ppermute | solution.py:542
  26.8 7.8 %collective-permute-start.4 = (f32[64,256]{1,0:T(8,128)S(1)}, f32[64,256]{1,0:T(8,128)S(1)}, u32[]{:S(2)}, u32[]{:S(2)}) collective-permute-start(f32[64,256]{1,0:T(8,128)S(1)} %get-tuple-element.45.near), channel_id=1, source_target_pairs={{0,8},{2,10},{4,12},{6,14},{8,0},{10,2},{12,4},{14,6},{1,9},{3,11}... | collective-permute-start | bytes 196616 | tf_op jit(solution)/shard_map/ppermute | solution.py:542
  32.2 6.6 %collective-permute-start.12 = (f32[64,256]{1,0:T(8,128)S(1)}, f32[64,256]{1,0:T(8,128)S(1)}, u32[]{:S(2)}, u32[]{:S(2)}) collective-permute-start(f32[64,256]{1,0:T(8,128)S(1)} %get-tuple-element.59.near), channel_id=1, source_target_pairs={{0,8},{2,10},{4,12},{6,14},{8,0},{10,2},{12,4},{14,6},{1,9},{3,11}... | collective-permute-start | bytes 196616 | tf_op jit(solution)/shard_map/ppermute | solution.py:542
  35.2 7.7 %copy-start.2 = (bf16[2,2,768,256]{3,2,1,0:T(8,128)(2,1)S(1)}, bf16[2,2,768,256]{3,2,1,0:T(8,128)(2,1)}, u32[]{:S(2)}) copy-start(bf16[2,2,768,256]{3,2,1,0:T(8,128)(2,1)} %constant.24.clone.table) | copy-start | bytes 4718596
  35.2 6.3 %collective-permute-start.5 = (f32[64,256]{1,0:T(8,128)S(1)}, f32[64,256]{1,0:T(8,128)S(1)}, u32[]{:S(2)}, u32[]{:S(2)}) collective-permute-start(f32[64,256]{1,0:T(8,128)S(1)} %get-tuple-element.47), channel_id=1, source_target_pairs={{0,2},{2,0},{4,6},{6,4},{8,10},{10,8},{12,14},{14,12},{1,3},{3,1},... | collective-permute-start | bytes 196616 | tf_op jit(solution)/shard_map/ppermute | solution.py:542
  35.8 7.2 %collective-permute-start.6 = (f32[64,256]{1,0:T(8,128)S(1)}, f32[64,256]{1,0:T(8,128)S(1)}, u32[]{:S(2)}, u32[]{:S(2)}) collective-permute-start(f32[64,256]{1,0:T(8,128)S(1)} %get-tuple-element.48), channel_id=1, source_target_pairs={{0,4},{2,6},{4,0},{6,2},{8,12},{10,14},{12,8},{14,10},{1,5},{3,7},... | collective-permute-start | bytes 196616 | tf_op jit(solution)/shard_map/ppermute | solution.py:542
  37.4 5.5 %collective-permute-start.7 = (f32[64,256]{1,0:T(8,128)S(1)}, f32[64,256]{1,0:T(8,128)S(1)}, u32[]{:S(2)}, u32[]{:S(2)}) collective-permute-start(f32[64,256]{1,0:T(8,128)S(1)} %get-tuple-element.49), channel_id=1, source_target_pairs={{0,6},{2,4},{4,2},{6,0},{8,14},{10,12},{12,10},{14,8},{1,7},{3,5},... | collective-permute-start | bytes 196616 | tf_op jit(solution)/shard_map/ppermute | solution.py:542
  39.4 6.9 %collective-permute-start.13 = (f32[64,256]{1,0:T(8,128)S(1)}, f32[64,256]{1,0:T(8,128)S(1)}, u32[]{:S(2)}, u32[]{:S(2)}) collective-permute-start(f32[64,256]{1,0:T(8,128)S(1)} %get-tuple-element.61), channel_id=1, source_target_pairs={{0,2},{2,0},{4,6},{6,4},{8,10},{10,8},{12,14},{14,12},{1,3},{3,1},... | collective-permute-start | bytes 196616 | tf_op jit(solution)/shard_map/ppermute | solution.py:542
  40.0 6.4 %collective-permute-start.14 = (f32[64,256]{1,0:T(8,128)S(1)}, f32[64,256]{1,0:T(8,128)S(1)}, u32[]{:S(2)}, u32[]{:S(2)}) collective-permute-start(f32[64,256]{1,0:T(8,128)S(1)} %get-tuple-element.62), channel_id=1, source_target_pairs={{0,4},{2,6},{4,0},{6,2},{8,12},{10,14},{12,8},{14,10},{1,5},{3,7},... | collective-permute-start | bytes 196616 | tf_op jit(solution)/shard_map/ppermute | solution.py:542
  41.6 5.2 %collective-permute-start.15 = (f32[64,256]{1,0:T(8,128)S(1)}, f32[64,256]{1,0:T(8,128)S(1)}, u32[]{:S(2)}, u32[]{:S(2)}) collective-permute-start(f32[64,256]{1,0:T(8,128)S(1)} %get-tuple-element.63), channel_id=1, source_target_pairs={{0,6},{2,4},{4,2},{6,0},{8,14},{10,12},{12,10},{14,8},{1,7},{3,5},... | collective-permute-start | bytes 196616 | tf_op jit(solution)/shard_map/ppermute | solution.py:542
  46.2 7.3 %collective-permute-start.16 = (f32[4224,128]{1,0:T(8,128)S(1)}, f32[4224,128]{1,0:T(8,128)S(1)}, u32[]{:S(2)}, u32[]{:S(2)}) collective-permute-start(f32[4224,128]{1,0:T(8,128)S(1)} %get-tuple-element.65), channel_id=1, source_target_pairs={{0,1},{1,0},{2,3},{3,2},{4,5},{5,4},{6,7},{7,6},{8,9},{9,8},{10,11... | collective-permute-start | bytes 6488072 | tf_op jit(solution)/shard_map/ppermute | solution.py:537
  46.8 3.2 %copy-start.1 = (bf16[2,768,256]{2,1,0:T(8,128)(2,1)S(1)}, bf16[2,768,256]{2,1,0:T(8,128)(2,1)}, u32[]{:S(2)}) copy-start(bf16[2,768,256]{2,1,0:T(8,128)(2,1)} %constant.25.clone.tables) | copy-start | bytes 2359300
  49.8 4.3 %collective-permute-start.17 = (f32[4224,128]{1,0:T(8,128)S(1)}, f32[4224,128]{1,0:T(8,128)S(1)}, u32[]{:S(2)}, u32[]{:S(2)}) collective-permute-start(f32[4224,128]{1,0:T(8,128)S(1)} %get-tuple-element.66), channel_id=1, source_target_pairs={{0,1},{1,0},{2,3},{3,2},{4,5},{5,4},{6,7},{7,6},{8,9},{9,8},{10,11... | collective-permute-start | bytes 6488072 | tf_op jit(solution)/shard_map/ppermute | solution.py:537

commit v15 on v14

--- a/solution.py
+++ b/solution.py
@@ -76,9 +76,21 @@
     return jnp.dot(rows, table, preferred_element_type=jnp.float32)
 
 
-def lanes_reversed(block):
-    index = LANES - 1 - lax.broadcasted_iota(jnp.int32, (block.shape[0], LANES), 1)
-    return jnp.take_along_axis(block, index, axis=1, mode="promise_in_bounds")
+ALONG_LANES = lax.GatherDimensionNumbers(
+    offset_dims=(),
+    collapsed_slice_dims=(1,),
+    start_index_map=(1,),
+    operand_batching_dims=(0,),
+    start_indices_batching_dims=(0,),
+)
+
+
+def reversal():
+    index = LANES - 1 - lax.broadcasted_iota(jnp.int32, (TILE, LANES), 1)
+    index = index.reshape(TILE, LANES, 1)
+    return lambda block: lax.gather(
+        block, index, ALONG_LANES, (1, 1), mode=lax.GatherScatterMode.PROMISE_IN_BOUNDS
+    )
 
 
 def store_rows_reversed(ref, start, block):
@@ -153,6 +165,8 @@
         for at in range(first, min(last, pieces)):
             for copy in copies(at):
                 copy.start()
+
+    lanes_reversed = reversal()
 
     def put(other, at, sums_at, cells):
         lower = cells[:, :half]
@@ -485,6 +499,8 @@
         here = pl.ds(at * piece, piece)
         return pltpu.make_async_copy(out.at[here], target.at[here], sems.at[at])
 
+    lanes_reversed = reversal()
+
     def product(at):
         split, result = scratch[2 * (at % count) : 2 * (at % count) + 2]
         for row in range(0, piece, group):

time: 60.4 us -> 60.3 us (level)
  no operation moved by 1% of the time
where the time goes in v15:
time: 60.3 us; the launch traced here: 60.2 us
  Pallas kernels  34.2 us (57%)
  starting transfers between devices  21.5 us (36%)
  waiting for transfers between devices  4.09 us (7%)
    ppermute x14, starting transfers between devices, with_partner(): lax.ppermute(block, 'tm', [(slab, slab ^ distance) for slab in range(slab...  20.6 us
    pallas_call x1, Pallas kernels, forward_second(): call(forward_second_kernel, 'forward_second', [IN_HBM] * 3, [IN_VMEM] * (...  6.92 us
    pallas_call x2, Pallas kernels, forward_first(): call(functools.partial(forward_first_kernel, slabs, chunk), 'forward_firs...  6.49 us
    pallas_call x2, Pallas kernels, inverse_first(): call(functools.partial(inverse_first_kernel, slabs, chunk), 'inverse_firs...  6.32 us
    pallas_call x1, Pallas kernels, inverse_second(): call(inverse_second_kernel, 'inverse_second', [IN_VMEM] * (2 + CHUNKS), I...  5.9 us
    pallas_call x1, Pallas kernels, keep_inverse(): call(functools.partial(keep_inverse_kernel, steps), 'keep_inverse', [IN_V...  3.54 us
    pallas_call x1, Pallas kernels, keep_second(): call(functools.partial(keep_second_kernel, steps), 'keep_second', [IN_VME...  2.68 us
    ppermute x14, waiting for transfers between devices, with_partner(): lax.ppermute(block, 'tm', [(slab, slab ^ distance) for slab in range(slab...  2.17 us
  transfers between devices with their start and end apart: 18, of which 4 were waited for; matrix products, arithmetic and copies ran while one was open for 0% of the time, Pallas kernels for 36%

profile of v15, /device:TPU:0, one launch (start us, length us, event | category | flops | bytes accessed | tf_op | source)
XLA Modules:
  0.0 60.2 jit_solution(12116082033254969013)
XLA Ops:
  0.0 0.1 pad_add_fusion.place
  0.1 6.9 %forward_second.1 = (f32[4352,256]{1,0:T(8,128)S(1)}, f32[4488,128]{1,0:T(8,128)S(1)}, f32[4488,128]{1,0:T(8,128)S(1)}) custom-call(s32[2]{0:T(128)S(1)} %pad_add_fusion.place, f32[256,16,512]{2,1,0:T(8,128)} %field_in.1, f32[256,512]{1,0:T(8,128)} %initial_in.1, bf16[2,768,256]{2,1,0:T(8,128)(2,1)} %constant.23.clone.tables), custom_call_target="tpu_custom_call" | custom-call | flops 4294967296 | bytes 8388608 | tf_op jit(solution)/shard_map/forward_second/pallas_call | solution.py:221
  7.0 0.6 collective-permute-start
  7.6 0.1 collective-permute-start.8
  7.6 2.7 %keep_second.1 = (f32[4488,128]{1,0:T(8,128)S(1)}, f32[4488,128]{1,0:T(8,128)S(1)}) custom-call(s32[2]{0:T(128)S(1)} %pad_add_fusion.place, bf16[2,768,256]{2,1,0:T(8,128)(2,1)S(1)} %copy-done.5, f32[4352,256]{1,0:T(8,128)S(1)} %get-tuple-element.36.sums), custom_call_target="tpu_custom_call" | custom-call | flops 2147483648 | bytes 8388608 | tf_op jit(solution)/shard_map/keep_second/pallas_call | solution.py:266
  10.3 1.3 %collective-permute-done.got = f32[4488,128]{1,0:T(8,128)S(1)} collective-permute-done((f32[4488,128]{1,0:T(8,128)S(1)}, f32[4488,128]{1,0:T(8,128)S(1)}, u32[]{:S(2)}, u32[]{:S(2)}) %collective-permute-start) | collective-permute-done | bytes 2297888 | tf_op jit(solution)/shard_map/ppermute | solution.py:553
  11.6 3.2 %forward_first.2 = (f32[16,2,128,256]{3,2,1,0:T(8,128)S(1)}, f32[64,256]{1,0:T(8,128)S(1)}, f32[64,256]{1,0:T(8,128)S(1)}, f32[64,256]{1,0:T(8,128)S(1)}, f32[64,256]{1,0:T(8,128)S(1)}) custom-call(s32[2]{0:T(128)S(1)} %pad_add_fusion.place, f32[4488,128]{1,0:T(8,128)S(1)} %get-tuple-element.37.keep, f32[4488,128]{1,0:T(8,128)S(1)} %collective-permute-done.got, ...), custom_call_target="tpu_custom_call" | custom-call | flops 2147483648 | bytes 8388608 | tf_op jit(solution)/shard_map/forward_first/pallas_call | solution.py:331
  14.9 2.9 %collective-permute-start.1 = (f32[64,256]{1,0:T(8,128)S(1)}, f32[64,256]{1,0:T(8,128)S(1)}, u32[]{:S(2)}, u32[]{:S(2)}) collective-permute-start(f32[64,256]{1,0:T(8,128)S(1)} %get-tuple-element.41), channel_id=1, source_target_pairs={{0,2},{2,0},{4,6},{6,4},{8,10},{10,8},{12,14},{14,12},{1,3},{3,1},... | collective-permute-start | bytes 196616 | tf_op jit(solution)/shard_map/ppermute | solution.py:558
  17.8 1.6 %collective-permute-start.2 = (f32[64,256]{1,0:T(8,128)S(1)}, f32[64,256]{1,0:T(8,128)S(1)}, u32[]{:S(2)}, u32[]{:S(2)}) collective-permute-start(f32[64,256]{1,0:T(8,128)S(1)} %get-tuple-element.42), channel_id=1, source_target_pairs={{0,4},{2,6},{4,0},{6,2},{8,12},{10,14},{12,8},{14,10},{1,5},{3,7},... | collective-permute-start | bytes 196616 | tf_op jit(solution)/shard_map/ppermute | solution.py:558
  19.4 3.2 %forward_first.3 = (f32[16,2,128,256]{3,2,1,0:T(8,128)S(1)}, f32[64,256]{1,0:T(8,128)S(1)}, f32[64,256]{1,0:T(8,128)S(1)}, f32[64,256]{1,0:T(8,128)S(1)}, f32[64,256]{1,0:T(8,128)S(1)}) custom-call(s32[2]{0:T(128)S(1)} %pad_add_fusion.place, f32[4488,128]{1,0:T(8,128)S(1)} %get-tuple-element.51.keep, f32[4488,128]{1,0:T(8,128)S(1)} %collective-permute-done.8.got, ...), custom_call_target="tpu_custom_call" | custom-call | flops 2147483648 | bytes 8388608 | tf_op jit(solution)/shard_map/forward_first/pallas_call | solution.py:331
  22.7 2.0 %collective-permute-start.9 = (f32[64,256]{1,0:T(8,128)S(1)}, f32[64,256]{1,0:T(8,128)S(1)}, u32[]{:S(2)}, u32[]{:S(2)}) collective-permute-start(f32[64,256]{1,0:T(8,128)S(1)} %get-tuple-element.55), channel_id=1, source_target_pairs={{0,2},{2,0},{4,6},{6,4},{8,10},{10,8},{12,14},{14,12},{1,3},{3,1},... | collective-permute-start | bytes 196616 | tf_op jit(solution)/shard_map/ppermute | solution.py:558
  24.6 1.6 %collective-permute-start.10 = (f32[64,256]{1,0:T(8,128)S(1)}, f32[64,256]{1,0:T(8,128)S(1)}, u32[]{:S(2)}, u32[]{:S(2)}) collective-permute-start(f32[64,256]{1,0:T(8,128)S(1)} %get-tuple-element.56), channel_id=1, source_target_pairs={{0,4},{2,6},{4,0},{6,2},{8,12},{10,14},{12,8},{14,10},{1,5},{3,7},... | collective-permute-start | bytes 196616 | tf_op jit(solution)/shard_map/ppermute | solution.py:558
  26.2 0.6 half_sum.2
  26.8 3.0 %collective-permute-start.4 = (f32[64,256]{1,0:T(8,128)S(1)}, f32[64,256]{1,0:T(8,128)S(1)}, u32[]{:S(2)}, u32[]{:S(2)}) collective-permute-start(f32[64,256]{1,0:T(8,128)S(1)} %get-tuple-element.45.near), channel_id=1, source_target_pairs={{0,8},{2,10},{4,12},{6,14},{8,0},{10,2},{12,4},{14,6},{1,9},{3,11}... | collective-permute-start | bytes 196616 | tf_op jit(solution)/shard_map/ppermute | solution.py:558
  29.9 1.7 %collective-permute-done.11.refs_3_ = f32[64,256]{1,0:T(8,128)S(1)} collective-permute-done((f32[64,256]{1,0:T(8,128)S(1)}, f32[64,256]{1,0:T(8,128)S(1)}, u32[]{:S(2)}, u32[]{:S(2)}) %collective-permute-start.11) | collective-permute-done | bytes 65568 | tf_op jit(solution)/shard_map/ppermute | solution.py:558
  31.6 0.6 half_sum.3
  32.2 2.4 %collective-permute-start.12 = (f32[64,256]{1,0:T(8,128)S(1)}, f32[64,256]{1,0:T(8,128)S(1)}, u32[]{:S(2)}, u32[]{:S(2)}) collective-permute-start(f32[64,256]{1,0:T(8,128)S(1)} %get-tuple-element.59.near), channel_id=1, source_target_pairs={{0,8},{2,10},{4,12},{6,14},{8,0},{10,2},{12,4},{14,6},{1,9},{3,11}... | collective-permute-start | bytes 196616 | tf_op jit(solution)/shard_map/ppermute | solution.py:558
  34.6 0.6 close.2
  35.2 0.6 collective-permute-start.5
  35.8 1.6 %collective-permute-start.6 = (f32[64,256]{1,0:T(8,128)S(1)}, f32[64,256]{1,0:T(8,128)S(1)}, u32[]{:S(2)}, u32[]{:S(2)}) collective-permute-start(f32[64,256]{1,0:T(8,128)S(1)} %get-tuple-element.48), channel_id=1, source_target_pairs={{0,4},{2,6},{4,0},{6,2},{8,12},{10,14},{12,8},{14,10},{1,5},{3,7},... | collective-permute-start | bytes 196616 | tf_op jit(solution)/shard_map/ppermute | solution.py:558
  37.4 1.4 %collective-permute-start.7 = (f32[64,256]{1,0:T(8,128)S(1)}, f32[64,256]{1,0:T(8,128)S(1)}, u32[]{:S(2)}, u32[]{:S(2)}) collective-permute-start(f32[64,256]{1,0:T(8,128)S(1)} %get-tuple-element.49), channel_id=1, source_target_pairs={{0,6},{2,4},{4,2},{6,0},{8,14},{10,12},{12,10},{14,8},{1,7},{3,5},... | collective-permute-start | bytes 196616 | tf_op jit(solution)/shard_map/ppermute | solution.py:558
  38.8 0.6 close.3
  39.4 0.6 collective-permute-start.13
  40.0 1.6 %collective-permute-start.14 = (f32[64,256]{1,0:T(8,128)S(1)}, f32[64,256]{1,0:T(8,128)S(1)}, u32[]{:S(2)}, u32[]{:S(2)}) collective-permute-start(f32[64,256]{1,0:T(8,128)S(1)} %get-tuple-element.62), channel_id=1, source_target_pairs={{0,4},{2,6},{4,0},{6,2},{8,12},{10,14},{12,8},{14,10},{1,5},{3,7},... | collective-permute-start | bytes 196616 | tf_op jit(solution)/shard_map/ppermute | solution.py:558
  41.6 1.4 %collective-permute-start.15 = (f32[64,256]{1,0:T(8,128)S(1)}, f32[64,256]{1,0:T(8,128)S(1)}, u32[]{:S(2)}, u32[]{:S(2)}) collective-permute-start(f32[64,256]{1,0:T(8,128)S(1)} %get-tuple-element.63), channel_id=1, source_target_pairs={{0,6},{2,4},{4,2},{6,0},{8,14},{10,12},{12,10},{14,8},{1,7},{3,5},... | collective-permute-start | bytes 196616 | tf_op jit(solution)/shard_map/ppermute | solution.py:558
  43.0 3.3 %inverse_first.2 = (f32[4224,128]{1,0:T(8,128)S(1)}, f32[4224,128]{1,0:T(8,128)S(1)}) custom-call(s32[2]{0:T(128)S(1)} %pad_add_fusion.place, f32[16,2,128,256]{3,2,1,0:T(8,128)S(1)} %get-tuple-element.39.modes, bf16[2,2,768,256]{3,2,1,0:T(8,128)(2,1)S(1)} %copy-done.2, f32[2,2,256,256]{3,2,1,0:T(8,128)S(1)} %copy-done.4, ...), custom_call_target="tpu_custom_call" | custom-call | flops 2147483648 | bytes 8388608 | tf_op jit(solution)/shard_map/inverse_first/pallas_call | solution.py:440
  46.3 0.4 collective-permute-done.15.refs_3_
  46.8 3.1 %inverse_first.3 = (f32[4224,128]{1,0:T(8,128)S(1)}, f32[4224,128]{1,0:T(8,128)S(1)}) custom-call(s32[2]{0:T(128)S(1)} %pad_add_fusion.place, f32[16,2,128,256]{3,2,1,0:T(8,128)S(1)} %get-tuple-element.53.modes, bf16[2,2,768,256]{3,2,1,0:T(8,128)(2,1)S(1)} %copy-done.2, f32[2,2,256,256]{3,2,1,0:T(8,128)S(1)} %copy-done.4, ...), custom_call_target="tpu_custom_call" | custom-call | flops 2147483648 | bytes 8388608 | tf_op jit(solution)/shard_map/inverse_first/pallas_call | solution.py:440
  49.8 0.2 collective-permute-start.17
  50.0 3.5 %keep_inverse.1.kept = f32[4096,256]{1,0:T(8,128)S(1)} custom-call(s32[2]{0:T(128)S(1)} %pad_add_fusion.place, bf16[2,768,256]{2,1,0:T(8,128)(2,1)S(1)} %copy-done.1, f32[4224,128]{1,0:T(8,128)S(1)} %get-tuple-element.50.refs_0_, f32[4224,128]{1,0:T(8,128)S(1)} %get-tuple-element.64.refs_1_), custom_call_target="tpu_custom_call" | custom-call | flops 2147483648 | bytes 8388608 | tf_op jit(solution)/shard_map/keep_inverse/pallas_call | solution.py:472
  53.5 0.6 %collective-permute-done.17.refs_1_ = f32[4224,128]{1,0:T(8,128)S(1)} collective-permute-done((f32[4224,128]{1,0:T(8,128)S(1)}, f32[4224,128]{1,0:T(8,128)S(1)}, u32[]{:S(2)}, u32[]{:S(2)}) %collective-permute-start.17) | collective-permute-done | bytes 2162720 | tf_op jit(solution)/shard_map/ppermute | solution.py:553
  54.1 5.9 %inverse_second.1 = f32[256,16,512]{2,1,0:T(8,128)} custom-call(s32[2]{0:T(128)S(1)} %pad_add_fusion.place, bf16[2,768,256]{2,1,0:T(8,128)(2,1)S(1)} %copy-done.1, f32[4096,256]{1,0:T(8,128)S(1)} %keep_inverse.1.kept, f32[4224,128]{1,0:T(8,128)S(1)} %collective-permute-done.16.refs_0_, f32[4224,128]{1,0:T(8,128)S(1)} %collective-permute-done.17.refs_1_), custom_call_target="tpu_custom_call" | custom-call | flops 4294967296 | bytes 8388608 | tf_op jit(solution)/shard_map/inverse_second/pallas_call | solution.py:539
  (29 shorter events, 0.1 us)
Async XLA Ops:
  0.1 7.6 %copy-start.5 = (bf16[2,768,256]{2,1,0:T(8,128)(2,1)S(1)}, bf16[2,768,256]{2,1,0:T(8,128)(2,1)}, u32[]{:S(2)}) copy-start(bf16[2,768,256]{2,1,0:T(8,128)(2,1)} %constant.23.clone.tables) | copy-start | bytes 2359300
  7.0 4.6 %collective-permute-start = (f32[4488,128]{1,0:T(8,128)S(1)}, f32[4488,128]{1,0:T(8,128)S(1)}, u32[]{:S(2)}, u32[]{:S(2)}) collective-permute-start(f32[4488,128]{1,0:T(8,128)S(1)} %get-tuple-element.38), channel_id=1, source_target_pairs={{0,1},{1,0},{2,3},{3,2},{4,5},{5,4},{6,7},{7,6},{8,9},{9,8},{10,11... | collective-permute-start | bytes 6893576 | tf_op jit(solution)/shard_map/ppermute | solution.py:553
  7.6 11.8 %collective-permute-start.8 = (f32[4488,128]{1,0:T(8,128)S(1)}, f32[4488,128]{1,0:T(8,128)S(1)}, u32[]{:S(2)}, u32[]{:S(2)}) collective-permute-start(f32[4488,128]{1,0:T(8,128)S(1)} %get-tuple-element.52), channel_id=1, source_target_pairs={{0,1},{1,0},{2,3},{3,2},{4,5},{5,4},{6,7},{7,6},{8,9},{9,8},{10,11... | collective-permute-start | bytes 6893576 | tf_op jit(solution)/shard_map/ppermute | solution.py:553
  7.6 4.0 %copy-start.3 = (bf16[2,2,768,256]{3,2,1,0:T(8,128)(2,1)S(1)}, bf16[2,2,768,256]{3,2,1,0:T(8,128)(2,1)}, u32[]{:S(2)}) copy-start(bf16[2,2,768,256]{3,2,1,0:T(8,128)(2,1)} %constant.21.clone.table) | copy-start | bytes 4718596
  7.6 4.0 %copy-start.4 = (f32[2,2,256,256]{3,2,1,0:T(8,128)S(1)}, f32[2,2,256,256]{3,2,1,0:T(8,128)}, u32[]{:S(2)}) copy-start(f32[2,2,256,256]{3,2,1,0:T(8,128)} %constant.22.clone.decay) | copy-start | bytes 3145732
  14.9 11.3 %collective-permute-start.1 = (f32[64,256]{1,0:T(8,128)S(1)}, f32[64,256]{1,0:T(8,128)S(1)}, u32[]{:S(2)}, u32[]{:S(2)}) collective-permute-start(f32[64,256]{1,0:T(8,128)S(1)} %get-tuple-element.41), channel_id=1, source_target_pairs={{0,2},{2,0},{4,6},{6,4},{8,10},{10,8},{12,14},{14,12},{1,3},{3,1},... | collective-permute-start | bytes 196616 | tf_op jit(solution)/shard_map/ppermute | solution.py:558
  17.8 8.4 %collective-permute-start.2 = (f32[64,256]{1,0:T(8,128)S(1)}, f32[64,256]{1,0:T(8,128)S(1)}, u32[]{:S(2)}, u32[]{:S(2)}) collective-permute-start(f32[64,256]{1,0:T(8,128)S(1)} %get-tuple-element.42), channel_id=1, source_target_pairs={{0,4},{2,6},{4,0},{6,2},{8,12},{10,14},{12,8},{14,10},{1,5},{3,7},... | collective-permute-start | bytes 196616 | tf_op jit(solution)/shard_map/ppermute | solution.py:558
  19.4 6.8 %collective-permute-start.3 = (f32[64,256]{1,0:T(8,128)S(1)}, f32[64,256]{1,0:T(8,128)S(1)}, u32[]{:S(2)}, u32[]{:S(2)}) collective-permute-start(f32[64,256]{1,0:T(8,128)S(1)} %get-tuple-element.43), channel_id=1, source_target_pairs={{0,6},{2,4},{4,2},{6,0},{8,14},{10,12},{12,10},{14,8},{1,7},{3,5},... | collective-permute-start | bytes 196616 | tf_op jit(solution)/shard_map/ppermute | solution.py:558
  19.4 6.8 %copy-start = (f32[2,2,3,256,256]{4,3,2,1,0:T(8,128)S(1)}, f32[2,2,3,256,256]{4,3,2,1,0:T(8,128)}, u32[]{:S(2)}) copy-start(f32[2,2,3,256,256]{4,3,2,1,0:T(8,128)} %constant.20.clone.closing) | copy-start | bytes 9437188
  22.7 7.2 %collective-permute-start.9 = (f32[64,256]{1,0:T(8,128)S(1)}, f32[64,256]{1,0:T(8,128)S(1)}, u32[]{:S(2)}, u32[]{:S(2)}) collective-permute-start(f32[64,256]{1,0:T(8,128)S(1)} %get-tuple-element.55), channel_id=1, source_target_pairs={{0,2},{2,0},{4,6},{6,4},{8,10},{10,8},{12,14},{14,12},{1,3},{3,1},... | collective-permute-start | bytes 196616 | tf_op jit(solution)/shard_map/ppermute | solution.py:558
  24.6 5.2 %collective-permute-start.10 = (f32[64,256]{1,0:T(8,128)S(1)}, f32[64,256]{1,0:T(8,128)S(1)}, u32[]{:S(2)}, u32[]{:S(2)}) collective-permute-start(f32[64,256]{1,0:T(8,128)S(1)} %get-tuple-element.56), channel_id=1, source_target_pairs={{0,4},{2,6},{4,0},{6,2},{8,12},{10,14},{12,8},{14,10},{1,5},{3,7},... | collective-permute-start | bytes 196616 | tf_op jit(solution)/shard_map/ppermute | solution.py:558
  26.2 5.4 %collective-permute-start.11 = (f32[64,256]{1,0:T(8,128)S(1)}, f32[64,256]{1,0:T(8,128)S(1)}, u32[]{:S(2)}, u32[]{:S(2)}) collective-permute-start(f32[64,256]{1,0:T(8,128)S(1)} %get-tuple-element.57), channel_id=1, source_target_pairs={{0,6},{2,4},{4,2},{6,0},{8,14},{10,12},{12,10},{14,8},{1,7},{3,5},... | collective-permute-start | bytes 196616 | tf_op jit(solution)/shard_map/ppermute | solution.py:558
  26.8 7.8 %collective-permute-start.4 = (f32[64,256]{1,0:T(8,128)S(1)}, f32[64,256]{1,0:T(8,128)S(1)}, u32[]{:S(2)}, u32[]{:S(2)}) collective-permute-start(f32[64,256]{1,0:T(8,128)S(1)} %get-tuple-element.45.near), channel_id=1, source_target_pairs={{0,8},{2,10},{4,12},{6,14},{8,0},{10,2},{12,4},{14,6},{1,9},{3,11}... | collective-permute-start | bytes 196616 | tf_op jit(solution)/shard_map/ppermute | solution.py:558
  32.2 6.6 %collective-permute-start.12 = (f32[64,256]{1,0:T(8,128)S(1)}, f32[64,256]{1,0:T(8,128)S(1)}, u32[]{:S(2)}, u32[]{:S(2)}) collective-permute-start(f32[64,256]{1,0:T(8,128)S(1)} %get-tuple-element.59.near), channel_id=1, source_target_pairs={{0,8},{2,10},{4,12},{6,14},{8,0},{10,2},{12,4},{14,6},{1,9},{3,11}... | collective-permute-start | bytes 196616 | tf_op jit(solution)/shard_map/ppermute | solution.py:558
  35.2 7.7 %copy-start.2 = (bf16[2,2,768,256]{3,2,1,0:T(8,128)(2,1)S(1)}, bf16[2,2,768,256]{3,2,1,0:T(8,128)(2,1)}, u32[]{:S(2)}) copy-start(bf16[2,2,768,256]{3,2,1,0:T(8,128)(2,1)} %constant.24.clone.table) | copy-start | bytes 4718596
  35.2 6.3 %collective-permute-start.5 = (f32[64,256]{1,0:T(8,128)S(1)}, f32[64,256]{1,0:T(8,128)S(1)}, u32[]{:S(2)}, u32[]{:S(2)}) collective-permute-start(f32[64,256]{1,0:T(8,128)S(1)} %get-tuple-element.47), channel_id=1, source_target_pairs={{0,2},{2,0},{4,6},{6,4},{8,10},{10,8},{12,14},{14,12},{1,3},{3,1},... | collective-permute-start | bytes 196616 | tf_op jit(solution)/shard_map/ppermute | solution.py:558
  35.8 7.2 %collective-permute-start.6 = (f32[64,256]{1,0:T(8,128)S(1)}, f32[64,256]{1,0:T(8,128)S(1)}, u32[]{:S(2)}, u32[]{:S(2)}) collective-permute-start(f32[64,256]{1,0:T(8,128)S(1)} %get-tuple-element.48), channel_id=1, source_target_pairs={{0,4},{2,6},{4,0},{6,2},{8,12},{10,14},{12,8},{14,10},{1,5},{3,7},... | collective-permute-start | bytes 196616 | tf_op jit(solution)/shard_map/ppermute | solution.py:558
  37.4 5.5 %collective-permute-start.7 = (f32[64,256]{1,0:T(8,128)S(1)}, f32[64,256]{1,0:T(8,128)S(1)}, u32[]{:S(2)}, u32[]{:S(2)}) collective-permute-start(f32[64,256]{1,0:T(8,128)S(1)} %get-tuple-element.49), channel_id=1, source_target_pairs={{0,6},{2,4},{4,2},{6,0},{8,14},{10,12},{12,10},{14,8},{1,7},{3,5},... | collective-permute-start | bytes 196616 | tf_op jit(solution)/shard_map/ppermute | solution.py:558
  39.4 6.9 %collective-permute-start.13 = (f32[64,256]{1,0:T(8,128)S(1)}, f32[64,256]{1,0:T(8,128)S(1)}, u32[]{:S(2)}, u32[]{:S(2)}) collective-permute-start(f32[64,256]{1,0:T(8,128)S(1)} %get-tuple-element.61), channel_id=1, source_target_pairs={{0,2},{2,0},{4,6},{6,4},{8,10},{10,8},{12,14},{14,12},{1,3},{3,1},... | collective-permute-start | bytes 196616 | tf_op jit(solution)/shard_map/ppermute | solution.py:558
  40.0 6.4 %collective-permute-start.14 = (f32[64,256]{1,0:T(8,128)S(1)}, f32[64,256]{1,0:T(8,128)S(1)}, u32[]{:S(2)}, u32[]{:S(2)}) collective-permute-start(f32[64,256]{1,0:T(8,128)S(1)} %get-tuple-element.62), channel_id=1, source_target_pairs={{0,4},{2,6},{4,0},{6,2},{8,12},{10,14},{12,8},{14,10},{1,5},{3,7},... | collective-permute-start | bytes 196616 | tf_op jit(solution)/shard_map/ppermute | solution.py:558
  41.6 5.2 %collective-permute-start.15 = (f32[64,256]{1,0:T(8,128)S(1)}, f32[64,256]{1,0:T(8,128)S(1)}, u32[]{:S(2)}, u32[]{:S(2)}) collective-permute-start(f32[64,256]{1,0:T(8,128)S(1)} %get-tuple-element.63), channel_id=1, source_target_pairs={{0,6},{2,4},{4,2},{6,0},{8,14},{10,12},{12,10},{14,8},{1,7},{3,5},... | collective-permute-start | bytes 196616 | tf_op jit(solution)/shard_map/ppermute | solution.py:558
  46.2 7.3 %collective-permute-start.16 = (f32[4224,128]{1,0:T(8,128)S(1)}, f32[4224,128]{1,0:T(8,128)S(1)}, u32[]{:S(2)}, u32[]{:S(2)}) collective-permute-start(f32[4224,128]{1,0:T(8,128)S(1)} %get-tuple-element.65), channel_id=1, source_target_pairs={{0,1},{1,0},{2,3},{3,2},{4,5},{5,4},{6,7},{7,6},{8,9},{9,8},{10,11... | collective-permute-start | bytes 6488072 | tf_op jit(solution)/shard_map/ppermute | solution.py:553
  46.7 3.2 %copy-start.1 = (bf16[2,768,256]{2,1,0:T(8,128)(2,1)S(1)}, bf16[2,768,256]{2,1,0:T(8,128)(2,1)}, u32[]{:S(2)}) copy-start(bf16[2,768,256]{2,1,0:T(8,128)(2,1)} %constant.25.clone.tables) | copy-start | bytes 2359300
  49.8 4.3 %collective-permute-start.17 = (f32[4224,128]{1,0:T(8,128)S(1)}, f32[4224,128]{1,0:T(8,128)S(1)}, u32[]{:S(2)}, u32[]{:S(2)}) collective-permute-start(f32[4224,128]{1,0:T(8,128)S(1)} %get-tuple-element.66), channel_id=1, source_target_pairs={{0,1},{1,0},{2,3},{3,2},{4,5},{5,4},{6,7},{7,6},{8,9},{9,8},{10,11... | collective-permute-start | bytes 6488072 | tf_op jit(solution)/shard_map/ppermute | solution.py:553

commit v16 on v15

--- a/solution.py
+++ b/solution.py
@@ -276,6 +276,10 @@
 
 def ranks(slabs):
     return slabs // 2
+
+
+def by_distance(blocks):
+    return [blocks[0], *blocks[:0:-1]]
 
 
 def forward_first_kernel(slabs, chunk, place, keep, got, table, decay, modes, *refs):
@@ -346,7 +350,7 @@
 
 def half_sum_kernel(slabs, chunk, place, closing, *refs):
     size = ranks(slabs)
-    lasts, ordered, total = refs[:size], refs[size], refs[size + 1]
+    lasts, ordered, total = by_distance(refs[:size]), refs[size], refs[size + 1]
     share = total.shape[0]
     rank = lax.rem(place[0], size)
     decay = closing[place[1], chunk, 0, pl.ds(pl.multiple_of(rank * share, share), share)]
@@ -369,7 +373,7 @@
         [floats(size, share, rows), floats(share, rows)],
         [],
         1 << 20,
-    )(place, closing, *lasts)
+    )(place, closing, *by_distance(lasts))
 
 
 def close_kernel(slabs, chunk, place, closing, ordered, near, far, *refs):
@@ -404,7 +408,7 @@
 
 def inverse_first_kernel(slabs, chunk, place, modes, table, decay, *refs):
     size = ranks(slabs)
-    befores, (keep, send, state, split) = refs[:size], refs[size:]
+    befores, (keep, send, state, split) = by_distance(refs[:size]), refs[size:]
     steps, _, part, rows = modes.shape
     pitch = keep.shape[0] // steps
     block = split.shape[1] // part
@@ -448,7 +452,7 @@
             pltpu.VMEM((2, block * part, 2 * rows), jnp.bfloat16),
         ],
         1 << 31,
-    )(place, modes, tables, decays, *befores)
+    )(place, modes, tables, decays, *by_distance(befores))
 
 
 def keep_inverse_kernel(steps, place, tables, *refs):
@@ -489,14 +493,15 @@
     part = half // CHUNKS
     pitch = gots[0].shape[0] // steps
     count = len(scratch) // 2
-    pieces = sems.shape[0]
-    piece = cells // pieces
+    piece = scratch[0].shape[0] // steps
+    pieces = cells // piece
+    flight = cells // sems.shape[0]
     group = max(TILE // steps, 1)
     strip = place[1]
     sign = 1.0 - 2.0 * strip.astype(jnp.float32)
 
     def copy(at):
-        here = pl.ds(at * piece, piece)
+        here = pl.ds(at * flight, flight)
         return pltpu.make_async_copy(out.at[here], target.at[here], sems.at[at])
 
     lanes_reversed = reversal()
@@ -521,14 +526,16 @@
             ][::-1]
             whole = jnp.concatenate([first + second, *parts], axis=1)
             out[pl.ds(at * piece + row, group)] = whole.reshape(group, TILE // group, width)
-        copy(at).start()
+            done = at * piece + row + group
+            if done % flight == 0:
+                copy(done // flight - 1).start()
 
     for at in range(pieces):
         product(at)
         if at:
             finish(at - 1)
     finish(pieces - 1)
-    for at in range(pieces):
+    for at in range(sems.shape[0]):
         copy(at).wait()
 
 
@@ -542,7 +549,10 @@
         [IN_VMEM] * (2 + CHUNKS),
         IN_HBM,
         floats(rows, steps, 2 * half),
-        [pltpu.VMEM((rows, steps, 2 * half), jnp.float32), pltpu.SemaphoreType.DMA((rows // piece,))]
+        [
+            pltpu.VMEM((rows, steps, 2 * half), jnp.float32),
+            pltpu.SemaphoreType.DMA((2 * rows // piece,)),
+        ]
         + [pltpu.VMEM((depth, 2 * half), jnp.bfloat16), pltpu.VMEM((depth, half), jnp.float32)]
         * pieces,
         1 << 32,

time: 60.3 us -> 58.9 us (0.977)
  waiting for transfers between devices: 4.09 us -> 2.4 us
    ppermute x14, waiting for transfers between devices: 2.17 us -> 0.77 us  [with_partner(): lax.ppermute(block, 'tm', [(slab, slab ^ distance) for slab in range(slab...]
  transfers between devices with their start and end apart: 18 -> 18, of which waited for: 4 -> 3; matrix products, arithmetic and copies ran while one was open for 0% -> 0% of each run, Pallas kernels for 36% -> 36%
where the time goes in v16:
time: 58.9 us; the launch traced here: 58.8 us
  Pallas kernels  34.1 us (58%)
  starting transfers between devices  21.9 us (37%)
  waiting for transfers between devices  2.4 us (4%)
    ppermute x14, starting transfers between devices, with_partner(): lax.ppermute(block, 'tm', [(slab, slab ^ distance) for slab in range(slab...  20.6 us
    pallas_call x1, Pallas kernels, forward_second(): call(forward_second_kernel, 'forward_second', [IN_HBM] * 3, [IN_VMEM] * (...  6.92 us
    pallas_call x2, Pallas kernels, forward_first(): call(functools.partial(forward_first_kernel, slabs, chunk), 'forward_firs...  6.49 us
    pallas_call x2, Pallas kernels, inverse_first(): call(functools.partial(inverse_first_kernel, slabs, chunk), 'inverse_firs...  6.32 us
    pallas_call x1, Pallas kernels, inverse_second(): call(inverse_second_kernel, 'inverse_second', [IN_VMEM] * (2 + CHUNKS), I...  5.79 us
    pallas_call x1, Pallas kernels, keep_inverse(): call(functools.partial(keep_inverse_kernel, steps), 'keep_inverse', [IN_V...  3.54 us
    pallas_call x1, Pallas kernels, keep_second(): call(functools.partial(keep_second_kernel, steps), 'keep_second', [IN_VME...  2.68 us
    ppermute x4, waiting for transfers between devices, swapped(): return lax.ppermute(block, 'space', [(0, 1), (1, 0)])  1.63 us
  transfers between devices with their start and end apart: 18, of which 3 were waited for; matrix products, arithmetic and copies ran while one was open for 0% of the time, Pallas kernels for 36%

profile of v16, /device:TPU:0, one launch (start us, length us, event | category | flops | bytes accessed | tf_op | source)
XLA Modules:
  0.0 58.8 jit_solution(259619347664289931)
XLA Ops:
  0.0 0.1 pad_add_fusion.place
  0.1 6.9 %forward_second.1 = (f32[4352,256]{1,0:T(8,128)S(1)}, f32[4488,128]{1,0:T(8,128)S(1)}, f32[4488,128]{1,0:T(8,128)S(1)}) custom-call(s32[2]{0:T(128)S(1)} %pad_add_fusion.place, f32[256,16,512]{2,1,0:T(8,128)} %field_in.1, f32[256,512]{1,0:T(8,128)} %initial_in.1, bf16[2,768,256]{2,1,0:T(8,128)(2,1)} %constant.23.clone.tables), custom_call_target="tpu_custom_call" | custom-call | flops 4294967296 | bytes 8388608 | tf_op jit(solution)/shard_map/forward_second/pallas_call | solution.py:221
  7.0 0.6 collective-permute-start
  7.6 0.1 collective-permute-start.8
  7.6 2.7 %keep_second.1 = (f32[4488,128]{1,0:T(8,128)S(1)}, f32[4488,128]{1,0:T(8,128)S(1)}) custom-call(s32[2]{0:T(128)S(1)} %pad_add_fusion.place, bf16[2,768,256]{2,1,0:T(8,128)(2,1)S(1)} %copy-done.5, f32[4352,256]{1,0:T(8,128)S(1)} %get-tuple-element.36.sums), custom_call_target="tpu_custom_call" | custom-call | flops 2147483648 | bytes 8388608 | tf_op jit(solution)/shard_map/keep_second/pallas_call | solution.py:266
  10.3 1.3 %collective-permute-done.got = f32[4488,128]{1,0:T(8,128)S(1)} collective-permute-done((f32[4488,128]{1,0:T(8,128)S(1)}, f32[4488,128]{1,0:T(8,128)S(1)}, u32[]{:S(2)}, u32[]{:S(2)}) %collective-permute-start) | collective-permute-done | bytes 2297888 | tf_op jit(solution)/shard_map/ppermute | solution.py:563
  11.6 3.2 %forward_first.2 = (f32[16,2,128,256]{3,2,1,0:T(8,128)S(1)}, f32[64,256]{1,0:T(8,128)S(1)}, f32[64,256]{1,0:T(8,128)S(1)}, f32[64,256]{1,0:T(8,128)S(1)}, f32[64,256]{1,0:T(8,128)S(1)}) custom-call(s32[2]{0:T(128)S(1)} %pad_add_fusion.place, f32[4488,128]{1,0:T(8,128)S(1)} %get-tuple-element.37.keep, f32[4488,128]{1,0:T(8,128)S(1)} %collective-permute-done.got, ...), custom_call_target="tpu_custom_call" | custom-call | flops 2147483648 | bytes 8388608 | tf_op jit(solution)/shard_map/forward_first/pallas_call | solution.py:335
  14.9 3.9 %collective-permute-start.1 = (f32[64,256]{1,0:T(8,128)S(1)}, f32[64,256]{1,0:T(8,128)S(1)}, u32[]{:S(2)}, u32[]{:S(2)}) collective-permute-start(f32[64,256]{1,0:T(8,128)S(1)} %get-tuple-element.41), channel_id=1, source_target_pairs={{0,6},{2,4},{4,2},{6,0},{8,14},{10,12},{12,10},{14,8},{1,7},{3,5},... | collective-permute-start | bytes 196616 | tf_op jit(solution)/shard_map/ppermute | solution.py:568
  18.8 0.5 collective-permute-start.2
  19.3 0.2 collective-permute-start.3
  19.5 3.2 %forward_first.3 = (f32[16,2,128,256]{3,2,1,0:T(8,128)S(1)}, f32[64,256]{1,0:T(8,128)S(1)}, f32[64,256]{1,0:T(8,128)S(1)}, f32[64,256]{1,0:T(8,128)S(1)}, f32[64,256]{1,0:T(8,128)S(1)}) custom-call(s32[2]{0:T(128)S(1)} %pad_add_fusion.place, f32[4488,128]{1,0:T(8,128)S(1)} %get-tuple-element.51.keep, f32[4488,128]{1,0:T(8,128)S(1)} %collective-permute-done.8.got, ...), custom_call_target="tpu_custom_call" | custom-call | flops 2147483648 | bytes 8388608 | tf_op jit(solution)/shard_map/forward_first/pallas_call | solution.py:335
  22.7 2.9 %collective-permute-start.9 = (f32[64,256]{1,0:T(8,128)S(1)}, f32[64,256]{1,0:T(8,128)S(1)}, u32[]{:S(2)}, u32[]{:S(2)}) collective-permute-start(f32[64,256]{1,0:T(8,128)S(1)} %get-tuple-element.55), channel_id=1, source_target_pairs={{0,6},{2,4},{4,2},{6,0},{8,14},{10,12},{12,10},{14,8},{1,7},{3,5},... | collective-permute-start | bytes 196616 | tf_op jit(solution)/shard_map/ppermute | solution.py:568
  25.6 0.5 collective-permute-start.10
  26.1 0.2 collective-permute-start.11
  26.3 0.6 half_sum.2
  26.9 3.0 %collective-permute-start.4 = (f32[64,256]{1,0:T(8,128)S(1)}, f32[64,256]{1,0:T(8,128)S(1)}, u32[]{:S(2)}, u32[]{:S(2)}) collective-permute-start(f32[64,256]{1,0:T(8,128)S(1)} %get-tuple-element.45.near), channel_id=1, source_target_pairs={{0,8},{2,10},{4,12},{6,14},{8,0},{10,2},{12,4},{14,6},{1,9},{3,11}... | collective-permute-start | bytes 196616 | tf_op jit(solution)/shard_map/ppermute | solution.py:568
  29.9 0.7 %collective-permute-done.10.refs_2_ = f32[64,256]{1,0:T(8,128)S(1)} collective-permute-done((f32[64,256]{1,0:T(8,128)S(1)}, f32[64,256]{1,0:T(8,128)S(1)}, u32[]{:S(2)}, u32[]{:S(2)}) %collective-permute-start.10) | collective-permute-done | bytes 65568 | tf_op jit(solution)/shard_map/ppermute | solution.py:568
  30.6 0.6 half_sum.3
  31.2 2.4 %collective-permute-start.12 = (f32[64,256]{1,0:T(8,128)S(1)}, f32[64,256]{1,0:T(8,128)S(1)}, u32[]{:S(2)}, u32[]{:S(2)}) collective-permute-start(f32[64,256]{1,0:T(8,128)S(1)} %get-tuple-element.59.near), channel_id=1, source_target_pairs={{0,8},{2,10},{4,12},{6,14},{8,0},{10,2},{12,4},{14,6},{1,9},{3,11}... | collective-permute-start | bytes 196616 | tf_op jit(solution)/shard_map/ppermute | solution.py:568
  33.6 0.6 %close.2 = (f32[64,256]{1,0:T(8,128)S(1)}, f32[64,256]{1,0:T(8,128)S(1)}, f32[64,256]{1,0:T(8,128)S(1)}, f32[64,256]{1,0:T(8,128)S(1)}) custom-call(s32[2]{0:T(128)S(1)} %pad_add_fusion.place, f32[2,2,3,256,256]{4,3,2,1,0:T(8,128)S(1)} %copy-done, f32[4,64,256]{2,1,0:T(8,128)S(1)} %get-tuple-element.44.ordered, f32[64,256]{1,0:T(8,128)S(1)} %get-tuple-element.45.near, ...), custom_call_target="tpu_custom_call" | custom-call | flops 1048576 | bytes 8388608 | tf_op jit(solution)/shard_map/close/pallas_call | solution.py:398
  34.2 2.2 %collective-permute-start.5 = (f32[64,256]{1,0:T(8,128)S(1)}, f32[64,256]{1,0:T(8,128)S(1)}, u32[]{:S(2)}, u32[]{:S(2)}) collective-permute-start(f32[64,256]{1,0:T(8,128)S(1)} %get-tuple-element.47), channel_id=1, source_target_pairs={{0,6},{2,4},{4,2},{6,0},{8,14},{10,12},{12,10},{14,8},{1,7},{3,5},... | collective-permute-start | bytes 196616 | tf_op jit(solution)/shard_map/ppermute | solution.py:568
  36.5 1.3 %collective-permute-start.7 = (f32[64,256]{1,0:T(8,128)S(1)}, f32[64,256]{1,0:T(8,128)S(1)}, u32[]{:S(2)}, u32[]{:S(2)}) collective-permute-start(f32[64,256]{1,0:T(8,128)S(1)} %get-tuple-element.49), channel_id=1, source_target_pairs={{0,2},{2,0},{4,6},{6,4},{8,10},{10,8},{12,14},{14,12},{1,3},{3,1},... | collective-permute-start | bytes 196616 | tf_op jit(solution)/shard_map/ppermute | solution.py:568
  37.8 0.6 %close.3 = (f32[64,256]{1,0:T(8,128)S(1)}, f32[64,256]{1,0:T(8,128)S(1)}, f32[64,256]{1,0:T(8,128)S(1)}, f32[64,256]{1,0:T(8,128)S(1)}) custom-call(s32[2]{0:T(128)S(1)} %pad_add_fusion.place, f32[2,2,3,256,256]{4,3,2,1,0:T(8,128)S(1)} %copy-done, f32[4,64,256]{2,1,0:T(8,128)S(1)} %get-tuple-element.58.ordered, f32[64,256]{1,0:T(8,128)S(1)} %get-tuple-element.59.near, ...), custom_call_target="tpu_custom_call" | custom-call | flops 1048576 | bytes 8388608 | tf_op jit(solution)/shard_map/close/pallas_call | solution.py:398
  38.4 2.2 %collective-permute-start.13 = (f32[64,256]{1,0:T(8,128)S(1)}, f32[64,256]{1,0:T(8,128)S(1)}, u32[]{:S(2)}, u32[]{:S(2)}) collective-permute-start(f32[64,256]{1,0:T(8,128)S(1)} %get-tuple-element.61), channel_id=1, source_target_pairs={{0,6},{2,4},{4,2},{6,0},{8,14},{10,12},{12,10},{14,8},{1,7},{3,5},... | collective-permute-start | bytes 196616 | tf_op jit(solution)/shard_map/ppermute | solution.py:568
  40.6 1.3 %collective-permute-start.15 = (f32[64,256]{1,0:T(8,128)S(1)}, f32[64,256]{1,0:T(8,128)S(1)}, u32[]{:S(2)}, u32[]{:S(2)}) collective-permute-start(f32[64,256]{1,0:T(8,128)S(1)} %get-tuple-element.63), channel_id=1, source_target_pairs={{0,2},{2,0},{4,6},{6,4},{8,10},{10,8},{12,14},{14,12},{1,3},{3,1},... | collective-permute-start | bytes 196616 | tf_op jit(solution)/shard_map/ppermute | solution.py:568
  42.0 3.3 %inverse_first.2 = (f32[4224,128]{1,0:T(8,128)S(1)}, f32[4224,128]{1,0:T(8,128)S(1)}) custom-call(s32[2]{0:T(128)S(1)} %pad_add_fusion.place, f32[16,2,128,256]{3,2,1,0:T(8,128)S(1)} %get-tuple-element.39.modes, bf16[2,2,768,256]{3,2,1,0:T(8,128)(2,1)S(1)} %copy-done.2, f32[2,2,256,256]{3,2,1,0:T(8,128)S(1)} %copy-done.4, ...), custom_call_target="tpu_custom_call" | custom-call | flops 2147483648 | bytes 8388608 | tf_op jit(solution)/shard_map/inverse_first/pallas_call | solution.py:444
  45.2 0.1 collective-permute-start.16
  45.3 3.1 %inverse_first.3 = (f32[4224,128]{1,0:T(8,128)S(1)}, f32[4224,128]{1,0:T(8,128)S(1)}) custom-call(s32[2]{0:T(128)S(1)} %pad_add_fusion.place, f32[16,2,128,256]{3,2,1,0:T(8,128)S(1)} %get-tuple-element.53.modes, bf16[2,2,768,256]{3,2,1,0:T(8,128)(2,1)S(1)} %copy-done.2, f32[2,2,256,256]{3,2,1,0:T(8,128)S(1)} %copy-done.4, ...), custom_call_target="tpu_custom_call" | custom-call | flops 2147483648 | bytes 8388608 | tf_op jit(solution)/shard_map/inverse_first/pallas_call | solution.py:444
  48.4 0.5 collective-permute-start.17
  49.0 3.5 %keep_inverse.1.kept = f32[4096,256]{1,0:T(8,128)S(1)} custom-call(s32[2]{0:T(128)S(1)} %pad_add_fusion.place, bf16[2,768,256]{2,1,0:T(8,128)(2,1)S(1)} %copy-done.1, f32[4224,128]{1,0:T(8,128)S(1)} %get-tuple-element.50.refs_0_, f32[4224,128]{1,0:T(8,128)S(1)} %get-tuple-element.64.refs_1_), custom_call_target="tpu_custom_call" | custom-call | flops 2147483648 | bytes 8388608 | tf_op jit(solution)/shard_map/keep_inverse/pallas_call | solution.py:476
  52.5 0.3 collective-permute-done.17.refs_1_
  52.8 5.8 %inverse_second.1 = f32[256,16,512]{2,1,0:T(8,128)} custom-call(s32[2]{0:T(128)S(1)} %pad_add_fusion.place, bf16[2,768,256]{2,1,0:T(8,128)(2,1)S(1)} %copy-done.1, f32[4096,256]{1,0:T(8,128)S(1)} %keep_inverse.1.kept, f32[4224,128]{1,0:T(8,128)S(1)} %collective-permute-done.16.refs_0_, f32[4224,128]{1,0:T(8,128)S(1)} %collective-permute-done.17.refs_1_), custom_call_target="tpu_custom_call" | custom-call | flops 4294967296 | bytes 8388608 | tf_op jit(solution)/shard_map/inverse_second/pallas_call | solution.py:546
  (29 shorter events, 0.1 us)
Async XLA Ops:
  0.1 7.6 %copy-start.5 = (bf16[2,768,256]{2,1,0:T(8,128)(2,1)S(1)}, bf16[2,768,256]{2,1,0:T(8,128)(2,1)}, u32[]{:S(2)}) copy-start(bf16[2,768,256]{2,1,0:T(8,128)(2,1)} %constant.23.clone.tables) | copy-start | bytes 2359300
  7.0 4.6 %collective-permute-start = (f32[4488,128]{1,0:T(8,128)S(1)}, f32[4488,128]{1,0:T(8,128)S(1)}, u32[]{:S(2)}, u32[]{:S(2)}) collective-permute-start(f32[4488,128]{1,0:T(8,128)S(1)} %get-tuple-element.38), channel_id=1, source_target_pairs={{0,1},{1,0},{2,3},{3,2},{4,5},{5,4},{6,7},{7,6},{8,9},{9,8},{10,11... | collective-permute-start | bytes 6893576 | tf_op jit(solution)/shard_map/ppermute | solution.py:563
  7.6 11.9 %collective-permute-start.8 = (f32[4488,128]{1,0:T(8,128)S(1)}, f32[4488,128]{1,0:T(8,128)S(1)}, u32[]{:S(2)}, u32[]{:S(2)}) collective-permute-start(f32[4488,128]{1,0:T(8,128)S(1)} %get-tuple-element.52), channel_id=1, source_target_pairs={{0,1},{1,0},{2,3},{3,2},{4,5},{5,4},{6,7},{7,6},{8,9},{9,8},{10,11... | collective-permute-start | bytes 6893576 | tf_op jit(solution)/shard_map/ppermute | solution.py:563
  7.6 4.0 %copy-start.3 = (bf16[2,2,768,256]{3,2,1,0:T(8,128)(2,1)S(1)}, bf16[2,2,768,256]{3,2,1,0:T(8,128)(2,1)}, u32[]{:S(2)}) copy-start(bf16[2,2,768,256]{3,2,1,0:T(8,128)(2,1)} %constant.21.clone.table) | copy-start | bytes 4718596
  7.6 4.0 %copy-start.4 = (f32[2,2,256,256]{3,2,1,0:T(8,128)S(1)}, f32[2,2,256,256]{3,2,1,0:T(8,128)}, u32[]{:S(2)}) copy-start(f32[2,2,256,256]{3,2,1,0:T(8,128)} %constant.22.clone.decay) | copy-start | bytes 3145732
  14.9 11.2 %collective-permute-start.1 = (f32[64,256]{1,0:T(8,128)S(1)}, f32[64,256]{1,0:T(8,128)S(1)}, u32[]{:S(2)}, u32[]{:S(2)}) collective-permute-start(f32[64,256]{1,0:T(8,128)S(1)} %get-tuple-element.41), channel_id=1, source_target_pairs={{0,6},{2,4},{4,2},{6,0},{8,14},{10,12},{12,10},{14,8},{1,7},{3,5},... | collective-permute-start | bytes 196616 | tf_op jit(solution)/shard_map/ppermute | solution.py:568
  18.8 7.5 %collective-permute-start.2 = (f32[64,256]{1,0:T(8,128)S(1)}, f32[64,256]{1,0:T(8,128)S(1)}, u32[]{:S(2)}, u32[]{:S(2)}) collective-permute-start(f32[64,256]{1,0:T(8,128)S(1)} %get-tuple-element.42), channel_id=1, source_target_pairs={{0,4},{2,6},{4,0},{6,2},{8,12},{10,14},{12,8},{14,10},{1,5},{3,7},... | collective-permute-start | bytes 196616 | tf_op jit(solution)/shard_map/ppermute | solution.py:568
  19.3 7.0 %collective-permute-start.3 = (f32[64,256]{1,0:T(8,128)S(1)}, f32[64,256]{1,0:T(8,128)S(1)}, u32[]{:S(2)}, u32[]{:S(2)}) collective-permute-start(f32[64,256]{1,0:T(8,128)S(1)} %get-tuple-element.43), channel_id=1, source_target_pairs={{0,2},{2,0},{4,6},{6,4},{8,10},{10,8},{12,14},{14,12},{1,3},{3,1},... | collective-permute-start | bytes 196616 | tf_op jit(solution)/shard_map/ppermute | solution.py:568
  19.5 6.8 %copy-start = (f32[2,2,3,256,256]{4,3,2,1,0:T(8,128)S(1)}, f32[2,2,3,256,256]{4,3,2,1,0:T(8,128)}, u32[]{:S(2)}) copy-start(f32[2,2,3,256,256]{4,3,2,1,0:T(8,128)} %constant.20.clone.closing) | copy-start | bytes 9437188
  22.7 7.1 %collective-permute-start.9 = (f32[64,256]{1,0:T(8,128)S(1)}, f32[64,256]{1,0:T(8,128)S(1)}, u32[]{:S(2)}, u32[]{:S(2)}) collective-permute-start(f32[64,256]{1,0:T(8,128)S(1)} %get-tuple-element.55), channel_id=1, source_target_pairs={{0,6},{2,4},{4,2},{6,0},{8,14},{10,12},{12,10},{14,8},{1,7},{3,5},... | collective-permute-start | bytes 196616 | tf_op jit(solution)/shard_map/ppermute | solution.py:568
  25.6 4.9 %collective-permute-start.10 = (f32[64,256]{1,0:T(8,128)S(1)}, f32[64,256]{1,0:T(8,128)S(1)}, u32[]{:S(2)}, u32[]{:S(2)}) collective-permute-start(f32[64,256]{1,0:T(8,128)S(1)} %get-tuple-element.56), channel_id=1, source_target_pairs={{0,4},{2,6},{4,0},{6,2},{8,12},{10,14},{12,8},{14,10},{1,5},{3,7},... | collective-permute-start | bytes 196616 | tf_op jit(solution)/shard_map/ppermute | solution.py:568
  26.1 4.5 %collective-permute-start.11 = (f32[64,256]{1,0:T(8,128)S(1)}, f32[64,256]{1,0:T(8,128)S(1)}, u32[]{:S(2)}, u32[]{:S(2)}) collective-permute-start(f32[64,256]{1,0:T(8,128)S(1)} %get-tuple-element.57), channel_id=1, source_target_pairs={{0,2},{2,0},{4,6},{6,4},{8,10},{10,8},{12,14},{14,12},{1,3},{3,1},... | collective-permute-start | bytes 196616 | tf_op jit(solution)/shard_map/ppermute | solution.py:568
  26.9 6.7 %collective-permute-start.4 = (f32[64,256]{1,0:T(8,128)S(1)}, f32[64,256]{1,0:T(8,128)S(1)}, u32[]{:S(2)}, u32[]{:S(2)}) collective-permute-start(f32[64,256]{1,0:T(8,128)S(1)} %get-tuple-element.45.near), channel_id=1, source_target_pairs={{0,8},{2,10},{4,12},{6,14},{8,0},{10,2},{12,4},{14,6},{1,9},{3,11}... | collective-permute-start | bytes 196616 | tf_op jit(solution)/shard_map/ppermute | solution.py:568
  31.2 6.6 %collective-permute-start.12 = (f32[64,256]{1,0:T(8,128)S(1)}, f32[64,256]{1,0:T(8,128)S(1)}, u32[]{:S(2)}, u32[]{:S(2)}) collective-permute-start(f32[64,256]{1,0:T(8,128)S(1)} %get-tuple-element.59.near), channel_id=1, source_target_pairs={{0,8},{2,10},{4,12},{6,14},{8,0},{10,2},{12,4},{14,6},{1,9},{3,11}... | collective-permute-start | bytes 196616 | tf_op jit(solution)/shard_map/ppermute | solution.py:568
  34.2 7.7 %copy-start.2 = (bf16[2,2,768,256]{3,2,1,0:T(8,128)(2,1)S(1)}, bf16[2,2,768,256]{3,2,1,0:T(8,128)(2,1)}, u32[]{:S(2)}) copy-start(bf16[2,2,768,256]{3,2,1,0:T(8,128)(2,1)} %constant.24.clone.table) | copy-start | bytes 4718596
  34.2 6.4 %collective-permute-start.5 = (f32[64,256]{1,0:T(8,128)S(1)}, f32[64,256]{1,0:T(8,128)S(1)}, u32[]{:S(2)}, u32[]{:S(2)}) collective-permute-start(f32[64,256]{1,0:T(8,128)S(1)} %get-tuple-element.47), channel_id=1, source_target_pairs={{0,6},{2,4},{4,2},{6,0},{8,14},{10,12},{12,10},{14,8},{1,7},{3,5},... | collective-permute-start | bytes 196616 | tf_op jit(solution)/shard_map/ppermute | solution.py:568
  36.5 5.5 %collective-permute-start.6 = (f32[64,256]{1,0:T(8,128)S(1)}, f32[64,256]{1,0:T(8,128)S(1)}, u32[]{:S(2)}, u32[]{:S(2)}) collective-permute-start(f32[64,256]{1,0:T(8,128)S(1)} %get-tuple-element.48), channel_id=1, source_target_pairs={{0,4},{2,6},{4,0},{6,2},{8,12},{10,14},{12,8},{14,10},{1,5},{3,7},... | collective-permute-start | bytes 196616 | tf_op jit(solution)/shard_map/ppermute | solution.py:568
  36.5 5.5 %collective-permute-start.7 = (f32[64,256]{1,0:T(8,128)S(1)}, f32[64,256]{1,0:T(8,128)S(1)}, u32[]{:S(2)}, u32[]{:S(2)}) collective-permute-start(f32[64,256]{1,0:T(8,128)S(1)} %get-tuple-element.49), channel_id=1, source_target_pairs={{0,2},{2,0},{4,6},{6,4},{8,10},{10,8},{12,14},{14,12},{1,3},{3,1},... | collective-permute-start | bytes 196616 | tf_op jit(solution)/shard_map/ppermute | solution.py:568
  38.4 6.9 %collective-permute-start.13 = (f32[64,256]{1,0:T(8,128)S(1)}, f32[64,256]{1,0:T(8,128)S(1)}, u32[]{:S(2)}, u32[]{:S(2)}) collective-permute-start(f32[64,256]{1,0:T(8,128)S(1)} %get-tuple-element.61), channel_id=1, source_target_pairs={{0,6},{2,4},{4,2},{6,0},{8,14},{10,12},{12,10},{14,8},{1,7},{3,5},... | collective-permute-start | bytes 196616 | tf_op jit(solution)/shard_map/ppermute | solution.py:568
  40.6 4.7 %collective-permute-start.14 = (f32[64,256]{1,0:T(8,128)S(1)}, f32[64,256]{1,0:T(8,128)S(1)}, u32[]{:S(2)}, u32[]{:S(2)}) collective-permute-start(f32[64,256]{1,0:T(8,128)S(1)} %get-tuple-element.62), channel_id=1, source_target_pairs={{0,4},{2,6},{4,0},{6,2},{8,12},{10,14},{12,8},{14,10},{1,5},{3,7},... | collective-permute-start | bytes 196616 | tf_op jit(solution)/shard_map/ppermute | solution.py:568
  40.6 4.7 %collective-permute-start.15 = (f32[64,256]{1,0:T(8,128)S(1)}, f32[64,256]{1,0:T(8,128)S(1)}, u32[]{:S(2)}, u32[]{:S(2)}) collective-permute-start(f32[64,256]{1,0:T(8,128)S(1)} %get-tuple-element.63), channel_id=1, source_target_pairs={{0,2},{2,0},{4,6},{6,4},{8,10},{10,8},{12,14},{14,12},{1,3},{3,1},... | collective-permute-start | bytes 196616 | tf_op jit(solution)/shard_map/ppermute | solution.py:568
  45.2 7.3 %collective-permute-start.16 = (f32[4224,128]{1,0:T(8,128)S(1)}, f32[4224,128]{1,0:T(8,128)S(1)}, u32[]{:S(2)}, u32[]{:S(2)}) collective-permute-start(f32[4224,128]{1,0:T(8,128)S(1)} %get-tuple-element.65), channel_id=1, source_target_pairs={{0,1},{1,0},{2,3},{3,2},{4,5},{5,4},{6,7},{7,6},{8,9},{9,8},{10,11... | collective-permute-start | bytes 6488072 | tf_op jit(solution)/shard_map/ppermute | solution.py:563
  45.3 3.6 %copy-start.1 = (bf16[2,768,256]{2,1,0:T(8,128)(2,1)S(1)}, bf16[2,768,256]{2,1,0:T(8,128)(2,1)}, u32[]{:S(2)}) copy-start(bf16[2,768,256]{2,1,0:T(8,128)(2,1)} %constant.25.clone.tables) | copy-start | bytes 2359300
  48.4 4.4 %collective-permute-start.17 = (f32[4224,128]{1,0:T(8,128)S(1)}, f32[4224,128]{1,0:T(8,128)S(1)}, u32[]{:S(2)}, u32[]{:S(2)}) collective-permute-start(f32[4224,128]{1,0:T(8,128)S(1)} %get-tuple-element.66), channel_id=1, source_target_pairs={{0,1},{1,0},{2,3},{3,2},{4,5},{5,4},{6,7},{7,6},{8,9},{9,8},{10,11... | collective-permute-start | bytes 6488072 | tf_op jit(solution)/shard_map/ppermute | solution.py:563

commit v17 on v16

--- a/solution.py
+++ b/solution.py
@@ -29,8 +29,8 @@
 
 
 def second_tables(width):
-    half = width // 2
-    return np.stack([sine_table(np.arange(half), np.arange(s, width, 2), width) for s in (0, 1)])
+    cells = np.arange(width)
+    return np.stack([sine_table(cells, np.arange(s, width, 2), width) for s in (0, 1)])
 
 
 def first_tables(total):
@@ -59,7 +59,20 @@
     table = np.asarray(table, np.float32)
     high = table.astype(jnp.bfloat16)
     low = (table - high.astype(np.float32)).astype(jnp.bfloat16)
-    return jnp.asarray(np.concatenate([high, high, low], axis=-2))
+    return np.concatenate([high, high, low], axis=-2)
+
+
+def mixed_constant(tables):
+    width = 2 * tables.shape[2]
+    quarter = width // 4
+    outer = tables[:, [*range(quarter), *range(width - quarter, width)]]
+    parts = [split_constant(outer), split_constant(tables[:, quarter : 2 * quarter])]
+    return np.concatenate(parts, axis=1)
+
+
+def mixed_dot(outer, inner, table):
+    rows = [outer, outer[:, : outer.shape[1] // 2], inner, inner[:, : inner.shape[1] // 2]]
+    return jnp.dot(jnp.concatenate(rows, axis=1), table, preferred_element_type=jnp.float32)
 
 
 def store_split(ref, at, lane, block):
@@ -138,7 +151,7 @@
     )
 
 
-def forward_second_kernel(place, field_in, initial_in, tables, sums, *refs):
+def forward_second_kernel(place, field_in, initial_in, tables, outer, sums, *refs):
     sends, refs = refs[:CHUNKS], refs[CHUNKS:]
     field, initial, table, sems, table_sem, *scratch = refs
     cells, steps, width = field.shape
@@ -168,13 +181,18 @@
 
     lanes_reversed = reversal()
 
-    def put(other, at, sums_at, cells):
-        lower = cells[:, :half]
-        upper = sign * jnp.concatenate(
-            [lanes_reversed(cells[:, lane : lane + LANES]) for lane in range(half, width, LANES)][::-1],
-            axis=1,
-        )
-        sums[pl.ds(sums_at, TILE), :] = lower + upper
+    def put(other, at, to, cells):
+        quarter = width // 4
+        to = pl.ds(to, TILE)
+        store_split(outer, (to,), 0, cells[:, :quarter])
+        store_split(outer, (to,), quarter, cells[:, width - quarter :])
+        lower = cells[:, quarter:half]
+        upper = [
+            lanes_reversed(cells[:, lane : lane + LANES])
+            for lane in range(half, width - quarter, LANES)
+        ]
+        upper = sign * jnp.concatenate(upper[::-1], axis=1)
+        sums[to, :] = lower + upper
         store_split(other, (pl.ds(at, TILE),), 0, lower - upper)
 
     def prepare(at):
@@ -190,7 +208,10 @@
             put(split, body + row, cells * steps + cell + row, ends)
 
     def transform(at):
-        sent = dot(scratch[at % len(scratch)][...], table[...])
+        here = [outer[pl.ds(at * body, body)], outer[pl.ds(cells * steps + at * piece, piece)]]
+        sent = mixed_dot(
+            jnp.concatenate(here, axis=0), scratch[at % len(scratch)][...], table[...]
+        )
         first = cells - (at + 1) * piece
         for chunk, send in enumerate(sends):
             lanes = slice(chunk * part, (chunk + 1) * part)
@@ -222,8 +243,11 @@
         forward_second_kernel,
         "forward_second",
         [IN_HBM] * 3,
-        [IN_VMEM] * (1 + CHUNKS),
-        [floats((steps + 1) * rows, half)]
+        [IN_VMEM] * (2 + CHUNKS),
+        [
+            jax.ShapeDtypeStruct(((steps + 1) * rows, 2 * half), jnp.bfloat16),
+            floats((steps + 1) * rows, half // 2),
+        ]
         + [floats((steps + 1) * pitch_of(rows), half // CHUNKS)] * CHUNKS,
         [
             pltpu.VMEM(field.shape, jnp.float32),
@@ -232,13 +256,13 @@
             pltpu.SemaphoreType.DMA((rows // piece, 2)),
             pltpu.SemaphoreType.DMA,
         ]
-        + [pltpu.VMEM(((steps + 1) * piece, 2 * half), jnp.bfloat16)] * pieces,
+        + [pltpu.VMEM(((steps + 1) * piece, half), jnp.bfloat16)] * pieces,
         1 << 32,
     )(place, in_hbm(field), in_hbm(initial), in_hbm(tables))
-    return outs[0], outs[1:]
-
-
-def keep_second_kernel(steps, place, tables, sums, *refs):
+    return outs[0], outs[1], outs[2:]
+
+
+def keep_second_kernel(steps, place, tables, outer, sums, *refs):
     keeps, scratch = refs[:CHUNKS], refs[CHUNKS:]
     depth = scratch[0].shape[0]
     cells = sums.shape[0] // (steps + 1)
@@ -247,7 +271,7 @@
         split = scratch[at // depth % 2]
         for row in range(0, depth, TILE):
             store_split(split, (pl.ds(row, TILE),), 0, sums[pl.ds(at + row, TILE)])
-        result = dot(split[...], tables[place[1]])
+        result = mixed_dot(outer[pl.ds(at, depth)], split[...], tables[place[1]])
         for chunk, keep in enumerate(keeps):
             part = keep.shape[1]
             lanes = slice(chunk * part, (chunk + 1) * part)
@@ -260,18 +284,18 @@
                 keep[ends, :] = result[body:, lanes]
 
 
-def keep_second(place, sums, tables, steps):
-    rows, half = sums.shape
+def keep_second(place, outer, sums, tables, steps):
+    rows, half = outer.shape[0], tables.shape[2]
     shape = ((steps + 1) * pitch_of(rows // (steps + 1)), half // CHUNKS)
     return call(
         functools.partial(keep_second_kernel, steps),
         "keep_second",
-        [IN_VMEM] * 2,
+        [IN_VMEM] * 3,
         [IN_VMEM] * CHUNKS,
         [floats(*shape)] * CHUNKS,
-        [pltpu.VMEM((rows // 8, 2 * half), jnp.bfloat16)] * 2,
+        [pltpu.VMEM((rows // 8, half), jnp.bfloat16)] * 2,
         1 << 31,
-    )(place, tables, sums)
+    )(place, tables, outer, sums)
 
 
 def ranks(slabs):
@@ -593,10 +617,10 @@
         np.stack([by_chunk(table) for table in (slab_decay, half_decay, gain)], axis=2)
     )
     first_table, decays = split_constant(first), constant(decay)
-    second_table = split_constant(REACTION_STEP * second)
-    sums, sends = forward_second(place, iterate, initial, second_table)
+    second_table = mixed_constant(REACTION_STEP * second)
+    outer, sums, sends = forward_second(place, iterate, initial, second_table)
     gots = [swapped(send) for send in sends]
-    keeps = keep_second(place, sums, second_table, steps)
+    keeps = keep_second(place, outer, sums, second_table, steps)
     modes, befores = [], []
     for chunk in range(CHUNKS):
         own_modes, lasts = forward_first(
@@ -614,7 +638,7 @@
         )
     )
     gots = [swapped(send) for send in sends]
-    inverse_table = split_constant(np.swapaxes(second, 1, 2))
+    inverse_table = split_constant(np.swapaxes(second[:, : width // 2], 1, 2))
     kept = keep_inverse(place, keeps, inverse_table, rows, steps)
     return inverse_second(place, kept, gots, inverse_table, steps)
 

time: 58.9 us -> 61.1 us (1.037)
  Pallas kernels: 34.1 us -> 37.3 us
  waiting for transfers between devices: 2.4 us -> 1.37 us
    pallas_call x1, Pallas kernels: 6.92 us -> 8.84 us  [forward_second(): call(forward_second_kernel, 'forward_second', [IN_HBM] * 3, [IN_VMEM] * (...]
    pallas_call x1, Pallas kernels: 2.68 us -> 3.73 us  [keep_second(): call(functools.partial(keep_second_kernel, steps), 'keep_second', [IN_VME...]
    ppermute x4, waiting for transfers between devices: 1.63 us -> 0.58 us  [swapped(): return lax.ppermute(block, 'space', [(0, 1), (1, 0)])]
  transfers between devices with their start and end apart: 18 -> 18, of which waited for: 3 -> 3; matrix products, arithmetic and copies ran while one was open for 0% -> 0% of each run, Pallas kernels for 36% -> 37%
where the time goes in v17:
time: 61.1 us; the launch traced here: 60.9 us
  Pallas kernels  37.3 us (61%)
  starting transfers between devices  21.8 us (36%)
  waiting for transfers between devices  1.37 us (2%)
    ppermute x14, starting transfers between devices, with_partner(): lax.ppermute(block, 'tm', [(slab, slab ^ distance) for slab in range(slab...  20.2 us
    pallas_call x1, Pallas kernels, forward_second(): call(forward_second_kernel, 'forward_second', [IN_HBM] * 3, [IN_VMEM] * (...  8.84 us
    pallas_call x2, Pallas kernels, forward_first(): call(functools.partial(forward_first_kernel, slabs, chunk), 'forward_firs...  6.68 us
    pallas_call x2, Pallas kernels, inverse_first(): call(functools.partial(inverse_first_kernel, slabs, chunk), 'inverse_firs...  6.34 us
    pallas_call x1, Pallas kernels, inverse_second(): call(inverse_second_kernel, 'inverse_second', [IN_VMEM] * (2 + CHUNKS), I...  5.78 us
    pallas_call x1, Pallas kernels, keep_second(): call(functools.partial(keep_second_kernel, steps), 'keep_second', [IN_VME...  3.73 us
    pallas_call x1, Pallas kernels, keep_inverse(): call(functools.partial(keep_inverse_kernel, steps), 'keep_inverse', [IN_V...  3.54 us
    ppermute x4, starting transfers between devices, swapped(): return lax.ppermute(block, 'space', [(0, 1), (1, 0)])  1.64 us
  transfers between devices with their start and end apart: 18, of which 3 were waited for; matrix products, arithmetic and copies ran while one was open for 0% of the time, Pallas kernels for 37%

profile of v17, /device:TPU:0, one launch (start us, length us, event | category | flops | bytes accessed | tf_op | source)
XLA Modules:
  0.0 60.9 jit_solution(8546495480988021789)
XLA Ops:
  0.0 0.1 pad_add_fusion.place
  0.1 8.8 %forward_second.1 = (bf16[4352,512]{1,0:T(8,128)(2,1)S(1)}, f32[4352,128]{1,0:T(8,128)S(1)}, f32[4488,128]{1,0:T(8,128)S(1)}, f32[4488,128]{1,0:T(8,128)S(1)}) custom-call(s32[2]{0:T(128)S(1)} %pad_add_fusion.place, f32[256,16,512]{2,1,0:T(8,128)} %field_in.1, f32[256,512]{1,0:T(8,128)} %initial_in.1, bf16[2,1152,256]{2,1,0:T(8,128)(2,1)} %constant.22.clone.tables), custom_call_target="tpu_custom_call" | custom-call | flops 4294967296 | bytes 8388608 | tf_op jit(solution)/shard_map/forward_second/pallas_call | solution.py:242
  8.9 0.9 %collective-permute-start = (f32[4488,128]{1,0:T(8,128)S(1)}, f32[4488,128]{1,0:T(8,128)S(1)}, u32[]{:S(2)}, u32[]{:S(2)}) collective-permute-start(f32[4488,128]{1,0:T(8,128)S(1)} %get-tuple-element.40), channel_id=1, source_target_pairs={{0,1},{1,0},{2,3},{3,2},{4,5},{5,4},{6,7},{7,6},{8,9},{9,8},{10,11... | collective-permute-start | bytes 6893576 | tf_op jit(solution)/shard_map/ppermute | solution.py:587
  9.9 0.1 collective-permute-start.8
  10.0 3.7 %keep_second.1 = (f32[4488,128]{1,0:T(8,128)S(1)}, f32[4488,128]{1,0:T(8,128)S(1)}) custom-call(s32[2]{0:T(128)S(1)} %pad_add_fusion.place, bf16[2,1152,256]{2,1,0:T(8,128)(2,1)S(1)} %copy-done.4, bf16[4352,512]{1,0:T(8,128)(2,1)S(1)} %get-tuple-element.37.outer, f32[4352,128]{1,0:T(8,128)S(1)} %get-tuple-element.38.sums), custom_call_target="tpu_custom_call" | custom-call | flops 2147483648 | bytes 8388608 | tf_op jit(solution)/shard_map/keep_second/pallas_call | solution.py:290
  13.7 0.3 collective-permute-done.got
  14.0 3.3 %forward_first.2 = (f32[16,2,128,256]{3,2,1,0:T(8,128)S(1)}, f32[64,256]{1,0:T(8,128)S(1)}, f32[64,256]{1,0:T(8,128)S(1)}, f32[64,256]{1,0:T(8,128)S(1)}, f32[64,256]{1,0:T(8,128)S(1)}) custom-call(s32[2]{0:T(128)S(1)} %pad_add_fusion.place, f32[4488,128]{1,0:T(8,128)S(1)} %get-tuple-element.39.keep, f32[4488,128]{1,0:T(8,128)S(1)} %collective-permute-done.got, ...), custom_call_target="tpu_custom_call" | custom-call | flops 2147483648 | bytes 8388608 | tf_op jit(solution)/shard_map/forward_first/pallas_call | solution.py:359
  17.2 3.5 %collective-permute-start.1 = (f32[64,256]{1,0:T(8,128)S(1)}, f32[64,256]{1,0:T(8,128)S(1)}, u32[]{:S(2)}, u32[]{:S(2)}) collective-permute-start(f32[64,256]{1,0:T(8,128)S(1)} %get-tuple-element.43), channel_id=1, source_target_pairs={{0,6},{2,4},{4,2},{6,0},{8,14},{10,12},{12,10},{14,8},{1,7},{3,5},... | collective-permute-start | bytes 196616 | tf_op jit(solution)/shard_map/ppermute | solution.py:592
  20.8 0.4 collective-permute-start.2
  21.2 0.2 collective-permute-start.3
  21.4 3.4 %forward_first.3 = (f32[16,2,128,256]{3,2,1,0:T(8,128)S(1)}, f32[64,256]{1,0:T(8,128)S(1)}, f32[64,256]{1,0:T(8,128)S(1)}, f32[64,256]{1,0:T(8,128)S(1)}, f32[64,256]{1,0:T(8,128)S(1)}) custom-call(s32[2]{0:T(128)S(1)} %pad_add_fusion.place, f32[4488,128]{1,0:T(8,128)S(1)} %get-tuple-element.53.keep, f32[4488,128]{1,0:T(8,128)S(1)} %collective-permute-done.8.got, ...), custom_call_target="tpu_custom_call" | custom-call | flops 2147483648 | bytes 8388608 | tf_op jit(solution)/shard_map/forward_first/pallas_call | solution.py:359
  24.8 2.9 %collective-permute-start.9 = (f32[64,256]{1,0:T(8,128)S(1)}, f32[64,256]{1,0:T(8,128)S(1)}, u32[]{:S(2)}, u32[]{:S(2)}) collective-permute-start(f32[64,256]{1,0:T(8,128)S(1)} %get-tuple-element.57), channel_id=1, source_target_pairs={{0,6},{2,4},{4,2},{6,0},{8,14},{10,12},{12,10},{14,8},{1,7},{3,5},... | collective-permute-start | bytes 196616 | tf_op jit(solution)/shard_map/ppermute | solution.py:592
  27.8 0.4 collective-permute-start.10
  28.2 0.2 collective-permute-start.11
  28.4 0.6 half_sum.2
  29.0 3.0 %collective-permute-start.4 = (f32[64,256]{1,0:T(8,128)S(1)}, f32[64,256]{1,0:T(8,128)S(1)}, u32[]{:S(2)}, u32[]{:S(2)}) collective-permute-start(f32[64,256]{1,0:T(8,128)S(1)} %get-tuple-element.47.near), channel_id=1, source_target_pairs={{0,8},{2,10},{4,12},{6,14},{8,0},{10,2},{12,4},{14,6},{1,9},{3,11}... | collective-permute-start | bytes 196616 | tf_op jit(solution)/shard_map/ppermute | solution.py:592
  32.0 0.8 %collective-permute-done.10.refs_2_ = f32[64,256]{1,0:T(8,128)S(1)} collective-permute-done((f32[64,256]{1,0:T(8,128)S(1)}, f32[64,256]{1,0:T(8,128)S(1)}, u32[]{:S(2)}, u32[]{:S(2)}) %collective-permute-start.10) | collective-permute-done | bytes 65568 | tf_op jit(solution)/shard_map/ppermute | solution.py:592
  32.7 0.6 half_sum.3
  33.3 2.4 %collective-permute-start.12 = (f32[64,256]{1,0:T(8,128)S(1)}, f32[64,256]{1,0:T(8,128)S(1)}, u32[]{:S(2)}, u32[]{:S(2)}) collective-permute-start(f32[64,256]{1,0:T(8,128)S(1)} %get-tuple-element.61.near), channel_id=1, source_target_pairs={{0,8},{2,10},{4,12},{6,14},{8,0},{10,2},{12,4},{14,6},{1,9},{3,11}... | collective-permute-start | bytes 196616 | tf_op jit(solution)/shard_map/ppermute | solution.py:592
  35.7 0.6 close.2
  36.4 2.4 %collective-permute-start.5 = (f32[64,256]{1,0:T(8,128)S(1)}, f32[64,256]{1,0:T(8,128)S(1)}, u32[]{:S(2)}, u32[]{:S(2)}) collective-permute-start(f32[64,256]{1,0:T(8,128)S(1)} %get-tuple-element.49), channel_id=1, source_target_pairs={{0,6},{2,4},{4,2},{6,0},{8,14},{10,12},{12,10},{14,8},{1,7},{3,5},... | collective-permute-start | bytes 196616 | tf_op jit(solution)/shard_map/ppermute | solution.py:592
  38.7 1.2 %collective-permute-start.7 = (f32[64,256]{1,0:T(8,128)S(1)}, f32[64,256]{1,0:T(8,128)S(1)}, u32[]{:S(2)}, u32[]{:S(2)}) collective-permute-start(f32[64,256]{1,0:T(8,128)S(1)} %get-tuple-element.51), channel_id=1, source_target_pairs={{0,2},{2,0},{4,6},{6,4},{8,10},{10,8},{12,14},{14,12},{1,3},{3,1},... | collective-permute-start | bytes 196616 | tf_op jit(solution)/shard_map/ppermute | solution.py:592
  39.9 0.6 close.3
  40.5 2.4 %collective-permute-start.13 = (f32[64,256]{1,0:T(8,128)S(1)}, f32[64,256]{1,0:T(8,128)S(1)}, u32[]{:S(2)}, u32[]{:S(2)}) collective-permute-start(f32[64,256]{1,0:T(8,128)S(1)} %get-tuple-element.63), channel_id=1, source_target_pairs={{0,6},{2,4},{4,2},{6,0},{8,14},{10,12},{12,10},{14,8},{1,7},{3,5},... | collective-permute-start | bytes 196616 | tf_op jit(solution)/shard_map/ppermute | solution.py:592
  42.9 1.2 %collective-permute-start.15 = (f32[64,256]{1,0:T(8,128)S(1)}, f32[64,256]{1,0:T(8,128)S(1)}, u32[]{:S(2)}, u32[]{:S(2)}) collective-permute-start(f32[64,256]{1,0:T(8,128)S(1)} %get-tuple-element.65), channel_id=1, source_target_pairs={{0,2},{2,0},{4,6},{6,4},{8,10},{10,8},{12,14},{14,12},{1,3},{3,1},... | collective-permute-start | bytes 196616 | tf_op jit(solution)/shard_map/ppermute | solution.py:592
  44.1 3.2 %inverse_first.2 = (f32[4224,128]{1,0:T(8,128)S(1)}, f32[4224,128]{1,0:T(8,128)S(1)}) custom-call(s32[2]{0:T(128)S(1)} %pad_add_fusion.place, f32[16,2,128,256]{3,2,1,0:T(8,128)S(1)} %get-tuple-element.41.modes, bf16[2,2,768,256]{3,2,1,0:T(8,128)(2,1)S(1)} %copy-done.2, f32[2,2,256,256]{3,2,1,0:T(8,128)S(1)} %copy-done.5, ...), custom_call_target="tpu_custom_call" | custom-call | flops 2147483648 | bytes 8388608 | tf_op jit(solution)/shard_map/inverse_first/pallas_call | solution.py:468
  47.3 0.1 collective-permute-start.16
  47.4 3.2 %inverse_first.3 = (f32[4224,128]{1,0:T(8,128)S(1)}, f32[4224,128]{1,0:T(8,128)S(1)}) custom-call(s32[2]{0:T(128)S(1)} %pad_add_fusion.place, f32[16,2,128,256]{3,2,1,0:T(8,128)S(1)} %get-tuple-element.55.modes, bf16[2,2,768,256]{3,2,1,0:T(8,128)(2,1)S(1)} %copy-done.2, f32[2,2,256,256]{3,2,1,0:T(8,128)S(1)} %copy-done.5, ...), custom_call_target="tpu_custom_call" | custom-call | flops 2147483648 | bytes 8388608 | tf_op jit(solution)/shard_map/inverse_first/pallas_call | solution.py:468
  50.6 0.5 collective-permute-start.17
  51.1 3.5 %keep_inverse.1.kept = f32[4096,256]{1,0:T(8,128)S(1)} custom-call(s32[2]{0:T(128)S(1)} %pad_add_fusion.place, bf16[2,768,256]{2,1,0:T(8,128)(2,1)S(1)} %copy-done.1, f32[4224,128]{1,0:T(8,128)S(1)} %get-tuple-element.52.refs_0_, f32[4224,128]{1,0:T(8,128)S(1)} %get-tuple-element.66.refs_1_), custom_call_target="tpu_custom_call" | custom-call | flops 2147483648 | bytes 8388608 | tf_op jit(solution)/shard_map/keep_inverse/pallas_call | solution.py:500
  54.7 0.3 collective-permute-done.17.refs_1_
  55.0 5.8 %inverse_second.1 = f32[256,16,512]{2,1,0:T(8,128)} custom-call(s32[2]{0:T(128)S(1)} %pad_add_fusion.place, bf16[2,768,256]{2,1,0:T(8,128)(2,1)S(1)} %copy-done.1, f32[4096,256]{1,0:T(8,128)S(1)} %keep_inverse.1.kept, f32[4224,128]{1,0:T(8,128)S(1)} %collective-permute-done.16.refs_0_, f32[4224,128]{1,0:T(8,128)S(1)} %collective-permute-done.17.refs_1_), custom_call_target="tpu_custom_call" | custom-call | flops 4294967296 | bytes 8388608 | tf_op jit(solution)/shard_map/inverse_second/pallas_call | solution.py:570
  (29 shorter events, 0.1 us)
Async XLA Ops:
  0.1 9.9 %copy-start.4 = (bf16[2,1152,256]{2,1,0:T(8,128)(2,1)S(1)}, bf16[2,1152,256]{2,1,0:T(8,128)(2,1)}, u32[]{:S(2)}) copy-start(bf16[2,1152,256]{2,1,0:T(8,128)(2,1)} %constant.22.clone.tables) | copy-start | bytes 3538948
  8.9 5.0 %collective-permute-start = (f32[4488,128]{1,0:T(8,128)S(1)}, f32[4488,128]{1,0:T(8,128)S(1)}, u32[]{:S(2)}, u32[]{:S(2)}) collective-permute-start(f32[4488,128]{1,0:T(8,128)S(1)} %get-tuple-element.40), channel_id=1, source_target_pairs={{0,1},{1,0},{2,3},{3,2},{4,5},{5,4},{6,7},{7,6},{8,9},{9,8},{10,11... | collective-permute-start | bytes 6893576 | tf_op jit(solution)/shard_map/ppermute | solution.py:587
  9.9 11.6 %collective-permute-start.8 = (f32[4488,128]{1,0:T(8,128)S(1)}, f32[4488,128]{1,0:T(8,128)S(1)}, u32[]{:S(2)}, u32[]{:S(2)}) collective-permute-start(f32[4488,128]{1,0:T(8,128)S(1)} %get-tuple-element.54), channel_id=1, source_target_pairs={{0,1},{1,0},{2,3},{3,2},{4,5},{5,4},{6,7},{7,6},{8,9},{9,8},{10,11... | collective-permute-start | bytes 6893576 | tf_op jit(solution)/shard_map/ppermute | solution.py:587
  10.0 4.0 %copy-start.3 = (bf16[2,2,768,256]{3,2,1,0:T(8,128)(2,1)S(1)}, bf16[2,2,768,256]{3,2,1,0:T(8,128)(2,1)}, u32[]{:S(2)}) copy-start(bf16[2,2,768,256]{3,2,1,0:T(8,128)(2,1)} %constant.23.clone.table) | copy-start | bytes 4718596
  10.0 4.0 %copy-start.5 = (f32[2,2,256,256]{3,2,1,0:T(8,128)S(1)}, f32[2,2,256,256]{3,2,1,0:T(8,128)}, u32[]{:S(2)}) copy-start(f32[2,2,256,256]{3,2,1,0:T(8,128)} %constant.21.clone.decay) | copy-start | bytes 3145732
  17.2 11.0 %collective-permute-start.1 = (f32[64,256]{1,0:T(8,128)S(1)}, f32[64,256]{1,0:T(8,128)S(1)}, u32[]{:S(2)}, u32[]{:S(2)}) collective-permute-start(f32[64,256]{1,0:T(8,128)S(1)} %get-tuple-element.43), channel_id=1, source_target_pairs={{0,6},{2,4},{4,2},{6,0},{8,14},{10,12},{12,10},{14,8},{1,7},{3,5},... | collective-permute-start | bytes 196616 | tf_op jit(solution)/shard_map/ppermute | solution.py:592
  20.8 7.6 %collective-permute-start.2 = (f32[64,256]{1,0:T(8,128)S(1)}, f32[64,256]{1,0:T(8,128)S(1)}, u32[]{:S(2)}, u32[]{:S(2)}) collective-permute-start(f32[64,256]{1,0:T(8,128)S(1)} %get-tuple-element.44), channel_id=1, source_target_pairs={{0,4},{2,6},{4,0},{6,2},{8,12},{10,14},{12,8},{14,10},{1,5},{3,7},... | collective-permute-start | bytes 196616 | tf_op jit(solution)/shard_map/ppermute | solution.py:592
  21.2 7.2 %collective-permute-start.3 = (f32[64,256]{1,0:T(8,128)S(1)}, f32[64,256]{1,0:T(8,128)S(1)}, u32[]{:S(2)}, u32[]{:S(2)}) collective-permute-start(f32[64,256]{1,0:T(8,128)S(1)} %get-tuple-element.45), channel_id=1, source_target_pairs={{0,2},{2,0},{4,6},{6,4},{8,10},{10,8},{12,14},{14,12},{1,3},{3,1},... | collective-permute-start | bytes 196616 | tf_op jit(solution)/shard_map/ppermute | solution.py:592
  21.4 7.0 %copy-start = (f32[2,2,3,256,256]{4,3,2,1,0:T(8,128)S(1)}, f32[2,2,3,256,256]{4,3,2,1,0:T(8,128)}, u32[]{:S(2)}) copy-start(f32[2,2,3,256,256]{4,3,2,1,0:T(8,128)} %constant.20.clone.closing) | copy-start | bytes 9437188
  24.8 7.1 %collective-permute-start.9 = (f32[64,256]{1,0:T(8,128)S(1)}, f32[64,256]{1,0:T(8,128)S(1)}, u32[]{:S(2)}, u32[]{:S(2)}) collective-permute-start(f32[64,256]{1,0:T(8,128)S(1)} %get-tuple-element.57), channel_id=1, source_target_pairs={{0,6},{2,4},{4,2},{6,0},{8,14},{10,12},{12,10},{14,8},{1,7},{3,5},... | collective-permute-start | bytes 196616 | tf_op jit(solution)/shard_map/ppermute | solution.py:592
  27.8 5.0 %collective-permute-start.10 = (f32[64,256]{1,0:T(8,128)S(1)}, f32[64,256]{1,0:T(8,128)S(1)}, u32[]{:S(2)}, u32[]{:S(2)}) collective-permute-start(f32[64,256]{1,0:T(8,128)S(1)} %get-tuple-element.58), channel_id=1, source_target_pairs={{0,4},{2,6},{4,0},{6,2},{8,12},{10,14},{12,8},{14,10},{1,5},{3,7},... | collective-permute-start | bytes 196616 | tf_op jit(solution)/shard_map/ppermute | solution.py:592
  28.2 4.5 %collective-permute-start.11 = (f32[64,256]{1,0:T(8,128)S(1)}, f32[64,256]{1,0:T(8,128)S(1)}, u32[]{:S(2)}, u32[]{:S(2)}) collective-permute-start(f32[64,256]{1,0:T(8,128)S(1)} %get-tuple-element.59), channel_id=1, source_target_pairs={{0,2},{2,0},{4,6},{6,4},{8,10},{10,8},{12,14},{14,12},{1,3},{3,1},... | collective-permute-start | bytes 196616 | tf_op jit(solution)/shard_map/ppermute | solution.py:592
  29.0 6.7 %collective-permute-start.4 = (f32[64,256]{1,0:T(8,128)S(1)}, f32[64,256]{1,0:T(8,128)S(1)}, u32[]{:S(2)}, u32[]{:S(2)}) collective-permute-start(f32[64,256]{1,0:T(8,128)S(1)} %get-tuple-element.47.near), channel_id=1, source_target_pairs={{0,8},{2,10},{4,12},{6,14},{8,0},{10,2},{12,4},{14,6},{1,9},{3,11}... | collective-permute-start | bytes 196616 | tf_op jit(solution)/shard_map/ppermute | solution.py:592
  33.3 6.6 %collective-permute-start.12 = (f32[64,256]{1,0:T(8,128)S(1)}, f32[64,256]{1,0:T(8,128)S(1)}, u32[]{:S(2)}, u32[]{:S(2)}) collective-permute-start(f32[64,256]{1,0:T(8,128)S(1)} %get-tuple-element.61.near), channel_id=1, source_target_pairs={{0,8},{2,10},{4,12},{6,14},{8,0},{10,2},{12,4},{14,6},{1,9},{3,11}... | collective-permute-start | bytes 196616 | tf_op jit(solution)/shard_map/ppermute | solution.py:592
  36.3 7.7 %copy-start.2 = (bf16[2,2,768,256]{3,2,1,0:T(8,128)(2,1)S(1)}, bf16[2,2,768,256]{3,2,1,0:T(8,128)(2,1)}, u32[]{:S(2)}) copy-start(bf16[2,2,768,256]{3,2,1,0:T(8,128)(2,1)} %constant.24.clone.table) | copy-start | bytes 4718596
  36.4 6.5 %collective-permute-start.5 = (f32[64,256]{1,0:T(8,128)S(1)}, f32[64,256]{1,0:T(8,128)S(1)}, u32[]{:S(2)}, u32[]{:S(2)}) collective-permute-start(f32[64,256]{1,0:T(8,128)S(1)} %get-tuple-element.49), channel_id=1, source_target_pairs={{0,6},{2,4},{4,2},{6,0},{8,14},{10,12},{12,10},{14,8},{1,7},{3,5},... | collective-permute-start | bytes 196616 | tf_op jit(solution)/shard_map/ppermute | solution.py:592
  38.7 5.4 %collective-permute-start.6 = (f32[64,256]{1,0:T(8,128)S(1)}, f32[64,256]{1,0:T(8,128)S(1)}, u32[]{:S(2)}, u32[]{:S(2)}) collective-permute-start(f32[64,256]{1,0:T(8,128)S(1)} %get-tuple-element.50), channel_id=1, source_target_pairs={{0,4},{2,6},{4,0},{6,2},{8,12},{10,14},{12,8},{14,10},{1,5},{3,7},... | collective-permute-start | bytes 196616 | tf_op jit(solution)/shard_map/ppermute | solution.py:592
  38.7 5.4 %collective-permute-start.7 = (f32[64,256]{1,0:T(8,128)S(1)}, f32[64,256]{1,0:T(8,128)S(1)}, u32[]{:S(2)}, u32[]{:S(2)}) collective-permute-start(f32[64,256]{1,0:T(8,128)S(1)} %get-tuple-element.51), channel_id=1, source_target_pairs={{0,2},{2,0},{4,6},{6,4},{8,10},{10,8},{12,14},{14,12},{1,3},{3,1},... | collective-permute-start | bytes 196616 | tf_op jit(solution)/shard_map/ppermute | solution.py:592
  40.5 6.8 %collective-permute-start.13 = (f32[64,256]{1,0:T(8,128)S(1)}, f32[64,256]{1,0:T(8,128)S(1)}, u32[]{:S(2)}, u32[]{:S(2)}) collective-permute-start(f32[64,256]{1,0:T(8,128)S(1)} %get-tuple-element.63), channel_id=1, source_target_pairs={{0,6},{2,4},{4,2},{6,0},{8,14},{10,12},{12,10},{14,8},{1,7},{3,5},... | collective-permute-start | bytes 196616 | tf_op jit(solution)/shard_map/ppermute | solution.py:592
  42.9 4.5 %collective-permute-start.14 = (f32[64,256]{1,0:T(8,128)S(1)}, f32[64,256]{1,0:T(8,128)S(1)}, u32[]{:S(2)}, u32[]{:S(2)}) collective-permute-start(f32[64,256]{1,0:T(8,128)S(1)} %get-tuple-element.64), channel_id=1, source_target_pairs={{0,4},{2,6},{4,0},{6,2},{8,12},{10,14},{12,8},{14,10},{1,5},{3,7},... | collective-permute-start | bytes 196616 | tf_op jit(solution)/shard_map/ppermute | solution.py:592
  42.9 4.5 %collective-permute-start.15 = (f32[64,256]{1,0:T(8,128)S(1)}, f32[64,256]{1,0:T(8,128)S(1)}, u32[]{:S(2)}, u32[]{:S(2)}) collective-permute-start(f32[64,256]{1,0:T(8,128)S(1)} %get-tuple-element.65), channel_id=1, source_target_pairs={{0,2},{2,0},{4,6},{6,4},{8,10},{10,8},{12,14},{14,12},{1,3},{3,1},... | collective-permute-start | bytes 196616 | tf_op jit(solution)/shard_map/ppermute | solution.py:592
  47.3 7.4 %collective-permute-start.16 = (f32[4224,128]{1,0:T(8,128)S(1)}, f32[4224,128]{1,0:T(8,128)S(1)}, u32[]{:S(2)}, u32[]{:S(2)}) collective-permute-start(f32[4224,128]{1,0:T(8,128)S(1)} %get-tuple-element.67), channel_id=1, source_target_pairs={{0,1},{1,0},{2,3},{3,2},{4,5},{5,4},{6,7},{7,6},{8,9},{9,8},{10,11... | collective-permute-start | bytes 6488072 | tf_op jit(solution)/shard_map/ppermute | solution.py:587
  47.4 3.7 %copy-start.1 = (bf16[2,768,256]{2,1,0:T(8,128)(2,1)S(1)}, bf16[2,768,256]{2,1,0:T(8,128)(2,1)}, u32[]{:S(2)}) copy-start(bf16[2,768,256]{2,1,0:T(8,128)(2,1)} %constant.25.clone.tables) | copy-start | bytes 2359300
  50.6 4.4 %collective-permute-start.17 = (f32[4224,128]{1,0:T(8,128)S(1)}, f32[4224,128]{1,0:T(8,128)S(1)}, u32[]{:S(2)}, u32[]{:S(2)}) collective-permute-start(f32[4224,128]{1,0:T(8,128)S(1)} %get-tuple-element.68), channel_id=1, source_target_pairs={{0,1},{1,0},{2,3},{3,2},{4,5},{5,4},{6,7},{7,6},{8,9},{9,8},{10,11... | collective-permute-start | bytes 6488072 | tf_op jit(solution)/shard_map/ppermute | solution.py:587

commit v18 on v16

--- a/solution.py
+++ b/solution.py
@@ -140,7 +140,7 @@
 
 def forward_second_kernel(place, field_in, initial_in, tables, sums, *refs):
     sends, refs = refs[:CHUNKS], refs[CHUNKS:]
-    field, initial, table, sems, table_sem, *scratch = refs
+    field, initial, table, sems, table_sem, result, *scratch = refs
     cells, steps, width = field.shape
     half = width // 2
     part = half // CHUNKS
@@ -190,14 +190,17 @@
             put(split, body + row, cells * steps + cell + row, ends)
 
     def transform(at):
-        sent = dot(scratch[at % len(scratch)][...], table[...])
+        result[...] = dot(scratch[at % len(scratch)][...], table[...])
+
+    def place_modes(at):
         first = cells - (at + 1) * piece
         for chunk, send in enumerate(sends):
-            lanes = slice(chunk * part, (chunk + 1) * part)
+            lanes = pl.ds(chunk * part, part)
             for row in range(piece):
-                line = sent[row * steps : (row + 1) * steps, lanes]
+                line = result[pl.ds(row * steps, steps), lanes]
                 send[pl.ds(first + piece - 1 - row, steps, stride=pitch), :] = line
-            store_rows_reversed(send, pitch * steps + first, sent[body:, lanes])
+            ends = result[pl.ds(body, piece), lanes]
+            store_rows_reversed(send, pitch * steps + first, ends)
 
     start(0, 1)
     table_copy.start()
@@ -211,7 +214,10 @@
         if at:
             transform(at - 1)
         prepare(at)
+        if at:
+            place_modes(at - 1)
     transform(pieces - 1)
+    place_modes(pieces - 1)
 
 
 def forward_second(place, field, initial, tables):
@@ -231,6 +237,7 @@
             pltpu.VMEM(tables.shape[1:], jnp.bfloat16),
             pltpu.SemaphoreType.DMA((rows // piece, 2)),
             pltpu.SemaphoreType.DMA,
+            pltpu.VMEM(((steps + 1) * piece, half), jnp.float32),
         ]
         + [pltpu.VMEM(((steps + 1) * piece, 2 * half), jnp.bfloat16)] * pieces,
         1 << 32,

time: 58.9 us -> 59 us (level)
  no operation moved by 1% of the time
where the time goes in v18:
time: 59 us; the launch traced here: 58.9 us
  Pallas kernels  34.2 us (58%)
  starting transfers between devices  21.9 us (37%)
  waiting for transfers between devices  2.4 us (4%)
    ppermute x14, starting transfers between devices, with_partner(): lax.ppermute(block, 'tm', [(slab, slab ^ distance) for slab in range(slab...  20.6 us
    pallas_call x1, Pallas kernels, forward_second(): call(forward_second_kernel, 'forward_second', [IN_HBM] * 3, [IN_VMEM] * (...  6.98 us
    pallas_call x2, Pallas kernels, forward_first(): call(functools.partial(forward_first_kernel, slabs, chunk), 'forward_firs...  6.49 us
    pallas_call x2, Pallas kernels, inverse_first(): call(functools.partial(inverse_first_kernel, slabs, chunk), 'inverse_firs...  6.33 us
    pallas_call x1, Pallas kernels, inverse_second(): call(inverse_second_kernel, 'inverse_second', [IN_VMEM] * (2 + CHUNKS), I...  5.78 us
    pallas_call x1, Pallas kernels, keep_inverse(): call(functools.partial(keep_inverse_kernel, steps), 'keep_inverse', [IN_V...  3.54 us
    pallas_call x1, Pallas kernels, keep_second(): call(functools.partial(keep_second_kernel, steps), 'keep_second', [IN_VME...  2.68 us
    ppermute x4, waiting for transfers between devices, swapped(): return lax.ppermute(block, 'space', [(0, 1), (1, 0)])  1.63 us
  transfers between devices with their start and end apart: 18, of which 3 were waited for; matrix products, arithmetic and copies ran while one was open for 0% of the time, Pallas kernels for 36%

profile of v18, /device:TPU:0, one launch (start us, length us, event | category | flops | bytes accessed | tf_op | source)
XLA Modules:
  0.0 58.9 jit_solution(9647660759470340258)
XLA Ops:
  0.0 0.1 pad_add_fusion.place
  0.1 7.0 %forward_second.1 = (f32[4352,256]{1,0:T(8,128)S(1)}, f32[4488,128]{1,0:T(8,128)S(1)}, f32[4488,128]{1,0:T(8,128)S(1)}) custom-call(s32[2]{0:T(128)S(1)} %pad_add_fusion.place, f32[256,16,512]{2,1,0:T(8,128)} %field_in.1, f32[256,512]{1,0:T(8,128)} %initial_in.1, bf16[2,768,256]{2,1,0:T(8,128)(2,1)} %constant.23.clone.tables), custom_call_target="tpu_custom_call" | custom-call | flops 4294967296 | bytes 8388608 | tf_op jit(solution)/shard_map/forward_second/pallas_call | solution.py:227
  7.1 0.6 collective-permute-start
  7.6 0.1 collective-permute-start.8
  7.7 2.7 %keep_second.1 = (f32[4488,128]{1,0:T(8,128)S(1)}, f32[4488,128]{1,0:T(8,128)S(1)}) custom-call(s32[2]{0:T(128)S(1)} %pad_add_fusion.place, bf16[2,768,256]{2,1,0:T(8,128)(2,1)S(1)} %copy-done.5, f32[4352,256]{1,0:T(8,128)S(1)} %get-tuple-element.36.sums), custom_call_target="tpu_custom_call" | custom-call | flops 2147483648 | bytes 8388608 | tf_op jit(solution)/shard_map/keep_second/pallas_call | solution.py:273
  10.4 1.3 %collective-permute-done.got = f32[4488,128]{1,0:T(8,128)S(1)} collective-permute-done((f32[4488,128]{1,0:T(8,128)S(1)}, f32[4488,128]{1,0:T(8,128)S(1)}, u32[]{:S(2)}, u32[]{:S(2)}) %collective-permute-start) | collective-permute-done | bytes 2297888 | tf_op jit(solution)/shard_map/ppermute | solution.py:570
  11.7 3.2 %forward_first.2 = (f32[16,2,128,256]{3,2,1,0:T(8,128)S(1)}, f32[64,256]{1,0:T(8,128)S(1)}, f32[64,256]{1,0:T(8,128)S(1)}, f32[64,256]{1,0:T(8,128)S(1)}, f32[64,256]{1,0:T(8,128)S(1)}) custom-call(s32[2]{0:T(128)S(1)} %pad_add_fusion.place, f32[4488,128]{1,0:T(8,128)S(1)} %get-tuple-element.37.keep, f32[4488,128]{1,0:T(8,128)S(1)} %collective-permute-done.got, ...), custom_call_target="tpu_custom_call" | custom-call | flops 2147483648 | bytes 8388608 | tf_op jit(solution)/shard_map/forward_first/pallas_call | solution.py:342
  15.0 3.9 %collective-permute-start.1 = (f32[64,256]{1,0:T(8,128)S(1)}, f32[64,256]{1,0:T(8,128)S(1)}, u32[]{:S(2)}, u32[]{:S(2)}) collective-permute-start(f32[64,256]{1,0:T(8,128)S(1)} %get-tuple-element.41), channel_id=1, source_target_pairs={{0,6},{2,4},{4,2},{6,0},{8,14},{10,12},{12,10},{14,8},{1,7},{3,5},... | collective-permute-start | bytes 196616 | tf_op jit(solution)/shard_map/ppermute | solution.py:575
  18.9 0.5 collective-permute-start.2
  19.3 0.2 collective-permute-start.3
  19.5 3.2 %forward_first.3 = (f32[16,2,128,256]{3,2,1,0:T(8,128)S(1)}, f32[64,256]{1,0:T(8,128)S(1)}, f32[64,256]{1,0:T(8,128)S(1)}, f32[64,256]{1,0:T(8,128)S(1)}, f32[64,256]{1,0:T(8,128)S(1)}) custom-call(s32[2]{0:T(128)S(1)} %pad_add_fusion.place, f32[4488,128]{1,0:T(8,128)S(1)} %get-tuple-element.51.keep, f32[4488,128]{1,0:T(8,128)S(1)} %collective-permute-done.8.got, ...), custom_call_target="tpu_custom_call" | custom-call | flops 2147483648 | bytes 8388608 | tf_op jit(solution)/shard_map/forward_first/pallas_call | solution.py:342
  22.8 2.9 %collective-permute-start.9 = (f32[64,256]{1,0:T(8,128)S(1)}, f32[64,256]{1,0:T(8,128)S(1)}, u32[]{:S(2)}, u32[]{:S(2)}) collective-permute-start(f32[64,256]{1,0:T(8,128)S(1)} %get-tuple-element.55), channel_id=1, source_target_pairs={{0,6},{2,4},{4,2},{6,0},{8,14},{10,12},{12,10},{14,8},{1,7},{3,5},... | collective-permute-start | bytes 196616 | tf_op jit(solution)/shard_map/ppermute | solution.py:575
  25.7 0.5 collective-permute-start.10
  26.2 0.2 collective-permute-start.11
  26.4 0.6 half_sum.2
  26.9 3.0 %collective-permute-start.4 = (f32[64,256]{1,0:T(8,128)S(1)}, f32[64,256]{1,0:T(8,128)S(1)}, u32[]{:S(2)}, u32[]{:S(2)}) collective-permute-start(f32[64,256]{1,0:T(8,128)S(1)} %get-tuple-element.45.near), channel_id=1, source_target_pairs={{0,8},{2,10},{4,12},{6,14},{8,0},{10,2},{12,4},{14,6},{1,9},{3,11}... | collective-permute-start | bytes 196616 | tf_op jit(solution)/shard_map/ppermute | solution.py:575
  29.9 0.7 %collective-permute-done.10.refs_2_ = f32[64,256]{1,0:T(8,128)S(1)} collective-permute-done((f32[64,256]{1,0:T(8,128)S(1)}, f32[64,256]{1,0:T(8,128)S(1)}, u32[]{:S(2)}, u32[]{:S(2)}) %collective-permute-start.10) | collective-permute-done | bytes 65568 | tf_op jit(solution)/shard_map/ppermute | solution.py:575
  30.6 0.6 half_sum.3
  31.2 2.4 %collective-permute-start.12 = (f32[64,256]{1,0:T(8,128)S(1)}, f32[64,256]{1,0:T(8,128)S(1)}, u32[]{:S(2)}, u32[]{:S(2)}) collective-permute-start(f32[64,256]{1,0:T(8,128)S(1)} %get-tuple-element.59.near), channel_id=1, source_target_pairs={{0,8},{2,10},{4,12},{6,14},{8,0},{10,2},{12,4},{14,6},{1,9},{3,11}... | collective-permute-start | bytes 196616 | tf_op jit(solution)/shard_map/ppermute | solution.py:575
  33.7 0.6 %close.2 = (f32[64,256]{1,0:T(8,128)S(1)}, f32[64,256]{1,0:T(8,128)S(1)}, f32[64,256]{1,0:T(8,128)S(1)}, f32[64,256]{1,0:T(8,128)S(1)}) custom-call(s32[2]{0:T(128)S(1)} %pad_add_fusion.place, f32[2,2,3,256,256]{4,3,2,1,0:T(8,128)S(1)} %copy-done, f32[4,64,256]{2,1,0:T(8,128)S(1)} %get-tuple-element.44.ordered, f32[64,256]{1,0:T(8,128)S(1)} %get-tuple-element.45.near, ...), custom_call_target="tpu_custom_call" | custom-call | flops 1048576 | bytes 8388608 | tf_op jit(solution)/shard_map/close/pallas_call | solution.py:405
  34.3 2.2 %collective-permute-start.5 = (f32[64,256]{1,0:T(8,128)S(1)}, f32[64,256]{1,0:T(8,128)S(1)}, u32[]{:S(2)}, u32[]{:S(2)}) collective-permute-start(f32[64,256]{1,0:T(8,128)S(1)} %get-tuple-element.47), channel_id=1, source_target_pairs={{0,6},{2,4},{4,2},{6,0},{8,14},{10,12},{12,10},{14,8},{1,7},{3,5},... | collective-permute-start | bytes 196616 | tf_op jit(solution)/shard_map/ppermute | solution.py:575
  36.5 1.3 %collective-permute-start.7 = (f32[64,256]{1,0:T(8,128)S(1)}, f32[64,256]{1,0:T(8,128)S(1)}, u32[]{:S(2)}, u32[]{:S(2)}) collective-permute-start(f32[64,256]{1,0:T(8,128)S(1)} %get-tuple-element.49), channel_id=1, source_target_pairs={{0,2},{2,0},{4,6},{6,4},{8,10},{10,8},{12,14},{14,12},{1,3},{3,1},... | collective-permute-start | bytes 196616 | tf_op jit(solution)/shard_map/ppermute | solution.py:575
  37.8 0.6 %close.3 = (f32[64,256]{1,0:T(8,128)S(1)}, f32[64,256]{1,0:T(8,128)S(1)}, f32[64,256]{1,0:T(8,128)S(1)}, f32[64,256]{1,0:T(8,128)S(1)}) custom-call(s32[2]{0:T(128)S(1)} %pad_add_fusion.place, f32[2,2,3,256,256]{4,3,2,1,0:T(8,128)S(1)} %copy-done, f32[4,64,256]{2,1,0:T(8,128)S(1)} %get-tuple-element.58.ordered, f32[64,256]{1,0:T(8,128)S(1)} %get-tuple-element.59.near, ...), custom_call_target="tpu_custom_call" | custom-call | flops 1048576 | bytes 8388608 | tf_op jit(solution)/shard_map/close/pallas_call | solution.py:405
  38.4 2.2 %collective-permute-start.13 = (f32[64,256]{1,0:T(8,128)S(1)}, f32[64,256]{1,0:T(8,128)S(1)}, u32[]{:S(2)}, u32[]{:S(2)}) collective-permute-start(f32[64,256]{1,0:T(8,128)S(1)} %get-tuple-element.61), channel_id=1, source_target_pairs={{0,6},{2,4},{4,2},{6,0},{8,14},{10,12},{12,10},{14,8},{1,7},{3,5},... | collective-permute-start | bytes 196616 | tf_op jit(solution)/shard_map/ppermute | solution.py:575
  40.7 1.3 %collective-permute-start.15 = (f32[64,256]{1,0:T(8,128)S(1)}, f32[64,256]{1,0:T(8,128)S(1)}, u32[]{:S(2)}, u32[]{:S(2)}) collective-permute-start(f32[64,256]{1,0:T(8,128)S(1)} %get-tuple-element.63), channel_id=1, source_target_pairs={{0,2},{2,0},{4,6},{6,4},{8,10},{10,8},{12,14},{14,12},{1,3},{3,1},... | collective-permute-start | bytes 196616 | tf_op jit(solution)/shard_map/ppermute | solution.py:575
  42.0 3.3 %inverse_first.2 = (f32[4224,128]{1,0:T(8,128)S(1)}, f32[4224,128]{1,0:T(8,128)S(1)}) custom-call(s32[2]{0:T(128)S(1)} %pad_add_fusion.place, f32[16,2,128,256]{3,2,1,0:T(8,128)S(1)} %get-tuple-element.39.modes, bf16[2,2,768,256]{3,2,1,0:T(8,128)(2,1)S(1)} %copy-done.2, f32[2,2,256,256]{3,2,1,0:T(8,128)S(1)} %copy-done.4, ...), custom_call_target="tpu_custom_call" | custom-call | flops 2147483648 | bytes 8388608 | tf_op jit(solution)/shard_map/inverse_first/pallas_call | solution.py:451
  45.3 0.1 collective-permute-start.16
  45.4 3.1 %inverse_first.3 = (f32[4224,128]{1,0:T(8,128)S(1)}, f32[4224,128]{1,0:T(8,128)S(1)}) custom-call(s32[2]{0:T(128)S(1)} %pad_add_fusion.place, f32[16,2,128,256]{3,2,1,0:T(8,128)S(1)} %get-tuple-element.53.modes, bf16[2,2,768,256]{3,2,1,0:T(8,128)(2,1)S(1)} %copy-done.2, f32[2,2,256,256]{3,2,1,0:T(8,128)S(1)} %copy-done.4, ...), custom_call_target="tpu_custom_call" | custom-call | flops 2147483648 | bytes 8388608 | tf_op jit(solution)/shard_map/inverse_first/pallas_call | solution.py:451
  48.5 0.5 collective-permute-start.17
  49.0 3.5 %keep_inverse.1.kept = f32[4096,256]{1,0:T(8,128)S(1)} custom-call(s32[2]{0:T(128)S(1)} %pad_add_fusion.place, bf16[2,768,256]{2,1,0:T(8,128)(2,1)S(1)} %copy-done.1, f32[4224,128]{1,0:T(8,128)S(1)} %get-tuple-element.50.refs_0_, f32[4224,128]{1,0:T(8,128)S(1)} %get-tuple-element.64.refs_1_), custom_call_target="tpu_custom_call" | custom-call | flops 2147483648 | bytes 8388608 | tf_op jit(solution)/shard_map/keep_inverse/pallas_call | solution.py:483
  52.6 0.3 collective-permute-done.17.refs_1_
  52.9 5.8 %inverse_second.1 = f32[256,16,512]{2,1,0:T(8,128)} custom-call(s32[2]{0:T(128)S(1)} %pad_add_fusion.place, bf16[2,768,256]{2,1,0:T(8,128)(2,1)S(1)} %copy-done.1, f32[4096,256]{1,0:T(8,128)S(1)} %keep_inverse.1.kept, f32[4224,128]{1,0:T(8,128)S(1)} %collective-permute-done.16.refs_0_, f32[4224,128]{1,0:T(8,128)S(1)} %collective-permute-done.17.refs_1_), custom_call_target="tpu_custom_call" | custom-call | flops 4294967296 | bytes 8388608 | tf_op jit(solution)/shard_map/inverse_second/pallas_call | solution.py:553
  (29 shorter events, 0.1 us)
Async XLA Ops:
  0.1 7.6 %copy-start.5 = (bf16[2,768,256]{2,1,0:T(8,128)(2,1)S(1)}, bf16[2,768,256]{2,1,0:T(8,128)(2,1)}, u32[]{:S(2)}) copy-start(bf16[2,768,256]{2,1,0:T(8,128)(2,1)} %constant.23.clone.tables) | copy-start | bytes 2359300
  7.1 4.6 %collective-permute-start = (f32[4488,128]{1,0:T(8,128)S(1)}, f32[4488,128]{1,0:T(8,128)S(1)}, u32[]{:S(2)}, u32[]{:S(2)}) collective-permute-start(f32[4488,128]{1,0:T(8,128)S(1)} %get-tuple-element.38), channel_id=1, source_target_pairs={{0,1},{1,0},{2,3},{3,2},{4,5},{5,4},{6,7},{7,6},{8,9},{9,8},{10,11... | collective-permute-start | bytes 6893576 | tf_op jit(solution)/shard_map/ppermute | solution.py:570
  7.6 11.9 %collective-permute-start.8 = (f32[4488,128]{1,0:T(8,128)S(1)}, f32[4488,128]{1,0:T(8,128)S(1)}, u32[]{:S(2)}, u32[]{:S(2)}) collective-permute-start(f32[4488,128]{1,0:T(8,128)S(1)} %get-tuple-element.52), channel_id=1, source_target_pairs={{0,1},{1,0},{2,3},{3,2},{4,5},{5,4},{6,7},{7,6},{8,9},{9,8},{10,11... | collective-permute-start | bytes 6893576 | tf_op jit(solution)/shard_map/ppermute | solution.py:570
  7.7 4.0 %copy-start.3 = (bf16[2,2,768,256]{3,2,1,0:T(8,128)(2,1)S(1)}, bf16[2,2,768,256]{3,2,1,0:T(8,128)(2,1)}, u32[]{:S(2)}) copy-start(bf16[2,2,768,256]{3,2,1,0:T(8,128)(2,1)} %constant.21.clone.table) | copy-start | bytes 4718596
  7.7 4.0 %copy-start.4 = (f32[2,2,256,256]{3,2,1,0:T(8,128)S(1)}, f32[2,2,256,256]{3,2,1,0:T(8,128)}, u32[]{:S(2)}) copy-start(f32[2,2,256,256]{3,2,1,0:T(8,128)} %constant.22.clone.decay) | copy-start | bytes 3145732
  15.0 11.2 %collective-permute-start.1 = (f32[64,256]{1,0:T(8,128)S(1)}, f32[64,256]{1,0:T(8,128)S(1)}, u32[]{:S(2)}, u32[]{:S(2)}) collective-permute-start(f32[64,256]{1,0:T(8,128)S(1)} %get-tuple-element.41), channel_id=1, source_target_pairs={{0,6},{2,4},{4,2},{6,0},{8,14},{10,12},{12,10},{14,8},{1,7},{3,5},... | collective-permute-start | bytes 196616 | tf_op jit(solution)/shard_map/ppermute | solution.py:575
  18.9 7.5 %collective-permute-start.2 = (f32[64,256]{1,0:T(8,128)S(1)}, f32[64,256]{1,0:T(8,128)S(1)}, u32[]{:S(2)}, u32[]{:S(2)}) collective-permute-start(f32[64,256]{1,0:T(8,128)S(1)} %get-tuple-element.42), channel_id=1, source_target_pairs={{0,4},{2,6},{4,0},{6,2},{8,12},{10,14},{12,8},{14,10},{1,5},{3,7},... | collective-permute-start | bytes 196616 | tf_op jit(solution)/shard_map/ppermute | solution.py:575
  19.3 7.0 %collective-permute-start.3 = (f32[64,256]{1,0:T(8,128)S(1)}, f32[64,256]{1,0:T(8,128)S(1)}, u32[]{:S(2)}, u32[]{:S(2)}) collective-permute-start(f32[64,256]{1,0:T(8,128)S(1)} %get-tuple-element.43), channel_id=1, source_target_pairs={{0,2},{2,0},{4,6},{6,4},{8,10},{10,8},{12,14},{14,12},{1,3},{3,1},... | collective-permute-start | bytes 196616 | tf_op jit(solution)/shard_map/ppermute | solution.py:575
  19.5 6.8 %copy-start = (f32[2,2,3,256,256]{4,3,2,1,0:T(8,128)S(1)}, f32[2,2,3,256,256]{4,3,2,1,0:T(8,128)}, u32[]{:S(2)}) copy-start(f32[2,2,3,256,256]{4,3,2,1,0:T(8,128)} %constant.20.clone.closing) | copy-start | bytes 9437188
  22.8 7.1 %collective-permute-start.9 = (f32[64,256]{1,0:T(8,128)S(1)}, f32[64,256]{1,0:T(8,128)S(1)}, u32[]{:S(2)}, u32[]{:S(2)}) collective-permute-start(f32[64,256]{1,0:T(8,128)S(1)} %get-tuple-element.55), channel_id=1, source_target_pairs={{0,6},{2,4},{4,2},{6,0},{8,14},{10,12},{12,10},{14,8},{1,7},{3,5},... | collective-permute-start | bytes 196616 | tf_op jit(solution)/shard_map/ppermute | solution.py:575
  25.7 4.9 %collective-permute-start.10 = (f32[64,256]{1,0:T(8,128)S(1)}, f32[64,256]{1,0:T(8,128)S(1)}, u32[]{:S(2)}, u32[]{:S(2)}) collective-permute-start(f32[64,256]{1,0:T(8,128)S(1)} %get-tuple-element.56), channel_id=1, source_target_pairs={{0,4},{2,6},{4,0},{6,2},{8,12},{10,14},{12,8},{14,10},{1,5},{3,7},... | collective-permute-start | bytes 196616 | tf_op jit(solution)/shard_map/ppermute | solution.py:575
  26.2 4.5 %collective-permute-start.11 = (f32[64,256]{1,0:T(8,128)S(1)}, f32[64,256]{1,0:T(8,128)S(1)}, u32[]{:S(2)}, u32[]{:S(2)}) collective-permute-start(f32[64,256]{1,0:T(8,128)S(1)} %get-tuple-element.57), channel_id=1, source_target_pairs={{0,2},{2,0},{4,6},{6,4},{8,10},{10,8},{12,14},{14,12},{1,3},{3,1},... | collective-permute-start | bytes 196616 | tf_op jit(solution)/shard_map/ppermute | solution.py:575
  26.9 6.7 %collective-permute-start.4 = (f32[64,256]{1,0:T(8,128)S(1)}, f32[64,256]{1,0:T(8,128)S(1)}, u32[]{:S(2)}, u32[]{:S(2)}) collective-permute-start(f32[64,256]{1,0:T(8,128)S(1)} %get-tuple-element.45.near), channel_id=1, source_target_pairs={{0,8},{2,10},{4,12},{6,14},{8,0},{10,2},{12,4},{14,6},{1,9},{3,11}... | collective-permute-start | bytes 196616 | tf_op jit(solution)/shard_map/ppermute | solution.py:575
  31.2 6.6 %collective-permute-start.12 = (f32[64,256]{1,0:T(8,128)S(1)}, f32[64,256]{1,0:T(8,128)S(1)}, u32[]{:S(2)}, u32[]{:S(2)}) collective-permute-start(f32[64,256]{1,0:T(8,128)S(1)} %get-tuple-element.59.near), channel_id=1, source_target_pairs={{0,8},{2,10},{4,12},{6,14},{8,0},{10,2},{12,4},{14,6},{1,9},{3,11}... | collective-permute-start | bytes 196616 | tf_op jit(solution)/shard_map/ppermute | solution.py:575
  34.3 7.7 %copy-start.2 = (bf16[2,2,768,256]{3,2,1,0:T(8,128)(2,1)S(1)}, bf16[2,2,768,256]{3,2,1,0:T(8,128)(2,1)}, u32[]{:S(2)}) copy-start(bf16[2,2,768,256]{3,2,1,0:T(8,128)(2,1)} %constant.24.clone.table) | copy-start | bytes 4718596
  34.3 6.4 %collective-permute-start.5 = (f32[64,256]{1,0:T(8,128)S(1)}, f32[64,256]{1,0:T(8,128)S(1)}, u32[]{:S(2)}, u32[]{:S(2)}) collective-permute-start(f32[64,256]{1,0:T(8,128)S(1)} %get-tuple-element.47), channel_id=1, source_target_pairs={{0,6},{2,4},{4,2},{6,0},{8,14},{10,12},{12,10},{14,8},{1,7},{3,5},... | collective-permute-start | bytes 196616 | tf_op jit(solution)/shard_map/ppermute | solution.py:575
  36.5 5.5 %collective-permute-start.6 = (f32[64,256]{1,0:T(8,128)S(1)}, f32[64,256]{1,0:T(8,128)S(1)}, u32[]{:S(2)}, u32[]{:S(2)}) collective-permute-start(f32[64,256]{1,0:T(8,128)S(1)} %get-tuple-element.48), channel_id=1, source_target_pairs={{0,4},{2,6},{4,0},{6,2},{8,12},{10,14},{12,8},{14,10},{1,5},{3,7},... | collective-permute-start | bytes 196616 | tf_op jit(solution)/shard_map/ppermute | solution.py:575
  36.5 5.5 %collective-permute-start.7 = (f32[64,256]{1,0:T(8,128)S(1)}, f32[64,256]{1,0:T(8,128)S(1)}, u32[]{:S(2)}, u32[]{:S(2)}) collective-permute-start(f32[64,256]{1,0:T(8,128)S(1)} %get-tuple-element.49), channel_id=1, source_target_pairs={{0,2},{2,0},{4,6},{6,4},{8,10},{10,8},{12,14},{14,12},{1,3},{3,1},... | collective-permute-start | bytes 196616 | tf_op jit(solution)/shard_map/ppermute | solution.py:575
  38.4 6.9 %collective-permute-start.13 = (f32[64,256]{1,0:T(8,128)S(1)}, f32[64,256]{1,0:T(8,128)S(1)}, u32[]{:S(2)}, u32[]{:S(2)}) collective-permute-start(f32[64,256]{1,0:T(8,128)S(1)} %get-tuple-element.61), channel_id=1, source_target_pairs={{0,6},{2,4},{4,2},{6,0},{8,14},{10,12},{12,10},{14,8},{1,7},{3,5},... | collective-permute-start | bytes 196616 | tf_op jit(solution)/shard_map/ppermute | solution.py:575
  40.7 4.7 %collective-permute-start.14 = (f32[64,256]{1,0:T(8,128)S(1)}, f32[64,256]{1,0:T(8,128)S(1)}, u32[]{:S(2)}, u32[]{:S(2)}) collective-permute-start(f32[64,256]{1,0:T(8,128)S(1)} %get-tuple-element.62), channel_id=1, source_target_pairs={{0,4},{2,6},{4,0},{6,2},{8,12},{10,14},{12,8},{14,10},{1,5},{3,7},... | collective-permute-start | bytes 196616 | tf_op jit(solution)/shard_map/ppermute | solution.py:575
  40.7 4.7 %collective-permute-start.15 = (f32[64,256]{1,0:T(8,128)S(1)}, f32[64,256]{1,0:T(8,128)S(1)}, u32[]{:S(2)}, u32[]{:S(2)}) collective-permute-start(f32[64,256]{1,0:T(8,128)S(1)} %get-tuple-element.63), channel_id=1, source_target_pairs={{0,2},{2,0},{4,6},{6,4},{8,10},{10,8},{12,14},{14,12},{1,3},{3,1},... | collective-permute-start | bytes 196616 | tf_op jit(solution)/shard_map/ppermute | solution.py:575
  45.3 7.3 %collective-permute-start.16 = (f32[4224,128]{1,0:T(8,128)S(1)}, f32[4224,128]{1,0:T(8,128)S(1)}, u32[]{:S(2)}, u32[]{:S(2)}) collective-permute-start(f32[4224,128]{1,0:T(8,128)S(1)} %get-tuple-element.65), channel_id=1, source_target_pairs={{0,1},{1,0},{2,3},{3,2},{4,5},{5,4},{6,7},{7,6},{8,9},{9,8},{10,11... | collective-permute-start | bytes 6488072 | tf_op jit(solution)/shard_map/ppermute | solution.py:570
  45.4 3.6 %copy-start.1 = (bf16[2,768,256]{2,1,0:T(8,128)(2,1)S(1)}, bf16[2,768,256]{2,1,0:T(8,128)(2,1)}, u32[]{:S(2)}) copy-start(bf16[2,768,256]{2,1,0:T(8,128)(2,1)} %constant.25.clone.tables) | copy-start | bytes 2359300
  48.5 4.4 %collective-permute-start.17 = (f32[4224,128]{1,0:T(8,128)S(1)}, f32[4224,128]{1,0:T(8,128)S(1)}, u32[]{:S(2)}, u32[]{:S(2)}) collective-permute-start(f32[4224,128]{1,0:T(8,128)S(1)} %get-tuple-element.66), channel_id=1, source_target_pairs={{0,1},{1,0},{2,3},{3,2},{4,5},{5,4},{6,7},{7,6},{8,9},{9,8},{10,11... | collective-permute-start | bytes 6488072 | tf_op jit(solution)/shard_map/ppermute | solution.py:570

commit v19 on v18

--- a/solution.py
+++ b/solution.py
@@ -177,20 +177,22 @@
         sums[pl.ds(sums_at, TILE), :] = lower + upper
         store_split(other, (pl.ds(at, TILE),), 0, lower - upper)
 
-    def prepare(at):
+    def prepare(at, first, last):
         split = scratch[at % len(scratch)]
         cell = at * piece
-        for row in range(0, piece, group):
+        for row in range(first, last, group):
             values = field[pl.ds(cell + row, group)]
             force = values - values * values * values
             put(split, row * steps, (cell + row) * steps, force.reshape(TILE, width))
-        for row in range(0, piece, TILE):
+        for row in range(first, last, TILE):
             here = pl.ds(cell + row, TILE)
             ends = jnp.where(is_first, initial[here], field[here, steps - 1, :])
             put(split, body + row, cells * steps + cell + row, ends)
 
-    def transform(at):
-        result[...] = dot(scratch[at % len(scratch)][...], table[...])
+    def transform(at, part_at):
+        rows = (piece * steps + piece) // 2
+        here = pl.ds(part_at * rows, rows)
+        result[here, :] = dot(scratch[at % len(scratch)][here, :], table[...])
 
     def place_modes(at):
         first = cells - (at + 1) * piece
@@ -211,12 +213,14 @@
         start(2 * at + 2, 2 * at + 4)
         if at == 1:
             table_copy.wait()
-        if at:
-            transform(at - 1)
-        prepare(at)
+        for part_at in (0, 1):
+            if at:
+                transform(at - 1, part_at)
+            prepare(at, part_at * piece // 2, (part_at + 1) * piece // 2)
         if at:
             place_modes(at - 1)
-    transform(pieces - 1)
+    transform(pieces - 1, 0)
+    transform(pieces - 1, 1)
     place_modes(pieces - 1)
 
 
@@ -513,18 +517,23 @@
 
     lanes_reversed = reversal()
 
-    def product(at):
+    def prepare(at):
         split, result = scratch[2 * (at % count) : 2 * (at % count) + 2]
         for row in range(0, piece, group):
             mirrors = [cells - 1 - at * piece - row - cell for cell in range(group)]
             for chunk, got in enumerate(gots):
                 values = steps_of(got, mirrors, steps, pitch)
                 store_split(split, (pl.ds(row * steps, TILE),), chunk * part, values)
-        result[...] = dot(split[...], tables[1 - strip])
-
-    def finish(at):
+
+    def product(at, part_at):
+        split, result = scratch[2 * (at % count) : 2 * (at % count) + 2]
+        rows = piece * steps // 2
+        here = pl.ds(part_at * rows, rows)
+        result[here, :] = dot(split[here, :], tables[1 - strip])
+
+    def finish(at, part_at):
         result = scratch[2 * (at % count) + 1]
-        for row in range(0, piece, group):
+        for row in range(part_at * piece // 2, (part_at + 1) * piece // 2, group):
             first = kept[pl.ds((at * piece + row) * steps, TILE)]
             second = result[pl.ds(row * steps, TILE)]
             upper = sign * (first - second)
@@ -538,10 +547,13 @@
                 copy(done // flight - 1).start()
 
     for at in range(pieces):
-        product(at)
-        if at:
-            finish(at - 1)
-    finish(pieces - 1)
+        prepare(at)
+        for part_at in (0, 1):
+            product(at, part_at)
+            if at:
+                finish(at - 1, part_at)
+    finish(pieces - 1, 0)
+    finish(pieces - 1, 1)
     for at in range(sems.shape[0]):
         copy(at).wait()
 

time: 59 us -> 58.1 us (0.985)
  Pallas kernels: 34.2 us -> 33.2 us
  transfers between devices with their start and end apart: 18 -> 18, of which waited for: 3 -> 3; matrix products, arithmetic and copies ran while one was open for 0% -> 0% of each run, Pallas kernels for 36% -> 37%
where the time goes in v19:
time: 58.1 us; the launch traced here: 57.9 us
  Pallas kernels  33.2 us (57%)
  starting transfers between devices  21.9 us (38%)
  waiting for transfers between devices  2.39 us (4%)
    ppermute x14, starting transfers between devices, with_partner(): lax.ppermute(block, 'tm', [(slab, slab ^ distance) for slab in range(slab...  20.7 us
    pallas_call x2, Pallas kernels, forward_first(): call(functools.partial(forward_first_kernel, slabs, chunk), 'forward_firs...  6.49 us
    pallas_call x1, Pallas kernels, forward_second(): call(forward_second_kernel, 'forward_second', [IN_HBM] * 3, [IN_VMEM] * (...  6.47 us
    pallas_call x2, Pallas kernels, inverse_first(): call(functools.partial(inverse_first_kernel, slabs, chunk), 'inverse_firs...  6.34 us
    pallas_call x1, Pallas kernels, inverse_second(): call(inverse_second_kernel, 'inverse_second', [IN_VMEM] * (2 + CHUNKS), I...  5.33 us
    pallas_call x1, Pallas kernels, keep_inverse(): call(functools.partial(keep_inverse_kernel, steps), 'keep_inverse', [IN_V...  3.54 us
    pallas_call x1, Pallas kernels, keep_second(): call(functools.partial(keep_second_kernel, steps), 'keep_second', [IN_VME...  2.68 us
    ppermute x4, waiting for transfers between devices, swapped(): return lax.ppermute(block, 'space', [(0, 1), (1, 0)])  1.62 us
  transfers between devices with their start and end apart: 18, of which 3 were waited for; matrix products, arithmetic and copies ran while one was open for 0% of the time, Pallas kernels for 37%

profile of v19, /device:TPU:0, one launch (start us, length us, event | category | flops | bytes accessed | tf_op | source)
XLA Modules:
  0.0 57.9 jit_solution(8034479643443315425)
XLA Ops:
  0.0 0.1 pad_add_fusion.place
  0.1 6.5 %forward_second.1 = (f32[4352,256]{1,0:T(8,128)S(1)}, f32[4488,128]{1,0:T(8,128)S(1)}, f32[4488,128]{1,0:T(8,128)S(1)}) custom-call(s32[2]{0:T(128)S(1)} %pad_add_fusion.place, f32[256,16,512]{2,1,0:T(8,128)} %field_in.1, f32[256,512]{1,0:T(8,128)} %initial_in.1, bf16[2,768,256]{2,1,0:T(8,128)(2,1)} %constant.23.clone.tables), custom_call_target="tpu_custom_call" | custom-call | flops 4294967296 | bytes 8388608 | tf_op jit(solution)/shard_map/forward_second/pallas_call | solution.py:231
  6.6 0.5 collective-permute-start
  7.1 0.1 collective-permute-start.8
  7.2 2.7 %keep_second.1 = (f32[4488,128]{1,0:T(8,128)S(1)}, f32[4488,128]{1,0:T(8,128)S(1)}) custom-call(s32[2]{0:T(128)S(1)} %pad_add_fusion.place, bf16[2,768,256]{2,1,0:T(8,128)(2,1)S(1)} %copy-done.5, f32[4352,256]{1,0:T(8,128)S(1)} %get-tuple-element.36.sums), custom_call_target="tpu_custom_call" | custom-call | flops 2147483648 | bytes 8388608 | tf_op jit(solution)/shard_map/keep_second/pallas_call | solution.py:277
  9.8 1.3 %collective-permute-done.got = f32[4488,128]{1,0:T(8,128)S(1)} collective-permute-done((f32[4488,128]{1,0:T(8,128)S(1)}, f32[4488,128]{1,0:T(8,128)S(1)}, u32[]{:S(2)}, u32[]{:S(2)}) %collective-permute-start) | collective-permute-done | bytes 2297888 | tf_op jit(solution)/shard_map/ppermute | solution.py:582
  11.2 3.2 %forward_first.2 = (f32[16,2,128,256]{3,2,1,0:T(8,128)S(1)}, f32[64,256]{1,0:T(8,128)S(1)}, f32[64,256]{1,0:T(8,128)S(1)}, f32[64,256]{1,0:T(8,128)S(1)}, f32[64,256]{1,0:T(8,128)S(1)}) custom-call(s32[2]{0:T(128)S(1)} %pad_add_fusion.place, f32[4488,128]{1,0:T(8,128)S(1)} %get-tuple-element.37.keep, f32[4488,128]{1,0:T(8,128)S(1)} %collective-permute-done.got, ...), custom_call_target="tpu_custom_call" | custom-call | flops 2147483648 | bytes 8388608 | tf_op jit(solution)/shard_map/forward_first/pallas_call | solution.py:346
  14.4 4.0 %collective-permute-start.1 = (f32[64,256]{1,0:T(8,128)S(1)}, f32[64,256]{1,0:T(8,128)S(1)}, u32[]{:S(2)}, u32[]{:S(2)}) collective-permute-start(f32[64,256]{1,0:T(8,128)S(1)} %get-tuple-element.41), channel_id=1, source_target_pairs={{0,6},{2,4},{4,2},{6,0},{8,14},{10,12},{12,10},{14,8},{1,7},{3,5},... | collective-permute-start | bytes 196616 | tf_op jit(solution)/shard_map/ppermute | solution.py:587
  18.4 0.5 collective-permute-start.2
  18.8 0.2 collective-permute-start.3
  19.0 3.2 %forward_first.3 = (f32[16,2,128,256]{3,2,1,0:T(8,128)S(1)}, f32[64,256]{1,0:T(8,128)S(1)}, f32[64,256]{1,0:T(8,128)S(1)}, f32[64,256]{1,0:T(8,128)S(1)}, f32[64,256]{1,0:T(8,128)S(1)}) custom-call(s32[2]{0:T(128)S(1)} %pad_add_fusion.place, f32[4488,128]{1,0:T(8,128)S(1)} %get-tuple-element.51.keep, f32[4488,128]{1,0:T(8,128)S(1)} %collective-permute-done.8.got, ...), custom_call_target="tpu_custom_call" | custom-call | flops 2147483648 | bytes 8388608 | tf_op jit(solution)/shard_map/forward_first/pallas_call | solution.py:346
  22.3 2.9 %collective-permute-start.9 = (f32[64,256]{1,0:T(8,128)S(1)}, f32[64,256]{1,0:T(8,128)S(1)}, u32[]{:S(2)}, u32[]{:S(2)}) collective-permute-start(f32[64,256]{1,0:T(8,128)S(1)} %get-tuple-element.55), channel_id=1, source_target_pairs={{0,6},{2,4},{4,2},{6,0},{8,14},{10,12},{12,10},{14,8},{1,7},{3,5},... | collective-permute-start | bytes 196616 | tf_op jit(solution)/shard_map/ppermute | solution.py:587
  25.2 0.5 collective-permute-start.10
  25.6 0.2 collective-permute-start.11
  25.9 0.6 %half_sum.2 = (f32[4,64,256]{2,1,0:T(8,128)S(1)}, f32[64,256]{1,0:T(8,128)S(1)}) custom-call(s32[2]{0:T(128)S(1)} %pad_add_fusion.place, f32[2,2,3,256,256]{4,3,2,1,0:T(8,128)S(1)} %copy-done, f32[64,256]{1,0:T(8,128)S(1)} %get-tuple-element.40.refs_0_, f32[64,256]{1,0:T(8,128)S(1)} %collective-permute-done.1.refs_1_, ...), custom_call_target="tpu_custom_call" | custom-call | flops 1048576 | bytes 8388608 | tf_op jit(solution)/shard_map/half_sum/pallas_call | solution.py:379
  26.4 3.0 %collective-permute-start.4 = (f32[64,256]{1,0:T(8,128)S(1)}, f32[64,256]{1,0:T(8,128)S(1)}, u32[]{:S(2)}, u32[]{:S(2)}) collective-permute-start(f32[64,256]{1,0:T(8,128)S(1)} %get-tuple-element.45.near), channel_id=1, source_target_pairs={{0,8},{2,10},{4,12},{6,14},{8,0},{10,2},{12,4},{14,6},{1,9},{3,11}... | collective-permute-start | bytes 196616 | tf_op jit(solution)/shard_map/ppermute | solution.py:587
  29.4 0.7 %collective-permute-done.10.refs_2_ = f32[64,256]{1,0:T(8,128)S(1)} collective-permute-done((f32[64,256]{1,0:T(8,128)S(1)}, f32[64,256]{1,0:T(8,128)S(1)}, u32[]{:S(2)}, u32[]{:S(2)}) %collective-permute-start.10) | collective-permute-done | bytes 65568 | tf_op jit(solution)/shard_map/ppermute | solution.py:587
  30.1 0.6 %half_sum.3 = (f32[4,64,256]{2,1,0:T(8,128)S(1)}, f32[64,256]{1,0:T(8,128)S(1)}) custom-call(s32[2]{0:T(128)S(1)} %pad_add_fusion.place, f32[2,2,3,256,256]{4,3,2,1,0:T(8,128)S(1)} %copy-done, f32[64,256]{1,0:T(8,128)S(1)} %get-tuple-element.54.refs_0_, f32[64,256]{1,0:T(8,128)S(1)} %collective-permute-done.9.refs_1_, ...), custom_call_target="tpu_custom_call" | custom-call | flops 1048576 | bytes 8388608 | tf_op jit(solution)/shard_map/half_sum/pallas_call | solution.py:379
  30.7 2.4 %collective-permute-start.12 = (f32[64,256]{1,0:T(8,128)S(1)}, f32[64,256]{1,0:T(8,128)S(1)}, u32[]{:S(2)}, u32[]{:S(2)}) collective-permute-start(f32[64,256]{1,0:T(8,128)S(1)} %get-tuple-element.59.near), channel_id=1, source_target_pairs={{0,8},{2,10},{4,12},{6,14},{8,0},{10,2},{12,4},{14,6},{1,9},{3,11}... | collective-permute-start | bytes 196616 | tf_op jit(solution)/shard_map/ppermute | solution.py:587
  33.2 0.6 %close.2 = (f32[64,256]{1,0:T(8,128)S(1)}, f32[64,256]{1,0:T(8,128)S(1)}, f32[64,256]{1,0:T(8,128)S(1)}, f32[64,256]{1,0:T(8,128)S(1)}) custom-call(s32[2]{0:T(128)S(1)} %pad_add_fusion.place, f32[2,2,3,256,256]{4,3,2,1,0:T(8,128)S(1)} %copy-done, f32[4,64,256]{2,1,0:T(8,128)S(1)} %get-tuple-element.44.ordered, f32[64,256]{1,0:T(8,128)S(1)} %get-tuple-element.45.near, ...), custom_call_target="tpu_custom_call" | custom-call | flops 1048576 | bytes 8388608 | tf_op jit(solution)/shard_map/close/pallas_call | solution.py:409
  33.8 2.2 %collective-permute-start.5 = (f32[64,256]{1,0:T(8,128)S(1)}, f32[64,256]{1,0:T(8,128)S(1)}, u32[]{:S(2)}, u32[]{:S(2)}) collective-permute-start(f32[64,256]{1,0:T(8,128)S(1)} %get-tuple-element.47), channel_id=1, source_target_pairs={{0,6},{2,4},{4,2},{6,0},{8,14},{10,12},{12,10},{14,8},{1,7},{3,5},... | collective-permute-start | bytes 196616 | tf_op jit(solution)/shard_map/ppermute | solution.py:587
  36.0 1.3 %collective-permute-start.7 = (f32[64,256]{1,0:T(8,128)S(1)}, f32[64,256]{1,0:T(8,128)S(1)}, u32[]{:S(2)}, u32[]{:S(2)}) collective-permute-start(f32[64,256]{1,0:T(8,128)S(1)} %get-tuple-element.49), channel_id=1, source_target_pairs={{0,2},{2,0},{4,6},{6,4},{8,10},{10,8},{12,14},{14,12},{1,3},{3,1},... | collective-permute-start | bytes 196616 | tf_op jit(solution)/shard_map/ppermute | solution.py:587
  37.3 0.6 %close.3 = (f32[64,256]{1,0:T(8,128)S(1)}, f32[64,256]{1,0:T(8,128)S(1)}, f32[64,256]{1,0:T(8,128)S(1)}, f32[64,256]{1,0:T(8,128)S(1)}) custom-call(s32[2]{0:T(128)S(1)} %pad_add_fusion.place, f32[2,2,3,256,256]{4,3,2,1,0:T(8,128)S(1)} %copy-done, f32[4,64,256]{2,1,0:T(8,128)S(1)} %get-tuple-element.58.ordered, f32[64,256]{1,0:T(8,128)S(1)} %get-tuple-element.59.near, ...), custom_call_target="tpu_custom_call" | custom-call | flops 1048576 | bytes 8388608 | tf_op jit(solution)/shard_map/close/pallas_call | solution.py:409
  37.9 2.2 %collective-permute-start.13 = (f32[64,256]{1,0:T(8,128)S(1)}, f32[64,256]{1,0:T(8,128)S(1)}, u32[]{:S(2)}, u32[]{:S(2)}) collective-permute-start(f32[64,256]{1,0:T(8,128)S(1)} %get-tuple-element.61), channel_id=1, source_target_pairs={{0,6},{2,4},{4,2},{6,0},{8,14},{10,12},{12,10},{14,8},{1,7},{3,5},... | collective-permute-start | bytes 196616 | tf_op jit(solution)/shard_map/ppermute | solution.py:587
  40.2 1.3 %collective-permute-start.15 = (f32[64,256]{1,0:T(8,128)S(1)}, f32[64,256]{1,0:T(8,128)S(1)}, u32[]{:S(2)}, u32[]{:S(2)}) collective-permute-start(f32[64,256]{1,0:T(8,128)S(1)} %get-tuple-element.63), channel_id=1, source_target_pairs={{0,2},{2,0},{4,6},{6,4},{8,10},{10,8},{12,14},{14,12},{1,3},{3,1},... | collective-permute-start | bytes 196616 | tf_op jit(solution)/shard_map/ppermute | solution.py:587
  41.5 3.3 %inverse_first.2 = (f32[4224,128]{1,0:T(8,128)S(1)}, f32[4224,128]{1,0:T(8,128)S(1)}) custom-call(s32[2]{0:T(128)S(1)} %pad_add_fusion.place, f32[16,2,128,256]{3,2,1,0:T(8,128)S(1)} %get-tuple-element.39.modes, bf16[2,2,768,256]{3,2,1,0:T(8,128)(2,1)S(1)} %copy-done.2, f32[2,2,256,256]{3,2,1,0:T(8,128)S(1)} %copy-done.4, ...), custom_call_target="tpu_custom_call" | custom-call | flops 2147483648 | bytes 8388608 | tf_op jit(solution)/shard_map/inverse_first/pallas_call | solution.py:455
  44.8 0.1 collective-permute-start.16
  44.9 3.1 %inverse_first.3 = (f32[4224,128]{1,0:T(8,128)S(1)}, f32[4224,128]{1,0:T(8,128)S(1)}) custom-call(s32[2]{0:T(128)S(1)} %pad_add_fusion.place, f32[16,2,128,256]{3,2,1,0:T(8,128)S(1)} %get-tuple-element.53.modes, bf16[2,2,768,256]{3,2,1,0:T(8,128)(2,1)S(1)} %copy-done.2, f32[2,2,256,256]{3,2,1,0:T(8,128)S(1)} %copy-done.4, ...), custom_call_target="tpu_custom_call" | custom-call | flops 2147483648 | bytes 8388608 | tf_op jit(solution)/shard_map/inverse_first/pallas_call | solution.py:455
  48.0 0.5 collective-permute-start.17
  48.5 3.5 %keep_inverse.1.kept = f32[4096,256]{1,0:T(8,128)S(1)} custom-call(s32[2]{0:T(128)S(1)} %pad_add_fusion.place, bf16[2,768,256]{2,1,0:T(8,128)(2,1)S(1)} %copy-done.1, f32[4224,128]{1,0:T(8,128)S(1)} %get-tuple-element.50.refs_0_, f32[4224,128]{1,0:T(8,128)S(1)} %get-tuple-element.64.refs_1_), custom_call_target="tpu_custom_call" | custom-call | flops 2147483648 | bytes 8388608 | tf_op jit(solution)/shard_map/keep_inverse/pallas_call | solution.py:487
  52.1 0.3 collective-permute-done.17.refs_1_
  52.4 5.3 %inverse_second.1 = f32[256,16,512]{2,1,0:T(8,128)} custom-call(s32[2]{0:T(128)S(1)} %pad_add_fusion.place, bf16[2,768,256]{2,1,0:T(8,128)(2,1)S(1)} %copy-done.1, f32[4096,256]{1,0:T(8,128)S(1)} %keep_inverse.1.kept, f32[4224,128]{1,0:T(8,128)S(1)} %collective-permute-done.16.refs_0_, f32[4224,128]{1,0:T(8,128)S(1)} %collective-permute-done.17.refs_1_), custom_call_target="tpu_custom_call" | custom-call | flops 4294967296 | bytes 8388608 | tf_op jit(solution)/shard_map/inverse_second/pallas_call | solution.py:565
  (29 shorter events, 0.1 us)
Async XLA Ops:
  0.1 7.1 %copy-start.5 = (bf16[2,768,256]{2,1,0:T(8,128)(2,1)S(1)}, bf16[2,768,256]{2,1,0:T(8,128)(2,1)}, u32[]{:S(2)}) copy-start(bf16[2,768,256]{2,1,0:T(8,128)(2,1)} %constant.23.clone.tables) | copy-start | bytes 2359300
  6.6 4.6 %collective-permute-start = (f32[4488,128]{1,0:T(8,128)S(1)}, f32[4488,128]{1,0:T(8,128)S(1)}, u32[]{:S(2)}, u32[]{:S(2)}) collective-permute-start(f32[4488,128]{1,0:T(8,128)S(1)} %get-tuple-element.38), channel_id=1, source_target_pairs={{0,1},{1,0},{2,3},{3,2},{4,5},{5,4},{6,7},{7,6},{8,9},{9,8},{10,11... | collective-permute-start | bytes 6893576 | tf_op jit(solution)/shard_map/ppermute | solution.py:582
  7.1 12.0 %collective-permute-start.8 = (f32[4488,128]{1,0:T(8,128)S(1)}, f32[4488,128]{1,0:T(8,128)S(1)}, u32[]{:S(2)}, u32[]{:S(2)}) collective-permute-start(f32[4488,128]{1,0:T(8,128)S(1)} %get-tuple-element.52), channel_id=1, source_target_pairs={{0,1},{1,0},{2,3},{3,2},{4,5},{5,4},{6,7},{7,6},{8,9},{9,8},{10,11... | collective-permute-start | bytes 6893576 | tf_op jit(solution)/shard_map/ppermute | solution.py:582
  7.2 4.0 %copy-start.3 = (bf16[2,2,768,256]{3,2,1,0:T(8,128)(2,1)S(1)}, bf16[2,2,768,256]{3,2,1,0:T(8,128)(2,1)}, u32[]{:S(2)}) copy-start(bf16[2,2,768,256]{3,2,1,0:T(8,128)(2,1)} %constant.21.clone.table) | copy-start | bytes 4718596
  7.2 4.0 %copy-start.4 = (f32[2,2,256,256]{3,2,1,0:T(8,128)S(1)}, f32[2,2,256,256]{3,2,1,0:T(8,128)}, u32[]{:S(2)}) copy-start(f32[2,2,256,256]{3,2,1,0:T(8,128)} %constant.22.clone.decay) | copy-start | bytes 3145732
  14.4 11.2 %collective-permute-start.1 = (f32[64,256]{1,0:T(8,128)S(1)}, f32[64,256]{1,0:T(8,128)S(1)}, u32[]{:S(2)}, u32[]{:S(2)}) collective-permute-start(f32[64,256]{1,0:T(8,128)S(1)} %get-tuple-element.41), channel_id=1, source_target_pairs={{0,6},{2,4},{4,2},{6,0},{8,14},{10,12},{12,10},{14,8},{1,7},{3,5},... | collective-permute-start | bytes 196616 | tf_op jit(solution)/shard_map/ppermute | solution.py:587
  18.4 7.5 %collective-permute-start.2 = (f32[64,256]{1,0:T(8,128)S(1)}, f32[64,256]{1,0:T(8,128)S(1)}, u32[]{:S(2)}, u32[]{:S(2)}) collective-permute-start(f32[64,256]{1,0:T(8,128)S(1)} %get-tuple-element.42), channel_id=1, source_target_pairs={{0,4},{2,6},{4,0},{6,2},{8,12},{10,14},{12,8},{14,10},{1,5},{3,7},... | collective-permute-start | bytes 196616 | tf_op jit(solution)/shard_map/ppermute | solution.py:587
  18.8 7.0 %collective-permute-start.3 = (f32[64,256]{1,0:T(8,128)S(1)}, f32[64,256]{1,0:T(8,128)S(1)}, u32[]{:S(2)}, u32[]{:S(2)}) collective-permute-start(f32[64,256]{1,0:T(8,128)S(1)} %get-tuple-element.43), channel_id=1, source_target_pairs={{0,2},{2,0},{4,6},{6,4},{8,10},{10,8},{12,14},{14,12},{1,3},{3,1},... | collective-permute-start | bytes 196616 | tf_op jit(solution)/shard_map/ppermute | solution.py:587
  19.0 6.8 %copy-start = (f32[2,2,3,256,256]{4,3,2,1,0:T(8,128)S(1)}, f32[2,2,3,256,256]{4,3,2,1,0:T(8,128)}, u32[]{:S(2)}) copy-start(f32[2,2,3,256,256]{4,3,2,1,0:T(8,128)} %constant.20.clone.closing) | copy-start | bytes 9437188
  22.3 7.1 %collective-permute-start.9 = (f32[64,256]{1,0:T(8,128)S(1)}, f32[64,256]{1,0:T(8,128)S(1)}, u32[]{:S(2)}, u32[]{:S(2)}) collective-permute-start(f32[64,256]{1,0:T(8,128)S(1)} %get-tuple-element.55), channel_id=1, source_target_pairs={{0,6},{2,4},{4,2},{6,0},{8,14},{10,12},{12,10},{14,8},{1,7},{3,5},... | collective-permute-start | bytes 196616 | tf_op jit(solution)/shard_map/ppermute | solution.py:587
  25.2 4.9 %collective-permute-start.10 = (f32[64,256]{1,0:T(8,128)S(1)}, f32[64,256]{1,0:T(8,128)S(1)}, u32[]{:S(2)}, u32[]{:S(2)}) collective-permute-start(f32[64,256]{1,0:T(8,128)S(1)} %get-tuple-element.56), channel_id=1, source_target_pairs={{0,4},{2,6},{4,0},{6,2},{8,12},{10,14},{12,8},{14,10},{1,5},{3,7},... | collective-permute-start | bytes 196616 | tf_op jit(solution)/shard_map/ppermute | solution.py:587
  25.6 4.5 %collective-permute-start.11 = (f32[64,256]{1,0:T(8,128)S(1)}, f32[64,256]{1,0:T(8,128)S(1)}, u32[]{:S(2)}, u32[]{:S(2)}) collective-permute-start(f32[64,256]{1,0:T(8,128)S(1)} %get-tuple-element.57), channel_id=1, source_target_pairs={{0,2},{2,0},{4,6},{6,4},{8,10},{10,8},{12,14},{14,12},{1,3},{3,1},... | collective-permute-start | bytes 196616 | tf_op jit(solution)/shard_map/ppermute | solution.py:587
  26.4 6.7 %collective-permute-start.4 = (f32[64,256]{1,0:T(8,128)S(1)}, f32[64,256]{1,0:T(8,128)S(1)}, u32[]{:S(2)}, u32[]{:S(2)}) collective-permute-start(f32[64,256]{1,0:T(8,128)S(1)} %get-tuple-element.45.near), channel_id=1, source_target_pairs={{0,8},{2,10},{4,12},{6,14},{8,0},{10,2},{12,4},{14,6},{1,9},{3,11}... | collective-permute-start | bytes 196616 | tf_op jit(solution)/shard_map/ppermute | solution.py:587
  30.7 6.6 %collective-permute-start.12 = (f32[64,256]{1,0:T(8,128)S(1)}, f32[64,256]{1,0:T(8,128)S(1)}, u32[]{:S(2)}, u32[]{:S(2)}) collective-permute-start(f32[64,256]{1,0:T(8,128)S(1)} %get-tuple-element.59.near), channel_id=1, source_target_pairs={{0,8},{2,10},{4,12},{6,14},{8,0},{10,2},{12,4},{14,6},{1,9},{3,11}... | collective-permute-start | bytes 196616 | tf_op jit(solution)/shard_map/ppermute | solution.py:587
  33.8 7.7 %copy-start.2 = (bf16[2,2,768,256]{3,2,1,0:T(8,128)(2,1)S(1)}, bf16[2,2,768,256]{3,2,1,0:T(8,128)(2,1)}, u32[]{:S(2)}) copy-start(bf16[2,2,768,256]{3,2,1,0:T(8,128)(2,1)} %constant.24.clone.table) | copy-start | bytes 4718596
  33.8 6.4 %collective-permute-start.5 = (f32[64,256]{1,0:T(8,128)S(1)}, f32[64,256]{1,0:T(8,128)S(1)}, u32[]{:S(2)}, u32[]{:S(2)}) collective-permute-start(f32[64,256]{1,0:T(8,128)S(1)} %get-tuple-element.47), channel_id=1, source_target_pairs={{0,6},{2,4},{4,2},{6,0},{8,14},{10,12},{12,10},{14,8},{1,7},{3,5},... | collective-permute-start | bytes 196616 | tf_op jit(solution)/shard_map/ppermute | solution.py:587
  36.0 5.5 %collective-permute-start.6 = (f32[64,256]{1,0:T(8,128)S(1)}, f32[64,256]{1,0:T(8,128)S(1)}, u32[]{:S(2)}, u32[]{:S(2)}) collective-permute-start(f32[64,256]{1,0:T(8,128)S(1)} %get-tuple-element.48), channel_id=1, source_target_pairs={{0,4},{2,6},{4,0},{6,2},{8,12},{10,14},{12,8},{14,10},{1,5},{3,7},... | collective-permute-start | bytes 196616 | tf_op jit(solution)/shard_map/ppermute | solution.py:587
  36.0 5.5 %collective-permute-start.7 = (f32[64,256]{1,0:T(8,128)S(1)}, f32[64,256]{1,0:T(8,128)S(1)}, u32[]{:S(2)}, u32[]{:S(2)}) collective-permute-start(f32[64,256]{1,0:T(8,128)S(1)} %get-tuple-element.49), channel_id=1, source_target_pairs={{0,2},{2,0},{4,6},{6,4},{8,10},{10,8},{12,14},{14,12},{1,3},{3,1},... | collective-permute-start | bytes 196616 | tf_op jit(solution)/shard_map/ppermute | solution.py:587
  37.9 6.9 %collective-permute-start.13 = (f32[64,256]{1,0:T(8,128)S(1)}, f32[64,256]{1,0:T(8,128)S(1)}, u32[]{:S(2)}, u32[]{:S(2)}) collective-permute-start(f32[64,256]{1,0:T(8,128)S(1)} %get-tuple-element.61), channel_id=1, source_target_pairs={{0,6},{2,4},{4,2},{6,0},{8,14},{10,12},{12,10},{14,8},{1,7},{3,5},... | collective-permute-start | bytes 196616 | tf_op jit(solution)/shard_map/ppermute | solution.py:587
  40.2 4.7 %collective-permute-start.14 = (f32[64,256]{1,0:T(8,128)S(1)}, f32[64,256]{1,0:T(8,128)S(1)}, u32[]{:S(2)}, u32[]{:S(2)}) collective-permute-start(f32[64,256]{1,0:T(8,128)S(1)} %get-tuple-element.62), channel_id=1, source_target_pairs={{0,4},{2,6},{4,0},{6,2},{8,12},{10,14},{12,8},{14,10},{1,5},{3,7},... | collective-permute-start | bytes 196616 | tf_op jit(solution)/shard_map/ppermute | solution.py:587
  40.2 4.7 %collective-permute-start.15 = (f32[64,256]{1,0:T(8,128)S(1)}, f32[64,256]{1,0:T(8,128)S(1)}, u32[]{:S(2)}, u32[]{:S(2)}) collective-permute-start(f32[64,256]{1,0:T(8,128)S(1)} %get-tuple-element.63), channel_id=1, source_target_pairs={{0,2},{2,0},{4,6},{6,4},{8,10},{10,8},{12,14},{14,12},{1,3},{3,1},... | collective-permute-start | bytes 196616 | tf_op jit(solution)/shard_map/ppermute | solution.py:587
  44.8 7.3 %collective-permute-start.16 = (f32[4224,128]{1,0:T(8,128)S(1)}, f32[4224,128]{1,0:T(8,128)S(1)}, u32[]{:S(2)}, u32[]{:S(2)}) collective-permute-start(f32[4224,128]{1,0:T(8,128)S(1)} %get-tuple-element.65), channel_id=1, source_target_pairs={{0,1},{1,0},{2,3},{3,2},{4,5},{5,4},{6,7},{7,6},{8,9},{9,8},{10,11... | collective-permute-start | bytes 6488072 | tf_op jit(solution)/shard_map/ppermute | solution.py:582
  44.9 3.6 %copy-start.1 = (bf16[2,768,256]{2,1,0:T(8,128)(2,1)S(1)}, bf16[2,768,256]{2,1,0:T(8,128)(2,1)}, u32[]{:S(2)}) copy-start(bf16[2,768,256]{2,1,0:T(8,128)(2,1)} %constant.25.clone.tables) | copy-start | bytes 2359300
  48.0 4.4 %collective-permute-start.17 = (f32[4224,128]{1,0:T(8,128)S(1)}, f32[4224,128]{1,0:T(8,128)S(1)}, u32[]{:S(2)}, u32[]{:S(2)}) collective-permute-start(f32[4224,128]{1,0:T(8,128)S(1)} %get-tuple-element.66), channel_id=1, source_target_pairs={{0,1},{1,0},{2,3},{3,2},{4,5},{5,4},{6,7},{7,6},{8,9},{9,8},{10,11... | collective-permute-start | bytes 6488072 | tf_op jit(solution)/shard_map/ppermute | solution.py:582

commit v20 on v19

--- a/solution.py
+++ b/solution.py
@@ -17,6 +17,7 @@
 SUBLANES = 8
 TILE = 16
 CHUNKS = 2
+PARTS = 4
 
 
 def sine_table(row_index, column_index, length):
@@ -69,6 +70,12 @@
     low = (block - high.astype(jnp.float32)).astype(jnp.bfloat16)
     ref[(*at, pl.ds(lane, width))] = high
     ref[(*at, pl.ds(depth + lane, width))] = low
+
+
+def part_of(at, rows):
+    tiles = rows // TILE
+    first, last = at * tiles // PARTS, (at + 1) * tiles // PARTS
+    return pl.ds(first * TILE, (last - first) * TILE)
 
 
 def dot(split, table):
@@ -184,14 +191,13 @@
             values = field[pl.ds(cell + row, group)]
             force = values - values * values * values
             put(split, row * steps, (cell + row) * steps, force.reshape(TILE, width))
-        for row in range(first, last, TILE):
+        for row in range(0, piece if last == piece else 0, TILE):
             here = pl.ds(cell + row, TILE)
             ends = jnp.where(is_first, initial[here], field[here, steps - 1, :])
             put(split, body + row, cells * steps + cell + row, ends)
 
     def transform(at, part_at):
-        rows = (piece * steps + piece) // 2
-        here = pl.ds(part_at * rows, rows)
+        here = part_of(part_at, piece * steps + piece)
         result[here, :] = dot(scratch[at % len(scratch)][here, :], table[...])
 
     def place_modes(at):
@@ -213,14 +219,14 @@
         start(2 * at + 2, 2 * at + 4)
         if at == 1:
             table_copy.wait()
-        for part_at in (0, 1):
+        for part_at in range(PARTS):
             if at:
                 transform(at - 1, part_at)
-            prepare(at, part_at * piece // 2, (part_at + 1) * piece // 2)
+            prepare(at, part_at * piece // PARTS, (part_at + 1) * piece // PARTS)
         if at:
             place_modes(at - 1)
-    transform(pieces - 1, 0)
-    transform(pieces - 1, 1)
+    for part_at in range(PARTS):
+        transform(pieces - 1, part_at)
     place_modes(pieces - 1)
 
 
@@ -527,13 +533,12 @@
 
     def product(at, part_at):
         split, result = scratch[2 * (at % count) : 2 * (at % count) + 2]
-        rows = piece * steps // 2
-        here = pl.ds(part_at * rows, rows)
+        here = part_of(part_at, piece * steps)
         result[here, :] = dot(split[here, :], tables[1 - strip])
 
     def finish(at, part_at):
         result = scratch[2 * (at % count) + 1]
-        for row in range(part_at * piece // 2, (part_at + 1) * piece // 2, group):
+        for row in range(part_at * piece // PARTS, (part_at + 1) * piece // PARTS, group):
             first = kept[pl.ds((at * piece + row) * steps, TILE)]
             second = result[pl.ds(row * steps, TILE)]
             upper = sign * (first - second)
@@ -548,12 +553,12 @@
 
     for at in range(pieces):
         prepare(at)
-        for part_at in (0, 1):
+        for part_at in range(PARTS):
             product(at, part_at)
             if at:
                 finish(at - 1, part_at)
-    finish(pieces - 1, 0)
-    finish(pieces - 1, 1)
+    for part_at in range(PARTS):
+        finish(pieces - 1, part_at)
     for at in range(sems.shape[0]):
         copy(at).wait()
 

time: 58.1 us -> 58.1 us (level)
  no operation moved by 1% of the time
where the time goes in v20:
time: 58.1 us; the launch traced here: 57.9 us
  Pallas kernels  33.2 us (57%)
  starting transfers between devices  21.9 us (38%)
  waiting for transfers between devices  2.39 us (4%)
    ppermute x14, starting transfers between devices, with_partner(): lax.ppermute(block, 'tm', [(slab, slab ^ distance) for slab in range(slab...  20.7 us
    pallas_call x1, Pallas kernels, forward_second(): call(forward_second_kernel, 'forward_second', [IN_HBM] * 3, [IN_VMEM] * (...  6.58 us
    pallas_call x2, Pallas kernels, forward_first(): call(functools.partial(forward_first_kernel, slabs, chunk), 'forward_firs...  6.49 us
    pallas_call x2, Pallas kernels, inverse_first(): call(functools.partial(inverse_first_kernel, slabs, chunk), 'inverse_firs...  6.33 us
    pallas_call x1, Pallas kernels, inverse_second(): call(inverse_second_kernel, 'inverse_second', [IN_VMEM] * (2 + CHUNKS), I...  5.24 us
    pallas_call x1, Pallas kernels, keep_inverse(): call(functools.partial(keep_inverse_kernel, steps), 'keep_inverse', [IN_V...  3.54 us
    pallas_call x1, Pallas kernels, keep_second(): call(functools.partial(keep_second_kernel, steps), 'keep_second', [IN_VME...  2.68 us
    ppermute x4, waiting for transfers between devices, swapped(): return lax.ppermute(block, 'space', [(0, 1), (1, 0)])  1.62 us
  transfers between devices with their start and end apart: 18, of which 3 were waited for; matrix products, arithmetic and copies ran while one was open for 0% of the time, Pallas kernels for 37%

profile of v20, /device:TPU:0, one launch (start us, length us, event | category | flops | bytes accessed | tf_op | source)
XLA Modules:
  0.0 57.9 jit_solution(17231345056255708541)
XLA Ops:
  0.0 0.1 pad_add_fusion.place
  0.1 6.6 %forward_second.1 = (f32[4352,256]{1,0:T(8,128)S(1)}, f32[4488,128]{1,0:T(8,128)S(1)}, f32[4488,128]{1,0:T(8,128)S(1)}) custom-call(s32[2]{0:T(128)S(1)} %pad_add_fusion.place, f32[256,16,512]{2,1,0:T(8,128)} %field_in.1, f32[256,512]{1,0:T(8,128)} %initial_in.1, bf16[2,768,256]{2,1,0:T(8,128)(2,1)} %constant.23.clone.tables), custom_call_target="tpu_custom_call" | custom-call | flops 4294967296 | bytes 8388608 | tf_op jit(solution)/shard_map/forward_second/pallas_call | solution.py:237
  6.7 0.5 collective-permute-start
  7.2 0.1 collective-permute-start.8
  7.3 2.7 %keep_second.1 = (f32[4488,128]{1,0:T(8,128)S(1)}, f32[4488,128]{1,0:T(8,128)S(1)}) custom-call(s32[2]{0:T(128)S(1)} %pad_add_fusion.place, bf16[2,768,256]{2,1,0:T(8,128)(2,1)S(1)} %copy-done.5, f32[4352,256]{1,0:T(8,128)S(1)} %get-tuple-element.36.sums), custom_call_target="tpu_custom_call" | custom-call | flops 2147483648 | bytes 8388608 | tf_op jit(solution)/shard_map/keep_second/pallas_call | solution.py:283
  10.0 1.3 %collective-permute-done.got = f32[4488,128]{1,0:T(8,128)S(1)} collective-permute-done((f32[4488,128]{1,0:T(8,128)S(1)}, f32[4488,128]{1,0:T(8,128)S(1)}, u32[]{:S(2)}, u32[]{:S(2)}) %collective-permute-start) | collective-permute-done | bytes 2297888 | tf_op jit(solution)/shard_map/ppermute | solution.py:587
  11.3 3.2 %forward_first.2 = (f32[16,2,128,256]{3,2,1,0:T(8,128)S(1)}, f32[64,256]{1,0:T(8,128)S(1)}, f32[64,256]{1,0:T(8,128)S(1)}, f32[64,256]{1,0:T(8,128)S(1)}, f32[64,256]{1,0:T(8,128)S(1)}) custom-call(s32[2]{0:T(128)S(1)} %pad_add_fusion.place, f32[4488,128]{1,0:T(8,128)S(1)} %get-tuple-element.37.keep, f32[4488,128]{1,0:T(8,128)S(1)} %collective-permute-done.got, ...), custom_call_target="tpu_custom_call" | custom-call | flops 2147483648 | bytes 8388608 | tf_op jit(solution)/shard_map/forward_first/pallas_call | solution.py:352
  14.5 4.0 %collective-permute-start.1 = (f32[64,256]{1,0:T(8,128)S(1)}, f32[64,256]{1,0:T(8,128)S(1)}, u32[]{:S(2)}, u32[]{:S(2)}) collective-permute-start(f32[64,256]{1,0:T(8,128)S(1)} %get-tuple-element.41), channel_id=1, source_target_pairs={{0,6},{2,4},{4,2},{6,0},{8,14},{10,12},{12,10},{14,8},{1,7},{3,5},... | collective-permute-start | bytes 196616 | tf_op jit(solution)/shard_map/ppermute | solution.py:592
  18.5 0.5 collective-permute-start.2
  18.9 0.2 collective-permute-start.3
  19.1 3.2 %forward_first.3 = (f32[16,2,128,256]{3,2,1,0:T(8,128)S(1)}, f32[64,256]{1,0:T(8,128)S(1)}, f32[64,256]{1,0:T(8,128)S(1)}, f32[64,256]{1,0:T(8,128)S(1)}, f32[64,256]{1,0:T(8,128)S(1)}) custom-call(s32[2]{0:T(128)S(1)} %pad_add_fusion.place, f32[4488,128]{1,0:T(8,128)S(1)} %get-tuple-element.51.keep, f32[4488,128]{1,0:T(8,128)S(1)} %collective-permute-done.8.got, ...), custom_call_target="tpu_custom_call" | custom-call | flops 2147483648 | bytes 8388608 | tf_op jit(solution)/shard_map/forward_first/pallas_call | solution.py:352
  22.4 2.9 %collective-permute-start.9 = (f32[64,256]{1,0:T(8,128)S(1)}, f32[64,256]{1,0:T(8,128)S(1)}, u32[]{:S(2)}, u32[]{:S(2)}) collective-permute-start(f32[64,256]{1,0:T(8,128)S(1)} %get-tuple-element.55), channel_id=1, source_target_pairs={{0,6},{2,4},{4,2},{6,0},{8,14},{10,12},{12,10},{14,8},{1,7},{3,5},... | collective-permute-start | bytes 196616 | tf_op jit(solution)/shard_map/ppermute | solution.py:592
  25.3 0.5 collective-permute-start.10
  25.8 0.2 collective-permute-start.11
  26.0 0.6 %half_sum.2 = (f32[4,64,256]{2,1,0:T(8,128)S(1)}, f32[64,256]{1,0:T(8,128)S(1)}) custom-call(s32[2]{0:T(128)S(1)} %pad_add_fusion.place, f32[2,2,3,256,256]{4,3,2,1,0:T(8,128)S(1)} %copy-done, f32[64,256]{1,0:T(8,128)S(1)} %get-tuple-element.40.refs_0_, f32[64,256]{1,0:T(8,128)S(1)} %collective-permute-done.1.refs_1_, ...), custom_call_target="tpu_custom_call" | custom-call | flops 1048576 | bytes 8388608 | tf_op jit(solution)/shard_map/half_sum/pallas_call | solution.py:385
  26.6 3.0 %collective-permute-start.4 = (f32[64,256]{1,0:T(8,128)S(1)}, f32[64,256]{1,0:T(8,128)S(1)}, u32[]{:S(2)}, u32[]{:S(2)}) collective-permute-start(f32[64,256]{1,0:T(8,128)S(1)} %get-tuple-element.45.near), channel_id=1, source_target_pairs={{0,8},{2,10},{4,12},{6,14},{8,0},{10,2},{12,4},{14,6},{1,9},{3,11}... | collective-permute-start | bytes 196616 | tf_op jit(solution)/shard_map/ppermute | solution.py:592
  29.5 0.7 %collective-permute-done.10.refs_2_ = f32[64,256]{1,0:T(8,128)S(1)} collective-permute-done((f32[64,256]{1,0:T(8,128)S(1)}, f32[64,256]{1,0:T(8,128)S(1)}, u32[]{:S(2)}, u32[]{:S(2)}) %collective-permute-start.10) | collective-permute-done | bytes 65568 | tf_op jit(solution)/shard_map/ppermute | solution.py:592
  30.3 0.6 %half_sum.3 = (f32[4,64,256]{2,1,0:T(8,128)S(1)}, f32[64,256]{1,0:T(8,128)S(1)}) custom-call(s32[2]{0:T(128)S(1)} %pad_add_fusion.place, f32[2,2,3,256,256]{4,3,2,1,0:T(8,128)S(1)} %copy-done, f32[64,256]{1,0:T(8,128)S(1)} %get-tuple-element.54.refs_0_, f32[64,256]{1,0:T(8,128)S(1)} %collective-permute-done.9.refs_1_, ...), custom_call_target="tpu_custom_call" | custom-call | flops 1048576 | bytes 8388608 | tf_op jit(solution)/shard_map/half_sum/pallas_call | solution.py:385
  30.8 2.4 %collective-permute-start.12 = (f32[64,256]{1,0:T(8,128)S(1)}, f32[64,256]{1,0:T(8,128)S(1)}, u32[]{:S(2)}, u32[]{:S(2)}) collective-permute-start(f32[64,256]{1,0:T(8,128)S(1)} %get-tuple-element.59.near), channel_id=1, source_target_pairs={{0,8},{2,10},{4,12},{6,14},{8,0},{10,2},{12,4},{14,6},{1,9},{3,11}... | collective-permute-start | bytes 196616 | tf_op jit(solution)/shard_map/ppermute | solution.py:592
  33.3 0.6 %close.2 = (f32[64,256]{1,0:T(8,128)S(1)}, f32[64,256]{1,0:T(8,128)S(1)}, f32[64,256]{1,0:T(8,128)S(1)}, f32[64,256]{1,0:T(8,128)S(1)}) custom-call(s32[2]{0:T(128)S(1)} %pad_add_fusion.place, f32[2,2,3,256,256]{4,3,2,1,0:T(8,128)S(1)} %copy-done, f32[4,64,256]{2,1,0:T(8,128)S(1)} %get-tuple-element.44.ordered, f32[64,256]{1,0:T(8,128)S(1)} %get-tuple-element.45.near, ...), custom_call_target="tpu_custom_call" | custom-call | flops 1048576 | bytes 8388608 | tf_op jit(solution)/shard_map/close/pallas_call | solution.py:415
  33.9 2.2 %collective-permute-start.5 = (f32[64,256]{1,0:T(8,128)S(1)}, f32[64,256]{1,0:T(8,128)S(1)}, u32[]{:S(2)}, u32[]{:S(2)}) collective-permute-start(f32[64,256]{1,0:T(8,128)S(1)} %get-tuple-element.47), channel_id=1, source_target_pairs={{0,6},{2,4},{4,2},{6,0},{8,14},{10,12},{12,10},{14,8},{1,7},{3,5},... | collective-permute-start | bytes 196616 | tf_op jit(solution)/shard_map/ppermute | solution.py:592
  36.2 1.3 %collective-permute-start.7 = (f32[64,256]{1,0:T(8,128)S(1)}, f32[64,256]{1,0:T(8,128)S(1)}, u32[]{:S(2)}, u32[]{:S(2)}) collective-permute-start(f32[64,256]{1,0:T(8,128)S(1)} %get-tuple-element.49), channel_id=1, source_target_pairs={{0,2},{2,0},{4,6},{6,4},{8,10},{10,8},{12,14},{14,12},{1,3},{3,1},... | collective-permute-start | bytes 196616 | tf_op jit(solution)/shard_map/ppermute | solution.py:592
  37.5 0.6 %close.3 = (f32[64,256]{1,0:T(8,128)S(1)}, f32[64,256]{1,0:T(8,128)S(1)}, f32[64,256]{1,0:T(8,128)S(1)}, f32[64,256]{1,0:T(8,128)S(1)}) custom-call(s32[2]{0:T(128)S(1)} %pad_add_fusion.place, f32[2,2,3,256,256]{4,3,2,1,0:T(8,128)S(1)} %copy-done, f32[4,64,256]{2,1,0:T(8,128)S(1)} %get-tuple-element.58.ordered, f32[64,256]{1,0:T(8,128)S(1)} %get-tuple-element.59.near, ...), custom_call_target="tpu_custom_call" | custom-call | flops 1048576 | bytes 8388608 | tf_op jit(solution)/shard_map/close/pallas_call | solution.py:415
  38.1 2.2 %collective-permute-start.13 = (f32[64,256]{1,0:T(8,128)S(1)}, f32[64,256]{1,0:T(8,128)S(1)}, u32[]{:S(2)}, u32[]{:S(2)}) collective-permute-start(f32[64,256]{1,0:T(8,128)S(1)} %get-tuple-element.61), channel_id=1, source_target_pairs={{0,6},{2,4},{4,2},{6,0},{8,14},{10,12},{12,10},{14,8},{1,7},{3,5},... | collective-permute-start | bytes 196616 | tf_op jit(solution)/shard_map/ppermute | solution.py:592
  40.3 1.3 %collective-permute-start.15 = (f32[64,256]{1,0:T(8,128)S(1)}, f32[64,256]{1,0:T(8,128)S(1)}, u32[]{:S(2)}, u32[]{:S(2)}) collective-permute-start(f32[64,256]{1,0:T(8,128)S(1)} %get-tuple-element.63), channel_id=1, source_target_pairs={{0,2},{2,0},{4,6},{6,4},{8,10},{10,8},{12,14},{14,12},{1,3},{3,1},... | collective-permute-start | bytes 196616 | tf_op jit(solution)/shard_map/ppermute | solution.py:592
  41.6 3.3 %inverse_first.2 = (f32[4224,128]{1,0:T(8,128)S(1)}, f32[4224,128]{1,0:T(8,128)S(1)}) custom-call(s32[2]{0:T(128)S(1)} %pad_add_fusion.place, f32[16,2,128,256]{3,2,1,0:T(8,128)S(1)} %get-tuple-element.39.modes, bf16[2,2,768,256]{3,2,1,0:T(8,128)(2,1)S(1)} %copy-done.2, f32[2,2,256,256]{3,2,1,0:T(8,128)S(1)} %copy-done.4, ...), custom_call_target="tpu_custom_call" | custom-call | flops 2147483648 | bytes 8388608 | tf_op jit(solution)/shard_map/inverse_first/pallas_call | solution.py:461
  44.9 0.1 collective-permute-start.16
  45.0 3.1 %inverse_first.3 = (f32[4224,128]{1,0:T(8,128)S(1)}, f32[4224,128]{1,0:T(8,128)S(1)}) custom-call(s32[2]{0:T(128)S(1)} %pad_add_fusion.place, f32[16,2,128,256]{3,2,1,0:T(8,128)S(1)} %get-tuple-element.53.modes, bf16[2,2,768,256]{3,2,1,0:T(8,128)(2,1)S(1)} %copy-done.2, f32[2,2,256,256]{3,2,1,0:T(8,128)S(1)} %copy-done.4, ...), custom_call_target="tpu_custom_call" | custom-call | flops 2147483648 | bytes 8388608 | tf_op jit(solution)/shard_map/inverse_first/pallas_call | solution.py:461
  48.1 0.5 collective-permute-start.17
  48.6 3.5 %keep_inverse.1.kept = f32[4096,256]{1,0:T(8,128)S(1)} custom-call(s32[2]{0:T(128)S(1)} %pad_add_fusion.place, bf16[2,768,256]{2,1,0:T(8,128)(2,1)S(1)} %copy-done.1, f32[4224,128]{1,0:T(8,128)S(1)} %get-tuple-element.50.refs_0_, f32[4224,128]{1,0:T(8,128)S(1)} %get-tuple-element.64.refs_1_), custom_call_target="tpu_custom_call" | custom-call | flops 2147483648 | bytes 8388608 | tf_op jit(solution)/shard_map/keep_inverse/pallas_call | solution.py:493
  52.2 0.3 collective-permute-done.17.refs_1_
  52.5 5.2 %inverse_second.1 = f32[256,16,512]{2,1,0:T(8,128)} custom-call(s32[2]{0:T(128)S(1)} %pad_add_fusion.place, bf16[2,768,256]{2,1,0:T(8,128)(2,1)S(1)} %copy-done.1, f32[4096,256]{1,0:T(8,128)S(1)} %keep_inverse.1.kept, f32[4224,128]{1,0:T(8,128)S(1)} %collective-permute-done.16.refs_0_, f32[4224,128]{1,0:T(8,128)S(1)} %collective-permute-done.17.refs_1_), custom_call_target="tpu_custom_call" | custom-call | flops 4294967296 | bytes 8388608 | tf_op jit(solution)/shard_map/inverse_second/pallas_call | solution.py:570
  (29 shorter events, 0.1 us)
Async XLA Ops:
  0.1 7.2 %copy-start.5 = (bf16[2,768,256]{2,1,0:T(8,128)(2,1)S(1)}, bf16[2,768,256]{2,1,0:T(8,128)(2,1)}, u32[]{:S(2)}) copy-start(bf16[2,768,256]{2,1,0:T(8,128)(2,1)} %constant.23.clone.tables) | copy-start | bytes 2359300
  6.7 4.6 %collective-permute-start = (f32[4488,128]{1,0:T(8,128)S(1)}, f32[4488,128]{1,0:T(8,128)S(1)}, u32[]{:S(2)}, u32[]{:S(2)}) collective-permute-start(f32[4488,128]{1,0:T(8,128)S(1)} %get-tuple-element.38), channel_id=1, source_target_pairs={{0,1},{1,0},{2,3},{3,2},{4,5},{5,4},{6,7},{7,6},{8,9},{9,8},{10,11... | collective-permute-start | bytes 6893576 | tf_op jit(solution)/shard_map/ppermute | solution.py:587
  7.2 11.9 %collective-permute-start.8 = (f32[4488,128]{1,0:T(8,128)S(1)}, f32[4488,128]{1,0:T(8,128)S(1)}, u32[]{:S(2)}, u32[]{:S(2)}) collective-permute-start(f32[4488,128]{1,0:T(8,128)S(1)} %get-tuple-element.52), channel_id=1, source_target_pairs={{0,1},{1,0},{2,3},{3,2},{4,5},{5,4},{6,7},{7,6},{8,9},{9,8},{10,11... | collective-permute-start | bytes 6893576 | tf_op jit(solution)/shard_map/ppermute | solution.py:587
  7.3 4.0 %copy-start.3 = (bf16[2,2,768,256]{3,2,1,0:T(8,128)(2,1)S(1)}, bf16[2,2,768,256]{3,2,1,0:T(8,128)(2,1)}, u32[]{:S(2)}) copy-start(bf16[2,2,768,256]{3,2,1,0:T(8,128)(2,1)} %constant.21.clone.table) | copy-start | bytes 4718596
  7.3 4.0 %copy-start.4 = (f32[2,2,256,256]{3,2,1,0:T(8,128)S(1)}, f32[2,2,256,256]{3,2,1,0:T(8,128)}, u32[]{:S(2)}) copy-start(f32[2,2,256,256]{3,2,1,0:T(8,128)} %constant.22.clone.decay) | copy-start | bytes 3145732
  14.5 11.2 %collective-permute-start.1 = (f32[64,256]{1,0:T(8,128)S(1)}, f32[64,256]{1,0:T(8,128)S(1)}, u32[]{:S(2)}, u32[]{:S(2)}) collective-permute-start(f32[64,256]{1,0:T(8,128)S(1)} %get-tuple-element.41), channel_id=1, source_target_pairs={{0,6},{2,4},{4,2},{6,0},{8,14},{10,12},{12,10},{14,8},{1,7},{3,5},... | collective-permute-start | bytes 196616 | tf_op jit(solution)/shard_map/ppermute | solution.py:592
  18.5 7.5 %collective-permute-start.2 = (f32[64,256]{1,0:T(8,128)S(1)}, f32[64,256]{1,0:T(8,128)S(1)}, u32[]{:S(2)}, u32[]{:S(2)}) collective-permute-start(f32[64,256]{1,0:T(8,128)S(1)} %get-tuple-element.42), channel_id=1, source_target_pairs={{0,4},{2,6},{4,0},{6,2},{8,12},{10,14},{12,8},{14,10},{1,5},{3,7},... | collective-permute-start | bytes 196616 | tf_op jit(solution)/shard_map/ppermute | solution.py:592
  18.9 7.0 %collective-permute-start.3 = (f32[64,256]{1,0:T(8,128)S(1)}, f32[64,256]{1,0:T(8,128)S(1)}, u32[]{:S(2)}, u32[]{:S(2)}) collective-permute-start(f32[64,256]{1,0:T(8,128)S(1)} %get-tuple-element.43), channel_id=1, source_target_pairs={{0,2},{2,0},{4,6},{6,4},{8,10},{10,8},{12,14},{14,12},{1,3},{3,1},... | collective-permute-start | bytes 196616 | tf_op jit(solution)/shard_map/ppermute | solution.py:592
  19.1 6.8 %copy-start = (f32[2,2,3,256,256]{4,3,2,1,0:T(8,128)S(1)}, f32[2,2,3,256,256]{4,3,2,1,0:T(8,128)}, u32[]{:S(2)}) copy-start(f32[2,2,3,256,256]{4,3,2,1,0:T(8,128)} %constant.20.clone.closing) | copy-start | bytes 9437188
  22.4 7.1 %collective-permute-start.9 = (f32[64,256]{1,0:T(8,128)S(1)}, f32[64,256]{1,0:T(8,128)S(1)}, u32[]{:S(2)}, u32[]{:S(2)}) collective-permute-start(f32[64,256]{1,0:T(8,128)S(1)} %get-tuple-element.55), channel_id=1, source_target_pairs={{0,6},{2,4},{4,2},{6,0},{8,14},{10,12},{12,10},{14,8},{1,7},{3,5},... | collective-permute-start | bytes 196616 | tf_op jit(solution)/shard_map/ppermute | solution.py:592
  25.3 4.9 %collective-permute-start.10 = (f32[64,256]{1,0:T(8,128)S(1)}, f32[64,256]{1,0:T(8,128)S(1)}, u32[]{:S(2)}, u32[]{:S(2)}) collective-permute-start(f32[64,256]{1,0:T(8,128)S(1)} %get-tuple-element.56), channel_id=1, source_target_pairs={{0,4},{2,6},{4,0},{6,2},{8,12},{10,14},{12,8},{14,10},{1,5},{3,7},... | collective-permute-start | bytes 196616 | tf_op jit(solution)/shard_map/ppermute | solution.py:592
  25.8 4.5 %collective-permute-start.11 = (f32[64,256]{1,0:T(8,128)S(1)}, f32[64,256]{1,0:T(8,128)S(1)}, u32[]{:S(2)}, u32[]{:S(2)}) collective-permute-start(f32[64,256]{1,0:T(8,128)S(1)} %get-tuple-element.57), channel_id=1, source_target_pairs={{0,2},{2,0},{4,6},{6,4},{8,10},{10,8},{12,14},{14,12},{1,3},{3,1},... | collective-permute-start | bytes 196616 | tf_op jit(solution)/shard_map/ppermute | solution.py:592
  26.6 6.7 %collective-permute-start.4 = (f32[64,256]{1,0:T(8,128)S(1)}, f32[64,256]{1,0:T(8,128)S(1)}, u32[]{:S(2)}, u32[]{:S(2)}) collective-permute-start(f32[64,256]{1,0:T(8,128)S(1)} %get-tuple-element.45.near), channel_id=1, source_target_pairs={{0,8},{2,10},{4,12},{6,14},{8,0},{10,2},{12,4},{14,6},{1,9},{3,11}... | collective-permute-start | bytes 196616 | tf_op jit(solution)/shard_map/ppermute | solution.py:592
  30.8 6.6 %collective-permute-start.12 = (f32[64,256]{1,0:T(8,128)S(1)}, f32[64,256]{1,0:T(8,128)S(1)}, u32[]{:S(2)}, u32[]{:S(2)}) collective-permute-start(f32[64,256]{1,0:T(8,128)S(1)} %get-tuple-element.59.near), channel_id=1, source_target_pairs={{0,8},{2,10},{4,12},{6,14},{8,0},{10,2},{12,4},{14,6},{1,9},{3,11}... | collective-permute-start | bytes 196616 | tf_op jit(solution)/shard_map/ppermute | solution.py:592
  33.9 7.7 %copy-start.2 = (bf16[2,2,768,256]{3,2,1,0:T(8,128)(2,1)S(1)}, bf16[2,2,768,256]{3,2,1,0:T(8,128)(2,1)}, u32[]{:S(2)}) copy-start(bf16[2,2,768,256]{3,2,1,0:T(8,128)(2,1)} %constant.24.clone.table) | copy-start | bytes 4718596
  33.9 6.4 %collective-permute-start.5 = (f32[64,256]{1,0:T(8,128)S(1)}, f32[64,256]{1,0:T(8,128)S(1)}, u32[]{:S(2)}, u32[]{:S(2)}) collective-permute-start(f32[64,256]{1,0:T(8,128)S(1)} %get-tuple-element.47), channel_id=1, source_target_pairs={{0,6},{2,4},{4,2},{6,0},{8,14},{10,12},{12,10},{14,8},{1,7},{3,5},... | collective-permute-start | bytes 196616 | tf_op jit(solution)/shard_map/ppermute | solution.py:592
  36.1 5.5 %collective-permute-start.6 = (f32[64,256]{1,0:T(8,128)S(1)}, f32[64,256]{1,0:T(8,128)S(1)}, u32[]{:S(2)}, u32[]{:S(2)}) collective-permute-start(f32[64,256]{1,0:T(8,128)S(1)} %get-tuple-element.48), channel_id=1, source_target_pairs={{0,4},{2,6},{4,0},{6,2},{8,12},{10,14},{12,8},{14,10},{1,5},{3,7},... | collective-permute-start | bytes 196616 | tf_op jit(solution)/shard_map/ppermute | solution.py:592
  36.2 5.5 %collective-permute-start.7 = (f32[64,256]{1,0:T(8,128)S(1)}, f32[64,256]{1,0:T(8,128)S(1)}, u32[]{:S(2)}, u32[]{:S(2)}) collective-permute-start(f32[64,256]{1,0:T(8,128)S(1)} %get-tuple-element.49), channel_id=1, source_target_pairs={{0,2},{2,0},{4,6},{6,4},{8,10},{10,8},{12,14},{14,12},{1,3},{3,1},... | collective-permute-start | bytes 196616 | tf_op jit(solution)/shard_map/ppermute | solution.py:592
  38.1 6.9 %collective-permute-start.13 = (f32[64,256]{1,0:T(8,128)S(1)}, f32[64,256]{1,0:T(8,128)S(1)}, u32[]{:S(2)}, u32[]{:S(2)}) collective-permute-start(f32[64,256]{1,0:T(8,128)S(1)} %get-tuple-element.61), channel_id=1, source_target_pairs={{0,6},{2,4},{4,2},{6,0},{8,14},{10,12},{12,10},{14,8},{1,7},{3,5},... | collective-permute-start | bytes 196616 | tf_op jit(solution)/shard_map/ppermute | solution.py:592
  40.3 4.7 %collective-permute-start.14 = (f32[64,256]{1,0:T(8,128)S(1)}, f32[64,256]{1,0:T(8,128)S(1)}, u32[]{:S(2)}, u32[]{:S(2)}) collective-permute-start(f32[64,256]{1,0:T(8,128)S(1)} %get-tuple-element.62), channel_id=1, source_target_pairs={{0,4},{2,6},{4,0},{6,2},{8,12},{10,14},{12,8},{14,10},{1,5},{3,7},... | collective-permute-start | bytes 196616 | tf_op jit(solution)/shard_map/ppermute | solution.py:592
  40.3 4.7 %collective-permute-start.15 = (f32[64,256]{1,0:T(8,128)S(1)}, f32[64,256]{1,0:T(8,128)S(1)}, u32[]{:S(2)}, u32[]{:S(2)}) collective-permute-start(f32[64,256]{1,0:T(8,128)S(1)} %get-tuple-element.63), channel_id=1, source_target_pairs={{0,2},{2,0},{4,6},{6,4},{8,10},{10,8},{12,14},{14,12},{1,3},{3,1},... | collective-permute-start | bytes 196616 | tf_op jit(solution)/shard_map/ppermute | solution.py:592
  44.9 7.3 %collective-permute-start.16 = (f32[4224,128]{1,0:T(8,128)S(1)}, f32[4224,128]{1,0:T(8,128)S(1)}, u32[]{:S(2)}, u32[]{:S(2)}) collective-permute-start(f32[4224,128]{1,0:T(8,128)S(1)} %get-tuple-element.65), channel_id=1, source_target_pairs={{0,1},{1,0},{2,3},{3,2},{4,5},{5,4},{6,7},{7,6},{8,9},{9,8},{10,11... | collective-permute-start | bytes 6488072 | tf_op jit(solution)/shard_map/ppermute | solution.py:587
  45.0 3.6 %copy-start.1 = (bf16[2,768,256]{2,1,0:T(8,128)(2,1)S(1)}, bf16[2,768,256]{2,1,0:T(8,128)(2,1)}, u32[]{:S(2)}) copy-start(bf16[2,768,256]{2,1,0:T(8,128)(2,1)} %constant.25.clone.tables) | copy-start | bytes 2359300
  48.1 4.4 %collective-permute-start.17 = (f32[4224,128]{1,0:T(8,128)S(1)}, f32[4224,128]{1,0:T(8,128)S(1)}, u32[]{:S(2)}, u32[]{:S(2)}) collective-permute-start(f32[4224,128]{1,0:T(8,128)S(1)} %get-tuple-element.66), channel_id=1, source_target_pairs={{0,1},{1,0},{2,3},{3,2},{4,5},{5,4},{6,7},{7,6},{8,9},{9,8},{10,11... | collective-permute-start | bytes 6488072 | tf_op jit(solution)/shard_map/ppermute | solution.py:587
